TPU v7x, 32 devices: a whole 2x2x4 slice. The times are simulated.
32 devices in a mesh: wide: 8 (over y, x, core), narrow: 4 (over z).
Axes of the slice: x: 2, y: 2, z: 4, core: 2. Of those that a mesh axis runs over, the one named last changes fastest.
Arguments:
- tokens: bfloat16 [10240, 2048], P(('wide', 'narrow')), may hold values from -6 to 6
- lengths: int32 [32], P(('wide', 'narrow')), may hold values from 80 to 320, as said below
- cotangent: bfloat16 [10240, 2048], P(('wide', 'narrow')), may hold values from -6 to 6
- norm_gain1: bfloat16 [2048], P(('wide', 'narrow')), may hold values from 0.5 to 1.5
- gate_in: bfloat16 [2048, 2560], P(('wide', 'narrow')), may hold values from -0.125 to 0.125
- x_in: bfloat16 [2048, 2560], P(('wide', 'narrow')), may hold values from -0.125 to 0.125
- conv_kernel: bfloat16 [4, 2560], P(None, ('wide', 'narrow')), may hold values from -3 to 3
- conv_bias: bfloat16 [2560], P(('wide', 'narrow')), may hold values from -3 to 3
- rate_weight: bfloat16 [160, 2560], P(None, ('wide', 'narrow')), may hold values from -0.5 to 0.5
- rate_bias: bfloat16 [2560], P(('wide', 'narrow')), may hold values from -3 to 3
- input_weight: bfloat16 [160, 2560], P(None, ('wide', 'narrow')), may hold values from -0.5 to 0.5
- input_bias: bfloat16 [2560], P(('wide', 'narrow')), may hold values from -3 to 3
- decay_param: bfloat16 [2560], P(('wide', 'narrow')), may hold values from 4.5 to 9.5
- out_proj: bfloat16 [2560, 2048], P(('wide', 'narrow')), may hold values from -0.3125 to 0.3125
- norm_gain2: bfloat16 [2048], P(('wide', 'narrow')), may hold values from 0.5 to 1.5
- mlp_gate: bfloat16 [2048, 6144], P(('wide', 'narrow')), may hold values from -0.125 to 0.125
- mlp_up: bfloat16 [2048, 6144], P(('wide', 'narrow')), may hold values from -0.125 to 0.125
- mlp_down: bfloat16 [6144, 2048], P(('wide', 'narrow')), may hold values from -0.109375 to 0.109375
Outputs:
- block_out: bfloat16 [10240, 2048], P(('wide', 'narrow'))
- input_grad: float32 [10240, 2048], P(('wide', 'narrow'))
- grad_norm_gain1: float32 [2048], P(('wide', 'narrow'))
- grad_gate_in: float32 [2048, 2560], P(('wide', 'narrow'))
- grad_x_in: float32 [2048, 2560], P(('wide', 'narrow'))
- grad_conv_kernel: float32 [4, 2560], P(None, ('wide', 'narrow'))
- grad_conv_bias: float32 [2560], P(('wide', 'narrow'))
- grad_rate_weight: float32 [160, 2560], P(None, ('wide', 'narrow'))
- grad_rate_bias: float32 [2560], P(('wide', 'narrow'))
- grad_input_weight: float32 [160, 2560], P(None, ('wide', 'narrow'))
- grad_input_bias: float32 [2560], P(('wide', 'narrow'))
- grad_decay_param: float32 [2560], P(('wide', 'narrow'))
- grad_out_proj: float32 [2560, 2048], P(('wide', 'narrow'))
- grad_norm_gain2: float32 [2048], P(('wide', 'narrow'))
- grad_mlp_gate: float32 [2048, 6144], P(('wide', 'narrow'))
- grad_mlp_up: float32 [2048, 6144], P(('wide', 'narrow'))
- grad_mlp_down: float32 [6144, 2048], P(('wide', 'narrow'))
Inputs may be any that keep to these rules, and one draw needn't show every extreme that they name: Sequence s has lengths[s] real tokens at the start of its 320 slots, the rest is padding; some sequence fills all its slots.
All inputs are finite; a program needn't handle non-finite values.
Results may differ from a plain program's by a relative error of at most 0.014.
Values may be sent and summed in bfloat16 or wider, within the bound.
A program may use at most 448 MiB of HBM per device.

v0:
```python
import jax
import jax.numpy as jnp
from jax import lax
from jax.sharding import PartitionSpec as P

EPSILON = 1e-06
RATE_SCALE = 8.0


def rms_scale(values, gain):
    inverse = lax.rsqrt(jnp.mean(values * values, axis=-1, keepdims=True) + EPSILON)
    return values * inverse * gain


def gelu_tanh(values):
    return jax.nn.gelu(values, approximate=True)


def conv_causal(inputs, kernel, conv_shift):
    width = kernel.shape[0]
    padded = jnp.pad(inputs, ((width - 1, 0), (0, 0)))
    totals = conv_shift + jnp.zeros_like(inputs)
    for offset in range(width):
        totals = totals + kernel[offset] * padded[offset : offset + inputs.shape[0]]
    return totals


def combine_steps(earlier, later):
    return (earlier[0] * later[0], later[0] * earlier[1] + later[1])


def lru_mix(conv_vals, rate_pre, input_pre, gate_pre, decay_vals):
    rate_gate = jax.nn.sigmoid(rate_pre)
    input_gate = jax.nn.sigmoid(input_pre)
    log_decay = -RATE_SCALE * rate_gate * jax.nn.softplus(-decay_vals)
    decay_now = jnp.exp(log_decay)
    scale_in = jnp.sqrt(-jnp.expm1(2.0 * log_decay))
    driven = scale_in * input_gate * conv_vals
    states = lax.associative_scan(combine_steps, (decay_now, driven), axis=0)[1]
    return states * gelu_tanh(gate_pre)


def gated_product(gate_two, up_two):
    return gelu_tanh(gate_two) * up_two


def block_mix(values, weight):
    head_size = weight.shape[0]
    row_count = values.shape[0]
    by_heads = values.reshape(row_count, -1, head_size)
    head_table = weight.reshape(head_size, -1, head_size)
    mixed_heads = jnp.einsum(
        "thi,ihj->thj", by_heads, head_table, preferred_element_type=jnp.float32
    )
    return mixed_heads.reshape(row_count, -1)


def block_back(values, grads, weight):
    head_size = weight.shape[0]
    row_count = values.shape[0]
    by_heads = values.reshape(row_count, -1, head_size)
    grad_heads = grads.reshape(row_count, -1, head_size)
    head_table = weight.reshape(head_size, -1, head_size)
    weight_grad = jnp.einsum(
        "thi,thj->ihj", by_heads, grad_heads, preferred_element_type=jnp.float32
    )
    value_grad = jnp.einsum(
        "thj,ihj->thi", grad_heads, head_table, preferred_element_type=jnp.float32
    )
    return (value_grad.reshape(row_count, -1), weight_grad.reshape(head_size, -1))


def matmul_low(left, right):
    return jnp.dot(left, right, preferred_element_type=jnp.float32)


def on_device(
    tokens,
    lengths,
    cotangent,
    norm_gain1,
    gate_in,
    x_in,
    conv_kernel,
    conv_bias,
    rate_weight,
    rate_bias,
    input_weight,
    input_bias,
    decay_param,
    out_proj,
    norm_gain2,
    mlp_gate,
    mlp_up,
    mlp_down,
):
    row_count = tokens.shape[0]
    live_mask = (jnp.arange(row_count, dtype=jnp.int32) < lengths[0]).astype(jnp.float32)[:, None]
    rec_parts = (
        lax.all_gather(norm_gain1, ("wide", "narrow"), axis=0, tiled=True),
        lax.all_gather(gate_in, ("wide", "narrow"), axis=0, tiled=True),
        lax.all_gather(x_in, ("wide", "narrow"), axis=0, tiled=True),
        lax.all_gather(conv_kernel, ("wide", "narrow"), axis=1, tiled=True),
        lax.all_gather(conv_bias, ("wide", "narrow"), axis=0, tiled=True),
        lax.all_gather(rate_weight, ("wide", "narrow"), axis=1, tiled=True),
        lax.all_gather(rate_bias, ("wide", "narrow"), axis=0, tiled=True),
        lax.all_gather(input_weight, ("wide", "narrow"), axis=1, tiled=True),
        lax.all_gather(input_bias, ("wide", "narrow"), axis=0, tiled=True),
        lax.all_gather(decay_param, ("wide", "narrow"), axis=0, tiled=True),
        lax.all_gather(out_proj, ("wide", "narrow"), axis=0, tiled=True),
    )
    (
        gain_one,
        w_gate,
        w_branch,
        kernel,
        conv_shift,
        w_rate,
        b_rate,
        w_input,
        b_input,
        decay_vals,
        w_out,
    ) = rec_parts
    inputs = tokens.astype(jnp.float32)
    gain_one_f = gain_one.astype(jnp.float32)
    kernel_f = kernel.astype(jnp.float32)
    shift_f = conv_shift.astype(jnp.float32)
    decay_f = decay_vals.astype(jnp.float32)
    normed1 = rms_scale(inputs, gain_one_f).astype(jnp.bfloat16)
    gate_pre = matmul_low(normed1, w_gate)
    branch_pre = matmul_low(normed1, w_branch)
    conv_vals = conv_causal(branch_pre, kernel_f, shift_f).astype(jnp.bfloat16)
    conv_f = conv_vals.astype(jnp.float32)
    rate_pre = block_mix(conv_vals, w_rate) + b_rate.astype(jnp.float32)
    input_pre = block_mix(conv_vals, w_input) + b_input.astype(jnp.float32)
    mixed = lru_mix(conv_f, rate_pre, input_pre, gate_pre, decay_f).astype(jnp.bfloat16)
    merged = inputs + matmul_low(mixed, w_out)
    mlp_parts = (
        lax.all_gather(norm_gain2, ("wide", "narrow"), axis=0, tiled=True),
        lax.all_gather(mlp_gate, ("wide", "narrow"), axis=0, tiled=True),
        lax.all_gather(mlp_up, ("wide", "narrow"), axis=0, tiled=True),
        lax.all_gather(mlp_down, ("wide", "narrow"), axis=0, tiled=True),
    )
    gain_two, w_mgate, w_mup, w_down = mlp_parts
    gain_two_f = gain_two.astype(jnp.float32)
    normed2 = rms_scale(merged, gain_two_f).astype(jnp.bfloat16)
    gate_two = matmul_low(normed2, w_mgate)
    up_two = matmul_low(normed2, w_mup)
    product = gated_product(gate_two, up_two).astype(jnp.bfloat16)
    result = merged + matmul_low(product, w_down)
    block_out = (result * live_mask).astype(jnp.bfloat16)
    grad_res = cotangent.astype(jnp.float32) * live_mask
    low_res = grad_res.astype(jnp.bfloat16)
    gain_two, w_mgate, w_mup, w_down = (
        lax.all_gather(norm_gain2, ("wide", "narrow"), axis=0, tiled=True),
        lax.all_gather(mlp_gate, ("wide", "narrow"), axis=0, tiled=True),
        lax.all_gather(mlp_up, ("wide", "narrow"), axis=0, tiled=True),
        lax.all_gather(mlp_down, ("wide", "narrow"), axis=0, tiled=True),
    )
    grad_down = matmul_low(product.T, low_res)
    down_out = lax.psum_scatter(grad_down, ("wide", "narrow"), scatter_dimension=0, tiled=True)
    d_product = matmul_low(low_res, w_down.T)
    unused, pullback = jax.vjp(gated_product, gate_two, up_two)
    d_gate_two, d_up_two = pullback(d_product)
    d_gate_two = d_gate_two.astype(jnp.bfloat16)
    d_up_two = d_up_two.astype(jnp.bfloat16)
    grad_mgate = matmul_low(normed2.T, d_gate_two)
    grad_mup = matmul_low(normed2.T, d_up_two)
    d_normed2 = matmul_low(d_gate_two, w_mgate.T) + matmul_low(d_up_two, w_mup.T)
    unused, pullback = jax.vjp(rms_scale, merged, gain_two_f)
    d_merged_norm, grad_gain_two = pullback(d_normed2)
    d_merged = grad_res + d_merged_norm
    mlp_grads = (grad_gain_two, grad_mgate, grad_mup)
    mlp_out = (
        lax.psum_scatter(mlp_grads[0], ("wide", "narrow"), scatter_dimension=0, tiled=True),
        lax.psum_scatter(mlp_grads[1], ("wide", "narrow"), scatter_dimension=0, tiled=True),
        lax.psum_scatter(mlp_grads[2], ("wide", "narrow"), scatter_dimension=0, tiled=True),
    )
    rec_parts = (
        lax.all_gather(norm_gain1, ("wide", "narrow"), axis=0, tiled=True),
        lax.all_gather(gate_in, ("wide", "narrow"), axis=0, tiled=True),
        lax.all_gather(x_in, ("wide", "narrow"), axis=0, tiled=True),
        lax.all_gather(conv_kernel, ("wide", "narrow"), axis=1, tiled=True),
        lax.all_gather(conv_bias, ("wide", "narrow"), axis=0, tiled=True),
        lax.all_gather(rate_weight, ("wide", "narrow"), axis=1, tiled=True),
        lax.all_gather(rate_bias, ("wide", "narrow"), axis=0, tiled=True),
        lax.all_gather(input_weight, ("wide", "narrow"), axis=1, tiled=True),
        lax.all_gather(input_bias, ("wide", "narrow"), axis=0, tiled=True),
        lax.all_gather(decay_param, ("wide", "narrow"), axis=0, tiled=True),
        lax.all_gather(out_proj, ("wide", "narrow"), axis=0, tiled=True),
    )
    (
        gain_one,
        w_gate,
        w_branch,
        kernel,
        conv_shift,
        w_rate,
        b_rate,
        w_input,
        b_input,
        decay_vals,
        w_out,
    ) = rec_parts
    low_merged = d_merged.astype(jnp.bfloat16)
    grad_out = matmul_low(mixed.T, low_merged)
    d_mixed = matmul_low(low_merged, w_out.T)
    unused, pullback = jax.vjp(lru_mix, conv_f, rate_pre, input_pre, gate_pre, decay_f)
    d_conv_lru, d_rate, d_input, d_gate, grad_decay = pullback(d_mixed)
    grad_rate_bias = jnp.sum(d_rate, axis=0)
    grad_input_bias = jnp.sum(d_input, axis=0)
    d_conv_rate, grad_rate_weight = block_back(conv_vals, d_rate.astype(jnp.bfloat16), w_rate)
    d_conv_input, grad_input_weight = block_back(conv_vals, d_input.astype(jnp.bfloat16), w_input)
    d_conv = d_conv_lru + d_conv_rate + d_conv_input
    unused, pullback = jax.vjp(conv_causal, branch_pre, kernel_f, shift_f)
    d_branch, grad_kernel, grad_shift = pullback(d_conv)
    low_gate = d_gate.astype(jnp.bfloat16)
    low_branch = d_branch.astype(jnp.bfloat16)
    grad_gate_in = matmul_low(normed1.T, low_gate)
    grad_x_in = matmul_low(normed1.T, low_branch)
    d_normed1 = matmul_low(low_gate, w_gate.T) + matmul_low(low_branch, w_branch.T)
    unused, pullback = jax.vjp(rms_scale, inputs, gain_one_f)
    d_inputs_norm, grad_gain_one = pullback(d_normed1)
    input_grad = d_merged + d_inputs_norm
    rec_grads = (
        grad_gain_one,
        grad_gate_in,
        grad_x_in,
        grad_kernel,
        grad_shift,
        grad_rate_weight,
        grad_rate_bias,
        grad_input_weight,
        grad_input_bias,
        grad_decay,
        grad_out,
    )
    rec_out = (
        lax.psum_scatter(rec_grads[0], ("wide", "narrow"), scatter_dimension=0, tiled=True),
        lax.psum_scatter(rec_grads[1], ("wide", "narrow"), scatter_dimension=0, tiled=True),
        lax.psum_scatter(rec_grads[2], ("wide", "narrow"), scatter_dimension=0, tiled=True),
        lax.psum_scatter(rec_grads[3], ("wide", "narrow"), scatter_dimension=1, tiled=True),
        lax.psum_scatter(rec_grads[4], ("wide", "narrow"), scatter_dimension=0, tiled=True),
        lax.psum_scatter(rec_grads[5], ("wide", "narrow"), scatter_dimension=1, tiled=True),
        lax.psum_scatter(rec_grads[6], ("wide", "narrow"), scatter_dimension=0, tiled=True),
        lax.psum_scatter(rec_grads[7], ("wide", "narrow"), scatter_dimension=1, tiled=True),
        lax.psum_scatter(rec_grads[8], ("wide", "narrow"), scatter_dimension=0, tiled=True),
        lax.psum_scatter(rec_grads[9], ("wide", "narrow"), scatter_dimension=0, tiled=True),
        lax.psum_scatter(rec_grads[10], ("wide", "narrow"), scatter_dimension=0, tiled=True),
    )
    return (
        block_out,
        input_grad,
        rec_out[0],
        rec_out[1],
        rec_out[2],
        rec_out[3],
        rec_out[4],
        rec_out[5],
        rec_out[6],
        rec_out[7],
        rec_out[8],
        rec_out[9],
        rec_out[10],
        mlp_out[0],
        mlp_out[1],
        mlp_out[2],
        down_out,
    )


def solution(mesh):
    placed = (
        P(("wide", "narrow"), None),
        P(("wide", "narrow")),
        P(("wide", "narrow"), None),
        P(("wide", "narrow")),
        P(("wide", "narrow"), None),
        P(("wide", "narrow"), None),
        P(None, ("wide", "narrow")),
        P(("wide", "narrow")),
        P(None, ("wide", "narrow")),
        P(("wide", "narrow")),
        P(None, ("wide", "narrow")),
        P(("wide", "narrow")),
        P(("wide", "narrow")),
        P(("wide", "narrow"), None),
        P(("wide", "narrow")),
        P(("wide", "narrow"), None),
        P(("wide", "narrow"), None),
        P(("wide", "narrow"), None),
    )
    return jax.shard_map(
        on_device,
        mesh=mesh,
        in_specs=placed,
        out_specs=(
            P(("wide", "narrow"), None),
            P(("wide", "narrow"), None),
            P(("wide", "narrow")),
            P(("wide", "narrow"), None),
            P(("wide", "narrow"), None),
            P(None, ("wide", "narrow")),
            P(("wide", "narrow")),
            P(None, ("wide", "narrow")),
            P(("wide", "narrow")),
            P(None, ("wide", "narrow")),
            P(("wide", "narrow")),
            P(("wide", "narrow")),
            P(("wide", "narrow"), None),
            P(("wide", "narrow")),
            P(("wide", "narrow"), None),
            P(("wide", "narrow"), None),
            P(("wide", "narrow"), None),
        ),
        check_vma=False,
    )
```

profile of v0, /device:TPU:0, one launch (start us, length us, event | category | flops | bytes accessed | tf_op | source)
XLA Modules:
  0.0 4179.4 jit_solution(13397751653147060598)
XLA Ops:
  12.8 42.9 %all-reduce.96 = (bf16[2048]{0:T(1024)(128)(2,1)S(1)}, bf16[2560]{0:T(1024)(128)(2,1)S(1)}, bf16[2560]{0:T(1024)(128)(2,1)S(1)}, bf16[2560]{0:T(1024)(128)(2,1)S...) all-reduce(bf16[2048]{0:T(1024)(128)(2,1)S(1)} %dynamic-update-slic, ...), channel_id=1, replica_groups=mesh['wide'=8,'narrow'=4] {'wide','narrow'}, use_global_device_ids=true, to_apply=%add.84 | all-reduce | flops 14336 | bytes 57344
  55.9 67.0 %all-gather = bf16[32,80,4]{1,2,0:T(4,128)(2,1)S(1)} all-gather(bf16[1,80,4]{1,2,0:T(4,128)(2,1)S(1)} %bitcast.102), channel_id=1, replica_groups=mesh['wide'=8,'narrow'=4] {'wide','narrow'}, dimensions={0}, use_global_device_ids=true | all-gather | bytes 21120 | tf_op jit(solution)/shard_map/all_gather | solution.py:103
  126.7 90.0 %all_gather.57 = bf16[160,2560]{0,1:T(8,128)(2,1)S(1)} all-gather(bf16[160,80]{0,1:T(8,128)(2,1)S(1)} %copy.83), channel_id=1, replica_groups=mesh['wide'=8,'narrow'=4] {'wide','narrow'}, dimensions={1}, use_global_device_ids=true | all-gather | bytes 844800 | tf_op jit(solution)/shard_map/all_gather | solution.py:105
  216.8 98.6 %all_gather.60 = bf16[160,2560]{0,1:T(8,128)(2,1)} all-gather(bf16[160,80]{0,1:T(8,128)(2,1)S(1)} %copy.85), channel_id=1, replica_groups=mesh['wide'=8,'narrow'=4] {'wide','narrow'}, dimensions={1}, use_global_device_ids=true | all-gather | bytes 844800 | tf_op jit(solution)/shard_map/all_gather | solution.py:107
  315.3 6.3 fusion.68
  336.1 5.9 fusion.105
  342.0 5.2 copy.86
  347.3 10.8 multiply_exponential_fusion
  358.1 6.8 slice.337
  368.6 5.4 slice.336
  373.9 6.9 slice.340
  380.9 4.6 fusion.75
  448.8 7.0 slice.335
  476.0 9.8 pad.353
  488.4 5.8 pad.352
  494.1 11.7 multiply_convert_fusion.2
  505.9 7.0 multiply_reduce_fusion.7
  514.8 15.4 fusion.94
  530.2 85.3 %all-gather.16.cloned.1.call-done = bf16[2048,6144]{1,0:T(8,128)(2,1)} async-done(((bf16[64,6144]{1,0:T(8,128)(2,1)}), bf16[2048,6144]{1,0:T(8,128)(2,1)}) %all-gather.16.cloned.1.call-update) | async-done | bytes 25165840 | tf_op jit(solution)/shard_map/all_gather | solution.py:142
  615.5 15.5 fusion.95
  631.0 140.1 %all-gather.18.cloned.1.call-done = bf16[6144,2048]{1,0:T(8,128)(2,1)} async-done(((bf16[192,2048]{1,0:T(8,128)(2,1)}), bf16[6144,2048]{1,0:T(8,128)(2,1)}) %all-gather.18.cloned.1.call-update) | async-done | bytes 25165840 | tf_op jit(solution)/shard_map/all_gather | solution.py:143
  771.1 24.1 multiply_convert_fusion
  795.3 15.4 fusion.96
  810.7 17.7 multiply_reduce_fusion.5
  832.3 9.3 fusion.29
  845.1 6.8 slice.392
  852.0 4.8 fusion.40
  856.8 5.4 slice.393
  941.5 5.6 pad.424
  947.1 5.3 pad.361
  952.4 5.3 pad.406
  957.6 7.6 multiply_add_fusion.1
  966.7 9.9 pad.403
  976.6 5.8 pad.404
  982.4 5.8 pad.356
  988.2 5.9 pad.425
  994.0 5.8 pad.426
  999.9 10.4 pad.405
  1010.4 13.8 fusion.70
  1024.3 11.9 multiply_reduce_fusion
  1044.2 4.8 fusion.98
  1049.0 5.3 copy.89
  1058.1 4.9 fusion.99
  1063.0 5.3 copy.92
  1068.3 13.8 multiply_reduce_fusion.4
  1098.2 10.2 fusion.62
  1109.8 11.9 fusion.32
  1123.2 10.2 fusion.64
  1134.7 22.1 fusion.102
  1156.9 22.0 fusion.103
  1180.3 22.2 fusion.36
  1204.0 6.4 fusion.97
  1210.5 9.4 fusion.23
  1219.9 40.2 all-reduce.95
  1263.6 4.9 fusion.25
  1268.5 14.2 fusion.21
  1284.2 74.4 %reduce-scatter.30.cloned.1.call-done = f32[80,160]{1,0:T(8,128)} async-done(((f32[2560,160]{1,0:T(8,128)}), f32[80,160]{1,0:T(8,128)}) %reduce-scatter.30.cloned.1.call-update) | async-done | bytes 51216
  1360.2 139.3 %reduce-scatter.32.cloned.1.call-done = f32[80,160]{1,0:T(8,128)} async-done(((f32[2560,160]{1,0:T(8,128)}), f32[80,160]{1,0:T(8,128)}) %reduce-scatter.32.cloned.1.call-update) | async-done | bytes 51216
  1501.1 450.6 %reduce-scatter.18.cloned.1.call-done = f32[64,2560]{1,0:T(8,128)} async-done(((f32[2048,2560]{1,0:T(8,128)}), f32[64,2560]{1,0:T(8,128)}) %reduce-scatter.18.cloned.1.call-update) | async-done | bytes 655376 | tf_op jit(solution)/shard_map/reduce_scatter | solution.py:242
  1951.7 452.5 %reduce-scatter.20.cloned.1.call-done = f32[80,2048]{1,0:T(8,128)} async-done(((f32[2560,2048]{1,0:T(8,128)}), f32[80,2048]{1,0:T(8,128)}) %reduce-scatter.20.cloned.1.call-update) | async-done | bytes 655376 | tf_op jit(solution)/shard_map/reduce_scatter | solution.py:250
  2404.2 452.3 %reduce-scatter.16.cloned.1.call-done = f32[64,2560]{1,0:T(8,128)} async-done(((f32[2048,2560]{1,0:T(8,128)}), f32[64,2560]{1,0:T(8,128)}) %reduce-scatter.16.cloned.1.call-update) | async-done | bytes 655376 | tf_op jit(solution)/shard_map/reduce_scatter | solution.py:241
  2856.5 438.6 %reduce-scatter.22.cloned.1.call-done = f32[64,6144]{1,0:T(8,128)} async-done(((f32[2048,6144]{1,0:T(8,128)}), f32[64,6144]{1,0:T(8,128)}) %reduce-scatter.22.cloned.1.call-update) | async-done | bytes 1572880 | tf_op jit(solution)/shard_map/reduce_scatter | solution.py:177
  3295.1 438.7 %reduce-scatter.24.cloned.1.call-done = f32[64,6144]{1,0:T(8,128)} async-done(((f32[2048,6144]{1,0:T(8,128)}), f32[64,6144]{1,0:T(8,128)}) %reduce-scatter.24.cloned.1.call-update) | async-done | bytes 1572880 | tf_op jit(solution)/shard_map/reduce_scatter | solution.py:178
  3733.8 438.6 %reduce-scatter.26.cloned.1.call-done = f32[192,2048]{1,0:T(8,128)} async-done(((f32[6144,2048]{1,0:T(8,128)}), f32[192,2048]{1,0:T(8,128)}) %reduce-scatter.26.cloned.1.call-update) | async-done | bytes 1572880 | tf_op jit(solution)/shard_map/reduce_scatter | solution.py:162
  (602 shorter events, 244.2 us)
Async XLA Ops:
  7.3 48.6 %copy-start.158 = (bf16[4,80]{1,0:T(4,128)(2,1)S(1)}, bf16[4,80]{1,0:T(4,128)(2,1)}, u32[]{:S(2)}) copy-start(bf16[4,80]{1,0:T(4,128)(2,1)} %param.24) | copy-start | bytes 1924
  7.3 115.7 %copy-start.145 = (bf16[160,80]{1,0:T(8,128)(2,1)S(1)}, bf16[160,80]{1,0:T(8,128)(2,1)}, u32[]{:S(2)}) copy-start(bf16[160,80]{1,0:T(8,128)(2,1)} %param.26) | copy-start | bytes 76804
  7.3 115.8 %copy-start.146 = (bf16[160,80]{1,0:T(8,128)(2,1)S(1)}, bf16[160,80]{1,0:T(8,128)(2,1)}, u32[]{:S(2)}) copy-start(bf16[160,80]{1,0:T(8,128)(2,1)} %param.28) | copy-start | bytes 76804
  7.3 117.9 %copy-start.14 = (bf16[320,2048]{1,0:T(8,128)(2,1)S(1)}, bf16[320,2048]{1,0:T(8,128)(2,1)}, u32[]{:S(2)}) copy-start(bf16[320,2048]{1,0:T(8,128)(2,1)} %param.18) | copy-start | bytes 3932164
  7.3 308.0 %all-gather.8.cloned.1.call-start = ((), (), s32[]{:S(2)}) async-start(), calls=%async_computation.9 | async-start | bytes 10813440 | tf_op jit(solution)/shard_map/all_gather | solution.py:102
  8.0 486.1 %all-gather.10.cloned.1.call-start = ((), (), s32[]{:S(2)}) async-start(), calls=%async_computation.10 | async-start | bytes 10813440 | tf_op jit(solution)/shard_map/all_gather | solution.py:101
  8.8 497.1 %all-gather.12.cloned.1.call-start = ((), (), s32[]{:S(2)}) async-start(), calls=%async_computation.11 | async-start | bytes 10813440 | tf_op jit(solution)/shard_map/all_gather | solution.py:110
  9.5 505.2 %all-gather.14.cloned.1.call-start = ((), (), s32[]{:S(2)}) async-start(), calls=%async_computation.12 | async-start | bytes 25952256 | tf_op jit(solution)/shard_map/all_gather | solution.py:141
  10.1 605.4 %all-gather.16.cloned.1.call-start = ((), (), s32[]{:S(2)}) async-start(), calls=%async_computation.13 | async-start | bytes 25952256 | tf_op jit(solution)/shard_map/all_gather | solution.py:142
  10.7 760.4 %all-gather.18.cloned.1.call-start = ((), (), s32[]{:S(2)}) async-start(), calls=%async_computation.14 | async-start | bytes 25952256 | tf_op jit(solution)/shard_map/all_gather | solution.py:143
  11.3 1271.5 %reduce-scatter.28.cloned.1.call-start = ((), (), s32[]{:S(2)}) async-start(), calls=%async_computation.21 | async-start | bytes 1351680
  55.8 265.9 %copy-start.151 = (bf16[2560]{0:T(1024)(128)(2,1)}, bf16[2560]{0:T(1024)(128)(2,1)S(1)}, u32[]{:S(2)}) copy-start(bf16[2560]{0:T(1024)(128)(2,1)S(1)} %get-tuple-element.40) | copy-start | bytes 15364
  55.8 438.3 %copy-start.106 = (f32[2048]{0:T(1024)}, f32[2048]{0:T(1024)S(1)}, u32[]{:S(2)}) copy-start(f32[2048]{0:T(1024)S(1)} %convert_element_type.84) | copy-start | bytes 24580
  55.8 291.4 %copy-start.125 = (f32[2560]{0:T(1024)}, f32[2560]{0:T(1024)S(1)}, u32[]{:S(2)}) copy-start(f32[2560]{0:T(1024)S(1)} %convert_element_type.82) | copy-start | bytes 30724
  123.2 224.0 %copy-start.108 = (f32[2560]{0:T(1024)}, f32[2560]{0:T(1024)S(1)}, u32[]{:S(2)}) copy-start(f32[2560]{0:T(1024)S(1)} %convert_element_type.87) | copy-start | bytes 30724
  123.2 224.0 %copy-start.121 = (f32[2560]{0:T(1024)}, f32[2560]{0:T(1024)S(1)}, u32[]{:S(2)}) copy-start(f32[2560]{0:T(1024)S(1)} %convert_element_type.89) | copy-start | bytes 30724
  125.2 222.1 %copy-start.110 = (f32[2560]{0:T(1024)}, f32[2560]{0:T(1024)S(1)}, u32[]{:S(2)}) copy-start(f32[2560]{0:T(1024)S(1)} %get-tuple-element.28) | copy-start | bytes 30724
  125.2 222.1 %copy-start.112 = (f32[2560]{0:T(1024)}, f32[2560]{0:T(1024)S(1)}, u32[]{:S(2)}) copy-start(f32[2560]{0:T(1024)S(1)} %get-tuple-element.29) | copy-start | bytes 30724
  125.2 222.1 %copy-start.114 = (f32[2560]{0:T(1024)}, f32[2560]{0:T(1024)S(1)}, u32[]{:S(2)}) copy-start(f32[2560]{0:T(1024)S(1)} %get-tuple-element.30) | copy-start | bytes 30724
  125.2 222.1 %copy-start.116 = (f32[2560]{0:T(1024)}, f32[2560]{0:T(1024)S(1)}, u32[]{:S(2)}) copy-start(f32[2560]{0:T(1024)S(1)} %get-tuple-element.31) | copy-start | bytes 30724
  126.1 368.0 %copy-start.130 = (f32[320]{0:T(512)}, f32[320]{0:T(512)S(1)}, u32[]{:S(2)}) copy-start(f32[320]{0:T(512)S(1)} %fusion.53) | copy-start | bytes 3844
  126.7 220.6 %copy-start.123 = (f32[2560]{0:T(1024)}, f32[2560]{0:T(1024)S(1)}, u32[]{:S(2)}) copy-start(f32[2560]{0:T(1024)S(1)} %get-tuple-element.137) | copy-start | bytes 30724
  216.8 113.0 %copy-start.32 = (bf16[160,2560]{0,1:T(8,128)(2,1)}, bf16[160,2560]{0,1:T(8,128)(2,1)S(1)}, u32[]{:S(2)}) copy-start(bf16[160,2560]{0,1:T(8,128)(2,1)S(1)} %all_gather.57) | copy-start | bytes 2457604
  404.4 29.6 copy-start.62
  408.1 22.7 copy-start.85
  408.2 30.2 copy-start.90
  409.9 28.5 copy-start.75
  411.0 27.5 copy-start.92
  414.9 23.5 copy-start.95
  422.1 39.2 copy-start.119
  434.0 32.7 copy-start.81
  439.0 16.8 copy-start.19
  471.8 13.9 copy-start.10
  514.7 100.8 %copy-start.20 = (bf16[320,2048]{1,0:T(8,128)(2,1)}, bf16[320,2048]{1,0:T(8,128)(2,1)S(1)}, u32[]{:S(2)}) copy-start(bf16[320,2048]{1,0:T(8,128)(2,1)S(1)} %multiply_convert_fusion.3) | copy-start | bytes 3932164
  530.2 240.9 %copy-start.54 = (bf16[320,2048]{1,0:T(8,128)(2,1)S(1)}, bf16[320,2048]{1,0:T(8,128)(2,1)}, u32[]{:S(2)}) copy-start(bf16[320,2048]{1,0:T(8,128)(2,1)} %param.20) | copy-start | bytes 3932164
  530.2 240.9 %copy-start.153 = (f32[320]{0:T(512)S(1)}, f32[320]{0:T(512)}, u32[]{:S(2)}) copy-start(f32[320]{0:T(512)} %fusion.52) | copy-start | bytes 3844
  795.3 15.4 copy-start.34
  810.7 17.8 copy-start.55
  829.3 12.4 copy-start.17
  877.8 34.9 copy-start.86
  880.6 16.1 copy-start.97
  894.3 13.1 copy-start.47
  894.3 13.1 copy-start.65
  894.3 13.1 copy-start.67
  912.7 14.7 copy-start.26
  912.7 14.7 copy-start.38
  912.7 14.7 copy-start.39
  912.8 14.7 slice-start.2
  941.5 16.1 copy-start.9
  941.5 16.1 copy-start.23
  941.5 16.1 slice-start.1
  1010.4 13.9 copy-start.2
  1010.4 13.9 copy-start.4
  1010.4 13.8 copy-start.27
  1010.4 13.8 copy-start.134
  1083.8 274.7 %reduce-scatter.30.cloned.1.call-start = ((), (), s32[]{:S(2)}) async-start(), calls=%async_computation.22 | async-start | bytes 2703360
  1087.7 411.8 %reduce-scatter.32.cloned.1.call-start = ((), (), s32[]{:S(2)}) async-start(), calls=%async_computation.23 | async-start | bytes 2703360
  1091.7 860.0 %reduce-scatter.18.cloned.1.call-start = ((), (), s32[]{:S(2)}) async-start(), calls=%async_computation.16 | async-start | bytes 21626880 | tf_op jit(solution)/shard_map/reduce_scatter | solution.py:242
  1108.4 1295.7 %reduce-scatter.20.cloned.1.call-start = ((), (), s32[]{:S(2)}) async-start(), calls=%async_computation.17 | async-start | bytes 21626880 | tf_op jit(solution)/shard_map/reduce_scatter | solution.py:250
  1121.8 1734.7 %reduce-scatter.16.cloned.1.call-start = ((), (), s32[]{:S(2)}) async-start(), calls=%async_computation.15 | async-start | bytes 21626880 | tf_op jit(solution)/shard_map/reduce_scatter | solution.py:241
  1133.4 2161.7 %reduce-scatter.22.cloned.1.call-start = ((), (), s32[]{:S(2)}) async-start(), calls=%async_computation.18 | async-start | bytes 51904512 | tf_op jit(solution)/shard_map/reduce_scatter | solution.py:177
  1156.9 2576.9 %reduce-scatter.24.cloned.1.call-start = ((), (), s32[]{:S(2)}) async-start(), calls=%async_computation.19 | async-start | bytes 51904512 | tf_op jit(solution)/shard_map/reduce_scatter | solution.py:178
  1179.0 2993.4 %reduce-scatter.26.cloned.1.call-start = ((), (), s32[]{:S(2)}) async-start(), calls=%async_computation.20 | async-start | bytes 51904512 | tf_op jit(solution)/shard_map/reduce_scatter | solution.py:162
  1210.5 53.1 %copy-start.156 = (f32[320]{0:T(512)S(1)}, f32[320]{0:T(512)}, u32[]{:S(2)}) copy-start(f32[320]{0:T(512)} %copy-done.155) | copy-start | bytes 3844
  (123 other events, 589.3 us)
Sparse Core Ops, SparseCore 0:
  11.0 90.0 all-gather.7
  103.8 97.2 all-gather.9
  203.9 97.7 all-gather.11
  304.5 155.3 all-gather.13
  462.6 152.8 all-gather.15
  618.2 152.8 all-gather.17
  1083.9 134.2 reduce-scatter.27
  1220.6 137.9 reduce-scatter.29
  1360.9 138.5 reduce-scatter.31
  1502.3 449.3 reduce-scatter.17
  1954.7 449.4 reduce-scatter.19
  2407.0 449.4 reduce-scatter.15
  2864.6 430.4 reduce-scatter.21
  3303.1 430.6 reduce-scatter.23
  3741.8 430.5 reduce-scatter.25
where the time goes:
time: 4190 us; the launch traced here: 4180 us
  waiting for transfers between devices  3110 us (74%)
  blocking collectives  339 us (8%)
  local copies, waits for them, and re-layouts  303 us (7%)
  matrix products  277 us (7%)
  other arithmetic  127 us (3%)
    reduce_scatter x1, waiting for transfers between devices, on_device(): lax.psum_scatter(rec_grads[10], ('wide', 'narrow'), scatter_dimension=0,...  452 us
    reduce_scatter x1, waiting for transfers between devices, on_device(): lax.psum_scatter(rec_grads[1], ('wide', 'narrow'), scatter_dimension=0, t...  452 us
    reduce_scatter x1, waiting for transfers between devices, on_device(): lax.psum_scatter(rec_grads[2], ('wide', 'narrow'), scatter_dimension=0, t...  451 us
    reduce_scatter x1, waiting for transfers between devices, on_device(): lax.psum_scatter(mlp_grads[2], ('wide', 'narrow'), scatter_dimension=0, t...  439 us
    reduce_scatter x1, waiting for transfers between devices, on_device(): lax.psum_scatter(mlp_grads[1], ('wide', 'narrow'), scatter_dimension=0, t...  439 us
    reduce_scatter x1, waiting for transfers between devices, on_device(): lax.psum_scatter(grad_down, ('wide', 'narrow'), scatter_dimension=0, tile...  439 us
    dot_general x18, matrix products, matmul_low(): return jnp.dot(left, right, preferred_element_type=jnp.float32)  251 us
    unnamed x18, waiting for transfers between devices  218 us
  transfers between devices with their start and end apart: 15, of which 10 were waited for; matrix products, arithmetic and copies ran while one was open for 9% of the time, Pallas kernels for 0%

commit v1 on v0

v1 whole, which is shorter than its diff:
```python
import functools
import math

import jax
import jax.numpy as jnp
from jax import lax
from jax.experimental import pallas as pl
from jax.experimental.pallas import tpu as pltpu
from jax.sharding import Mesh
from jax.sharding import PartitionSpec as P

EPSILON = 1e-06
RATE_SCALE = 8.0
GELU_ROOT = 0.7978845608028654
GELU_CUBE = 0.044715
LANES = 128
HEADS = 16


def matmul_low(left, right):
    return jnp.dot(left, right, preferred_element_type=jnp.float32)


def matmul_nt(left, right):
    return lax.dot_general(left, right, (((1,), (1,)), ((), ())), preferred_element_type=jnp.float32)


def matmul_tn(left, right):
    return lax.dot_general(left, right, (((0,), (0,)), ((), ())), preferred_element_type=jnp.float32)


def rms_inverse(values):
    return lax.rsqrt(jnp.mean(values * values, axis=-1, keepdims=True) + EPSILON)


def rms_back(values, inverse, gain, grads):
    scaled = grads * gain
    dots = jnp.mean(scaled * values, axis=-1, keepdims=True)
    return inverse * scaled - values * (inverse * inverse * inverse * dots)


def gelu_pair(values):
    square = values * values
    slope = jnp.tanh(GELU_ROOT * values * (1.0 + GELU_CUBE * square))
    half = 0.5 * (1.0 + slope)
    grad = half + 0.5 * values * (1.0 - slope * slope) * (GELU_ROOT * (1.0 + 3.0 * GELU_CUBE * square))
    return values * half, grad


def minus_expm1(values):
    series = 1.0 + values * (1.0 / 6.0) * (1.0 + values * (1.0 / 7.0))
    for order in (5.0, 4.0, 3.0, 2.0):
        series = 1.0 + values * (1.0 / order) * series
    return jnp.where(values > -0.25, -values * series, 1.0 - jnp.exp(values))


def softplus_minus(values):
    return jnp.maximum(-values, 0.0) + jnp.log(1.0 + jnp.exp(-jnp.abs(values)))


def lru_terms(conv, rate_pre, input_pre, soft):
    rate_gate = 1.0 / (1.0 + jnp.exp(-rate_pre))
    input_gate = 1.0 / (1.0 + jnp.exp(-input_pre))
    log_decay = -RATE_SCALE * rate_gate * soft
    decay_now = jnp.exp(log_decay)
    scale_in = jnp.sqrt(minus_expm1(2.0 * log_decay))
    return rate_gate, input_gate, decay_now, scale_in


CHUNK = 64
UNROLL = 8


def lru_forward_kernel(seqs, conv_ref, rate_ref, input_ref, gate_ref, soft_ref, states_ref, mixed_ref, decay_s, drive_s):
    rows = conv_ref.shape[0]
    length = rows // seqs
    soft = soft_ref[0:1, :]

    def prepare(i, carry):
        at = pl.ds(pl.multiple_of(i * CHUNK, CHUNK), CHUNK)
        conv = conv_ref[at, :].astype(jnp.float32)
        _, input_gate, decay_now, scale_in = lru_terms(conv, rate_ref[at, :], input_ref[at, :], soft)
        decay_s[at, :] = decay_now
        drive_s[at, :] = scale_in * input_gate * conv
        return carry

    lax.fori_loop(0, rows // CHUNK, prepare, 0)

    def advance(i, state):
        for j in range(UNROLL):
            at = pl.ds(i * UNROLL + j, seqs, stride=length)
            state = decay_s[at, :] * state + drive_s[at, :]
            states_ref[at, :] = state
        return state

    lax.fori_loop(0, length // UNROLL, advance, jnp.zeros((seqs, LANES), jnp.float32))

    def finish(i, carry):
        at = pl.ds(pl.multiple_of(i * CHUNK, CHUNK), CHUNK)
        value, _ = gelu_pair(gate_ref[at, :])
        mixed_ref[at, :] = (states_ref[at, :] * value).astype(jnp.bfloat16)
        return carry

    lax.fori_loop(0, rows // CHUNK, finish, 0)


def lru_backward_kernel(
    seqs,
    conv_ref,
    rate_ref,
    input_ref,
    gate_ref,
    soft_ref,
    states_ref,
    grad_ref,
    d_conv_ref,
    d_rate_ref,
    d_input_ref,
    d_gate_ref,
    sums_ref,
    decay_s,
    flow_s,
    before_s,
):
    rows = conv_ref.shape[0]
    length = rows // seqs
    soft = soft_ref[0:1, :]

    def prepare(i, carry):
        at = pl.ds(pl.multiple_of(i * CHUNK, CHUNK), CHUNK)
        value, slope = gelu_pair(gate_ref[at, :])
        grad = grad_ref[at, :]
        d_gate_ref[at, :] = (grad * states_ref[at, :] * slope).astype(jnp.bfloat16)
        flow_s[at, :] = grad * value
        rate_gate = 1.0 / (1.0 + jnp.exp(-rate_ref[at, :]))
        decay_s[at, :] = jnp.exp(-RATE_SCALE * rate_gate * soft)
        return carry

    lax.fori_loop(0, rows // CHUNK, prepare, 0)

    def retreat(i, carry):
        flow, decay = carry
        for j in range(UNROLL):
            step = length - 1 - (i * UNROLL + j)
            at = pl.ds(step, seqs, stride=length)
            flow = flow_s[at, :] + decay * flow
            flow_s[at, :] = flow
            decay = decay_s[at, :]
        return flow, decay

    nothing = jnp.zeros((seqs, LANES), jnp.float32)
    lax.fori_loop(0, length // UNROLL, retreat, (nothing, nothing))

    def shift(i, last):
        for j in range(UNROLL):
            at = pl.ds(i * UNROLL + j, seqs, stride=length)
            before_s[at, :] = last
            last = states_ref[at, :]
        return last

    lax.fori_loop(0, length // UNROLL, shift, nothing)

    def finish(i, carry):
        rate_sum, input_sum, soft_sum = carry
        at = pl.ds(pl.multiple_of(i * CHUNK, CHUNK), CHUNK)
        conv = conv_ref[at, :].astype(jnp.float32)
        rate_gate, input_gate, decay_now, scale_in = lru_terms(conv, rate_ref[at, :], input_ref[at, :], soft)
        flow = flow_s[at, :]
        d_scale = flow * input_gate * conv
        d_log = decay_now * (flow * before_s[at, :] - d_scale * decay_now / scale_in)
        d_input = flow * scale_in * conv * input_gate * (1.0 - input_gate)
        d_rate = d_log * (-RATE_SCALE) * soft * rate_gate * (1.0 - rate_gate)
        d_conv_ref[at, :] = flow * scale_in * input_gate
        d_rate_ref[at, :] = d_rate.astype(jnp.bfloat16)
        d_input_ref[at, :] = d_input.astype(jnp.bfloat16)

        def fold(total, part):
            for k in range(CHUNK // 8):
                total = total + part[k * 8 : (k + 1) * 8, :]
            return total

        return (fold(rate_sum, d_rate), fold(input_sum, d_input), fold(soft_sum, d_log * (-RATE_SCALE) * rate_gate))

    blank = jnp.zeros((8, LANES), jnp.float32)
    rate_sum, input_sum, soft_sum = lax.fori_loop(0, rows // CHUNK, finish, (blank, blank, blank))
    sums_ref[0:8, :] = rate_sum
    sums_ref[8:16, :] = input_sum
    sums_ref[16:24, :] = soft_sum


def lru_forward(seqs, conv, rate_pre, input_pre, gate_pre, soft):
    rows, channels = conv.shape
    block = pl.BlockSpec((rows, LANES), lambda i: (0, i))
    return pl.pallas_call(
        functools.partial(lru_forward_kernel, seqs),
        grid=(pl.cdiv(channels, LANES),),
        out_shape=(
            jax.ShapeDtypeStruct((rows, channels), jnp.float32),
            jax.ShapeDtypeStruct((rows, channels), jnp.bfloat16),
        ),
        in_specs=[block, block, block, block, pl.BlockSpec((8, LANES), lambda i: (0, i))],
        out_specs=(block, block),
        scratch_shapes=[pltpu.VMEM((rows, LANES), jnp.float32)] * 2,
        compiler_params=pltpu.CompilerParams(vmem_limit_bytes=48 * 2**20),
        name="lru_forward",
    )(conv, rate_pre, input_pre, gate_pre, soft)


def lru_backward(seqs, conv, rate_pre, input_pre, gate_pre, soft, states, grads):
    rows, channels = conv.shape
    block = pl.BlockSpec((rows, LANES), lambda i: (0, i))
    return pl.pallas_call(
        functools.partial(lru_backward_kernel, seqs),
        grid=(pl.cdiv(channels, LANES),),
        out_shape=(
            jax.ShapeDtypeStruct((rows, channels), jnp.float32),
            jax.ShapeDtypeStruct((rows, channels), jnp.bfloat16),
            jax.ShapeDtypeStruct((rows, channels), jnp.bfloat16),
            jax.ShapeDtypeStruct((rows, channels), jnp.bfloat16),
            jax.ShapeDtypeStruct((24, channels), jnp.float32),
        ),
        in_specs=[block, block, block, block, pl.BlockSpec((8, LANES), lambda i: (0, i)), block, block],
        out_specs=(block, block, block, block, pl.BlockSpec((24, LANES), lambda i: (0, i))),
        scratch_shapes=[pltpu.VMEM((rows, LANES), jnp.float32)] * 3,
        compiler_params=pltpu.CompilerParams(vmem_limit_bytes=48 * 2**20),
        name="lru_backward",
    )(conv, rate_pre, input_pre, gate_pre, soft, states, grads)


def block_diagonal(table):
    size, channels = table.shape
    tall = jnp.concatenate([table] * (channels // size), axis=0)
    row_head = lax.broadcasted_iota(jnp.int32, tall.shape, 0) // size
    column_head = lax.broadcasted_iota(jnp.int32, tall.shape, 1) // size
    return jnp.where(row_head == column_head, tall, jnp.zeros_like(tall))


def diagonal_blocks(square, size):
    channels = square.shape[0]
    cube = square.reshape(channels // size, size, channels)
    row_head = lax.broadcasted_iota(jnp.int32, cube.shape, 0)
    column_head = lax.broadcasted_iota(jnp.int32, cube.shape, 2) // size
    return jnp.sum(jnp.where(row_head == column_head, cube, jnp.zeros_like(cube)), axis=0)


def shift_rows(values, seqs, by):
    rows, channels = values.shape
    length = rows // seqs
    cube = values.reshape(seqs, length, channels)
    if by > 0:
        cube = jnp.pad(cube, ((0, 0), (by, 0), (0, 0)))[:, :length]
    elif by < 0:
        cube = jnp.pad(cube, ((0, 0), (0, -by), (0, 0)))[:, -by:]
    return cube.reshape(rows, channels)


def make_block(tp, dp, tp_size, dp_size):
    every = (tp,) + dp

    def gather_rows(values):
        return lax.all_gather(values, tp, axis=0, tiled=True)

    def scatter_rows(values):
        return lax.psum_scatter(values, tp, scatter_dimension=0, tiled=True)

    def columns_out(shard):
        rows, columns = shard.shape
        cut = shard.reshape(rows, tp_size, columns // tp_size)
        return lax.all_to_all(cut, tp, 1, 0, tiled=False)

    def gather_weight(part):
        whole = lax.all_gather(part.reshape(-1, part.shape[-1]), dp, axis=0, tiled=True)
        whole = whole.reshape((dp_size,) + part.shape)
        return whole.swapaxes(0, 1).reshape(-1, part.shape[-1])

    def scatter_weight(grad, rows):
        columns = grad.shape[-1]
        cut = grad.reshape(tp_size, dp_size, rows, columns).swapaxes(0, 1).reshape(-1, columns)
        mine = lax.psum_scatter(cut, dp, scatter_dimension=0, tiled=True)
        return lax.all_to_all(mine.reshape(tp_size, rows, columns), tp, 0, 1, tiled=False)

    def on_device(
        tokens,
        lengths,
        cotangent,
        norm_gain1,
        gate_in,
        x_in,
        conv_kernel,
        conv_bias,
        rate_weight,
        rate_bias,
        input_weight,
        input_bias,
        decay_param,
        out_proj,
        norm_gain2,
        mlp_gate,
        mlp_up,
        mlp_down,
    ):
        bf16, f32 = jnp.bfloat16, jnp.float32
        row_count, width = tokens.shape
        head = rate_weight.shape[0]
        shard_rows = gate_in.shape[0]
        taps = conv_kernel.shape[0]
        seqs = tp_size
        live = (jnp.arange(row_count, dtype=jnp.int32) < lengths[0]).astype(f32)[:, None]

        low_res = (cotangent.astype(f32) * live).astype(bf16)
        tokens_all = gather_rows(tokens)
        low_res_all = gather_rows(low_res)

        gains = lax.all_gather(jnp.stack([norm_gain1, norm_gain2]), every, axis=1, tiled=True).astype(f32)
        gain_one, gain_two = gains[0:1], gains[1:2]

        w_gate = gather_weight(columns_out(gate_in))
        w_branch = gather_weight(columns_out(x_in))
        table = jnp.concatenate(
            [
                conv_kernel,
                conv_bias[None],
                rate_weight,
                rate_bias[None],
                input_weight,
                input_bias[None],
                decay_param[None],
            ],
            axis=0,
        )
        table = lax.all_gather(table.T, dp, axis=0, tiled=True).T
        w_out = lax.all_gather(out_proj, dp, axis=0, tiled=True)
        w_mgate = gather_weight(columns_out(mlp_gate))
        w_mup = gather_weight(columns_out(mlp_up))
        w_down = lax.all_gather(mlp_down, dp, axis=0, tiled=True)

        cuts = [taps, 1, head, 1, head, 1, 1]
        places = [sum(cuts[:i]) for i in range(len(cuts) + 1)]
        kernel, shift, rate_table, b_rate, input_table, b_input, decay = (
            table[places[i] : places[i + 1]] for i in range(len(cuts))
        )
        kernel_f, shift_f, b_rate, b_input, decay_f = (v.astype(f32) for v in (kernel, shift, b_rate, b_input, decay))
        w_rate = block_diagonal(rate_table)
        w_input = block_diagonal(input_table)
        soft = softplus_minus(decay_f)
        soft_rows = jnp.broadcast_to(soft, (8, soft.shape[1]))

        tokens_f = tokens_all.astype(f32)
        normed1 = (tokens_f * rms_inverse(tokens_f) * gain_one).astype(bf16)
        gate_pre = matmul_low(normed1, w_gate)
        branch_pre = matmul_low(normed1, w_branch)
        conv = shift_f
        for tap in range(taps):
            conv = conv + kernel_f[tap] * shift_rows(branch_pre, seqs, taps - 1 - tap)
        conv = conv.astype(bf16)
        rate_pre = matmul_low(conv, w_rate) + b_rate
        input_pre = matmul_low(conv, w_input) + b_input
        states, mixed = lru_forward(seqs, conv, rate_pre, input_pre, gate_pre, soft_rows)
        merged = tokens.astype(f32) + scatter_rows(matmul_low(mixed, w_out).astype(bf16)).astype(f32)

        inverse2 = rms_inverse(merged)
        normed2 = (merged * inverse2 * gain_two).astype(bf16)
        normed2_all = gather_rows(normed2)
        gate_two = matmul_low(normed2_all, w_mgate)
        up_two = matmul_low(normed2_all, w_mup)
        value, slope = gelu_pair(gate_two)
        product = (value * up_two).astype(bf16)
        result = merged + scatter_rows(matmul_low(product, w_down).astype(bf16)).astype(f32)
        block_out = (result * live).astype(bf16)

        grad_down = matmul_tn(product, low_res_all).astype(bf16)
        down_out = lax.psum_scatter(grad_down, dp, scatter_dimension=0, tiled=True).astype(f32)
        d_product = matmul_nt(low_res_all, w_down)
        d_gate_two = (d_product * up_two * slope).astype(bf16)
        d_up_two = (d_product * value).astype(bf16)
        mgate_out = scatter_weight(matmul_tn(normed2_all, d_gate_two).astype(bf16), shard_rows)
        mup_out = scatter_weight(matmul_tn(normed2_all, d_up_two).astype(bf16), shard_rows)
        d_normed2 = scatter_rows((matmul_nt(d_gate_two, w_mgate) + matmul_nt(d_up_two, w_mup)).astype(bf16)).astype(f32)
        grad_gain2 = jnp.sum(d_normed2 * merged * inverse2, axis=0)
        d_merged = low_res.astype(f32) + rms_back(merged, inverse2, gain_two, d_normed2)

        low_merged_all = gather_rows(d_merged.astype(bf16))
        grad_out = matmul_tn(mixed, low_merged_all).astype(bf16)
        out_out = lax.psum_scatter(grad_out, dp, scatter_dimension=0, tiled=True).astype(f32)
        d_mixed = matmul_nt(low_merged_all, w_out)
        d_conv_lru, d_rate, d_input, d_gate, sums = lru_backward(
            seqs, conv, rate_pre, input_pre, gate_pre, soft_rows, states, d_mixed
        )
        sums = sums.reshape(3, 8, -1).sum(axis=1)
        grad_decay = sums[2] * (-1.0 / (1.0 + jnp.exp(decay_f[0])))
        d_conv = d_conv_lru + matmul_nt(d_rate, w_rate) + matmul_nt(d_input, w_input)
        grad_rate_weight = diagonal_blocks(matmul_tn(conv, d_rate), head)
        grad_input_weight = diagonal_blocks(matmul_tn(conv, d_input), head)
        d_branch = jnp.zeros_like(d_conv)
        grad_taps = []
        for tap in range(taps):
            moved = shift_rows(d_conv, seqs, tap - (taps - 1))
            d_branch = d_branch + kernel_f[tap] * moved
            grad_taps.append(jnp.sum(branch_pre * moved, axis=0))
        d_branch = d_branch.astype(bf16)
        gate_out = scatter_weight(matmul_tn(normed1, d_gate).astype(bf16), shard_rows)
        branch_out = scatter_weight(matmul_tn(normed1, d_branch).astype(bf16), shard_rows)
        d_normed1 = scatter_rows((matmul_nt(d_gate, w_gate) + matmul_nt(d_branch, w_branch)).astype(bf16)).astype(f32)
        own = tokens.astype(f32)
        inverse1 = rms_inverse(own)
        grad_gain1 = jnp.sum(d_normed1 * own * inverse1, axis=0)
        input_grad = d_merged + rms_back(own, inverse1, gain_one, d_normed1)

        table_grad = jnp.concatenate(
            [
                jnp.stack(grad_taps),
                jnp.sum(d_conv, axis=0)[None],
                grad_rate_weight,
                sums[0:1],
                grad_input_weight,
                sums[1:2],
                grad_decay[None],
            ],
            axis=0,
        )
        table_out = lax.psum_scatter(table_grad.T, dp, scatter_dimension=0, tiled=True).T
        kernel_out, shift_out, rate_out, rate_bias_out, input_out, input_bias_out, decay_out = (
            table_out[places[i] : places[i + 1]] for i in range(len(cuts))
        )
        gain_out = lax.psum_scatter(jnp.stack([grad_gain1, grad_gain2]), every, scatter_dimension=1, tiled=True)

        def flat(values):
            return values.reshape(shard_rows, -1).astype(f32)

        return (
            block_out,
            input_grad,
            gain_out[0],
            flat(gate_out),
            flat(branch_out),
            kernel_out,
            shift_out[0],
            rate_out,
            rate_bias_out[0],
            input_out,
            input_bias_out[0],
            decay_out[0],
            out_out,
            gain_out[1],
            flat(mgate_out),
            flat(mup_out),
            down_out,
        )

    return on_device


def split_mesh(mesh):
    wide, narrow = mesh.shape["wide"], mesh.shape["narrow"]
    group = math.gcd(wide, HEADS)
    if group == wide:
        return mesh, ("narrow",), group, narrow
    places = mesh.devices.reshape(group, wide // group, narrow)
    return Mesh(places, ("wide", "rest", "narrow")), ("rest", "narrow"), group, wide // group * narrow


def solution(mesh):
    mesh, dp, tp_size, dp_size = split_mesh(mesh)
    every = ("wide",) + dp
    rows, columns, vector = P(every, None), P(None, every), P(every)
    return jax.shard_map(
        make_block("wide", dp, tp_size, dp_size),
        mesh=mesh,
        in_specs=(
            rows,
            vector,
            rows,
            vector,
            rows,
            rows,
            columns,
            vector,
            columns,
            vector,
            columns,
            vector,
            vector,
            rows,
            vector,
            rows,
            rows,
            rows,
        ),
        out_specs=(
            rows,
            rows,
            vector,
            rows,
            rows,
            columns,
            vector,
            columns,
            vector,
            columns,
            vector,
            vector,
            rows,
            vector,
            rows,
            rows,
            rows,
        ),
        check_vma=False,
    )
```

time: 4190 us -> 1490 us (0.36)
  waiting for transfers between devices: 3110 us -> 905 us
  local copies, waits for them, and re-layouts: 303 us -> 61.3 us
  blocking collectives: 339 us -> 141 us
  other arithmetic: 127 us -> 47.4 us
  Pallas kernels: 0 us -> 61.5 us
    reduce_scatter x6 -> x10, waiting for transfers between devices: 2670 us -> 397 us  [the longest x4 291 us: scatter_rows(): return lax.psum_scatter(values, tp, scatter_dimension=0, tiled=True)]
    dot_general x18 -> x7, matrix products: 251 us -> 64.7 us  [matmul_low(): return jnp.dot(left, right, preferred_element_type=jnp.float32)]
    all_gather x3 -> x2, blocking collectives: 256 us -> 81.3 us  [the longest x1 65.1 us: on_device(): lax.all_gather(jnp.stack([norm_gain1, norm_gain2]), every, axis=1, tiled=...]
    dot_general x6 -> x16, matrix products: 26.1 us -> 167 us  [the longest x8 100 us: matmul_nt(): lax.dot_general(left, right, (((1,), (1,)), ((), ())), preferred_element_...]
    pad x63 -> x0, local copies, waits for them, and re-layouts: 133 us -> none  [lru_mix(): states = lax.associative_scan(combine_steps, (decay_now, driven), axis=0)[1]]
    all_gather x6 -> x10, waiting for transfers between devices: 225 us -> 342 us  [the longest x4 184 us: gather_rows(): return lax.all_gather(values, tp, axis=0, tiled=True)]
    slice x64 -> x7, local copies, waits for them, and re-layouts: 111 us -> 15.9 us  [the longest x1 9.36 us: shift_rows(): cube = jnp.pad(cube, ((0, 0), (0, -by), (0, 0)))[:, -by:]]
    unnamed x2 -> x0, blocking collectives: 83.1 us -> none
  transfers between devices with their start and end apart: 15 -> 26, of which waited for: 10 -> 18; matrix products, arithmetic and copies ran while one was open for 9% -> 18% of each run, Pallas kernels for 0% -> 4%
where the time goes in v1:
time: 1490 us
  waiting for transfers between devices  905 us (61%)
  matrix products  238 us (16%)
  blocking collectives  141 us (9%)
  Pallas kernels  61.5 us (4%)
  local copies, waits for them, and re-layouts  61.3 us (4%)
  other arithmetic  47.4 us (3%)
  between operations  16.3 us (1%)
  starting transfers between devices  15.5 us (1%)
    reduce_scatter x4, waiting for transfers between devices, scatter_rows(): return lax.psum_scatter(values, tp, scatter_dimension=0, tiled=True)  291 us
    all_gather x4, waiting for transfers between devices, gather_rows(): return lax.all_gather(values, tp, axis=0, tiled=True)  184 us
    unnamed x24, waiting for transfers between devices  154 us
    all_gather x4, waiting for transfers between devices, gather_weight(): lax.all_gather(part.reshape(-1, part.shape[-1]), dp, axis=0, tiled=True)  117 us
    dot_general x8, matrix products, matmul_nt(): lax.dot_general(left, right, (((1,), (1,)), ((), ())), preferred_element_...  100 us
    dot_general x8, matrix products, matmul_tn(): lax.dot_general(left, right, (((0,), (0,)), ((), ())), preferred_element_...  67.3 us
    reduce_scatter x4, waiting for transfers between devices, scatter_weight(): mine = lax.psum_scatter(cut, dp, scatter_dimension=0, tiled=True)  67.1 us
    all_gather x1, blocking collectives, on_device(): lax.all_gather(jnp.stack([norm_gain1, norm_gain2]), every, axis=1, tiled=...  65.1 us
  transfers between devices with their start and end apart: 26, of which 18 were waited for; matrix products, arithmetic and copies ran while one was open for 18% of the time, Pallas kernels for 4%

profile of v1, /device:TPU:0, one launch (start us, length us, event | category | flops | bytes accessed | tf_op | source)
XLA Modules:
  0.0 1486.4 jit_solution(6162076748238219538)
XLA Ops:
  8.7 13.4 all_to_all.96
  23.5 11.4 all_to_all.97
  37.4 16.2 %all_gather.36 = bf16[320,328]{1,0:T(8,128)(2,1)S(1)} all-gather(bf16[80,328]{1,0:T(8,128)(2,1)S(1)} %bitcast.298), channel_id=1, replica_groups=mesh['wide'=8,'narrow'=4] {'narrow'}, dimensions={0}, use_global_device_ids=true | all-gather | bytes 262400 | tf_op jit(solution)/shard_map/all_gather | solution.py:331
  54.0 65.1 %all-gather = bf16[32,64,2]{1,2,0:T(2,128)(2,1)S(1)} all-gather(bf16[1,64,2]{1,2,0:T(2,128)(2,1)S(1)} %maximum_bitcast_fusion), channel_id=1, replica_groups=mesh['wide'=8,'narrow'=4] {'wide','narrow'}, dimensions={0}, use_global_device_ids=true | all-gather | bytes 8448 | tf_op jit(solution)/shard_map/all_gather | solution.py:314
  119.3 2.7 copy.274
  123.7 40.8 %all-gather.12.cloned.1.call-done = bf16[2560,2048]{1,0:T(8,128)(2,1)} async-done(((bf16[320,2048]{1,0:T(8,128)(2,1)}), bf16[2560,2048]{1,0:T(8,128)(2,1)}) %all-gather.12.cloned.1.call-update) | async-done | bytes 10485776 | tf_op jit(solution)/shard_map/all_gather | solution.py:261
  164.5 6.2 fusion
  171.4 3.7 fusion.2
  175.2 5.8 fusion.53
  181.0 4.3 pad_slice_fusion.5
  185.4 4.6 fusion.13.conv_ref
  190.0 3.4 convolution_add_fusion.2.input_ref
  193.4 3.4 convolution_add_fusion.3.rate_ref
  196.8 10.1 fusion.54.gate_ref
  206.9 21.4 %lru_forward.1 = (f32[2560,320]{1,0:T(8,128)}, bf16[2560,320]{1,0:T(8,128)(2,1)S(1)}) custom-call(bf16[2560,320]{1,0:T(8,128)(2,1)S(1)} %fusion.13.conv_ref, f32[2560,320]{1,0:T(8,128)} %convolution_add_fusion.3.rate_ref, f32[2560,320]{1,0:T(8,128)} %convolution_add_fusion.2.input_ref, f32[2560,320]{1,0:T(8,128)} %fusion.54.gate_ref, ...), custom_call_target="tpu_custom_call" | custom-call | tf_op jit(solution)/shard_map/lru_forward/pallas_call | solution.py:194
  228.9 10.2 convolution_convert_fusion.1
  240.5 15.7 %all_to_all.98 = bf16[1,64,8,768]{3,1,0,2:T(8,128)(2,1)} all-to-all(bf16[1,64,8,768]{3,1,0,2:T(8,128)(2,1)S(1)} %copy.276), channel_id=1, replica_groups=mesh['wide'=8,'narrow'=4] {'wide'}, dimensions={2} | all-to-all | bytes 1572864 | tf_op jit(solution)/shard_map/all_to_all | solution.py:269
  256.6 19.5 %all_to_all.99 = bf16[1,64,8,768]{3,1,0,2:T(8,128)(2,1)} all-to-all(bf16[1,64,8,768]{3,1,0,2:T(8,128)(2,1)S(1)} %copy.278), channel_id=1, replica_groups=mesh['wide'=8,'narrow'=4] {'wide'}, dimensions={2} | all-to-all | bytes 1572864 | tf_op jit(solution)/shard_map/all_to_all | solution.py:269
  276.1 48.1 %reduce-scatter.17.cloned.1.call-done = bf16[320,2048]{1,0:T(8,128)(2,1)} async-done(((bf16[2560,2048]{1,0:T(8,128)(2,1)}), bf16[320,2048]{1,0:T(8,128)(2,1)}) %reduce-scatter.17.cloned.1.call-update) | async-done | bytes 1310736 | tf_op jit(solution)/shard_map/reduce_scatter | solution.py:264
  332.0 57.1 %all-gather.22.cloned.1.call-done = bf16[2048,768]{1,0:T(8,128)(2,1)} async-done(((bf16[512,768]{1,0:T(8,128)(2,1)}), bf16[2048,768]{1,0:T(8,128)(2,1)}) %all-gather.22.cloned.1.call-update) | async-done | bytes 3145744 | tf_op jit(solution)/shard_map/all_gather | solution.py:272
  389.1 3.8 copy.277
  393.0 59.9 %all-gather.24.cloned.1.call-done = bf16[2048,768]{1,0:T(8,128)(2,1)} async-done(((bf16[512,768]{1,0:T(8,128)(2,1)}), bf16[2048,768]{1,0:T(8,128)(2,1)}) %all-gather.24.cloned.1.call-update) | async-done | bytes 3145744 | tf_op jit(solution)/shard_map/all_gather | solution.py:272
  452.9 3.8 copy.279
  456.7 60.6 %all-gather.20.cloned.1.call-done = bf16[2560,2048]{1,0:T(8,128)(2,1)} async-done(((bf16[320,2048]{1,0:T(8,128)(2,1)}), bf16[2560,2048]{1,0:T(8,128)(2,1)}) %all-gather.20.cloned.1.call-update) | async-done | bytes 10485776 | tf_op jit(solution)/shard_map/all_gather | solution.py:261
  517.3 14.0 fusion.56
  531.3 10.6 fusion.55
  541.9 40.5 %all-gather.26.cloned.1.call-done = bf16[768,2048]{1,0:T(8,128)(2,1)} async-done(((bf16[192,2048]{1,0:T(8,128)(2,1)}), bf16[768,2048]{1,0:T(8,128)(2,1)}) %all-gather.26.cloned.1.call-update) | async-done | bytes 3145744 | tf_op jit(solution)/shard_map/all_gather | solution.py:335
  582.4 64.2 %all-gather.28.cloned.1.call-done = bf16[2560,2048]{1,0:T(8,128)(2,1)} async-done(((bf16[320,2048]{1,0:T(8,128)(2,1)}), bf16[2560,2048]{1,0:T(8,128)(2,1)}) %all-gather.28.cloned.1.call-update) | async-done | bytes 10485776 | tf_op jit(solution)/shard_map/all_gather | solution.py:261
  646.6 23.2 %multiply_convert_fusion = (bf16[2560,768]{1,0:T(8,128)(2,1)}, bf16[2560,768]{1,0:T(8,128)(2,1)}, bf16[2560,768]{1,0:T(8,128)(2,1)}) fusion(f32[2560,768]{1,0:T(8,128)} %fusion.55, f32[2560,768]{1,0:T(8,128)} %fusion.56, bf16[2560,2048]{1,0:T(8,128)(2,1)} %all-gather.28.cloned.1.call-done, bf16[768,2048]{1,0:T(8,128)(2,1)} %all-gather.26.cloned.1.call-done), kind=kOutput, calls=%fused_computation.9 | convolution fusion | flops 8100249600 | bytes 41156608 | tf_op jit(solution)/shard_map/dot_general | solution.py:25
  669.9 15.1 %fusion.57 = f32[2560,2048]{1,0:T(8,128)} fusion(bf16[2560,768]{1,0:T(8,128)(2,1)} %get-tuple-element.53, bf16[2048,768]{1,0:T(8,128)(2,1)} %bitcast.266), kind=kOutput, calls=%fused_computation.139 | convolution fusion | flops 8053063680 | bytes 28049408 | tf_op jit(solution)/shard_map/dot_general | solution.py:25
  684.9 16.8 %add_convert_fusion.1 = bf16[2560,2048]{1,0:T(8,128)(2,1)} fusion(f32[2560,2048]{1,0:T(8,128)} %fusion.57, bf16[2560,768]{1,0:T(8,128)(2,1)} %get-tuple-element.52, bf16[2048,768]{1,0:T(8,128)(2,1)} %bitcast.269), kind=kOutput, calls=%fused_computation.6 | convolution fusion | flops 8063549440 | bytes 38535168 | tf_op jit(solution)/shard_map/dot_general | solution.py:25
  701.8 81.7 %reduce-scatter.21.cloned.1.call-done = bf16[320,2048]{1,0:T(8,128)(2,1)} async-done(((bf16[2560,2048]{1,0:T(8,128)(2,1)}), bf16[320,2048]{1,0:T(8,128)(2,1)}) %reduce-scatter.21.cloned.1.call-update) | async-done | bytes 1310736 | tf_op jit(solution)/shard_map/reduce_scatter | solution.py:264
  783.5 3.2 fusion.25
  788.9 12.4 convolution_convert_fusion.2
  803.3 12.8 convolution_convert_fusion.3
  818.1 15.2 %convolution_convert_fusion.4 = bf16[768,2048]{1,0:T(8,128)(2,1)} fusion(bf16[2560,768]{1,0:T(8,128)(2,1)} %get-tuple-element.54, bf16[2560,2048]{1,0:T(8,128)(2,1)} %all-gather.28.cloned.1.call-done), kind=kOutput, calls=%fused_computation.54 | convolution fusion | flops 8054636544 | bytes 17563648 | tf_op jit(solution)/shard_map/dot_general | solution.py:29
  833.4 18.9 %all-gather.30.cloned.1.call-done = bf16[2560,2048]{1,0:T(8,128)(2,1)} async-done(((bf16[320,2048]{1,0:T(8,128)(2,1)}), bf16[2560,2048]{1,0:T(8,128)(2,1)}) %all-gather.30.cloned.1.call-update) | async-done | bytes 10485776 | tf_op jit(solution)/shard_map/all_gather | solution.py:261
  852.3 9.8 fusion.58.grad_ref
  862.0 40.0 %lru_backward.1 = (f32[2560,320]{1,0:T(8,128)}, bf16[2560,320]{1,0:T(8,128)(2,1)S(1)}, bf16[2560,320]{1,0:T(8,128)(2,1)S(1)}, bf16[2560,320]{1,0:T(8,128)(2,1)S(1)}, f32[24,320]{1,0:T(8,128)S(1)}) custom-call(bf16[2560,320]{1,0:T(8,128)(2,1)} %copy-done, f32[2560,320]{1,0:T(8,128)} %convolution_add_fusion.3.rate_ref, ...), custom_call_target="tpu_custom_call" | custom-call | tf_op jit(solution)/shard_map/lru_backward/pallas_call | solution.py:212
  904.6 7.7 convolution_convert_fusion.7
  913.9 3.0 copy.285
  916.9 5.6 convolution_add_fusion.1
  922.6 5.9 convolution_add_fusion
  928.5 9.4 pad_slice_fusion.2
  937.9 8.3 fusion.46
  951.0 7.7 convolution_convert_fusion.6
  961.0 9.4 convolution_convert_fusion.5
  970.5 10.4 fusion.59
  980.9 13.3 add_convert_fusion
  996.1 13.0 convolution_convert_fusion
  1009.2 3.6 all-to-all-start.7
  1012.8 12.5 all-to-all-done.7
  1025.3 3.5 all-to-all-start.6
  1028.8 10.9 reduce-scatter.35.cloned.1.call-done
  1045.1 32.2 %reduce-scatter.25.cloned.1.call-done = bf16[512,320]{1,0:T(8,128)(2,1)} async-done(((bf16[2048,320]{1,0:T(8,128)(2,1)}), bf16[512,320]{1,0:T(8,128)(2,1)}) %reduce-scatter.25.cloned.1.call-update) | async-done | bytes 327696 | tf_op jit(solution)/shard_map/reduce_scatter | solution.py:279
  1077.3 3.7 all-to-all-start.4
  1081.0 19.3 %reduce-scatter.39.cloned.1.call-done = f32[80,328]{1,0:T(8,128)} async-done(((f32[320,328]{1,0:T(8,128)}), f32[80,328]{1,0:T(8,128)}) %reduce-scatter.39.cloned.1.call-update) | async-done | bytes 104976
  1102.0 34.8 %reduce-scatter.27.cloned.1.call-done = bf16[512,320]{1,0:T(8,128)(2,1)} async-done(((bf16[2048,320]{1,0:T(8,128)(2,1)}), bf16[512,320]{1,0:T(8,128)(2,1)}) %reduce-scatter.27.cloned.1.call-update) | async-done | bytes 327696 | tf_op jit(solution)/shard_map/reduce_scatter | solution.py:279
  1136.8 3.7 all-to-all-start.5
  1141.8 28.2 %reduce-scatter.29.cloned.1.call-done = bf16[80,2048]{1,0:T(8,128)(2,1)} async-done(((bf16[320,2048]{1,0:T(8,128)(2,1)}), bf16[80,2048]{1,0:T(8,128)(2,1)}) %reduce-scatter.29.cloned.1.call-update) | async-done | bytes 327696 | tf_op jit(solution)/shard_map/reduce_scatter | solution.py:384
  1175.1 79.1 %reduce-scatter.23.cloned.1.call-done = bf16[320,2048]{1,0:T(8,128)(2,1)} async-done(((bf16[2560,2048]{1,0:T(8,128)(2,1)}), bf16[320,2048]{1,0:T(8,128)(2,1)}) %reduce-scatter.23.cloned.1.call-update) | async-done | bytes 1310736 | tf_op jit(solution)/shard_map/reduce_scatter | solution.py:264
  1257.8 81.9 %reduce-scatter.19.cloned.1.call-done = bf16[320,2048]{1,0:T(8,128)(2,1)} async-done(((bf16[2560,2048]{1,0:T(8,128)(2,1)}), bf16[320,2048]{1,0:T(8,128)(2,1)}) %reduce-scatter.19.cloned.1.call-update) | async-done | bytes 1310736 | tf_op jit(solution)/shard_map/reduce_scatter | solution.py:264
  1339.7 5.2 fusion.20
  1344.9 132.4 %reduce-scatter.37.cloned.1.call-done = f32[64,2]{1,0:T(8,128)} async-done(((f32[2048,2]{1,0:T(8,128)}), f32[64,2]{1,0:T(8,128)}) %reduce-scatter.37.cloned.1.call-update) | async-done | bytes 528
  (271 shorter events, 55.9 us)
Async XLA Ops:
  7.2 112.1 %all-gather.16.cloned.1.call-start = ((), (), s32[]{:S(2)}) async-start(), calls=%async_computation.22 | async-start | bytes 1966080 | tf_op jit(solution)/shard_map/all_gather | solution.py:272
  8.5 27.9 %copy-start.61 = (bf16[4,80]{1,0:T(4,128)(2,1)S(1)}, bf16[4,80]{1,0:T(4,128)(2,1)}, u32[]{:S(2)}) copy-start(bf16[4,80]{1,0:T(4,128)(2,1)} %param.24) | copy-start | bytes 1924
  8.5 28.0 %copy-start.62 = (bf16[80]{0:T(256)(128)(2,1)S(1)}, bf16[80]{0:T(256)(128)(2,1)}, u32[]{:S(2)}) copy-start(bf16[80]{0:T(256)(128)(2,1)} %param.25) | copy-start | bytes 484
  8.6 28.1 %copy-start.63 = (bf16[80]{0:T(256)(128)(2,1)S(1)}, bf16[80]{0:T(256)(128)(2,1)}, u32[]{:S(2)}) copy-start(bf16[80]{0:T(256)(128)(2,1)} %param.27) | copy-start | bytes 484
  8.6 28.2 %copy-start.64 = (bf16[80]{0:T(256)(128)(2,1)S(1)}, bf16[80]{0:T(256)(128)(2,1)}, u32[]{:S(2)}) copy-start(bf16[80]{0:T(256)(128)(2,1)} %param.29) | copy-start | bytes 484
  8.6 28.3 %copy-start.65 = (bf16[80]{0:T(256)(128)(2,1)S(1)}, bf16[80]{0:T(256)(128)(2,1)}, u32[]{:S(2)}) copy-start(bf16[80]{0:T(256)(128)(2,1)} %param.30) | copy-start | bytes 484
  8.6 28.4 %copy-start.45 = (bf16[160,80]{1,0:T(8,128)(2,1)S(1)}, bf16[160,80]{1,0:T(8,128)(2,1)}, u32[]{:S(2)}) copy-start(bf16[160,80]{1,0:T(8,128)(2,1)} %param.26) | copy-start | bytes 76804
  8.6 28.5 %copy-start.46 = (bf16[160,80]{1,0:T(8,128)(2,1)S(1)}, bf16[160,80]{1,0:T(8,128)(2,1)}, u32[]{:S(2)}) copy-start(bf16[160,80]{1,0:T(8,128)(2,1)} %param.28) | copy-start | bytes 76804
  22.1 31.8 %copy-start.69 = (bf16[64]{0:T(256)(128)(2,1)S(1)}, bf16[64]{0:T(256)(128)(2,1)}, u32[]{:S(2)}) copy-start(bf16[64]{0:T(256)(128)(2,1)} %param.32) | copy-start | bytes 388
  22.1 31.8 %copy-start.70 = (bf16[64]{0:T(256)(128)(2,1)S(1)}, bf16[64]{0:T(256)(128)(2,1)}, u32[]{:S(2)}) copy-start(bf16[64]{0:T(256)(128)(2,1)} %param.21) | copy-start | bytes 388
  22.1 100.0 %all-gather.14.cloned.1.call-start = ((), (), s32[]{:S(2)}) async-start(), calls=%async_computation.21 | async-start | bytes 1966080 | tf_op jit(solution)/shard_map/all_gather | solution.py:272
  35.0 129.5 %all-gather.12.cloned.1.call-start = ((), (), s32[]{:S(2)}) async-start(), calls=%async_computation.20 | async-start | bytes 11796480 | tf_op jit(solution)/shard_map/all_gather | solution.py:261
  35.7 193.2 %all-gather.18.cloned.1.call-start = ((), (), s32[]{:S(2)}) async-start(), calls=%async_computation.23 | async-start | bytes 1638400 | tf_op jit(solution)/shard_map/all_gather | solution.py:332
  36.3 287.9 %reduce-scatter.17.cloned.1.call-start = ((), (), s32[]{:S(2)}) async-start(), calls=%async_computation.24 | async-start | bytes 11796480 | tf_op jit(solution)/shard_map/reduce_scatter | solution.py:264
  36.4 157.0 %copy-start.43 = (pred[320]{0:T(512)(128)(4,1)}, pred[320]{0:T(512)(128)(4,1)S(1)}, u32[]{:S(2)}) copy-start(pred[320]{0:T(512)(128)(4,1)S(1)} %fusion.36) | copy-start | bytes 964
  36.4 157.0 %copy-start.33 = (s32[320]{0:T(512)}, s32[320]{0:T(512)S(1)}, u32[]{:S(2)}) copy-start(s32[320]{0:T(512)S(1)} %get-tuple-element.82) | copy-start | bytes 3844
  36.4 157.0 %copy-start.35 = (s32[320]{0:T(512)}, s32[320]{0:T(512)S(1)}, u32[]{:S(2)}) copy-start(s32[320]{0:T(512)S(1)} %get-tuple-element.83) | copy-start | bytes 3844
  53.8 69.9 %copy-start.30 = (bf16[320,328]{0,1:T(8,128)(2,1)}, bf16[320,328]{0,1:T(8,128)(2,1)S(1)}, u32[]{:S(2)}) copy-start(bf16[320,328]{0,1:T(8,128)(2,1)S(1)} %copy.263) | copy-start | bytes 629764
  53.9 136.1 %copy-start.26 = (bf16[160,320]{1,0:T(8,128)(2,1)}, bf16[160,320]{1,0:T(8,128)(2,1)S(1)}, u32[]{:S(2)}) copy-start(bf16[160,320]{1,0:T(8,128)(2,1)S(1)} %get-tuple-element.63) | copy-start | bytes 307204
  53.9 139.5 %copy-start.28 = (bf16[160,320]{1,0:T(8,128)(2,1)}, bf16[160,320]{1,0:T(8,128)(2,1)S(1)}, u32[]{:S(2)}) copy-start(bf16[160,320]{1,0:T(8,128)(2,1)S(1)} %get-tuple-element.64) | copy-start | bytes 307204
  119.2 51.5 %copy-start.39 = (f32[1,2048]{1,0:T(1,128)}, f32[1,2048]{1,0:T(1,128)S(1)}, u32[]{:S(2)}) copy-start(f32[1,2048]{1,0:T(1,128)S(1)} %get-tuple-element.74) | copy-start | bytes 24580
  119.2 667.5 %copy-start.37 = (f32[1,2048]{1,0:T(1,128)}, f32[1,2048]{1,0:T(1,128)S(1)}, u32[]{:S(2)}) copy-start(f32[1,2048]{1,0:T(1,128)S(1)} %get-tuple-element.73) | copy-start | bytes 24580
  119.3 66.1 %copy-start.50 = (f32[320]{0:T(512)}, f32[320]{0:T(512)S(1)}, u32[]{:S(2)}) copy-start(f32[320]{0:T(512)S(1)} %get-tuple-element.45) | copy-start | bytes 3844
  119.3 66.1 %copy-start.52 = (f32[320]{0:T(512)}, f32[320]{0:T(512)S(1)}, u32[]{:S(2)}) copy-start(f32[320]{0:T(512)S(1)} %get-tuple-element.46) | copy-start | bytes 3844
  119.3 66.1 %copy-start.54 = (f32[320]{0:T(512)}, f32[320]{0:T(512)S(1)}, u32[]{:S(2)}) copy-start(f32[320]{0:T(512)S(1)} %get-tuple-element.47) | copy-start | bytes 3844
  119.3 66.1 %copy-start.56 = (f32[320]{0:T(512)}, f32[320]{0:T(512)S(1)}, u32[]{:S(2)}) copy-start(f32[320]{0:T(512)S(1)} %get-tuple-element.48) | copy-start | bytes 3844
  123.7 51.5 %copy-start.24 = (bf16[4,8,64,320]{3,2,0,1:T(8,128)(2,1)}, bf16[4,8,64,320]{3,2,0,1:T(8,128)(2,1)S(1)}, u32[]{:S(2)}) copy-start(bf16[4,8,64,320]{3,2,0,1:T(8,128)(2,1)S(1)} %copy.266) | copy-start | bytes 3932164
  190.0 16.9 %copy-start = (bf16[2560,320]{1,0:T(8,128)(2,1)}, bf16[2560,320]{1,0:T(8,128)(2,1)S(1)}, u32[]{:S(2)}) copy-start(bf16[2560,320]{1,0:T(8,128)(2,1)S(1)} %fusion.13.conv_ref) | copy-start | bytes 4915204
  239.2 17.1 %copy-start.32 = (bf16[64,6144]{1,0:T(8,128)(2,1)S(1)}, bf16[64,6144]{1,0:T(8,128)(2,1)}, u32[]{:S(2)}) copy-start(bf16[64,6144]{1,0:T(8,128)(2,1)} %param.34) | copy-start | bytes 2359300
  239.2 150.0 %all-gather.22.cloned.1.call-start = ((), (), s32[]{:S(2)}) async-start(), calls=%async_computation.26 | async-start | bytes 3932160 | tf_op jit(solution)/shard_map/all_gather | solution.py:272
  256.2 68.0 %copy-start.10 = (bf16[320,2048]{1,0:T(8,128)(2,1)S(1)}, bf16[320,2048]{1,0:T(8,128)(2,1)}, u32[]{:S(2)}) copy-start(bf16[320,2048]{1,0:T(8,128)(2,1)} %param.18) | copy-start | bytes 3932164
  256.2 196.6 %all-gather.24.cloned.1.call-start = ((), (), s32[]{:S(2)}) async-start(), calls=%async_computation.27 | async-start | bytes 3932160 | tf_op jit(solution)/shard_map/all_gather | solution.py:272
  276.1 241.2 %all-gather.20.cloned.1.call-start = ((), (), s32[]{:S(2)}) async-start(), calls=%async_computation.25 | async-start | bytes 11796480 | tf_op jit(solution)/shard_map/all_gather | solution.py:261
  326.1 460.5 %copy-start.41 = (f32[320]{0:T(512)}, f32[320]{0:T(512)S(1)}, u32[]{:S(2)}) copy-start(f32[320]{0:T(512)S(1)} %add_rsqrt_fusion.2) | copy-start | bytes 3844
  327.8 254.6 %all-gather.26.cloned.1.call-start = ((), (), s32[]{:S(2)}) async-start(), calls=%async_computation.28 | async-start | bytes 3932160 | tf_op jit(solution)/shard_map/all_gather | solution.py:335
  328.6 318.1 %all-gather.28.cloned.1.call-start = ((), (), s32[]{:S(2)}) async-start(), calls=%async_computation.30 | async-start | bytes 11796480 | tf_op jit(solution)/shard_map/all_gather | solution.py:261
  329.3 457.4 %copy-start.48 = (f32[320]{0:T(512)}, f32[320]{0:T(512)S(1)}, u32[]{:S(2)}) copy-start(f32[320]{0:T(512)S(1)} %fusion.37) | copy-start | bytes 3844
  331.9 451.5 %reduce-scatter.21.cloned.1.call-start = ((), (), s32[]{:S(2)}) async-start(), calls=%async_computation.31 | async-start | bytes 11796480 | tf_op jit(solution)/shard_map/reduce_scatter | solution.py:264
  701.7 150.5 %all-gather.30.cloned.1.call-start = ((), (), s32[]{:S(2)}) async-start(), calls=%async_computation.32 | async-start | bytes 11796480 | tf_op jit(solution)/shard_map/all_gather | solution.py:261
  788.9 220.3 %reduce-scatter.33.cloned.1.call-start = ((), (), s32[]{:S(2)}) async-start(), calls=%async_computation.38 | async-start | bytes 3932160 | tf_op jit(solution)/shard_map/reduce_scatter | solution.py:279
  803.3 209.5 %reduce-scatter.31.cloned.1.call-start = ((), (), s32[]{:S(2)}) async-start(), calls=%async_computation.37 | async-start | bytes 3932160 | tf_op jit(solution)/shard_map/reduce_scatter | solution.py:279
  818.1 221.7 %reduce-scatter.35.cloned.1.call-start = ((), (), s32[]{:S(2)}) async-start(), calls=%async_computation.39 | async-start | bytes 3932160 | tf_op jit(solution)/shard_map/reduce_scatter | solution.py:372
  833.3 19.0 %copy-start.68 = (bf16[320,2048]{1,0:T(8,128)(2,1)S(1)}, bf16[320,2048]{1,0:T(8,128)(2,1)}, u32[]{:S(2)}) copy-start(bf16[320,2048]{1,0:T(8,128)(2,1)} %all-gather.18.cloned.1.call-done) | copy-start | bytes 3932164
  833.3 28.7 %copy-start.8 = (f32[8,320]{1,0:T(8,128)S(1)}, f32[8,320]{1,0:T(8,128)}, u32[]{:S(2)}) copy-start(f32[8,320]{1,0:T(8,128)} %copy-done.7) | copy-start | bytes 30724
  833.3 244.0 %reduce-scatter.25.cloned.1.call-start = ((), (), s32[]{:S(2)}) async-start(), calls=%async_computation.34 | async-start | bytes 1966080 | tf_op jit(solution)/shard_map/reduce_scatter | solution.py:279
  922.6 177.7 %reduce-scatter.39.cloned.1.call-start = ((), (), s32[]{:S(2)}) async-start(), calls=%async_computation.41 | async-start | bytes 614400
  951.0 185.9 %reduce-scatter.27.cloned.1.call-start = ((), (), s32[]{:S(2)}) async-start(), calls=%async_computation.35 | async-start | bytes 1966080 | tf_op jit(solution)/shard_map/reduce_scatter | solution.py:279
  960.9 209.1 %reduce-scatter.29.cloned.1.call-start = ((), (), s32[]{:S(2)}) async-start(), calls=%async_computation.36 | async-start | bytes 1638400 | tf_op jit(solution)/shard_map/reduce_scatter | solution.py:384
  970.5 283.7 %reduce-scatter.23.cloned.1.call-start = ((), (), s32[]{:S(2)}) async-start(), calls=%async_computation.33 | async-start | bytes 11796480 | tf_op jit(solution)/shard_map/reduce_scatter | solution.py:264
  994.3 345.4 %reduce-scatter.19.cloned.1.call-start = ((), (), s32[]{:S(2)}) async-start(), calls=%async_computation.29 | async-start | bytes 11796480 | tf_op jit(solution)/shard_map/reduce_scatter | solution.py:264
  1009.2 16.1 %all-to-all-start.7 = ((bf16[8,64,1,768]{3,1,2,0:T(8,128)(2,1)}), bf16[8,64,1,768]{3,1,2,0:T(8,128)(2,1)S(1)}, u32[]{:S(2)}, u32[]{:S(2)}) async-start(bf16[8,64,1,768]{3,1,2,0:T(8,128)(2,1)} %bitcast.290), calls=%async_computation.16 | async-start | bytes 1572864 | tf_op jit(solution)/shard_map/all_to_all | solution.py:280
  1025.3 18.4 %all-to-all-start.6 = ((bf16[8,64,1,768]{3,1,2,0:T(8,128)(2,1)}), bf16[8,64,1,768]{3,1,2,0:T(8,128)(2,1)S(1)}, u32[]{:S(2)}, u32[]{:S(2)}) async-start(bf16[8,64,1,768]{3,1,2,0:T(8,128)(2,1)} %bitcast.289), calls=%async_computation.14 | async-start | bytes 1572864 | tf_op jit(solution)/shard_map/all_to_all | solution.py:280
  1043.7 37.3 %copy-start.58 = (f32[320]{0:T(512)S(1)}, f32[320]{0:T(512)}, u32[]{:S(2)}) copy-start(f32[320]{0:T(512)} %get-tuple-element.40) | copy-start | bytes 3844
  1077.3 59.5 %all-to-all-start.4 = ((bf16[8,64,1,320]{3,1,2,0:T(8,128)(2,1)}), bf16[8,64,1,320]{3,1,2,0:T(8,128)(2,1)S(1)}, u32[]{:S(2)}, u32[]{:S(2)}) async-start(bf16[8,64,1,320]{3,1,2,0:T(8,128)(2,1)} %bitcast.296), calls=%async_computation.9 | async-start | bytes 786432 | tf_op jit(solution)/shard_map/all_to_all | solution.py:280
  1136.8 36.7 %all-to-all-start.5 = ((bf16[8,64,1,320]{3,1,2,0:T(8,128)(2,1)}), bf16[8,64,1,320]{3,1,2,0:T(8,128)(2,1)S(1)}, u32[]{:S(2)}, u32[]{:S(2)}) async-start(bf16[8,64,1,320]{3,1,2,0:T(8,128)(2,1)} %bitcast.297), calls=%async_computation.11 | async-start | bytes 786432 | tf_op jit(solution)/shard_map/all_to_all | solution.py:280
  1140.5 336.8 %reduce-scatter.37.cloned.1.call-start = ((), (), s32[]{:S(2)}) async-start(), calls=%async_computation.40 | async-start | bytes 1081344
  1172.4 81.8 %copy-start.11 = (bf16[320,2048]{1,0:T(8,128)(2,1)S(1)}, bf16[320,2048]{1,0:T(8,128)(2,1)}, u32[]{:S(2)}) copy-start(bf16[320,2048]{1,0:T(8,128)(2,1)} %param.18) | copy-start | bytes 3932164
  1172.4 81.8 %copy-start.40 = (f32[1,2048]{1,0:T(1,128)S(1)}, f32[1,2048]{1,0:T(1,128)}, u32[]{:S(2)}) copy-start(f32[1,2048]{1,0:T(1,128)} %copy-done.39) | copy-start | bytes 24580
  1173.5 82.8 %copy-start.47 = (f32[2048]{0:T(1024)S(1)}, f32[2048]{0:T(1024)}, u32[]{:S(2)}) copy-start(f32[2048]{0:T(1024)} %get-tuple-element.36) | copy-start | bytes 24580
  1174.0 165.7 %copy-start.16 = (bf16[320,2048]{1,0:T(8,128)(2,1)S(1)}, bf16[320,2048]{1,0:T(8,128)(2,1)}, u32[]{:S(2)}) copy-start(bf16[320,2048]{1,0:T(8,128)(2,1)} %reduce-scatter.17.cloned.1.call-done) | copy-start | bytes 3932164
  1174.0 165.6 %copy-start.38 = (f32[1,2048]{1,0:T(1,128)S(1)}, f32[1,2048]{1,0:T(1,128)}, u32[]{:S(2)}) copy-start(f32[1,2048]{1,0:T(1,128)} %copy-done.37) | copy-start | bytes 24580
  1174.0 165.6 %copy-start.42 = (f32[320]{0:T(512)S(1)}, f32[320]{0:T(512)}, u32[]{:S(2)}) copy-start(f32[320]{0:T(512)} %copy-done.41) | copy-start | bytes 3844
  1174.1 165.6 %copy-start.49 = (f32[320]{0:T(512)S(1)}, f32[320]{0:T(512)}, u32[]{:S(2)}) copy-start(f32[320]{0:T(512)} %copy-done.48) | copy-start | bytes 3844
  1174.1 165.6 %copy-start.60 = (f32[320]{0:T(512)S(1)}, f32[320]{0:T(512)}, u32[]{:S(2)}) copy-start(f32[320]{0:T(512)} %copy-done.59) | copy-start | bytes 3844
  (33 other events, 198.3 us)
Sparse Core Ops, SparseCore 0:
  22.2 40.4 all-gather.15
  64.3 36.1 all-gather.13
  102.3 62.1 all-gather.11
  165.9 32.6 all-gather.17
  239.3 84.8 reduce-scatter.16
  325.6 63.4 all-gather.21
  390.7 62.1 all-gather.23
  455.3 61.8 all-gather.19
  518.8 63.4 all-gather.25
  584.7 61.8 all-gather.27
  701.8 81.5 reduce-scatter.20
  789.0 63.2 all-gather.29
  854.5 60.2 reduce-scatter.32
  917.0 60.2 reduce-scatter.30
  979.5 60.2 reduce-scatter.34
  1041.9 35.3 reduce-scatter.24
  1080.0 20.2 reduce-scatter.38
  1103.1 33.6 reduce-scatter.26
  1139.8 30.1 reduce-scatter.28
  1173.8 80.3 reduce-scatter.22
  1258.1 81.5 reduce-scatter.18
  1342.0 135.2 reduce-scatter.36

commit v2 on v1

--- a/solution.py
+++ b/solution.py
@@ -1,5 +1,4 @@
 import functools
-import math
 
 import jax
 import jax.numpy as jnp
@@ -14,7 +13,7 @@
 GELU_ROOT = 0.7978845608028654
 GELU_CUBE = 0.044715
 LANES = 128
-HEADS = 16
+PLANE = 4
 
 
 def matmul_low(left, right):
@@ -254,30 +253,72 @@
     return cube.reshape(rows, channels)
 
 
-def make_block(tp, dp, tp_size, dp_size):
-    every = (tp,) + dp
-
-    def gather_rows(values):
-        return lax.all_gather(values, tp, axis=0, tiled=True)
-
-    def scatter_rows(values):
-        return lax.psum_scatter(values, tp, scatter_dimension=0, tiled=True)
-
-    def columns_out(shard):
-        rows, columns = shard.shape
-        cut = shard.reshape(rows, tp_size, columns // tp_size)
-        return lax.all_to_all(cut, tp, 1, 0, tiled=False)
-
-    def gather_weight(part):
-        whole = lax.all_gather(part.reshape(-1, part.shape[-1]), dp, axis=0, tiled=True)
-        whole = whole.reshape((dp_size,) + part.shape)
-        return whole.swapaxes(0, 1).reshape(-1, part.shape[-1])
-
-    def scatter_weight(grad, rows):
+def make_block(rest_size, narrow_size):
+    bf16, f32 = jnp.bfloat16, jnp.float32
+    spread = ("rest", "narrow")
+
+    def swap(values, mask):
+        return lax.ppermute(values, "wide", [(i, i ^ mask) for i in range(PLANE)])
+
+    def gather_rows(shard):
+        half = shard.shape[0] // 2
+        one, two = swap(shard, 1), swap(shard, 2)
+        far = [swap(one[:half], 2), swap(two[half:], 1)]
+        return jnp.concatenate(far + [one, two, shard], axis=0)
+
+    def scatter_rows(parts):
+        far, one, two, own = parts
+        half = own.shape[0] // 2
+        via_one, via_two = swap(far[:half], 1), swap(far[half:], 2)
+        one_low, two_high = swap(one[:half], 1), swap(two[half:], 2)
+        one_high = swap((one[half:].astype(f32) + via_two.astype(f32)).astype(bf16), 1)
+        two_low = swap((two[:half].astype(f32) + via_one.astype(f32)).astype(bf16), 2)
+        low = own[:half].astype(f32) + one_low.astype(f32) + two_low.astype(f32)
+        high = own[half:].astype(f32) + one_high.astype(f32) + two_high.astype(f32)
+        return jnp.concatenate([low, high], axis=0)
+
+    def rows_to_parts(values):
+        return jnp.split(values, PLANE, axis=0)
+
+    def gather_columns(blocks):
+        part = lax.all_to_all(blocks, "wide", 0, 0, tiled=False)
+        plane, rows, columns = part.shape
+        whole = lax.all_gather(part.reshape(plane * rows, columns), spread, axis=0, tiled=True)
+        whole = whole.reshape(rest_size * narrow_size, plane, rows, columns)
+        return whole.swapaxes(0, 1).reshape(-1, columns)
+
+    def reduce_spread(values):
+        if rest_size == 2:
+            me = lax.axis_index("rest")
+            theirs = lax.dynamic_index_in_dim(values, 1 - me, 0, keepdims=False)
+            mine = lax.dynamic_index_in_dim(values, me, 0, keepdims=False)
+            other = lax.ppermute(theirs, "rest", [(0, 1), (1, 0)])
+            total = (mine.astype(f32) + other.astype(f32)).astype(values.dtype)
+        else:
+            total = lax.psum_scatter(values, "rest", scatter_dimension=0, tiled=False)
+        flat = total.reshape(-1, total.shape[-1])
+        return lax.psum_scatter(flat, "narrow", scatter_dimension=0, tiled=True)
+
+    def reduce_columns(grad, rows):
         columns = grad.shape[-1]
-        cut = grad.reshape(tp_size, dp_size, rows, columns).swapaxes(0, 1).reshape(-1, columns)
-        mine = lax.psum_scatter(cut, dp, scatter_dimension=0, tiled=True)
-        return lax.all_to_all(mine.reshape(tp_size, rows, columns), tp, 0, 1, tiled=False)
+        cut = grad.reshape(PLANE, rest_size, narrow_size, rows, columns)
+        mine = reduce_spread(cut.transpose(1, 2, 0, 3, 4))
+        return lax.all_to_all(mine.reshape(PLANE, rows, columns), "wide", 0, 1, tiled=False)
+
+    def reduce_rows(grad):
+        return reduce_spread(grad.reshape(rest_size, narrow_size, -1, grad.shape[-1]))
+
+    def sum_all(values):
+        values = values + swap(values, 1)
+        values = values + swap(values, 2)
+        if rest_size == 2:
+            values = values + lax.ppermute(values, "rest", [(0, 1), (1, 0)])
+        else:
+            values = lax.psum(values, "rest")
+        total = values
+        for step in range(1, narrow_size):
+            total = total + lax.ppermute(values, "narrow", [(i, (i + step) % narrow_size) for i in range(narrow_size)])
+        return total
 
     def on_device(
         tokens,
@@ -299,23 +340,22 @@
         mlp_up,
         mlp_down,
     ):
-        bf16, f32 = jnp.bfloat16, jnp.float32
         row_count, width = tokens.shape
         head = rate_weight.shape[0]
-        shard_rows = gate_in.shape[0]
+        rows = gate_in.shape[0]
         taps = conv_kernel.shape[0]
-        seqs = tp_size
+        seqs = PLANE
+        channels = gate_in.shape[1] // PLANE
+        hidden = mlp_gate.shape[1] // PLANE
         live = (jnp.arange(row_count, dtype=jnp.int32) < lengths[0]).astype(f32)[:, None]
 
-        low_res = (cotangent.astype(f32) * live).astype(bf16)
-        tokens_all = gather_rows(tokens)
-        low_res_all = gather_rows(low_res)
-
-        gains = lax.all_gather(jnp.stack([norm_gain1, norm_gain2]), every, axis=1, tiled=True).astype(f32)
-        gain_one, gain_two = gains[0:1], gains[1:2]
-
-        w_gate = gather_weight(columns_out(gate_in))
-        w_branch = gather_weight(columns_out(x_in))
+        def by_plane(*weights):
+            cut = [w.reshape(rows, PLANE, -1).swapaxes(0, 1) for w in weights]
+            return jnp.concatenate(cut, axis=2)
+
+        gains = jnp.pad(jnp.stack([norm_gain1, norm_gain2], axis=1), ((0, 0), (0, LANES - 2)))
+        gains = jnp.broadcast_to(gains[None], (PLANE, rows, LANES))
+        w_rec = gather_columns(jnp.concatenate([by_plane(gate_in, x_in), gains], axis=2))
         table = jnp.concatenate(
             [
                 conv_kernel,
@@ -328,14 +368,22 @@
             ],
             axis=0,
         )
-        table = lax.all_gather(table.T, dp, axis=0, tiled=True).T
-        w_out = lax.all_gather(out_proj, dp, axis=0, tiled=True)
-        w_mgate = gather_weight(columns_out(mlp_gate))
-        w_mup = gather_weight(columns_out(mlp_up))
-        w_down = lax.all_gather(mlp_down, dp, axis=0, tiled=True)
-
         cuts = [taps, 1, head, 1, head, 1, 1]
         places = [sum(cuts[:i]) for i in range(len(cuts) + 1)]
+        table = jnp.pad(table, ((0, -places[-1] % LANES), (0, 0)))
+        out_and_table = lax.all_gather(jnp.concatenate([out_proj, table.T], axis=1), spread, axis=0, tiled=True)
+        w_mlp = gather_columns(by_plane(mlp_gate, mlp_up))
+        w_down = lax.all_gather(mlp_down, spread, axis=0, tiled=True)
+
+        low_res = (cotangent.astype(f32) * live).astype(bf16)
+        tokens_all = gather_rows(tokens)
+        low_res_all = gather_rows(low_res)
+
+        gain_one = w_rec[:, 2 * channels].astype(f32)[None]
+        gain_two = w_rec[:, 2 * channels + 1].astype(f32)[None]
+        w_rec = w_rec[:, : 2 * channels]
+        w_out = out_and_table[:, :width]
+        table = out_and_table[:, width:].T
         kernel, shift, rate_table, b_rate, input_table, b_input, decay = (
             table[places[i] : places[i + 1]] for i in range(len(cuts))
         )
@@ -347,8 +395,8 @@
 
         tokens_f = tokens_all.astype(f32)
         normed1 = (tokens_f * rms_inverse(tokens_f) * gain_one).astype(bf16)
-        gate_pre = matmul_low(normed1, w_gate)
-        branch_pre = matmul_low(normed1, w_branch)
+        gate_pre = matmul_low(normed1, w_rec[:, :channels])
+        branch_pre = matmul_low(normed1, w_rec[:, channels:])
         conv = shift_f
         for tap in range(taps):
             conv = conv + kernel_f[tap] * shift_rows(branch_pre, seqs, taps - 1 - tap)
@@ -356,33 +404,31 @@
         rate_pre = matmul_low(conv, w_rate) + b_rate
         input_pre = matmul_low(conv, w_input) + b_input
         states, mixed = lru_forward(seqs, conv, rate_pre, input_pre, gate_pre, soft_rows)
-        merged = tokens.astype(f32) + scatter_rows(matmul_low(mixed, w_out).astype(bf16)).astype(f32)
+        merged = tokens.astype(f32) + scatter_rows(rows_to_parts(matmul_low(mixed, w_out).astype(bf16)))
 
         inverse2 = rms_inverse(merged)
         normed2 = (merged * inverse2 * gain_two).astype(bf16)
         normed2_all = gather_rows(normed2)
-        gate_two = matmul_low(normed2_all, w_mgate)
-        up_two = matmul_low(normed2_all, w_mup)
+        gate_two = matmul_low(normed2_all, w_mlp[:, :hidden])
+        up_two = matmul_low(normed2_all, w_mlp[:, hidden:])
         value, slope = gelu_pair(gate_two)
         product = (value * up_two).astype(bf16)
-        result = merged + scatter_rows(matmul_low(product, w_down).astype(bf16)).astype(f32)
+        result = merged + scatter_rows(rows_to_parts(matmul_low(product, w_down).astype(bf16)))
         block_out = (result * live).astype(bf16)
 
-        grad_down = matmul_tn(product, low_res_all).astype(bf16)
-        down_out = lax.psum_scatter(grad_down, dp, scatter_dimension=0, tiled=True).astype(f32)
+        down_out = reduce_rows(matmul_tn(product, low_res_all).astype(bf16)).astype(f32)
         d_product = matmul_nt(low_res_all, w_down)
         d_gate_two = (d_product * up_two * slope).astype(bf16)
         d_up_two = (d_product * value).astype(bf16)
-        mgate_out = scatter_weight(matmul_tn(normed2_all, d_gate_two).astype(bf16), shard_rows)
-        mup_out = scatter_weight(matmul_tn(normed2_all, d_up_two).astype(bf16), shard_rows)
-        d_normed2 = scatter_rows((matmul_nt(d_gate_two, w_mgate) + matmul_nt(d_up_two, w_mup)).astype(bf16)).astype(f32)
+        d_mlp = jnp.concatenate([d_gate_two, d_up_two], axis=1)
+        d_normed2 = scatter_rows(rows_to_parts(matmul_nt(d_mlp, w_mlp).astype(bf16)))
+        mlp_out = reduce_columns(matmul_tn(normed2_all, d_mlp).astype(bf16), rows)
         grad_gain2 = jnp.sum(d_normed2 * merged * inverse2, axis=0)
         d_merged = low_res.astype(f32) + rms_back(merged, inverse2, gain_two, d_normed2)
 
         low_merged_all = gather_rows(d_merged.astype(bf16))
-        grad_out = matmul_tn(mixed, low_merged_all).astype(bf16)
-        out_out = lax.psum_scatter(grad_out, dp, scatter_dimension=0, tiled=True).astype(f32)
         d_mixed = matmul_nt(low_merged_all, w_out)
+        out_out = reduce_rows(matmul_tn(mixed, low_merged_all).astype(bf16)).astype(f32)
         d_conv_lru, d_rate, d_input, d_gate, sums = lru_backward(
             seqs, conv, rate_pre, input_pre, gate_pre, soft_rows, states, d_mixed
         )
@@ -397,10 +443,9 @@
             moved = shift_rows(d_conv, seqs, tap - (taps - 1))
             d_branch = d_branch + kernel_f[tap] * moved
             grad_taps.append(jnp.sum(branch_pre * moved, axis=0))
-        d_branch = d_branch.astype(bf16)
-        gate_out = scatter_weight(matmul_tn(normed1, d_gate).astype(bf16), shard_rows)
-        branch_out = scatter_weight(matmul_tn(normed1, d_branch).astype(bf16), shard_rows)
-        d_normed1 = scatter_rows((matmul_nt(d_gate, w_gate) + matmul_nt(d_branch, w_branch)).astype(bf16)).astype(f32)
+        d_rec = jnp.concatenate([d_gate, d_branch.astype(bf16)], axis=1)
+        rec_out = reduce_columns(matmul_tn(normed1, d_rec).astype(bf16), rows)
+        d_normed1 = scatter_rows(rows_to_parts(matmul_nt(d_rec, w_rec).astype(bf16)))
         own = tokens.astype(f32)
         inverse1 = rms_inverse(own)
         grad_gain1 = jnp.sum(d_normed1 * own * inverse1, axis=0)
@@ -418,21 +463,23 @@
             ],
             axis=0,
         )
-        table_out = lax.psum_scatter(table_grad.T, dp, scatter_dimension=0, tiled=True).T
+        table_out = reduce_rows(jnp.pad(table_grad, ((0, -places[-1] % LANES), (0, 0))).T).T
         kernel_out, shift_out, rate_out, rate_bias_out, input_out, input_bias_out, decay_out = (
             table_out[places[i] : places[i + 1]] for i in range(len(cuts))
         )
-        gain_out = lax.psum_scatter(jnp.stack([grad_gain1, grad_gain2]), every, scatter_dimension=1, tiled=True)
-
-        def flat(values):
-            return values.reshape(shard_rows, -1).astype(f32)
+        index = lax.axis_index(("wide",) + spread)
+        gain_sums = sum_all(jnp.stack([grad_gain1, grad_gain2]))
+        gain_out = lax.dynamic_slice_in_dim(gain_sums, index * rows, rows, axis=1)
+
+        def whole_rows(cut):
+            return cut.reshape(rows, -1).astype(f32)
 
         return (
             block_out,
             input_grad,
             gain_out[0],
-            flat(gate_out),
-            flat(branch_out),
+            whole_rows(rec_out[:, :, :channels]),
+            whole_rows(rec_out[:, :, channels:]),
             kernel_out,
             shift_out[0],
             rate_out,
@@ -442,29 +489,21 @@
             decay_out[0],
             out_out,
             gain_out[1],
-            flat(mgate_out),
-            flat(mup_out),
+            whole_rows(mlp_out[:, :, :hidden]),
+            whole_rows(mlp_out[:, :, hidden:]),
             down_out,
         )
 
     return on_device
 
 
-def split_mesh(mesh):
+def solution(mesh):
     wide, narrow = mesh.shape["wide"], mesh.shape["narrow"]
-    group = math.gcd(wide, HEADS)
-    if group == wide:
-        return mesh, ("narrow",), group, narrow
-    places = mesh.devices.reshape(group, wide // group, narrow)
-    return Mesh(places, ("wide", "rest", "narrow")), ("rest", "narrow"), group, wide // group * narrow
-
-
-def solution(mesh):
-    mesh, dp, tp_size, dp_size = split_mesh(mesh)
-    every = ("wide",) + dp
+    mesh = Mesh(mesh.devices.reshape(PLANE, wide // PLANE, narrow), ("wide", "rest", "narrow"))
+    every = mesh.axis_names
     rows, columns, vector = P(every, None), P(None, every), P(every)
     return jax.shard_map(
-        make_block("wide", dp, tp_size, dp_size),
+        make_block(wide // PLANE, narrow),
         mesh=mesh,
         in_specs=(
             rows,

time: 1490 us -> 893 us (0.60)
  waiting for transfers between devices: 905 us -> 368 us
  blocking collectives: 141 us -> 38 us
  matrix products: 238 us -> 184 us
  starting transfers between devices: 15.5 us -> 63.4 us
  local copies, waits for them, and re-layouts: 61.3 us -> 89.8 us
  other arithmetic: 47.4 us -> 72.2 us
    all_gather x10 -> x4, waiting for transfers between devices: 342 us -> 10.9 us  [the longest x2 10.9 us: gather_columns(): lax.all_gather(part.reshape(plane * rows, columns), spread, axis=0, tiled...]
    reduce_scatter x10 -> x5, waiting for transfers between devices: 397 us -> 91 us  [reduce_spread(): return lax.psum_scatter(flat, 'narrow', scatter_dimension=0, tiled=True)]
    ppermute x0 -> x51, waiting for transfers between devices: none -> 263 us  [the longest x42 258 us: swap(): return lax.ppermute(values, 'wide', [(i, i ^ mask) for i in range(PLANE)])]
    unnamed x24 -> x9, waiting for transfers between devices: 154 us -> 0.81 us
    all_gather x2 -> x0, blocking collectives: 81.3 us -> none  [the longest x1 65.1 us: on_device(): lax.all_gather(jnp.stack([norm_gain1, norm_gain2]), every, axis=1, tiled=...]
    ppermute x0 -> x51, starting transfers between devices: none -> 55.2 us  [the longest x42 50.9 us: swap(): return lax.ppermute(values, 'wide', [(i, i ^ mask) for i in range(PLANE)])]
    dot_general x8 -> x6, matrix products: 100 us -> 58 us  [matmul_nt(): lax.dot_general(left, right, (((1,), (1,)), ((), ())), preferred_element_...]
    convert_element_type x6 -> x11, other arithmetic: 8.16 us -> 32.6 us  [the longest x4 22.7 us: reduce_spread(): total = (mine.astype(f32) + other.astype(f32)).astype(values.dtype)]
  transfers between devices with their start and end apart: 26 -> 62, of which waited for: 18 -> 31; matrix products, arithmetic and copies ran while one was open for 18% -> 25% of each run, Pallas kernels for 4% -> 2%
where the time goes in v2:
time: 893 us; the launch traced here: 886 us
  waiting for transfers between devices  368 us (41%)
  matrix products  184 us (21%)
  local copies, waits for them, and re-layouts  89.8 us (10%)
  other arithmetic  72.2 us (8%)
  starting transfers between devices  63.4 us (7%)
  Pallas kernels  53.2 us (6%)
  blocking collectives  38 us (4%)
  between operations  16.6 us (2%)
    ppermute x42, waiting for transfers between devices, swap(): return lax.ppermute(values, 'wide', [(i, i ^ mask) for i in range(PLANE)])  258 us
    reduce_scatter x5, waiting for transfers between devices, reduce_spread(): return lax.psum_scatter(flat, 'narrow', scatter_dimension=0, tiled=True)  91 us
    dot_general x8, matrix products, matmul_low(): return jnp.dot(left, right, preferred_element_type=jnp.float32)  70.9 us
    dot_general x6, matrix products, matmul_nt(): lax.dot_general(left, right, (((1,), (1,)), ((), ())), preferred_element_...  58 us
    dot_general x6, matrix products, matmul_tn(): lax.dot_general(left, right, (((0,), (0,)), ((), ())), preferred_element_...  55.5 us
    ppermute x42, starting transfers between devices, swap(): return lax.ppermute(values, 'wide', [(i, i ^ mask) for i in range(PLANE)])  50.9 us
    all_to_all x2, blocking collectives, gather_columns(): part = lax.all_to_all(blocks, 'wide', 0, 0, tiled=False)  38 us
    pallas_call x1, Pallas kernels, lru_backward(): pl.pallas_call(functools.partial(lru_backward_kernel, seqs), grid=(pl.cdi...  34.9 us
  transfers between devices with their start and end apart: 62, of which 31 were waited for; matrix products, arithmetic and copies ran while one was open for 25% of the time, Pallas kernels for 2%

profile of v2, /device:TPU:0, one launch (start us, length us, event | category | flops | bytes accessed | tf_op | source)
XLA Modules:
  0.0 885.9 jit_solution(929099323982103350)
XLA Ops:
  17.3 16.0 %all_to_all.40 = bf16[4,64,1408]{2,1,0:T(8,128)(2,1)} all-to-all(bf16[4,64,1408]{2,1,0:T(8,128)(2,1)S(1)} %copy.124), channel_id=1, replica_groups=mesh['wide'=4,'rest'=2,'narrow'=4] {'wide'}, dimensions={0} | all-to-all | bytes 1441792 | tf_op jit(solution)/shard_map/all_to_all | solution.py:284
  36.5 22.0 %all_to_all.41 = bf16[4,64,3072]{2,1,0:T(8,128)(2,1)} all-to-all(bf16[4,64,3072]{2,1,0:T(8,128)(2,1)S(1)} %copy.126), channel_id=1, replica_groups=mesh['wide'=4,'rest'=2,'narrow'=4] {'wide'}, dimensions={0} | all-to-all | bytes 3145728 | tf_op jit(solution)/shard_map/all_to_all | solution.py:284
  60.1 26.2 %collective-permute-done = bf16[320,2048]{1,0:T(8,128)(2,1)S(1)} collective-permute-done((bf16[320,2048]{1,0:T(8,128)(2,1)S(1)}, bf16[320,2048]{1,0:T(8,128)(2,1)S(1)}, u32[]{:S(2)}, u32[]{:S(2)}) %collective-permute-start) | collective-permute-done | bytes 1310752 | tf_op jit(solution)/shard_map/ppermute | solution.py:261
  89.6 11.7 %collective-permute-done.1 = bf16[160,2048]{1,0:T(8,128)(2,1)S(1)} collective-permute-done((bf16[160,2048]{1,0:T(8,128)(2,1)S(1)}, bf16[160,2048]{1,0:T(8,128)(2,1)S(1)}, u32[]{:S(2)}, u32[]{:S(2)}) %collective-permute-start.1) | collective-permute-done | bytes 655392 | tf_op jit(solution)/shard_map/ppermute | solution.py:261
  105.7 10.9 %all-gather.7.cloned.1.call-done = bf16[2048,1408]{1,0:T(8,128)(2,1)} async-done(((bf16[256,1408]{1,0:T(8,128)(2,1)}), bf16[2048,1408]{1,0:T(8,128)(2,1)}) %all-gather.7.cloned.1.call-update) | async-done | bytes 5767184 | tf_op jit(solution)/shard_map/all_gather | solution.py:286
  116.6 3.1 copy.125
  120.3 8.1 fusion.32
  128.5 2.7 pad_slice_fusion.5
  131.2 3.2 fusion.21.conv_ref
  134.4 3.5 convolution_add_fusion.3.rate_ref
  137.9 3.5 convolution_add_fusion.2.input_ref
  141.4 7.8 fusion.30.gate_ref
  149.2 18.3 %lru_forward.1 = (f32[1280,640]{1,0:T(8,128)}, bf16[1280,640]{1,0:T(8,128)(2,1)S(1)}) custom-call(bf16[1280,640]{1,0:T(8,128)(2,1)S(1)} %fusion.21.conv_ref, f32[1280,640]{1,0:T(8,128)} %convolution_add_fusion.3.rate_ref, f32[1280,640]{1,0:T(8,128)} %convolution_add_fusion.2.input_ref, f32[1280,640]{1,0:T(8,128)} %fusion.30.gate_ref, ...), custom_call_target="tpu_custom_call" | custom-call | tf_op jit(solution)/shard_map/lru_forward/pallas_call | solution.py:193
  167.5 4.6 convolution_convert_fusion.6
  176.7 13.4 %collective-permute-done.5 = bf16[160,2048]{1,0:T(8,128)(2,1)S(1)} collective-permute-done((bf16[160,2048]{1,0:T(8,128)(2,1)S(1)}, bf16[160,2048]{1,0:T(8,128)(2,1)S(1)}, u32[]{:S(2)}, u32[]{:S(2)}) %collective-permute-start.5) | collective-permute-done | bytes 655392 | tf_op jit(solution)/shard_map/ppermute | solution.py:261
  194.2 10.0 %collective-permute-done.4 = bf16[160,2048]{1,0:T(8,128)(2,1)S(1)} collective-permute-done((bf16[160,2048]{1,0:T(8,128)(2,1)S(1)}, bf16[160,2048]{1,0:T(8,128)(2,1)S(1)}, u32[]{:S(2)}, u32[]{:S(2)}) %collective-permute-start.4) | collective-permute-done | bytes 655392 | tf_op jit(solution)/shard_map/ppermute | solution.py:261
  205.6 2.5 collective-permute-done.6
  210.1 22.2 %collective-permute-done.20 = bf16[320,2048]{1,0:T(8,128)(2,1)S(1)} collective-permute-done((bf16[320,2048]{1,0:T(8,128)(2,1)S(1)}, bf16[320,2048]{1,0:T(8,128)(2,1)S(1)}, u32[]{:S(2)}, u32[]{:S(2)}) %collective-permute-start.20) | collective-permute-done | bytes 1310752 | tf_op jit(solution)/shard_map/ppermute | solution.py:261
  237.7 12.5 %collective-permute-done.9 = bf16[160,2048]{1,0:T(8,128)(2,1)S(1)} collective-permute-done((bf16[160,2048]{1,0:T(8,128)(2,1)S(1)}, bf16[160,2048]{1,0:T(8,128)(2,1)S(1)}, u32[]{:S(2)}, u32[]{:S(2)}) %collective-permute-start.9) | collective-permute-done | bytes 655392 | tf_op jit(solution)/shard_map/ppermute | solution.py:261
  254.9 9.3 %collective-permute-done.21 = bf16[160,2048]{1,0:T(8,128)(2,1)S(1)} collective-permute-done((bf16[160,2048]{1,0:T(8,128)(2,1)S(1)}, bf16[160,2048]{1,0:T(8,128)(2,1)S(1)}, u32[]{:S(2)}, u32[]{:S(2)}) %collective-permute-start.21) | collective-permute-done | bytes 655392 | tf_op jit(solution)/shard_map/ppermute | solution.py:261
  264.9 22.8 %collective-permute-done.10 = bf16[320,2048]{1,0:T(8,128)(2,1)S(1)} collective-permute-done((bf16[320,2048]{1,0:T(8,128)(2,1)S(1)}, bf16[320,2048]{1,0:T(8,128)(2,1)S(1)}, u32[]{:S(2)}, u32[]{:S(2)}) %collective-permute-start.10) | collective-permute-done | bytes 1310752 | tf_op jit(solution)/shard_map/ppermute | solution.py:261
  293.5 14.0 %fusion.74 = f32[1280,1536]{1,0:T(8,128)} fusion(bf16[1280,2048]{1,0:T(8,128)(2,1)} %copy-done.43, bf16[1536,2048]{1,0:T(8,128)(2,1)} %all-gather.11.cloned.1.call-done), kind=kOutput, calls=%fused_computation.217 | convolution fusion | flops 8053063680 | bytes 19398656 | tf_op jit(solution)/shard_map/dot_general | solution.py:24
  314.3 6.3 copy.127
  320.6 4.6 copy-done.19
  325.2 12.6 %fusion.5 = f32[1280,1536]{1,0:T(8,128)} fusion(bf16[1280,2048]{1,0:T(8,128)(2,1)} %constant_dynamic-update-slice_fusion.5, bf16[2048,3072]{1,0:T(8,128)(2,1)S(1)} %bitcast.188), kind=kOutput, calls=%fused_computation.21 | convolution fusion | flops 8053063680 | bytes 19398656 | tf_op jit(solution)/shard_map/dot_general | solution.py:20
  337.8 22.3 %multiply_convert_fusion.1 = (bf16[1280,1536]{1,0:T(8,128)(2,1)S(1)}, bf16[1280,1536]{1,0:T(8,128)(2,1)}, bf16[1280,1536]{1,0:T(8,128)(2,1)}) fusion(f32[1280,1536]{1,0:T(8,128)} %fusion.74, f32[1280,1536]{1,0:T(8,128)} %fusion.5, bf16[1280,2048]{1,0:T(8,128)(2,1)} %constant_dynamic-update-slice_fusion.5, bf16[2048,3072]{1,0:T(8,128)(2,1)} %bitcast.189), kind=kOutput, calls=%fused_computation.10 | convolution fusion | flops 8100249600 | bytes 39059456 | tf_op jit(solution)/shard_map/dot_general | solution.py:20
  360.1 21.9 %convolution_convert_fusion.4 = bf16[1280,2048]{1,0:T(8,128)(2,1)S(1)} fusion(bf16[2048,3072]{1,0:T(8,128)(2,1)} %bitcast.190, bf16[1280,1536]{1,0:T(8,128)(2,1)} %get-tuple-element.127, bf16[1280,1536]{1,0:T(8,128)(2,1)S(1)} %get-tuple-element.126), kind=kOutput, calls=%fused_computation.18 | convolution fusion | flops 16124477440 | bytes 25690112 | tf_op jit(solution)/shard_map/dot_general | solution.py:24
  385.9 14.2 %collective-permute-done.25 = bf16[160,2048]{1,0:T(8,128)(2,1)S(1)} collective-permute-done((bf16[160,2048]{1,0:T(8,128)(2,1)S(1)}, bf16[160,2048]{1,0:T(8,128)(2,1)S(1)}, u32[]{:S(2)}, u32[]{:S(2)}) %collective-permute-start.25) | collective-permute-done | bytes 655392 | tf_op jit(solution)/shard_map/ppermute | solution.py:261
  402.4 9.8 %collective-permute-done.24 = bf16[160,2048]{1,0:T(8,128)(2,1)S(1)} collective-permute-done((bf16[160,2048]{1,0:T(8,128)(2,1)S(1)}, bf16[160,2048]{1,0:T(8,128)(2,1)S(1)}, u32[]{:S(2)}, u32[]{:S(2)}) %collective-permute-start.24) | collective-permute-done | bytes 655392 | tf_op jit(solution)/shard_map/ppermute | solution.py:261
  412.1 5.9 collective-permute-done.26
  420.0 7.7 collective-permute-done.29
  432.4 2.5 collective-permute-start.30
  436.3 24.0 %collective-permute-done.30 = bf16[320,2048]{1,0:T(8,128)(2,1)S(1)} collective-permute-done((bf16[320,2048]{1,0:T(8,128)(2,1)S(1)}, bf16[320,2048]{1,0:T(8,128)(2,1)S(1)}, u32[]{:S(2)}, u32[]{:S(2)}) %collective-permute-start.30) | collective-permute-done | bytes 1310752 | tf_op jit(solution)/shard_map/ppermute | solution.py:261
  464.2 23.8 %convolution_convert_fusion = bf16[2048,3072]{1,0:T(8,128)(2,1)} fusion(bf16[1280,2048]{1,0:T(8,128)(2,1)} %constant_dynamic-update-slice_fusion.5, bf16[1280,1536]{1,0:T(8,128)(2,1)} %get-tuple-element.127, bf16[1280,1536]{1,0:T(8,128)(2,1)} %copy-done.73), kind=kOutput, calls=%fused_computation.4 | convolution fusion | flops 16128147456 | bytes 25690112 | tf_op jit(solution)/shard_map/dot_general | solution.py:28
  490.5 5.9 fusion.37.grad_ref
  496.4 34.9 %lru_backward.1 = (f32[1280,640]{1,0:T(8,128)}, bf16[1280,640]{1,0:T(8,128)(2,1)S(1)}, bf16[1280,640]{1,0:T(8,128)(2,1)S(1)}, bf16[1280,640]{1,0:T(8,128)(2,1)S(1)}, f32[24,640]{1,0:T(8,128)S(1)}) custom-call(bf16[1280,640]{1,0:T(8,128)(2,1)} %copy-done, f32[1280,640]{1,0:T(8,128)} %convolution_add_fusion.3.rate_ref, ...), custom_call_target="tpu_custom_call" | custom-call | tf_op jit(solution)/shard_map/lru_backward/pallas_call | solution.py:211
  531.4 4.9 convolution_add_fusion.1
  540.9 3.4 fusion.67
  544.3 10.3 %convolution_convert_fusion.2 = bf16[2048,1280]{1,0:T(8,128)(2,1)S(1)} fusion(bf16[1280,640]{1,0:T(8,128)(2,1)S(1)} %get-tuple-element.129, bf16[1280,640]{1,0:T(8,128)(2,1)S(1)} %get-tuple-element.26, bf16[1280,2048]{1,0:T(8,128)(2,1)} %copy-done.23, f32[2048]{0:T(1024)S(1)} %copy-done.48, f32[1280]{0:T(1024)S(1)} %copy-done.69), kind=kOutput, calls=%fused_computation.16 | convolution fusion | flops 6730547200 | bytes 13775872 | tf_op jit(solution)/shard_map/dot_general | solution.py:28
  558.2 11.2 %constant_dynamic-slice_fusion.4 = (bf16[4,1,4,64,3072]{4,3,2,1,0:T(8,128)(2,1)}, bf16[4,1,4,64,3072]{4,3,2,1,0:T(8,128)(2,1)}) fusion(bf16[4,2,4,64,3072]{4,3,2,1,0:T(8,128)(2,1)} %bitcast.187, s32[]{:T(128)S(6)} %select_n.63, s32[]{:T(128)S(6)} %select_n.64), kind=kLoop, calls=%fused_computation.172 | loop fusion | bytes 25165832 | tf_op jit(solution)/shard_map/jit(dynamic_index_in_dim)/dynamic_slice | solution.py:294
  569.5 6.2 copy.156
  583.4 3.2 collective-permute-done.47
  588.6 4.8 fusion.11
  593.4 10.2 %fusion = bf16[4,4,64,3072]{3,2,1,0:T(8,128)(2,1)} fusion(bf16[4,4,64,3072]{3,2,1,0:T(8,128)(2,1)} %collective-permute-done.49, bf16[4,1,4,64,3072]{4,3,2,1,0:T(8,128)(2,1)} %get-tuple-element.130), kind=kLoop, calls=%fused_computation.3 | loop fusion | flops 12582912 | bytes 18874368 | tf_op jit(solution)/shard_map/convert_element_type | solution.py:296
  603.7 11.8 %convolution_convert_fusion.1 = bf16[1536,2048]{1,0:T(8,128)(2,1)S(1)} fusion(bf16[1280,1536]{1,0:T(8,128)(2,1)} %get-tuple-element.128, bf16[1280,2048]{1,0:T(8,128)(2,1)} %copy-done.43), kind=kOutput, calls=%fused_computation.15 | convolution fusion | flops 8056209408 | bytes 15466496 | tf_op jit(solution)/shard_map/dot_general | solution.py:28
  617.4 2.7 copy-done.24
  620.5 6.7 convolution_convert_fusion.7
  627.5 8.6 convolution_convert_fusion.5
  644.3 9.3 %convolution_convert_fusion.3 = bf16[1280,2048]{1,0:T(8,128)(2,1)S(1)} fusion(bf16[2048,1408]{1,0:T(8,128)(2,1)} %bitcast.196, bf16[1280,640]{1,0:T(8,128)(2,1)S(1)} %copy-done.31, bf16[1280,640]{1,0:T(8,128)(2,1)S(1)} %get-tuple-element.26), kind=kOutput, calls=%fused_computation.17 | convolution fusion | flops 6720061440 | bytes 13762560 | tf_op jit(solution)/shard_map/dot_general | solution.py:24
  656.4 6.2 fusion.9
  667.4 17.7 %collective-permute-done.35 = bf16[160,2048]{1,0:T(8,128)(2,1)} collective-permute-done((bf16[160,2048]{1,0:T(8,128)(2,1)}, bf16[160,2048]{1,0:T(8,128)(2,1)}, u32[]{:S(2)}, u32[]{:S(2)}) %collective-permute-start.35) | collective-permute-done | bytes 655392 | tf_op jit(solution)/shard_map/ppermute | solution.py:261
  691.0 3.6 convert_add_fusion.8
  694.7 4.3 collective-permute-done.34
  702.8 14.0 %collective-permute-done.36 = bf16[160,2048]{1,0:T(8,128)(2,1)} collective-permute-done((bf16[160,2048]{1,0:T(8,128)(2,1)}, bf16[160,2048]{1,0:T(8,128)(2,1)}, u32[]{:S(2)}, u32[]{:S(2)}) %collective-permute-start.36) | collective-permute-done | bytes 655392 | tf_op jit(solution)/shard_map/ppermute | solution.py:261
  719.9 11.0 %collective-permute-done.19 = bf16[160,2048]{1,0:T(8,128)(2,1)S(1)} collective-permute-done((bf16[160,2048]{1,0:T(8,128)(2,1)S(1)}, bf16[160,2048]{1,0:T(8,128)(2,1)S(1)}, u32[]{:S(2)}, u32[]{:S(2)}) %collective-permute-start.19) | collective-permute-done | bytes 655392 | tf_op jit(solution)/shard_map/ppermute | solution.py:261
  730.8 2.5 convert_add_fusion.7
  733.3 9.8 %collective-permute-done.39 = bf16[160,2048]{1,0:T(8,128)(2,1)S(1)} collective-permute-done((bf16[160,2048]{1,0:T(8,128)(2,1)S(1)}, bf16[160,2048]{1,0:T(8,128)(2,1)S(1)}, u32[]{:S(2)}, u32[]{:S(2)}) %collective-permute-start.39) | collective-permute-done | bytes 655392 | tf_op jit(solution)/shard_map/ppermute | solution.py:261
  755.6 3.5 all-to-all-start.2
  763.6 2.7 all-to-all-done.2
  766.3 8.3 reduce-scatter.12.cloned.1.call-done
  774.6 4.3 all-to-all-start.3
  779.0 6.0 fusion.27
  785.7 23.1 %reduce-scatter.10.cloned.1.call-done = bf16[80,2048]{1,0:T(8,128)(2,1)} async-done(((bf16[320,2048]{1,0:T(8,128)(2,1)}), bf16[80,2048]{1,0:T(8,128)(2,1)}) %reduce-scatter.10.cloned.1.call-update) | async-done | bytes 327696 | tf_op jit(solution)/shard_map/reduce_scatter | solution.py:300
  810.6 59.6 %reduce-scatter.14.cloned.1.call-done = bf16[192,2048]{1,0:T(8,128)(2,1)} async-done(((bf16[768,2048]{1,0:T(8,128)(2,1)}), bf16[192,2048]{1,0:T(8,128)(2,1)}) %reduce-scatter.14.cloned.1.call-update) | async-done | bytes 786448 | tf_op jit(solution)/shard_map/reduce_scatter | solution.py:300
  (390 shorter events, 155.0 us)
Async XLA Ops:
  7.2 96.8 %all-gather.5.cloned.1.call-start = ((), (), s32[]{:S(2)}) async-start(), calls=%async_computation.9 | async-start | bytes 3502080 | tf_op jit(solution)/shard_map/all_gather | solution.py:374
  14.8 101.8 %all-gather.7.cloned.1.call-start = ((), (), s32[]{:S(2)}) async-start(), calls=%async_computation.10 | async-start | bytes 6488064 | tf_op jit(solution)/shard_map/all_gather | solution.py:286
  33.4 260.2 %all-gather.11.cloned.1.call-start = ((), (), s32[]{:S(2)}) async-start(), calls=%async_computation.12 | async-start | bytes 7077888 | tf_op jit(solution)/shard_map/all_gather | solution.py:376
  34.1 280.2 %all-gather.9.cloned.1.call-start = ((), (), s32[]{:S(2)}) async-start(), calls=%async_computation.11 | async-start | bytes 14155776 | tf_op jit(solution)/shard_map/all_gather | solution.py:286
  58.5 687.8 %reduce-scatter.8.cloned.1.call-start = ((), (), s32[]{:S(2)}) async-start(), calls=%async_computation.14 | async-start | bytes 614400 | tf_op jit(solution)/shard_map/reduce_scatter | solution.py:300
  58.6 27.7 %collective-permute-start = (bf16[320,2048]{1,0:T(8,128)(2,1)S(1)}, bf16[320,2048]{1,0:T(8,128)(2,1)S(1)}, u32[]{:S(2)}, u32[]{:S(2)}) collective-permute-start(bf16[320,2048]{1,0:T(8,128)(2,1)S(1)} %copy-done.16), channel_id=1, source_target_pairs={{0,8},{8,0},{16,24},{24,16},{1,9},{9,1},{17,25},{25,17},{2,10},{10... | collective-permute-start | bytes 3932168 | tf_op jit(solution)/shard_map/ppermute | solution.py:261
  59.5 29.3 %collective-permute-start.2 = (bf16[320,2048]{1,0:T(8,128)(2,1)S(1)}, bf16[320,2048]{1,0:T(8,128)(2,1)S(1)}, u32[]{:S(2)}, u32[]{:S(2)}) collective-permute-start(bf16[320,2048]{1,0:T(8,128)(2,1)S(1)} %copy-done.16), channel_id=1, source_target_pairs={{0,16},{8,24},{16,0},{24,8},{1,17},{9,25},{17,1},{25,9},{2,18},{10... | collective-permute-start | bytes 3932168 | tf_op jit(solution)/shard_map/ppermute | solution.py:261
  86.4 14.9 %collective-permute-start.1 = (bf16[160,2048]{1,0:T(8,128)(2,1)S(1)}, bf16[160,2048]{1,0:T(8,128)(2,1)S(1)}, u32[]{:S(2)}, u32[]{:S(2)}) collective-permute-start(bf16[160,2048]{1,0:T(8,128)(2,1)S(1)} %slice.370), channel_id=1, source_target_pairs={{0,16},{8,24},{16,0},{24,8},{1,17},{9,25},{17,1},{25,9},{2,18},{10... | collective-permute-start | bytes 1966088 | tf_op jit(solution)/shard_map/ppermute | solution.py:261
  88.9 12.4 %collective-permute-start.3 = (bf16[160,2048]{1,0:T(8,128)(2,1)S(1)}, bf16[160,2048]{1,0:T(8,128)(2,1)S(1)}, u32[]{:S(2)}, u32[]{:S(2)}) collective-permute-start(bf16[160,2048]{1,0:T(8,128)(2,1)S(1)} %slice.371), channel_id=1, source_target_pairs={{0,8},{8,0},{16,24},{24,16},{1,9},{9,1},{17,25},{25,17},{2,10},{10... | collective-permute-start | bytes 1966088 | tf_op jit(solution)/shard_map/ppermute | solution.py:261
  120.3 311.2 %copy-start.36 = (f32[2048]{0:T(1024)}, f32[2048]{0:T(1024)S(1)}, u32[]{:S(2)}) copy-start(f32[2048]{0:T(1024)S(1)} %get-tuple-element.99) | copy-start | bytes 24580
  172.5 17.6 %collective-permute-start.5 = (bf16[160,2048]{1,0:T(8,128)(2,1)S(1)}, bf16[160,2048]{1,0:T(8,128)(2,1)S(1)}, u32[]{:S(2)}, u32[]{:S(2)}) collective-permute-start(bf16[160,2048]{1,0:T(8,128)(2,1)S(1)} %get-tuple-element.157), channel_id=1, source_target_pairs={{0,8},{8,0},{16,24},{24,16},{1,9},{9,1},{17,25},{25,17},{2,10},{10... | collective-permute-start | bytes 1966088 | tf_op jit(solution)/shard_map/ppermute | solution.py:261
  174.6 29.6 %collective-permute-start.4 = (bf16[160,2048]{1,0:T(8,128)(2,1)S(1)}, bf16[160,2048]{1,0:T(8,128)(2,1)S(1)}, u32[]{:S(2)}, u32[]{:S(2)}) collective-permute-start(bf16[160,2048]{1,0:T(8,128)(2,1)S(1)} %get-tuple-element.154), channel_id=1, source_target_pairs={{0,8},{8,0},{16,24},{24,16},{1,9},{9,1},{17,25},{25,17},{2,10},{10... | collective-permute-start | bytes 1966088 | tf_op jit(solution)/shard_map/ppermute | solution.py:261
  175.3 30.2 %collective-permute-start.7 = (bf16[160,2048]{1,0:T(8,128)(2,1)S(1)}, bf16[160,2048]{1,0:T(8,128)(2,1)S(1)}, u32[]{:S(2)}, u32[]{:S(2)}) collective-permute-start(bf16[160,2048]{1,0:T(8,128)(2,1)S(1)} %get-tuple-element.156), channel_id=1, source_target_pairs={{0,16},{8,24},{16,0},{24,8},{1,17},{9,25},{17,1},{25,9},{2,18},{10... | collective-permute-start | bytes 1966088 | tf_op jit(solution)/shard_map/ppermute | solution.py:261
  190.3 17.7 %collective-permute-start.6 = (bf16[160,2048]{1,0:T(8,128)(2,1)S(1)}, bf16[160,2048]{1,0:T(8,128)(2,1)S(1)}, u32[]{:S(2)}, u32[]{:S(2)}) collective-permute-start(bf16[160,2048]{1,0:T(8,128)(2,1)S(1)} %add_convert_fusion.7), channel_id=1, source_target_pairs={{0,16},{8,24},{16,0},{24,8},{1,17},{9,25},{17,1},{25,9},{2,18},{10... | collective-permute-start | bytes 1966088 | tf_op jit(solution)/shard_map/ppermute | solution.py:261
  191.8 239.7 %copy-start.51 = (f32[320]{0:T(512)}, f32[320]{0:T(512)S(1)}, u32[]{:S(2)}) copy-start(f32[320]{0:T(512)S(1)} %fusion.50) | copy-start | bytes 3844
  192.1 40.2 %collective-permute-start.20 = (bf16[320,2048]{1,0:T(8,128)(2,1)S(1)}, bf16[320,2048]{1,0:T(8,128)(2,1)S(1)}, u32[]{:S(2)}, u32[]{:S(2)}) collective-permute-start(bf16[320,2048]{1,0:T(8,128)(2,1)S(1)} %multiply_convert_fusion.3), channel_id=1, source_target_pairs={{0,8},{8,0},{16,24},{24,16},{1,9},{9,1},{17,25},{25,17},{2,10},{10... | collective-permute-start | bytes 3932168 | tf_op jit(solution)/shard_map/ppermute | solution.py:261
  193.6 42.6 %collective-permute-start.22 = (bf16[320,2048]{1,0:T(8,128)(2,1)S(1)}, bf16[320,2048]{1,0:T(8,128)(2,1)S(1)}, u32[]{:S(2)}, u32[]{:S(2)}) collective-permute-start(bf16[320,2048]{1,0:T(8,128)(2,1)S(1)} %multiply_convert_fusion.3), channel_id=1, source_target_pairs={{0,16},{8,24},{16,0},{24,8},{1,17},{9,25},{17,1},{25,9},{2,18},{10... | collective-permute-start | bytes 3932168 | tf_op jit(solution)/shard_map/ppermute | solution.py:261
  204.2 46.0 %collective-permute-start.9 = (bf16[160,2048]{1,0:T(8,128)(2,1)S(1)}, bf16[160,2048]{1,0:T(8,128)(2,1)S(1)}, u32[]{:S(2)}, u32[]{:S(2)}) collective-permute-start(bf16[160,2048]{1,0:T(8,128)(2,1)S(1)} %get-tuple-element.155), channel_id=1, source_target_pairs={{0,16},{8,24},{16,0},{24,8},{1,17},{9,25},{17,1},{25,9},{2,18},{10... | collective-permute-start | bytes 1966088 | tf_op jit(solution)/shard_map/ppermute | solution.py:261
  208.6 41.6 %collective-permute-start.8 = (bf16[160,2048]{1,0:T(8,128)(2,1)S(1)}, bf16[160,2048]{1,0:T(8,128)(2,1)S(1)}, u32[]{:S(2)}, u32[]{:S(2)}) collective-permute-start(bf16[160,2048]{1,0:T(8,128)(2,1)S(1)} %get-tuple-element.153), channel_id=1, source_target_pairs={{0,8},{8,0},{16,24},{24,16},{1,9},{9,1},{17,25},{25,17},{2,10},{10... | collective-permute-start | bytes 1966088 | tf_op jit(solution)/shard_map/ppermute | solution.py:261
  232.3 31.9 %collective-permute-start.21 = (bf16[160,2048]{1,0:T(8,128)(2,1)S(1)}, bf16[160,2048]{1,0:T(8,128)(2,1)S(1)}, u32[]{:S(2)}, u32[]{:S(2)}) collective-permute-start(bf16[160,2048]{1,0:T(8,128)(2,1)S(1)} %slice.405), channel_id=1, source_target_pairs={{0,16},{8,24},{16,0},{24,8},{1,17},{9,25},{17,1},{25,9},{2,18},{10... | collective-permute-start | bytes 1966088 | tf_op jit(solution)/shard_map/ppermute | solution.py:261
  236.2 28.1 %collective-permute-start.23 = (bf16[160,2048]{1,0:T(8,128)(2,1)S(1)}, bf16[160,2048]{1,0:T(8,128)(2,1)S(1)}, u32[]{:S(2)}, u32[]{:S(2)}) collective-permute-start(bf16[160,2048]{1,0:T(8,128)(2,1)S(1)} %slice.406), channel_id=1, source_target_pairs={{0,8},{8,0},{16,24},{24,16},{1,9},{9,1},{17,25},{25,17},{2,10},{10... | collective-permute-start | bytes 1966088 | tf_op jit(solution)/shard_map/ppermute | solution.py:261
  252.0 35.8 %collective-permute-start.10 = (bf16[320,2048]{1,0:T(8,128)(2,1)S(1)}, bf16[320,2048]{1,0:T(8,128)(2,1)S(1)}, u32[]{:S(2)}, u32[]{:S(2)}) collective-permute-start(bf16[320,2048]{1,0:T(8,128)(2,1)S(1)} %multiply_convert_fusion.4), channel_id=1, source_target_pairs={{0,8},{8,0},{16,24},{24,16},{1,9},{9,1},{17,25},{25,17},{2,10},{10... | collective-permute-start | bytes 3932168 | tf_op jit(solution)/shard_map/ppermute | solution.py:261
  253.5 36.6 %collective-permute-start.12 = (bf16[320,2048]{1,0:T(8,128)(2,1)S(1)}, bf16[320,2048]{1,0:T(8,128)(2,1)S(1)}, u32[]{:S(2)}, u32[]{:S(2)}) collective-permute-start(bf16[320,2048]{1,0:T(8,128)(2,1)S(1)} %multiply_convert_fusion.4), channel_id=1, source_target_pairs={{0,16},{8,24},{16,0},{24,8},{1,17},{9,25},{17,1},{25,9},{2,18},{10... | collective-permute-start | bytes 3932168 | tf_op jit(solution)/shard_map/ppermute | solution.py:261
  288.7 18.8 %collective-permute-start.11 = (bf16[160,2048]{1,0:T(8,128)(2,1)}, bf16[160,2048]{1,0:T(8,128)(2,1)S(1)}, u32[]{:S(2)}, u32[]{:S(2)}) collective-permute-start(bf16[160,2048]{1,0:T(8,128)(2,1)} %slice.393), channel_id=1, source_target_pairs={{0,16},{8,24},{16,0},{24,8},{1,17},{9,25},{17,1},{25,9},{2,18},{10... | collective-permute-start | bytes 1966088 | tf_op jit(solution)/shard_map/ppermute | solution.py:261
  292.1 16.4 %collective-permute-start.13 = (bf16[160,2048]{1,0:T(8,128)(2,1)}, bf16[160,2048]{1,0:T(8,128)(2,1)}, u32[]{:S(2)}, u32[]{:S(2)}) collective-permute-start(bf16[160,2048]{1,0:T(8,128)(2,1)} %slice.394), channel_id=1, source_target_pairs={{0,8},{8,0},{16,24},{24,16},{1,9},{9,1},{17,25},{25,17},{2,10},{10... | collective-permute-start | bytes 1966088 | tf_op jit(solution)/shard_map/ppermute | solution.py:261
  382.3 17.7 %collective-permute-start.25 = (bf16[160,2048]{1,0:T(8,128)(2,1)S(1)}, bf16[160,2048]{1,0:T(8,128)(2,1)S(1)}, u32[]{:S(2)}, u32[]{:S(2)}) collective-permute-start(bf16[160,2048]{1,0:T(8,128)(2,1)S(1)} %get-tuple-element.145), channel_id=1, source_target_pairs={{0,8},{8,0},{16,24},{24,16},{1,9},{9,1},{17,25},{25,17},{2,10},{10... | collective-permute-start | bytes 1966088 | tf_op jit(solution)/shard_map/ppermute | solution.py:261
  383.7 28.4 %collective-permute-start.24 = (bf16[160,2048]{1,0:T(8,128)(2,1)S(1)}, bf16[160,2048]{1,0:T(8,128)(2,1)S(1)}, u32[]{:S(2)}, u32[]{:S(2)}) collective-permute-start(bf16[160,2048]{1,0:T(8,128)(2,1)S(1)} %get-tuple-element.142), channel_id=1, source_target_pairs={{0,8},{8,0},{16,24},{24,16},{1,9},{9,1},{17,25},{25,17},{2,10},{10... | collective-permute-start | bytes 1966088 | tf_op jit(solution)/shard_map/ppermute | solution.py:261
  384.4 27.7 %collective-permute-start.27 = (bf16[160,2048]{1,0:T(8,128)(2,1)S(1)}, bf16[160,2048]{1,0:T(8,128)(2,1)S(1)}, u32[]{:S(2)}, u32[]{:S(2)}) collective-permute-start(bf16[160,2048]{1,0:T(8,128)(2,1)S(1)} %get-tuple-element.144), channel_id=1, source_target_pairs={{0,16},{8,24},{16,0},{24,8},{1,17},{9,25},{17,1},{25,9},{2,18},{10... | collective-permute-start | bytes 1966088 | tf_op jit(solution)/shard_map/ppermute | solution.py:261
  400.3 17.7 %collective-permute-start.26 = (bf16[160,2048]{1,0:T(8,128)(2,1)S(1)}, bf16[160,2048]{1,0:T(8,128)(2,1)S(1)}, u32[]{:S(2)}, u32[]{:S(2)}) collective-permute-start(bf16[160,2048]{1,0:T(8,128)(2,1)S(1)} %add_convert_fusion.3), channel_id=1, source_target_pairs={{0,16},{8,24},{16,0},{24,8},{1,17},{9,25},{17,1},{25,9},{2,18},{10... | collective-permute-start | bytes 1966088 | tf_op jit(solution)/shard_map/ppermute | solution.py:261
  401.8 25.8 %collective-permute-start.29 = (bf16[160,2048]{1,0:T(8,128)(2,1)S(1)}, bf16[160,2048]{1,0:T(8,128)(2,1)S(1)}, u32[]{:S(2)}, u32[]{:S(2)}) collective-permute-start(bf16[160,2048]{1,0:T(8,128)(2,1)S(1)} %get-tuple-element.143), channel_id=1, source_target_pairs={{0,16},{8,24},{16,0},{24,8},{1,17},{9,25},{17,1},{25,9},{2,18},{10... | collective-permute-start | bytes 1966088 | tf_op jit(solution)/shard_map/ppermute | solution.py:261
  418.6 11.3 %collective-permute-start.28 = (bf16[160,2048]{1,0:T(8,128)(2,1)S(1)}, bf16[160,2048]{1,0:T(8,128)(2,1)S(1)}, u32[]{:S(2)}, u32[]{:S(2)}) collective-permute-start(bf16[160,2048]{1,0:T(8,128)(2,1)S(1)} %get-tuple-element.141), channel_id=1, source_target_pairs={{0,8},{8,0},{16,24},{24,16},{1,9},{9,1},{17,25},{25,17},{2,10},{10... | collective-permute-start | bytes 1966088 | tf_op jit(solution)/shard_map/ppermute | solution.py:261
  432.4 28.0 %collective-permute-start.30 = (bf16[320,2048]{1,0:T(8,128)(2,1)S(1)}, bf16[320,2048]{1,0:T(8,128)(2,1)S(1)}, u32[]{:S(2)}, u32[]{:S(2)}) collective-permute-start(bf16[320,2048]{1,0:T(8,128)(2,1)S(1)} %fusion.63), channel_id=1, source_target_pairs={{0,8},{8,0},{16,24},{24,16},{1,9},{9,1},{17,25},{25,17},{2,10},{10... | collective-permute-start | bytes 3932168 | tf_op jit(solution)/shard_map/ppermute | solution.py:261
  434.8 26.8 %collective-permute-start.32 = (bf16[320,2048]{1,0:T(8,128)(2,1)S(1)}, bf16[320,2048]{1,0:T(8,128)(2,1)}, u32[]{:S(2)}, u32[]{:S(2)}) collective-permute-start(bf16[320,2048]{1,0:T(8,128)(2,1)S(1)} %fusion.63), channel_id=1, source_target_pairs={{0,16},{8,24},{16,0},{24,8},{1,17},{9,25},{17,1},{25,9},{2,18},{10... | collective-permute-start | bytes 3932168 | tf_op jit(solution)/shard_map/ppermute | solution.py:261
  460.4 27.6 %collective-permute-start.31 = (bf16[160,2048]{1,0:T(8,128)(2,1)S(1)}, bf16[160,2048]{1,0:T(8,128)(2,1)S(1)}, u32[]{:S(2)}, u32[]{:S(2)}) collective-permute-start(bf16[160,2048]{1,0:T(8,128)(2,1)S(1)} %slice.415), channel_id=1, source_target_pairs={{0,16},{8,24},{16,0},{24,8},{1,17},{9,25},{17,1},{25,9},{2,18},{10... | collective-permute-start | bytes 1966088 | tf_op jit(solution)/shard_map/ppermute | solution.py:261
  462.8 25.2 %collective-permute-start.33 = (bf16[160,2048]{1,0:T(8,128)(2,1)S(1)}, bf16[160,2048]{1,0:T(8,128)(2,1)S(1)}, u32[]{:S(2)}, u32[]{:S(2)}) collective-permute-start(bf16[160,2048]{1,0:T(8,128)(2,1)S(1)} %slice.416), channel_id=1, source_target_pairs={{0,8},{8,0},{16,24},{24,16},{1,9},{9,1},{17,25},{25,17},{2,10},{10... | collective-permute-start | bytes 1966088 | tf_op jit(solution)/shard_map/ppermute | solution.py:261
  558.2 30.3 %collective-permute-start.46 = (bf16[4,4,64,1280]{3,2,1,0:T(8,128)(2,1)}, bf16[4,4,64,1280]{3,2,1,0:T(8,128)(2,1)}, u32[]{:S(2)}, u32[]{:S(2)}) collective-permute-start(bf16[4,4,64,1280]{3,2,1,0:T(8,128)(2,1)} %bitcast.181), channel_id=1, source_target_pairs={{0,4},{4,0},{1,5},{5,1},{2,6},{6,2},{3,7},{7,3},{8,12},{12,8},{9,1... | collective-permute-start | bytes 7864328 | tf_op jit(solution)/shard_map/ppermute | solution.py:295
  575.6 17.8 %collective-permute-start.49 = (bf16[4,4,64,3072]{3,2,1,0:T(8,128)(2,1)}, bf16[4,4,64,3072]{3,2,1,0:T(8,128)(2,1)}, u32[]{:S(2)}, u32[]{:S(2)}) collective-permute-start(bf16[4,4,64,3072]{3,2,1,0:T(8,128)(2,1)} %bitcast.180), channel_id=1, source_target_pairs={{0,4},{4,0},{1,5},{5,1},{2,6},{6,2},{3,7},{7,3},{8,12},{12,8},{9,1... | collective-permute-start | bytes 18874376 | tf_op jit(solution)/shard_map/ppermute | solution.py:295
  583.3 3.3 collective-permute-start.47
  588.5 167.1 %reduce-scatter.6.cloned.1.call-start = ((), (), s32[]{:S(2)}) async-start(), calls=%async_computation.13 | async-start | bytes 3276800 | tf_op jit(solution)/shard_map/reduce_scatter | solution.py:300
  593.3 181.3 %reduce-scatter.12.cloned.1.call-start = ((), (), s32[]{:S(2)}) async-start(), calls=%async_computation.16 | async-start | bytes 7864320 | tf_op jit(solution)/shard_map/reduce_scatter | solution.py:300
  603.6 205.2 %reduce-scatter.10.cloned.1.call-start = ((), (), s32[]{:S(2)}) async-start(), calls=%async_computation.15 | async-start | bytes 1638400 | tf_op jit(solution)/shard_map/reduce_scatter | solution.py:300
  620.1 36.2 %collective-permute-start.50 = (bf16[4,192,2048]{2,1,0:T(8,128)(2,1)}, bf16[4,192,2048]{2,1,0:T(8,128)(2,1)}, u32[]{:S(2)}, u32[]{:S(2)}) collective-permute-start(bf16[4,192,2048]{2,1,0:T(8,128)(2,1)} %dynamic-slice_bitcast_fusion), channel_id=1, source_target_pairs={{0,4},{4,0},{1,5},{5,1},{2,6},{6,2},{3,7},{7,3},{8,12},{12,8},{9,1... | collective-permute-start | bytes 9437192 | tf_op jit(solution)/shard_map/ppermute | solution.py:295
  627.4 15.3 %collective-permute-start.48 = (bf16[4,80,2048]{2,1,0:T(8,128)(2,1)S(1)}, bf16[4,80,2048]{2,1,0:T(8,128)(2,1)S(1)}, u32[]{:S(2)}, u32[]{:S(2)}) collective-permute-start(bf16[4,80,2048]{2,1,0:T(8,128)(2,1)S(1)} %dynamic-slice_bitcast_fusion.1), channel_id=1, source_target_pairs={{0,4},{4,0},{1,5},{5,1},{2,6},{6,2},{3,7},{7,3},{8,12},{12,8},{9,1... | collective-permute-start | bytes 3932168 | tf_op jit(solution)/shard_map/ppermute | solution.py:295
  639.1 23.5 %collective-permute-start.15 = (bf16[160,2048]{1,0:T(8,128)(2,1)}, bf16[160,2048]{1,0:T(8,128)(2,1)}, u32[]{:S(2)}, u32[]{:S(2)}) collective-permute-start(bf16[160,2048]{1,0:T(8,128)(2,1)} %get-tuple-element.151), channel_id=1, source_target_pairs={{0,8},{8,0},{16,24},{24,16},{1,9},{9,1},{17,25},{25,17},{2,10},{10... | collective-permute-start | bytes 1966088 | tf_op jit(solution)/shard_map/ppermute | solution.py:261
  639.8 49.1 %collective-permute-start.14 = (bf16[160,2048]{1,0:T(8,128)(2,1)}, bf16[160,2048]{1,0:T(8,128)(2,1)}, u32[]{:S(2)}, u32[]{:S(2)}) collective-permute-start(bf16[160,2048]{1,0:T(8,128)(2,1)} %get-tuple-element.148), channel_id=1, source_target_pairs={{0,8},{8,0},{16,24},{24,16},{1,9},{9,1},{17,25},{25,17},{2,10},{10... | collective-permute-start | bytes 1966088 | tf_op jit(solution)/shard_map/ppermute | solution.py:261
  641.1 48.3 %collective-permute-start.17 = (bf16[160,2048]{1,0:T(8,128)(2,1)}, bf16[160,2048]{1,0:T(8,128)(2,1)}, u32[]{:S(2)}, u32[]{:S(2)}) collective-permute-start(bf16[160,2048]{1,0:T(8,128)(2,1)} %get-tuple-element.150), channel_id=1, source_target_pairs={{0,16},{8,24},{16,0},{24,8},{1,17},{9,25},{17,1},{25,9},{2,18},{10... | collective-permute-start | bytes 1966088 | tf_op jit(solution)/shard_map/ppermute | solution.py:261
  644.2 226.0 %reduce-scatter.14.cloned.1.call-start = ((), (), s32[]{:S(2)}) async-start(), calls=%async_computation.17 | async-start | bytes 3932160 | tf_op jit(solution)/shard_map/reduce_scatter | solution.py:300
  656.2 28.9 %collective-permute-start.35 = (bf16[160,2048]{1,0:T(8,128)(2,1)}, bf16[160,2048]{1,0:T(8,128)(2,1)}, u32[]{:S(2)}, u32[]{:S(2)}) collective-permute-start(bf16[160,2048]{1,0:T(8,128)(2,1)} %get-tuple-element.139), channel_id=1, source_target_pairs={{0,8},{8,0},{16,24},{24,16},{1,9},{9,1},{17,25},{25,17},{2,10},{10... | collective-permute-start | bytes 1966088 | tf_op jit(solution)/shard_map/ppermute | solution.py:261
  665.0 26.0 %collective-permute-start.16 = (bf16[160,2048]{1,0:T(8,128)(2,1)}, bf16[160,2048]{1,0:T(8,128)(2,1)}, u32[]{:S(2)}, u32[]{:S(2)}) collective-permute-start(bf16[160,2048]{1,0:T(8,128)(2,1)} %add_convert_fusion.5), channel_id=1, source_target_pairs={{0,16},{8,24},{16,0},{24,8},{1,17},{9,25},{17,1},{25,9},{2,18},{10... | collective-permute-start | bytes 1966088 | tf_op jit(solution)/shard_map/ppermute | solution.py:261
  666.1 32.9 %collective-permute-start.34 = (bf16[160,2048]{1,0:T(8,128)(2,1)S(1)}, bf16[160,2048]{1,0:T(8,128)(2,1)S(1)}, u32[]{:S(2)}, u32[]{:S(2)}) collective-permute-start(bf16[160,2048]{1,0:T(8,128)(2,1)S(1)} %get-tuple-element.136), channel_id=1, source_target_pairs={{0,8},{8,0},{16,24},{24,16},{1,9},{9,1},{17,25},{25,17},{2,10},{10... | collective-permute-start | bytes 1966088 | tf_op jit(solution)/shard_map/ppermute | solution.py:261
  685.1 17.8 %collective-permute-start.37 = (bf16[160,2048]{1,0:T(8,128)(2,1)S(1)}, bf16[160,2048]{1,0:T(8,128)(2,1)}, u32[]{:S(2)}, u32[]{:S(2)}) collective-permute-start(bf16[160,2048]{1,0:T(8,128)(2,1)S(1)} %get-tuple-element.138), channel_id=1, source_target_pairs={{0,16},{8,24},{16,0},{24,8},{1,17},{9,25},{17,1},{25,9},{2,18},{10... | collective-permute-start | bytes 1966088 | tf_op jit(solution)/shard_map/ppermute | solution.py:261
  688.9 28.0 %collective-permute-start.36 = (bf16[160,2048]{1,0:T(8,128)(2,1)}, bf16[160,2048]{1,0:T(8,128)(2,1)}, u32[]{:S(2)}, u32[]{:S(2)}) collective-permute-start(bf16[160,2048]{1,0:T(8,128)(2,1)} %add_convert_fusion.1), channel_id=1, source_target_pairs={{0,16},{8,24},{16,0},{24,8},{1,17},{9,25},{17,1},{25,9},{2,18},{10... | collective-permute-start | bytes 1966088 | tf_op jit(solution)/shard_map/ppermute | solution.py:261
  689.4 41.4 %collective-permute-start.19 = (bf16[160,2048]{1,0:T(8,128)(2,1)S(1)}, bf16[160,2048]{1,0:T(8,128)(2,1)S(1)}, u32[]{:S(2)}, u32[]{:S(2)}) collective-permute-start(bf16[160,2048]{1,0:T(8,128)(2,1)S(1)} %copy-done.34), channel_id=1, source_target_pairs={{0,16},{8,24},{16,0},{24,8},{1,17},{9,25},{17,1},{25,9},{2,18},{10... | collective-permute-start | bytes 1966088 | tf_op jit(solution)/shard_map/ppermute | solution.py:261
  694.5 36.3 %collective-permute-start.18 = (bf16[160,2048]{1,0:T(8,128)(2,1)S(1)}, bf16[160,2048]{1,0:T(8,128)(2,1)S(1)}, u32[]{:S(2)}, u32[]{:S(2)}) collective-permute-start(bf16[160,2048]{1,0:T(8,128)(2,1)S(1)} %get-tuple-element.147), channel_id=1, source_target_pairs={{0,8},{8,0},{16,24},{24,16},{1,9},{9,1},{17,25},{25,17},{2,10},{10... | collective-permute-start | bytes 1966088 | tf_op jit(solution)/shard_map/ppermute | solution.py:261
  699.0 44.1 %collective-permute-start.39 = (bf16[160,2048]{1,0:T(8,128)(2,1)S(1)}, bf16[160,2048]{1,0:T(8,128)(2,1)S(1)}, u32[]{:S(2)}, u32[]{:S(2)}) collective-permute-start(bf16[160,2048]{1,0:T(8,128)(2,1)S(1)} %get-tuple-element.137), channel_id=1, source_target_pairs={{0,16},{8,24},{16,0},{24,8},{1,17},{9,25},{17,1},{25,9},{2,18},{10... | collective-permute-start | bytes 1966088 | tf_op jit(solution)/shard_map/ppermute | solution.py:261
  719.1 24.0 %collective-permute-start.38 = (bf16[160,2048]{1,0:T(8,128)(2,1)S(1)}, bf16[160,2048]{1,0:T(8,128)(2,1)S(1)}, u32[]{:S(2)}, u32[]{:S(2)}) collective-permute-start(bf16[160,2048]{1,0:T(8,128)(2,1)S(1)} %get-tuple-element.135), channel_id=1, source_target_pairs={{0,8},{8,0},{16,24},{24,16},{1,9},{9,1},{17,25},{25,17},{2,10},{10... | collective-permute-start | bytes 1966088 | tf_op jit(solution)/shard_map/ppermute | solution.py:261
  745.6 3.8 collective-permute-start.40
  749.4 9.7 %collective-permute-start.41 = (f32[2,2048]{1,0:T(2,128)S(1)}, f32[2,2048]{1,0:T(2,128)S(1)}, u32[]{:S(2)}, u32[]{:S(2)}) collective-permute-start(f32[2,2048]{1,0:T(2,128)S(1)} %fusion.58), channel_id=1, source_target_pairs={{0,16},{8,24},{16,0},{24,8},{1,17},{9,25},{17,1},{25,9},{2,18},{10... | collective-permute-start | bytes 49160 | tf_op jit(solution)/shard_map/ppermute | solution.py:261
  755.6 10.8 %all-to-all-start.2 = ((bf16[4,64,1,1280]{3,1,2,0:T(8,128)(2,1)}), bf16[4,64,1,1280]{3,1,2,0:T(8,128)(2,1)S(1)}, u32[]{:S(2)}, u32[]{:S(2)}) async-start(bf16[4,64,1,1280]{3,1,2,0:T(8,128)(2,1)} %bitcast.228), calls=%async_computation.3 | async-start | bytes 1310720 | tf_op jit(solution)/shard_map/all_to_all | solution.py:306
  759.1 1.2 collective-permute-start.42
  760.4 24.7 %collective-permute-start.45 = (f32[2,2048]{1,0:T(2,128)S(1)}, f32[2,2048]{1,0:T(2,128)S(1)}, u32[]{:S(2)}, u32[]{:S(2)}) collective-permute-start(f32[2,2048]{1,0:T(2,128)S(1)} %add.363), channel_id=1, source_target_pairs={{0,3},{1,0},{2,1},{3,2},{4,7},{5,4},{6,5},{7,6},{8,11},{9,8},{10,9... | collective-permute-start | bytes 49160 | tf_op jit(solution)/shard_map/ppermute | solution.py:320
  761.6 23.5 %collective-permute-start.43 = (f32[2,2048]{1,0:T(2,128)S(1)}, f32[2,2048]{1,0:T(2,128)S(1)}, u32[]{:S(2)}, u32[]{:S(2)}) collective-permute-start(f32[2,2048]{1,0:T(2,128)S(1)} %add.363), channel_id=1, source_target_pairs={{0,1},{1,2},{2,3},{3,0},{4,5},{5,6},{6,7},{7,4},{8,9},{9,10},{10,1... | collective-permute-start | bytes 49160 | tf_op jit(solution)/shard_map/ppermute | solution.py:320
  762.4 22.6 %collective-permute-start.44 = (f32[2,2048]{1,0:T(2,128)S(1)}, f32[2,2048]{1,0:T(2,128)S(1)}, u32[]{:S(2)}, u32[]{:S(2)}) collective-permute-start(f32[2,2048]{1,0:T(2,128)S(1)} %add.363), channel_id=1, source_target_pairs={{0,2},{1,3},{2,0},{3,1},{4,6},{5,7},{6,4},{7,5},{8,10},{9,11},{10,... | collective-permute-start | bytes 49160 | tf_op jit(solution)/shard_map/ppermute | solution.py:320
  774.6 100.0 %all-to-all-start.3 = ((bf16[4,64,1,3072]{3,1,2,0:T(8,128)(2,1)}), bf16[4,64,1,3072]{3,1,2,0:T(8,128)(2,1)}, u32[]{:S(2)}, u32[]{:S(2)}) async-start(bf16[4,64,1,3072]{3,1,2,0:T(8,128)(2,1)} %bitcast.220), calls=%async_computation.7 | async-start | bytes 3145728 | tf_op jit(solution)/shard_map/all_to_all | solution.py:306
  (76 other events, 1320.4 us)
Sparse Core Ops, SparseCore 0:
  15.0 40.7 all-gather.4
  57.3 59.2 all-gather.6
  118.2 63.4 all-gather.10
  183.2 115.3 all-gather.8
  588.6 19.1 reduce-scatter.7
  610.0 50.5 reduce-scatter.5
  663.1 111.4 reduce-scatter.11
  777.0 31.7 reduce-scatter.9
  811.2 59.0 reduce-scatter.13

commit v3 on v2

--- a/solution.py
+++ b/solution.py
@@ -201,6 +201,7 @@
         out_specs=(block, block),
         scratch_shapes=[pltpu.VMEM((rows, LANES), jnp.float32)] * 2,
         compiler_params=pltpu.CompilerParams(vmem_limit_bytes=48 * 2**20),
+        cost_estimate=pl.CostEstimate(flops=200000 * rows * channels // 10, bytes_accessed=20 * rows * channels, transcendentals=8 * rows * channels),
         name="lru_forward",
     )(conv, rate_pre, input_pre, gate_pre, soft)
 
@@ -222,8 +223,208 @@
         out_specs=(block, block, block, block, pl.BlockSpec((24, LANES), lambda i: (0, i))),
         scratch_shapes=[pltpu.VMEM((rows, LANES), jnp.float32)] * 3,
         compiler_params=pltpu.CompilerParams(vmem_limit_bytes=48 * 2**20),
+        cost_estimate=pl.CostEstimate(flops=200000 * rows * channels // 10, bytes_accessed=20 * rows * channels, transcendentals=16 * rows * channels),
         name="lru_backward",
     )(conv, rate_pre, input_pre, gate_pre, soft, states, grads)
+
+
+CONSTANT = pl.Buffered(1)
+VMEM_BYTES = 56 * 2**20
+
+
+def column_block(columns, most):
+    return max(w for w in range(LANES, most + 1, LANES) if columns % w == 0)
+
+
+def mlp_kernel(slots, n2_ref, low_ref, gate_ref, up_ref, down_ref, product_ref, d_gate_ref, d_up_ref, w_s):
+    groups, rows = gate_ref.shape[1], gate_ref.shape[2]
+    stride = gate_ref.shape[0] * rows
+    for c in range(groups):
+        for k in range(gate_ref.shape[0]):
+            at = pl.ds(c * stride + k * rows, rows)
+            w_s[0, at, :] = gate_ref[k, c]
+            w_s[1, at, :] = up_ref[k, c]
+    length = n2_ref.shape[0] // slots
+
+    for i in range(slots):
+        at = pl.ds(i * length, length)
+        here = n2_ref[at, :]
+        gate = jnp.dot(here, w_s[0], preferred_element_type=jnp.float32)
+        up = jnp.dot(here, w_s[1], preferred_element_type=jnp.float32)
+        grad = matmul_nt(low_ref[at, :], down_ref[...])
+        value, slope = gelu_pair(gate)
+        product_ref[at, :] = (value * up).astype(jnp.bfloat16)
+        d_gate_ref[at, :] = (grad * up * slope).astype(jnp.bfloat16)
+        d_up_ref[at, :] = (grad * value).astype(jnp.bfloat16)
+
+
+def mlp_both(slots, normed, low_res, weights, w_down):
+    tokens, width = normed.shape
+    hidden = w_down.shape[0]
+    block = column_block(hidden, 256)
+    steps = hidden // block
+    lead = weights.shape[:3]
+    return pl.pallas_call(
+        functools.partial(mlp_kernel, slots),
+        grid=(steps,),
+        out_shape=(jax.ShapeDtypeStruct((tokens, hidden), jnp.bfloat16),) * 3,
+        in_specs=[
+            pl.BlockSpec((tokens, width), lambda j: (0, 0), pipeline_mode=CONSTANT),
+            pl.BlockSpec((tokens, width), lambda j: (0, 0), pipeline_mode=CONSTANT),
+            pl.BlockSpec(lead + (block,), lambda j: (0, 0, 0, j)),
+            pl.BlockSpec(lead + (block,), lambda j: (0, 0, 0, j + steps)),
+            pl.BlockSpec((block, width), lambda j: (j, 0)),
+        ],
+        out_specs=(pl.BlockSpec((tokens, block), lambda j: (0, j)),) * 3,
+        scratch_shapes=[pltpu.VMEM((2, width, block), jnp.bfloat16)],
+        compiler_params=pltpu.CompilerParams(vmem_limit_bytes=VMEM_BYTES),
+        cost_estimate=pl.CostEstimate(
+            flops=6 * tokens * width * hidden, bytes_accessed=2 * (2 * tokens * width + 3 * width * hidden), transcendentals=tokens * hidden
+        ),
+        name="mlp_both",
+    )(normed, low_res, weights, weights, w_down)
+
+
+def store_parts(refs, length, part, value):
+    value = value.astype(jnp.bfloat16)
+    if part == 0:
+        refs[0][...] = value[: length // 2]
+        refs[1][...] = value[length // 2 :]
+    else:
+        refs[part + 1][...] = value
+
+
+def store_all(refs, total):
+    length = refs[-1].shape[0]
+    for part in range(PLANE):
+        store_parts(refs, length, part, total[part * length : (part + 1) * length])
+
+
+def back_kernel(pieces, *refs):
+    grads, w_ref, outs = refs[:pieces], refs[pieces], refs[pieces + 1 :]
+    shares, _, rows, _ = w_ref.shape
+    total = None
+    start = 0
+    for grads_ref in grads:
+        cut = grads_ref.shape[1]
+        weight = w_ref[:, 0, :, start : start + cut].reshape(shares * rows, cut)
+        term = matmul_nt(grads_ref[...], weight)
+        total = term if total is None else total + term
+        start += cut
+    store_all(outs, total)
+
+
+def parts_out(length, width, block):
+    heights = (length // 2, length // 2, length, length, length)
+    return (
+        tuple(jax.ShapeDtypeStruct((h, width), jnp.bfloat16) for h in heights),
+        tuple(pl.BlockSpec((h, block), lambda j: (0, j)) for h in heights),
+    )
+
+
+def back_parts(grads, weights):
+    tokens = grads[0].shape[0]
+    inner = sum(g.shape[1] for g in grads)
+    shares, groups, rows, columns = weights.shape
+    block = shares * rows
+    shapes, specs = parts_out(tokens // PLANE, groups * block, block)
+    return pl.pallas_call(
+        functools.partial(back_kernel, len(grads)),
+        grid=(groups,),
+        out_shape=shapes,
+        in_specs=[pl.BlockSpec(g.shape, lambda j: (0, 0), pipeline_mode=CONSTANT) for g in grads]
+        + [pl.BlockSpec((shares, 1, rows, columns), lambda j: (0, j, 0, 0))],
+        out_specs=specs,
+        compiler_params=pltpu.CompilerParams(vmem_limit_bytes=VMEM_BYTES),
+        cost_estimate=pl.CostEstimate(
+            flops=2 * tokens * inner * groups * block,
+            bytes_accessed=2 * (tokens * inner + groups * block * (columns + tokens)),
+            transcendentals=0,
+        ),
+        name="back_parts",
+    )(*grads, weights)
+
+
+def out_kernel(values_ref, w_ref, *refs):
+    store_all(refs, jnp.dot(values_ref[...], w_ref[...], preferred_element_type=jnp.float32))
+
+
+def out_parts(values, weight):
+    tokens, inner = values.shape
+    width = weight.shape[1]
+    block = column_block(width, 512)
+    shapes, specs = parts_out(tokens // PLANE, width, block)
+    return pl.pallas_call(
+        out_kernel,
+        grid=(width // block,),
+        out_shape=shapes,
+        in_specs=[
+            pl.BlockSpec((tokens, inner), lambda j: (0, 0), pipeline_mode=CONSTANT),
+            pl.BlockSpec((inner, block), lambda j: (0, j)),
+        ],
+        out_specs=specs,
+        compiler_params=pltpu.CompilerParams(vmem_limit_bytes=VMEM_BYTES),
+        cost_estimate=pl.CostEstimate(
+            flops=2 * tokens * inner * width, bytes_accessed=2 * (tokens * inner + inner * width + tokens * width), transcendentals=0
+        ),
+        name="out_parts",
+    )(values, weight)
+
+
+def weight_grad_kernel(rows, me_ref, left_ref, right_ref, mine_ref, theirs_ref, left_s):
+    @pl.when(pl.program_id(1) == 0)
+    def _():
+        left_s[...] = left_ref[...].T
+
+    narrow, groups, _, block = mine_ref.shape
+    height = narrow * rows
+    total = jnp.dot(left_s[...], right_ref[0], preferred_element_type=jnp.float32).astype(jnp.bfloat16)
+
+    def store(first_ref, second_ref):
+        for g in range(groups):
+            for share, ref in enumerate((first_ref, second_ref)):
+                start = (g * 2 + share) * height
+                ref[:, g] = total[start : start + height].reshape(narrow, rows, block)
+
+    @pl.when(me_ref[0] == 0)
+    def _():
+        store(mine_ref, theirs_ref)
+
+    @pl.when(me_ref[0] != 0)
+    def _():
+        store(theirs_ref, mine_ref)
+
+
+def weight_grad(me, left, right, narrow, groups, rows):
+    tokens = left.shape[0]
+    pieces, _, piece = right.shape
+    block = column_block(piece, 768)
+    steps = piece // block
+    together = 2 if groups % 2 == 0 else 1
+    height = together * 2 * narrow * rows
+    place = pl.BlockSpec((narrow, together, rows, block), lambda g, j, me_ref: (0, g, 0, j))
+    shape = jax.ShapeDtypeStruct((narrow, groups, rows, pieces * piece), jnp.bfloat16)
+    return pl.pallas_call(
+        functools.partial(weight_grad_kernel, rows),
+        grid_spec=pltpu.PrefetchScalarGridSpec(
+            num_scalar_prefetch=1,
+            grid=(groups // together, pieces * steps),
+            in_specs=[
+                pl.BlockSpec((tokens, height), lambda g, j, me_ref: (0, g)),
+                pl.BlockSpec((1, tokens, block), lambda g, j, me_ref: (j // steps, 0, j % steps)),
+            ],
+            out_specs=(place, place),
+            scratch_shapes=[pltpu.VMEM((height, tokens), jnp.bfloat16)],
+        ),
+        out_shape=(shape, shape),
+        compiler_params=pltpu.CompilerParams(vmem_limit_bytes=VMEM_BYTES),
+        cost_estimate=pl.CostEstimate(
+            flops=2 * tokens * left.shape[1] * pieces * piece,
+            bytes_accessed=2 * (left.size + groups // together * right.size + left.shape[1] * pieces * piece),
+            transcendentals=0,
+        ),
+        name="weight_grad",
+    )(me, left, right)
 
 
 def block_diagonal(table):
@@ -266,47 +467,67 @@
         far = [swap(one[:half], 2), swap(two[half:], 1)]
         return jnp.concatenate(far + [one, two, shard], axis=0)
 
-    def scatter_rows(parts):
-        far, one, two, own = parts
+    def scatter_rows(parts, *hold):
+        far_low, far_high, one, two, own = parts
         half = own.shape[0] // 2
-        via_one, via_two = swap(far[:half], 1), swap(far[half:], 2)
-        one_low, two_high = swap(one[:half], 1), swap(two[half:], 2)
-        one_high = swap((one[half:].astype(f32) + via_two.astype(f32)).astype(bf16), 1)
-        two_low = swap((two[:half].astype(f32) + via_one.astype(f32)).astype(bf16), 2)
-        low = own[:half].astype(f32) + one_low.astype(f32) + two_low.astype(f32)
-        high = own[half:].astype(f32) + one_high.astype(f32) + two_high.astype(f32)
-        return jnp.concatenate([low, high], axis=0)
-
-    def rows_to_parts(values):
-        return jnp.split(values, PLANE, axis=0)
-
-    def gather_columns(blocks):
-        part = lax.all_to_all(blocks, "wide", 0, 0, tiled=False)
-        plane, rows, columns = part.shape
-        whole = lax.all_gather(part.reshape(plane * rows, columns), spread, axis=0, tiled=True)
-        whole = whole.reshape(rest_size * narrow_size, plane, rows, columns)
-        return whole.swapaxes(0, 1).reshape(-1, columns)
-
-    def reduce_spread(values):
-        if rest_size == 2:
-            me = lax.axis_index("rest")
-            theirs = lax.dynamic_index_in_dim(values, 1 - me, 0, keepdims=False)
-            mine = lax.dynamic_index_in_dim(values, me, 0, keepdims=False)
-            other = lax.ppermute(theirs, "rest", [(0, 1), (1, 0)])
-            total = (mine.astype(f32) + other.astype(f32)).astype(values.dtype)
-        else:
-            total = lax.psum_scatter(values, "rest", scatter_dimension=0, tiled=False)
-        flat = total.reshape(-1, total.shape[-1])
-        return lax.psum_scatter(flat, "narrow", scatter_dimension=0, tiled=True)
-
-    def reduce_columns(grad, rows):
-        columns = grad.shape[-1]
-        cut = grad.reshape(PLANE, rest_size, narrow_size, rows, columns)
-        mine = reduce_spread(cut.transpose(1, 2, 0, 3, 4))
-        return lax.all_to_all(mine.reshape(PLANE, rows, columns), "wide", 0, 1, tiled=False)
-
-    def reduce_rows(grad):
-        return reduce_spread(grad.reshape(rest_size, narrow_size, -1, grad.shape[-1]))
+        via_one, via_two = swap(far_low, 1), swap(far_high, 2)
+        one, two = after(one, *hold), after(two, *hold)
+        one = jnp.concatenate([one[:half], (one[half:].astype(f32) + via_two.astype(f32)).astype(bf16)], axis=0)
+        two = jnp.concatenate([(two[:half].astype(f32) + via_one.astype(f32)).astype(bf16), two[half:]], axis=0)
+        return own.astype(f32) + swap(one, 1).astype(f32) + swap(two, 2).astype(f32)
+
+    def cut_columns(blocks):
+        return lax.all_to_all(blocks, "wide", 0, 0, tiled=False)
+
+    def gather_spread(part):
+        whole = lax.all_gather(part.reshape(-1, part.shape[-1]), spread, axis=0, tiled=True)
+        return whole.reshape((rest_size * narrow_size,) + part.shape)
+
+    def grad_shares(left, right, rows, groups):
+        if rest_size != 2:
+            grad = matmul_tn(left, right.swapaxes(0, 1).reshape(right.shape[1], -1)).astype(bf16)
+            cut = grad.reshape(groups, rest_size, narrow_size, rows, -1).transpose(1, 2, 0, 3, 4)
+            return grad, lambda *waits: lax.psum_scatter(after(cut, *waits), "rest", scatter_dimension=0, tiled=False)
+        me = lax.axis_index("rest").astype(jnp.int32)[None]
+        mine, theirs = weight_grad(me, left, right, narrow_size, groups, rows)
+        other = lax.ppermute(theirs, "rest", [(0, 1), (1, 0)])
+        return theirs, lambda *waits: (after(mine, *waits).astype(f32) + other.astype(f32)).astype(bf16)
+
+    def sum_rest(values):
+        if rest_size != 2:
+            return lax.psum_scatter(values, "rest", scatter_dimension=0, tiled=False)
+        me = lax.axis_index("rest")
+        theirs = lax.dynamic_index_in_dim(values, 1 - me, 0, keepdims=False)
+        mine = lax.dynamic_index_in_dim(values, me, 0, keepdims=False)
+        other = lax.ppermute(theirs, "rest", [(0, 1), (1, 0)])
+        return (mine.astype(f32) + other.astype(f32)).astype(values.dtype)
+
+    def sum_narrow(values):
+        return lax.psum_scatter(values.reshape(-1, values.shape[-1]), "narrow", scatter_dimension=0, tiled=True)
+
+    def columns_home(mine, rows):
+        return lax.all_to_all(mine.reshape(PLANE, rows, -1), "wide", 0, 1, tiled=False)
+
+    def sum_narrow_direct(values):
+        me = lax.axis_index("narrow")
+        total = lax.dynamic_index_in_dim(values, me, 0, keepdims=False).astype(f32)
+        for step in range(1, narrow_size):
+            part = lax.dynamic_index_in_dim(values, lax.rem(me + step, narrow_size), 0, keepdims=False)
+            pairs = [(i, (i + step) % narrow_size) for i in range(narrow_size)]
+            total = total + lax.ppermute(part, "narrow", pairs).astype(f32)
+        return total
+
+    def to_all(values, axes, count):
+        return lax.all_to_all(jnp.broadcast_to(values[None], (count,) + values.shape), axes, 0, 0, tiled=False)
+
+    def rows_cut(grad):
+        return grad.reshape(rest_size, narrow_size, -1, grad.shape[-1])
+
+    def fence(*values):
+        return lax.optimization_barrier(values)
+
+    def after(values, *others):
+        return lax.optimization_barrier((values,) + others)[0]
 
     def sum_all(values):
         values = values + swap(values, 1)
@@ -353,9 +574,6 @@
             cut = [w.reshape(rows, PLANE, -1).swapaxes(0, 1) for w in weights]
             return jnp.concatenate(cut, axis=2)
 
-        gains = jnp.pad(jnp.stack([norm_gain1, norm_gain2], axis=1), ((0, 0), (0, LANES - 2)))
-        gains = jnp.broadcast_to(gains[None], (PLANE, rows, LANES))
-        w_rec = gather_columns(jnp.concatenate([by_plane(gate_in, x_in), gains], axis=2))
         table = jnp.concatenate(
             [
                 conv_kernel,
@@ -370,20 +588,30 @@
         )
         cuts = [taps, 1, head, 1, head, 1, 1]
         places = [sum(cuts[:i]) for i in range(len(cuts) + 1)]
-        table = jnp.pad(table, ((0, -places[-1] % LANES), (0, 0)))
-        out_and_table = lax.all_gather(jnp.concatenate([out_proj, table.T], axis=1), spread, axis=0, tiled=True)
-        w_mlp = gather_columns(by_plane(mlp_gate, mlp_up))
-        w_down = lax.all_gather(mlp_down, spread, axis=0, tiled=True)
-
+        columns = 2 * channels
+        shares = rest_size * narrow_size
+        part_rec = cut_columns(by_plane(gate_in, x_in)).reshape(PLANE, rows, columns)
+        w_rec = gather_spread(part_rec)
+        tokens_all = gather_rows(after(tokens, part_rec))
+        table = jnp.pad(table, ((0, -places[-1] % LANES), (0, 0))).T
+        table = to_all(after(table, part_rec), spread, shares)
+        gains = to_all(after(jnp.stack([norm_gain1, norm_gain2]), table), ("wide",) + spread, PLANE * shares)
+        cut_mlp = by_plane(mlp_gate, mlp_up)
+        w_rec, tokens_all, table, gains, cut_mlp = fence(w_rec, tokens_all, table, gains, cut_mlp)
+
+        out_and_down = lax.all_gather(
+            after(jnp.concatenate([out_proj, mlp_down], axis=0), w_rec), spread, axis=0, tiled=True
+        ).reshape(rest_size * narrow_size, -1, width)
         low_res = (cotangent.astype(f32) * live).astype(bf16)
-        tokens_all = gather_rows(tokens)
-        low_res_all = gather_rows(low_res)
-
-        gain_one = w_rec[:, 2 * channels].astype(f32)[None]
-        gain_two = w_rec[:, 2 * channels + 1].astype(f32)[None]
-        w_rec = w_rec[:, : 2 * channels]
-        w_out = out_and_table[:, :width]
-        table = out_and_table[:, width:].T
+        low_res_all = gather_rows(after(low_res, w_rec))
+        gains = gains.swapaxes(0, 1).reshape(2, width).astype(f32)
+        gain_one, gain_two = gains[0:1], gains[1:2]
+        table = table.reshape(channels, -1).T
+        w_flat = w_rec.swapaxes(0, 1).reshape(width, columns)
+        tokens_f = tokens_all.astype(f32)
+        normed1 = (tokens_f * rms_inverse(tokens_f) * gain_one).astype(bf16)
+        gate_pre = matmul_low(normed1, w_flat[:, :channels])
+        branch_pre = matmul_low(normed1, w_flat[:, channels:])
         kernel, shift, rate_table, b_rate, input_table, b_input, decay = (
             table[places[i] : places[i + 1]] for i in range(len(cuts))
         )
@@ -392,11 +620,8 @@
         w_input = block_diagonal(input_table)
         soft = softplus_minus(decay_f)
         soft_rows = jnp.broadcast_to(soft, (8, soft.shape[1]))
-
-        tokens_f = tokens_all.astype(f32)
-        normed1 = (tokens_f * rms_inverse(tokens_f) * gain_one).astype(bf16)
-        gate_pre = matmul_low(normed1, w_rec[:, :channels])
-        branch_pre = matmul_low(normed1, w_rec[:, channels:])
+        part_mlp = cut_columns(after(cut_mlp, low_res_all))
+
         conv = shift_f
         for tap in range(taps):
             conv = conv + kernel_f[tap] * shift_rows(branch_pre, seqs, taps - 1 - tap)
@@ -404,48 +629,66 @@
         rate_pre = matmul_low(conv, w_rate) + b_rate
         input_pre = matmul_low(conv, w_input) + b_input
         states, mixed = lru_forward(seqs, conv, rate_pre, input_pre, gate_pre, soft_rows)
-        merged = tokens.astype(f32) + scatter_rows(rows_to_parts(matmul_low(mixed, w_out).astype(bf16)))
-
+        mixed, part_mlp, out_and_down = fence(mixed, part_mlp, out_and_down)
+        w_out = out_and_down[:, : out_proj.shape[0]].reshape(-1, width)
+        w_down = out_and_down[:, out_proj.shape[0] :].reshape(-1, width)
+
+        w_mlp = gather_spread(part_mlp)
+        merged = tokens.astype(f32) + scatter_rows(out_parts(mixed, w_out))
         inverse2 = rms_inverse(merged)
         normed2 = (merged * inverse2 * gain_two).astype(bf16)
         normed2_all = gather_rows(normed2)
-        gate_two = matmul_low(normed2_all, w_mlp[:, :hidden])
-        up_two = matmul_low(normed2_all, w_mlp[:, hidden:])
-        value, slope = gelu_pair(gate_two)
-        product = (value * up_two).astype(bf16)
-        result = merged + scatter_rows(rows_to_parts(matmul_low(product, w_down).astype(bf16)))
-        block_out = (result * live).astype(bf16)
-
-        down_out = reduce_rows(matmul_tn(product, low_res_all).astype(bf16)).astype(f32)
-        d_product = matmul_nt(low_res_all, w_down)
-        d_gate_two = (d_product * up_two * slope).astype(bf16)
-        d_up_two = (d_product * value).astype(bf16)
-        d_mlp = jnp.concatenate([d_gate_two, d_up_two], axis=1)
-        d_normed2 = scatter_rows(rows_to_parts(matmul_nt(d_mlp, w_mlp).astype(bf16)))
-        mlp_out = reduce_columns(matmul_tn(normed2_all, d_mlp).astype(bf16), rows)
+        normed2_all, w_mlp = fence(normed2_all, w_mlp)
+
+        product, d_gate_two, d_up_two = mlp_both(PLANE, normed2_all, low_res_all, w_mlp, w_down)
+        first, finish_down = grad_shares(product, low_res_all[None], mlp_down.shape[0], 1)
+        parts2 = back_parts((after(d_gate_two, first), d_up_two), w_mlp)
+        grad_down = finish_down(parts2[0])
+        down_out = sum_narrow(grad_down)
+        d_normed2 = scatter_rows(parts2)
+        _, finish = grad_shares(normed2_all, after(d_gate_two, parts2)[None], rows, PLANE)
+        grad_mgate = finish()
+        d_normed2, grad_mgate, down_out = fence(d_normed2, grad_mgate, down_out)
+
+        mgate_sum = sum_narrow(grad_mgate)
         grad_gain2 = jnp.sum(d_normed2 * merged * inverse2, axis=0)
         d_merged = low_res.astype(f32) + rms_back(merged, inverse2, gain_two, d_normed2)
-
         low_merged_all = gather_rows(d_merged.astype(bf16))
+        _, finish = grad_shares(normed2_all, after(d_up_two, d_normed2)[None], rows, PLANE)
+        grad_mup = finish()
+        parts_result = out_parts(after(product, d_normed2), w_down)
+        low_merged_all, parts_result, grad_mup, mgate_sum = fence(low_merged_all, parts_result, grad_mup, mgate_sum)
+        mup_sum = sum_narrow(grad_mup)
         d_mixed = matmul_nt(low_merged_all, w_out)
-        out_out = reduce_rows(matmul_tn(mixed, low_merged_all).astype(bf16)).astype(f32)
         d_conv_lru, d_rate, d_input, d_gate, sums = lru_backward(
             seqs, conv, rate_pre, input_pre, gate_pre, soft_rows, states, d_mixed
         )
+        result = merged + scatter_rows(parts_result, d_conv_lru)
+        mgate_out = columns_home(after(mgate_sum, d_conv_lru), rows)
         sums = sums.reshape(3, 8, -1).sum(axis=1)
         grad_decay = sums[2] * (-1.0 / (1.0 + jnp.exp(decay_f[0])))
         d_conv = d_conv_lru + matmul_nt(d_rate, w_rate) + matmul_nt(d_input, w_input)
-        grad_rate_weight = diagonal_blocks(matmul_tn(conv, d_rate), head)
-        grad_input_weight = diagonal_blocks(matmul_tn(conv, d_input), head)
         d_branch = jnp.zeros_like(d_conv)
         grad_taps = []
         for tap in range(taps):
             moved = shift_rows(d_conv, seqs, tap - (taps - 1))
             d_branch = d_branch + kernel_f[tap] * moved
             grad_taps.append(jnp.sum(branch_pre * moved, axis=0))
-        d_rec = jnp.concatenate([d_gate, d_branch.astype(bf16)], axis=1)
-        rec_out = reduce_columns(matmul_tn(normed1, d_rec).astype(bf16), rows)
-        d_normed1 = scatter_rows(rows_to_parts(matmul_nt(d_rec, w_rec).astype(bf16)))
+        d_rec = jnp.stack([d_gate, d_branch.astype(bf16)])
+        grad_out = sum_rest(rows_cut(matmul_tn(mixed, after(low_merged_all, d_conv_lru)).astype(bf16)))
+
+        d_rec, mup_sum, grad_out = fence(d_rec, mup_sum, grad_out)
+        out_out = sum_narrow(grad_out)
+        first, finish = grad_shares(normed1, d_rec, rows, PLANE)
+        parts1 = back_parts((after(d_rec[0], first), d_rec[1]), w_rec)
+        grad_rec = finish(parts1[0])
+        mup_out = columns_home(after(mup_sum, d_rec), rows)
+        grad_rec, parts1, out_out, mup_out, mgate_out = fence(grad_rec, parts1, out_out, mup_out, mgate_out)
+        rec_sum = sum_narrow(grad_rec)
+        d_normed1 = scatter_rows(parts1)
+        block_out = (after(result, d_normed1) * live).astype(bf16)
+        grad_rate_weight = diagonal_blocks(matmul_tn(conv, after(d_rate, grad_rec)), head)
+        grad_input_weight = diagonal_blocks(matmul_tn(conv, after(d_input, grad_rec)), head)
         own = tokens.astype(f32)
         inverse1 = rms_inverse(own)
         grad_gain1 = jnp.sum(d_normed1 * own * inverse1, axis=0)
@@ -463,7 +706,9 @@
             ],
             axis=0,
         )
-        table_out = reduce_rows(jnp.pad(table_grad, ((0, -places[-1] % LANES), (0, 0))).T).T
+        table_grad = sum_rest(rows_cut(jnp.pad(table_grad, ((0, -places[-1] % LANES), (0, 0))).T))
+        table_out = sum_narrow(after(table_grad, rec_sum)).T
+        rec_out = columns_home(rec_sum, rows)
         kernel_out, shift_out, rate_out, rate_bias_out, input_out, input_bias_out, decay_out = (
             table_out[places[i] : places[i + 1]] for i in range(len(cuts))
         )
@@ -487,11 +732,11 @@
             input_out,
             input_bias_out[0],
             decay_out[0],
-            out_out,
+            out_out.astype(f32),
             gain_out[1],
-            whole_rows(mlp_out[:, :, :hidden]),
-            whole_rows(mlp_out[:, :, hidden:]),
-            down_out,
+            whole_rows(mgate_out),
+            whole_rows(mup_out),
+            down_out.astype(f32),
         )
 
     return on_device

time: 893 us -> 760 us (0.85)
  waiting for transfers between devices: 368 us -> 211 us
  Pallas kernels: 53.2 us -> 202 us
  matrix products: 184 us -> 44.7 us
  blocking collectives: 38 us -> 15 us
  local copies, waits for them, and re-layouts: 89.8 us -> 109 us
  other arithmetic: 72.2 us -> 83.7 us
    pallas_call x0 -> x9, Pallas kernels: none -> 150 us  [the longest x4 60.1 us: weight_grad(): pl.pallas_call(functools.partial(weight_grad_kernel, rows), grid_spec=plt...]
    reduce_scatter x5 -> x6, waiting for transfers between devices: 91 us -> 4.53 us  [sum_narrow(): lax.psum_scatter(values.reshape(-1, values.shape[-1]), 'narrow', scatter_...]
    ppermute x42 -> x34, waiting for transfers between devices: 258 us -> 173 us  [swap(): return lax.ppermute(values, 'wide', [(i, i ^ mask) for i in range(PLANE)])]
    dot_general x8 -> x4, matrix products: 70.9 us -> 20.2 us  [matmul_low(): return jnp.dot(left, right, preferred_element_type=jnp.float32)]
    dot_general x6 -> x3, matrix products: 58 us -> 12.1 us  [matmul_nt(): lax.dot_general(left, right, (((1,), (1,)), ((), ())), preferred_element_...]
    dot_general x6 -> x3, matrix products: 55.5 us -> 12.4 us  [matmul_tn(): lax.dot_general(left, right, (((0,), (0,)), ((), ())), preferred_element_...]
    all_to_all x2 -> x1, blocking collectives: 38 us -> 15 us  [cut_columns(): return lax.all_to_all(blocks, 'wide', 0, 0, tiled=False)]
    all_to_all x2 -> x6, waiting for transfers between devices: 2.74 us -> 23.5 us  [the longest x3 23.5 us: columns_home(): lax.all_to_all(mine.reshape(PLANE, rows, -1), 'wide', 0, 1, tiled=False)]
  transfers between devices with their start and end apart: 62 -> 59, of which waited for: 31 -> 24; matrix products, arithmetic and copies ran while one was open for 25% -> 28% of each run, Pallas kernels for 2% -> 20%
where the time goes in v3:
time: 760 us; the launch traced here: 754 us
  waiting for transfers between devices  211 us (28%)
  Pallas kernels  202 us (27%)
  local copies, waits for them, and re-layouts  109 us (14%)
  other arithmetic  83.7 us (11%)
  starting transfers between devices  72.2 us (10%)
  matrix products  44.7 us (6%)
  between operations  16.1 us (2%)
  blocking collectives  15 us (2%)
    ppermute x34, waiting for transfers between devices, swap(): return lax.ppermute(values, 'wide', [(i, i ^ mask) for i in range(PLANE)])  173 us
    pallas_call x4, Pallas kernels, weight_grad(): pl.pallas_call(functools.partial(weight_grad_kernel, rows), grid_spec=plt...  60.1 us
    unnamed x197, local copies, waits for them, and re-layouts  41.2 us
    ppermute x34, starting transfers between devices, swap(): return lax.ppermute(values, 'wide', [(i, i ^ mask) for i in range(PLANE)])  39.4 us
    pallas_call x2, Pallas kernels, back_parts(): pl.pallas_call(functools.partial(back_kernel, len(grads)), grid=(groups,)...  34.9 us
    pallas_call x1, Pallas kernels, mlp_both(): pl.pallas_call(functools.partial(mlp_kernel, slots), grid=(steps,), out_s...  34.6 us
    pallas_call x1, Pallas kernels, lru_backward(): pl.pallas_call(functools.partial(lru_backward_kernel, seqs), grid=(pl.cdi...  34.5 us
    all_to_all x3, waiting for transfers between devices, columns_home(): lax.all_to_all(mine.reshape(PLANE, rows, -1), 'wide', 0, 1, tiled=False)  23.5 us
  transfers between devices with their start and end apart: 59, of which 24 were waited for; matrix products, arithmetic and copies ran while one was open for 28% of the time, Pallas kernels for 20%

profile of v3, /device:TPU:0, one launch (start us, length us, event | category | flops | bytes accessed | tf_op | source)
XLA Modules:
  0.0 753.5 jit_solution(15180435803566402141)
XLA Ops:
  9.9 15.0 %all_to_all.65 = bf16[4,64,1280]{2,1,0:T(8,128)(2,1)} all-to-all(bf16[4,64,1280]{2,1,0:T(8,128)(2,1)S(1)} %copy.76), channel_id=1, replica_groups=mesh['wide'=4,'rest'=2,'narrow'=4] {'wide'}, dimensions={0} | all-to-all | bytes 1310720 | tf_op jit(solution)/shard_map/all_to_all | solution.py:480
  28.1 4.9 all-to-all-start.1
  33.0 21.0 %collective-permute-done = bf16[320,2048]{1,0:T(8,128)(2,1)S(1)} collective-permute-done((bf16[320,2048]{1,0:T(8,128)(2,1)S(1)}, bf16[320,2048]{1,0:T(8,128)(2,1)S(1)}, u32[]{:S(2)}, u32[]{:S(2)}) %collective-permute-start) | collective-permute-done | bytes 1310752 | tf_op jit(solution)/shard_map/ppermute | solution.py:462
  68.2 5.2 all-to-all-start.2
  78.8 2.6 constant_dynamic-update-slice_fusion.1
  82.6 8.9 %all-gather.4.cloned.1.call-done = bf16[2048,1280]{1,0:T(8,128)(2,1)} async-done(((bf16[256,1280]{1,0:T(8,128)(2,1)}), bf16[2048,1280]{1,0:T(8,128)(2,1)}) %all-gather.4.cloned.1.call-update) | async-done | bytes 5242896 | tf_op jit(solution)/shard_map/all_gather | solution.py:483
  97.3 5.9 copy.79
  103.6 3.7 fusion
  107.4 3.9 fusion.2.left_ref
  111.3 4.3 fusion.23
  115.7 2.7 pad_slice_fusion.5
  118.4 3.6 fusion.12.conv_ref
  122.2 8.8 %fusion.21.gate_ref = f32[1280,640]{1,0:T(8,128)} fusion(bf16[1280,2048]{1,0:T(8,128)(2,1)S(1)} %copy-done.20, bf16[2048,1280]{1,0:T(8,128)(2,1)} %bitcast.175), kind=kOutput, calls=%fused_computation.54 | convolution fusion | flops 3355443200 | bytes 11141120 | tf_op jit(solution)/shard_map/dot_general | solution.py:20
  131.3 3.6 convolution_add_fusion.2.input_ref
  137.1 3.5 convolution_add_fusion.3.rate_ref
  140.6 6.8 collective-permute-done.5
  148.3 4.1 collective-permute-done.7
  154.6 2.7 constant_dynamic-update-slice_fusion.6
  157.2 2.5 constant_dynamic-update-slice_fusion.5.low_ref
  161.4 3.6 all-to-all-start.3
  165.0 18.1 %lru_forward.1 = (f32[1280,640]{1,0:T(8,128)}, bf16[1280,640]{1,0:T(8,128)(2,1)S(1)}) custom-call(bf16[1280,640]{1,0:T(8,128)(2,1)S(1)} %fusion.12.conv_ref, f32[1280,640]{1,0:T(8,128)} %convolution_add_fusion.3.rate_ref, f32[1280,640]{1,0:T(8,128)} %convolution_add_fusion.2.input_ref, f32[1280,640]{1,0:T(8,128)} %fusion.21.gate_ref, ...), custom_call_target="tpu_custom_call" | custom-call | flops 16384000000 | bytes 16384000 | tf_op jit(solution)/shard_map/lru_forward/pallas_call | solution.py:193
  185.6 3.6 slice.216
  189.2 7.5 out_parts.2
  202.6 9.8 %collective-permute-done.8 = bf16[160,2048]{1,0:T(8,128)(2,1)S(1)} collective-permute-done((bf16[160,2048]{1,0:T(8,128)(2,1)}, bf16[160,2048]{1,0:T(8,128)(2,1)S(1)}, u32[]{:S(2)}, u32[]{:S(2)}) %collective-permute-start.8) | collective-permute-done | bytes 655392 | tf_op jit(solution)/shard_map/ppermute | solution.py:462
  218.3 24.8 %collective-permute-done.9 = bf16[320,2048]{1,0:T(8,128)(2,1)S(1)} collective-permute-done((bf16[320,2048]{1,0:T(8,128)(2,1)}, bf16[320,2048]{1,0:T(8,128)(2,1)S(1)}, u32[]{:S(2)}, u32[]{:S(2)}) %collective-permute-start.9) | collective-permute-done | bytes 1310752 | tf_op jit(solution)/shard_map/ppermute | solution.py:462
  246.1 3.5 multiply_reduce_fusion.3
  252.3 25.2 %collective-permute-done.12 = bf16[320,2048]{1,0:T(8,128)(2,1)S(1)} collective-permute-done((bf16[320,2048]{1,0:T(8,128)(2,1)S(1)}, bf16[320,2048]{1,0:T(8,128)(2,1)S(1)}, u32[]{:S(2)}, u32[]{:S(2)}) %collective-permute-start.12) | collective-permute-done | bytes 1310752 | tf_op jit(solution)/shard_map/ppermute | solution.py:462
  283.8 6.6 slice.224
  301.7 34.6 %mlp_both.1 = (bf16[1280,1536]{1,0:T(8,128)(2,1)}, bf16[1280,1536]{1,0:T(8,128)(2,1)}, bf16[1280,1536]{1,0:T(8,128)(2,1)}) custom-call(bf16[1280,2048]{1,0:T(8,128)(2,1)} %constant_dynamic-update-slice_fusion.10.n2_ref.left_ref, bf16[1280,2048]{1,0:T(8,128)(2,1)} %constant_dynamic-update-slice_fusion.5.low_ref, bf16[8,4,64,3072]{3,2,1,0:T(8,128)(2,1)} %bitcast.219, ...), custom_call_target="tpu_custom_call" | custom-call | flops 24159191040 | bytes 29360128 | tf_op jit(solution)/shard_map/mlp_both/pallas_call | solution.py:267
  336.3 14.4 %weight_grad.4 = (bf16[4,1,192,2048]{3,2,1,0:T(8,128)(2,1)}, bf16[4,1,192,2048]{3,2,1,0:T(8,128)(2,1)}) custom-call(s32[1]{0:T(128)} %bitcast.28.me_ref, bf16[1280,1536]{1,0:T(8,128)(2,1)} %get-tuple-element.148.left_ref.values_ref, bf16[1,1280,2048]{2,1,0:T(8,128)(2,1)} %bitcast.29.right_ref), custom_call_target="tpu_custom_call" | custom-call | flops 8053063680 | bytes 15466496 | tf_op jit(solution)/shard_map/weight_grad/pallas_call | solution.py:407
  350.9 22.5 %back_parts.2 = (bf16[160,2048]{1,0:T(8,128)(2,1)}, bf16[160,2048]{1,0:T(8,128)(2,1)}, bf16[320,2048]{1,0:T(8,128)(2,1)}, bf16[320,2048]{1,0:T(8,128)(2,1)}, bf16[320,2048]{1,0:T(8,128)(2,1)}) custom-call(bf16[1280,1536]{1,0:T(8,128)(2,1)} %get-tuple-element.142.refs_0_, bf16[1280,1536]{1,0:T(8,128)(2,1)} %get-tuple-element.154.refs_1_, ...), custom_call_target="tpu_custom_call" | custom-call | flops 16106127360 | bytes 25690112 | tf_op jit(solution)/shard_map/back_parts/pallas_call | solution.py:331
  373.5 5.1 add_convert_fusion.1
  382.6 15.5 %weight_grad.5 = (bf16[4,4,64,1536]{3,2,1,0:T(8,128)(2,1)}, bf16[4,4,64,1536]{3,2,1,0:T(8,128)(2,1)}) custom-call(s32[1]{0:T(128)} %bitcast.28.me_ref, bf16[1280,2048]{1,0:T(8,128)(2,1)} %constant_dynamic-update-slice_fusion.10.n2_ref.left_ref, bf16[1,1280,1536]{2,1,0:T(8,128)(2,1)} %bitcast.225), custom_call_target="tpu_custom_call" | custom-call | flops 8053063680 | bytes 19398656 | tf_op jit(solution)/shard_map/weight_grad/pallas_call | solution.py:407
  400.9 29.0 %collective-permute-done.17 = bf16[320,2048]{1,0:T(8,128)(2,1)S(1)} collective-permute-done((bf16[320,2048]{1,0:T(8,128)(2,1)S(1)}, bf16[320,2048]{1,0:T(8,128)(2,1)S(1)}, u32[]{:S(2)}, u32[]{:S(2)}) %collective-permute-start.17) | collective-permute-done | bytes 1310752 | tf_op jit(solution)/shard_map/ppermute | solution.py:462
  433.0 2.7 add_convert_fusion.2
  437.4 2.7 multiply_reduce_fusion.1
  445.0 15.6 %weight_grad.6 = (bf16[4,4,64,1536]{3,2,1,0:T(8,128)(2,1)}, bf16[4,4,64,1536]{3,2,1,0:T(8,128)(2,1)}) custom-call(s32[1]{0:T(128)} %bitcast.28.me_ref, bf16[1280,2048]{1,0:T(8,128)(2,1)} %constant_dynamic-update-slice_fusion.10.n2_ref.left_ref, bf16[1,1280,1536]{2,1,0:T(8,128)(2,1)} %bitcast.224), custom_call_target="tpu_custom_call" | custom-call | flops 8053063680 | bytes 19398656 | tf_op jit(solution)/shard_map/weight_grad/pallas_call | solution.py:407
  463.1 9.7 %collective-permute-done.22 = bf16[320,2048]{1,0:T(8,128)(2,1)} collective-permute-done((bf16[320,2048]{1,0:T(8,128)(2,1)}, bf16[320,2048]{1,0:T(8,128)(2,1)}, u32[]{:S(2)}, u32[]{:S(2)}) %collective-permute-start.22) | collective-permute-done | bytes 1310752 | tf_op jit(solution)/shard_map/ppermute | solution.py:462
  478.2 12.4 %out_parts.3 = (bf16[160,2048]{1,0:T(8,128)(2,1)}, bf16[160,2048]{1,0:T(8,128)(2,1)}, bf16[320,2048]{1,0:T(8,128)(2,1)}, bf16[320,2048]{1,0:T(8,128)(2,1)}, bf16[320,2048]{1,0:T(8,128)(2,1)}) custom-call(bf16[1280,1536]{1,0:T(8,128)(2,1)} %get-tuple-element.148.left_ref.values_ref, bf16[1536,2048]{1,0:T(8,128)(2,1)} %bitcast.171), custom_call_target="tpu_custom_call" | custom-call | flops 8053063680 | bytes 15466496 | tf_op jit(solution)/shard_map/out_parts/pallas_call | solution.py:357
  492.8 2.5 constant_dynamic-update-slice_fusion.17
  495.3 2.7 constant_dynamic-update-slice_fusion.16
  498.0 2.6 constant_dynamic-update-slice_fusion.15
  500.6 2.6 add_convert_fusion
  504.9 8.4 %fusion.49.grad_ref = f32[1280,640]{1,0:T(8,128)} fusion(bf16[1280,2048]{1,0:T(8,128)(2,1)} %constant_dynamic-update-slice_fusion.15, bf16[640,2048]{1,0:T(8,128)(2,1)S(1)} %bitcast.185), kind=kOutput, calls=%fused_computation.180 | convolution fusion | flops 3355443200 | bytes 11141120 | tf_op jit(solution)/shard_map/dot_general | solution.py:24
  513.4 34.5 %lru_backward.1 = (f32[1280,640]{1,0:T(8,128)}, bf16[1280,640]{1,0:T(8,128)(2,1)S(1)}, bf16[1280,640]{1,0:T(8,128)(2,1)S(1)}, bf16[1280,640]{1,0:T(8,128)(2,1)S(1)}, f32[24,640]{1,0:T(8,128)S(1)}) custom-call(bf16[1280,640]{1,0:T(8,128)(2,1)} %copy-done, f32[1280,640]{1,0:T(8,128)} %convolution_add_fusion.3.rate_ref, ...), custom_call_target="tpu_custom_call" | custom-call | flops 16384000000 | bytes 16384000 | tf_op jit(solution)/shard_map/lru_backward/pallas_call | solution.py:212
  549.1 4.2 all-to-all-start.5
  553.8 6.8 convolution_convert_fusion
  569.8 3.7 fusion.46
  582.3 2.9 fusion.25
  585.2 14.7 %weight_grad.7 = (bf16[4,4,64,1280]{3,2,1,0:T(8,128)(2,1)}, bf16[4,4,64,1280]{3,2,1,0:T(8,128)(2,1)}) custom-call(s32[1]{0:T(128)} %bitcast.28.me_ref, bf16[1280,2048]{1,0:T(8,128)(2,1)} %copy-done.19, bf16[2,1280,640]{2,1,0:T(8,128)(2,1)} %pad_maximum_fusion.right_ref), custom_call_target="tpu_custom_call" | custom-call | flops 6710886400 | bytes 17039360 | tf_op jit(solution)/shard_map/weight_grad/pallas_call | solution.py:407
  608.0 12.4 %back_parts.3 = (bf16[160,2048]{1,0:T(8,128)(2,1)}, bf16[160,2048]{1,0:T(8,128)(2,1)}, bf16[320,2048]{1,0:T(8,128)(2,1)}, bf16[320,2048]{1,0:T(8,128)(2,1)}, bf16[320,2048]{1,0:T(8,128)(2,1)}) custom-call(bf16[1280,640]{1,0:T(8,128)(2,1)} %get-tuple-element.176.refs_0_, bf16[1280,640]{1,0:T(8,128)(2,1)} %get-tuple-element.300.refs_1_, ...), custom_call_target="tpu_custom_call" | custom-call | flops 6710886400 | bytes 13762560 | tf_op jit(solution)/shard_map/back_parts/pallas_call | solution.py:331
  620.3 4.2 all-to-all-start.4
  624.6 4.9 add_convert_fusion.3
  629.5 15.9 %all-to-all-done.4 = bf16[4,64,1,1536]{3,1,2,0:T(8,128)(2,1)} async-done(((bf16[4,64,1,1536]{3,1,2,0:T(8,128)(2,1)}), bf16[4,64,1,1536]{3,1,2,0:T(8,128)(2,1)}, u32[]{:S(2)}, u32[]{:S(2)}) %all-to-all-start.4) | async-done | bytes 786464 | tf_op jit(solution)/shard_map/all_to_all | solution.py:509
  645.5 4.1 fusion.50
  658.5 7.6 %collective-permute-done.33 = bf16[160,2048]{1,0:T(8,128)(2,1)} collective-permute-done((bf16[160,2048]{1,0:T(8,128)(2,1)}, bf16[160,2048]{1,0:T(8,128)(2,1)}, u32[]{:S(2)}, u32[]{:S(2)}) %collective-permute-start.33) | collective-permute-done | bytes 655392 | tf_op jit(solution)/shard_map/ppermute | solution.py:462
  680.0 18.2 %collective-permute-done.34 = bf16[320,2048]{1,0:T(8,128)(2,1)S(1)} collective-permute-done((bf16[320,2048]{1,0:T(8,128)(2,1)}, bf16[320,2048]{1,0:T(8,128)(2,1)S(1)}, u32[]{:S(2)}, u32[]{:S(2)}) %collective-permute-start.34) | collective-permute-done | bytes 1310752 | tf_op jit(solution)/shard_map/ppermute | solution.py:462
  698.1 3.8 collective-permute-done.36
  701.9 3.2 fusion.20
  709.6 3.2 collective-permute-done.38
  713.0 4.5 fusion.18
  723.3 3.5 all-to-all-start.6
  728.7 7.6 %all-to-all-done.6 = bf16[4,64,1,1280]{3,1,2,0:T(8,128)(2,1)S(1)} async-done(((bf16[4,64,1,1280]{3,1,2,0:T(8,128)(2,1)}), bf16[4,64,1,1280]{3,1,2,0:T(8,128)(2,1)S(1)}, u32[]{:S(2)}, u32[]{:S(2)}) %all-to-all-start.6) | async-done | bytes 655392 | tf_op jit(solution)/shard_map/all_to_all | solution.py:509
  738.2 3.0 reduce-scatter.17.cloned.1.call-done
  (408 shorter events, 175.4 us)
Async XLA Ops:
  7.2 84.4 %all-gather.4.cloned.1.call-start = ((), (), s32[]{:S(2)}) async-start(), calls=%async_computation.13 | async-start | bytes 5898240 | tf_op jit(solution)/shard_map/all_gather | solution.py:483
  24.9 29.0 %collective-permute-start = (bf16[320,2048]{1,0:T(8,128)(2,1)S(1)}, bf16[320,2048]{1,0:T(8,128)(2,1)S(1)}, u32[]{:S(2)}, u32[]{:S(2)}) collective-permute-start(bf16[320,2048]{1,0:T(8,128)(2,1)S(1)} %copy-done.11), channel_id=1, source_target_pairs={{0,8},{8,0},{16,24},{24,16},{1,9},{9,1},{17,25},{25,17},{2,10},{10... | collective-permute-start | bytes 3932168 | tf_op jit(solution)/shard_map/ppermute | solution.py:462
  25.9 32.6 %collective-permute-start.2 = (bf16[320,2048]{1,0:T(8,128)(2,1)S(1)}, bf16[320,2048]{1,0:T(8,128)(2,1)}, u32[]{:S(2)}, u32[]{:S(2)}) collective-permute-start(bf16[320,2048]{1,0:T(8,128)(2,1)S(1)} %copy-done.11), channel_id=1, source_target_pairs={{0,16},{8,24},{16,0},{24,8},{1,17},{9,25},{17,1},{25,9},{2,18},{10... | collective-permute-start | bytes 3932168 | tf_op jit(solution)/shard_map/ppermute | solution.py:462
  28.1 39.5 %all-to-all-start.1 = ((bf16[8,80,384]{2,1,0:T(8,128)(2,1)}), bf16[8,80,384]{2,1,0:T(8,128)(2,1)S(1)}, u32[]{:S(2)}, u32[]{:S(2)}) async-start(bf16[8,80,384]{2,1,0:T(8,128)(2,1)} %broadcast_in_dim.60), calls=%async_computation.1 | async-start | bytes 983040 | tf_op jit(solution)/shard_map/all_to_all | solution.py:521
  54.9 18.7 %collective-permute-start.1 = (bf16[160,2048]{1,0:T(8,128)(2,1)}, bf16[160,2048]{1,0:T(8,128)(2,1)}, u32[]{:S(2)}, u32[]{:S(2)}) collective-permute-start(bf16[160,2048]{1,0:T(8,128)(2,1)} %slice.258), channel_id=1, source_target_pairs={{0,16},{8,24},{16,0},{24,8},{1,17},{9,25},{17,1},{25,9},{2,18},{10... | collective-permute-start | bytes 1966088 | tf_op jit(solution)/shard_map/ppermute | solution.py:462
  60.5 15.1 %collective-permute-start.3 = (bf16[160,2048]{1,0:T(8,128)(2,1)}, bf16[160,2048]{1,0:T(8,128)(2,1)}, u32[]{:S(2)}, u32[]{:S(2)}) collective-permute-start(bf16[160,2048]{1,0:T(8,128)(2,1)} %slice.259), channel_id=1, source_target_pairs={{0,8},{8,0},{16,24},{24,16},{1,9},{9,1},{17,25},{25,17},{2,10},{10... | collective-permute-start | bytes 1966088 | tf_op jit(solution)/shard_map/ppermute | solution.py:462
  68.2 14.4 %all-to-all-start.2 = ((bf16[32,2,64]{2,1,0:T(2,128)(2,1)}), bf16[32,2,64]{2,1,0:T(2,128)(2,1)S(1)}, u32[]{:S(2)}, u32[]{:S(2)}) async-start(bf16[32,2,64]{2,1,0:T(2,128)(2,1)} %broadcast_in_dim.61), calls=%async_computation.2 | async-start | bytes 32768 | tf_op jit(solution)/shard_map/all_to_all | solution.py:521
  73.4 111.1 %all-gather.6.cloned.1.call-start = ((), (), s32[]{:S(2)}) async-start(), calls=%async_computation.14 | async-start | bytes 10027008 | tf_op jit(solution)/shard_map/all_gather | solution.py:602
  92.2 44.9 %copy-start.77 = (pred[640]{0:T(1024)(128)(4,1)}, pred[640]{0:T(1024)(128)(4,1)S(1)}, u32[]{:S(2)}) copy-start(pred[640]{0:T(1024)(128)(4,1)S(1)} %fusion.30) | copy-start | bytes 1924
  92.8 44.3 %copy-start.72 = (s32[640]{0:T(1024)}, s32[640]{0:T(1024)S(1)}, u32[]{:S(2)}) copy-start(s32[640]{0:T(1024)S(1)} %get-tuple-element.326) | copy-start | bytes 7684
  92.8 44.3 %copy-start.74 = (s32[640]{0:T(1024)}, s32[640]{0:T(1024)S(1)}, u32[]{:S(2)}) copy-start(s32[640]{0:T(1024)S(1)} %get-tuple-element.327) | copy-start | bytes 7684
  94.2 36.8 %collective-permute-start.4 = (bf16[320,2048]{1,0:T(8,128)(2,1)}, bf16[320,2048]{1,0:T(8,128)(2,1)S(1)}, u32[]{:S(2)}, u32[]{:S(2)}) collective-permute-start(bf16[320,2048]{1,0:T(8,128)(2,1)} %multiply_convert_fusion.2), channel_id=1, source_target_pairs={{0,8},{8,0},{16,24},{24,16},{1,9},{9,1},{17,25},{25,17},{2,10},{10... | collective-permute-start | bytes 3932168 | tf_op jit(solution)/shard_map/ppermute | solution.py:462
  95.6 39.2 %collective-permute-start.6 = (bf16[320,2048]{1,0:T(8,128)(2,1)}, bf16[320,2048]{1,0:T(8,128)(2,1)}, u32[]{:S(2)}, u32[]{:S(2)}) collective-permute-start(bf16[320,2048]{1,0:T(8,128)(2,1)} %multiply_convert_fusion.2), channel_id=1, source_target_pairs={{0,16},{8,24},{16,0},{24,8},{1,17},{9,25},{17,1},{25,9},{2,18},{10... | collective-permute-start | bytes 3932168 | tf_op jit(solution)/shard_map/ppermute | solution.py:462
  122.0 43.0 %copy-start = (bf16[1280,640]{1,0:T(8,128)(2,1)}, bf16[1280,640]{1,0:T(8,128)(2,1)S(1)}, u32[]{:S(2)}) copy-start(bf16[1280,640]{1,0:T(8,128)(2,1)S(1)} %fusion.12.conv_ref) | copy-start | bytes 4915204
  131.0 16.4 %collective-permute-start.5 = (bf16[160,2048]{1,0:T(8,128)(2,1)S(1)}, bf16[160,2048]{1,0:T(8,128)(2,1)S(1)}, u32[]{:S(2)}, u32[]{:S(2)}) collective-permute-start(bf16[160,2048]{1,0:T(8,128)(2,1)S(1)} %slice.274), channel_id=1, source_target_pairs={{0,16},{8,24},{16,0},{24,8},{1,17},{9,25},{17,1},{25,9},{2,18},{10... | collective-permute-start | bytes 1966088 | tf_op jit(solution)/shard_map/ppermute | solution.py:462
  136.0 16.4 %collective-permute-start.7 = (bf16[160,2048]{1,0:T(8,128)(2,1)S(1)}, bf16[160,2048]{1,0:T(8,128)(2,1)S(1)}, u32[]{:S(2)}, u32[]{:S(2)}) collective-permute-start(bf16[160,2048]{1,0:T(8,128)(2,1)S(1)} %slice.275), channel_id=1, source_target_pairs={{0,8},{8,0},{16,24},{24,16},{1,9},{9,1},{17,25},{25,17},{2,10},{10... | collective-permute-start | bytes 1966088 | tf_op jit(solution)/shard_map/ppermute | solution.py:462
  161.4 23.0 %all-to-all-start.3 = ((bf16[4,64,3072]{2,1,0:T(8,128)(2,1)}), bf16[4,64,3072]{2,1,0:T(8,128)(2,1)S(1)}, u32[]{:S(2)}, u32[]{:S(2)}) async-start(bf16[4,64,3072]{2,1,0:T(8,128)(2,1)} %copy.80), calls=%async_computation.3 | async-start | bytes 3145728 | tf_op jit(solution)/shard_map/all_to_all | solution.py:480
  165.0 136.7 %all-gather.8.cloned.1.call-start = ((), (), s32[]{:S(2)}) async-start(), calls=%async_computation.15 | async-start | bytes 14155776 | tf_op jit(solution)/shard_map/all_gather | solution.py:483
  185.6 251.7 %reduce-scatter.7.cloned.1.call-start = ((), (), s32[]{:S(2)}) async-start(), calls=%async_computation.16 | async-start | bytes 3932160 | tf_op jit(solution)/shard_map/reduce_scatter | solution.py:506
  196.7 15.7 %collective-permute-start.8 = (bf16[160,2048]{1,0:T(8,128)(2,1)}, bf16[160,2048]{1,0:T(8,128)(2,1)S(1)}, u32[]{:S(2)}, u32[]{:S(2)}) collective-permute-start(bf16[160,2048]{1,0:T(8,128)(2,1)} %get-tuple-element.126), channel_id=1, source_target_pairs={{0,16},{8,24},{16,0},{24,8},{1,17},{9,25},{17,1},{25,9},{2,18},{10... | collective-permute-start | bytes 1966088 | tf_op jit(solution)/shard_map/ppermute | solution.py:462
  199.9 15.6 %collective-permute-start.10 = (bf16[160,2048]{1,0:T(8,128)(2,1)}, bf16[160,2048]{1,0:T(8,128)(2,1)S(1)}, u32[]{:S(2)}, u32[]{:S(2)}) collective-permute-start(bf16[160,2048]{1,0:T(8,128)(2,1)} %get-tuple-element.128), channel_id=1, source_target_pairs={{0,8},{8,0},{16,24},{24,16},{1,9},{9,1},{17,25},{25,17},{2,10},{10... | collective-permute-start | bytes 1966088 | tf_op jit(solution)/shard_map/ppermute | solution.py:462
  213.8 29.3 %collective-permute-start.9 = (bf16[320,2048]{1,0:T(8,128)(2,1)}, bf16[320,2048]{1,0:T(8,128)(2,1)S(1)}, u32[]{:S(2)}, u32[]{:S(2)}) collective-permute-start(bf16[320,2048]{1,0:T(8,128)(2,1)} %pad_maximum_fusion.2), channel_id=1, source_target_pairs={{0,8},{8,0},{16,24},{24,16},{1,9},{9,1},{17,25},{25,17},{2,10},{10... | collective-permute-start | bytes 3932168 | tf_op jit(solution)/shard_map/ppermute | solution.py:462
  216.8 28.3 %collective-permute-start.11 = (bf16[320,2048]{1,0:T(8,128)(2,1)}, bf16[320,2048]{1,0:T(8,128)(2,1)S(1)}, u32[]{:S(2)}, u32[]{:S(2)}) collective-permute-start(bf16[320,2048]{1,0:T(8,128)(2,1)} %pad_maximum_fusion.3), channel_id=1, source_target_pairs={{0,16},{8,24},{16,0},{24,8},{1,17},{9,25},{17,1},{25,9},{2,18},{10... | collective-permute-start | bytes 3932168 | tf_op jit(solution)/shard_map/ppermute | solution.py:462
  249.6 190.4 %copy-start.5 = (f32[320,2048]{1,0:T(8,128)}, f32[320,2048]{1,0:T(8,128)S(1)}, u32[]{:S(2)}) copy-start(f32[320,2048]{1,0:T(8,128)S(1)} %get-tuple-element.298) | copy-start | bytes 7864324
  250.0 27.5 %collective-permute-start.12 = (bf16[320,2048]{1,0:T(8,128)(2,1)S(1)}, bf16[320,2048]{1,0:T(8,128)(2,1)S(1)}, u32[]{:S(2)}, u32[]{:S(2)}) collective-permute-start(bf16[320,2048]{1,0:T(8,128)(2,1)S(1)} %multiply_convert_fusion.1), channel_id=1, source_target_pairs={{0,8},{8,0},{16,24},{24,16},{1,9},{9,1},{17,25},{25,17},{2,10},{10... | collective-permute-start | bytes 3932168 | tf_op jit(solution)/shard_map/ppermute | solution.py:462
  251.1 29.7 %collective-permute-start.14 = (bf16[320,2048]{1,0:T(8,128)(2,1)S(1)}, bf16[320,2048]{1,0:T(8,128)(2,1)S(1)}, u32[]{:S(2)}, u32[]{:S(2)}) collective-permute-start(bf16[320,2048]{1,0:T(8,128)(2,1)S(1)} %multiply_convert_fusion.1), channel_id=1, source_target_pairs={{0,16},{8,24},{16,0},{24,8},{1,17},{9,25},{17,1},{25,9},{2,18},{10... | collective-permute-start | bytes 3932168 | tf_op jit(solution)/shard_map/ppermute | solution.py:462
  279.5 13.2 %collective-permute-start.13 = (bf16[160,2048]{1,0:T(8,128)(2,1)}, bf16[160,2048]{1,0:T(8,128)(2,1)S(1)}, u32[]{:S(2)}, u32[]{:S(2)}) collective-permute-start(bf16[160,2048]{1,0:T(8,128)(2,1)} %slice.281), channel_id=1, source_target_pairs={{0,16},{8,24},{16,0},{24,8},{1,17},{9,25},{17,1},{25,9},{2,18},{10... | collective-permute-start | bytes 1966088 | tf_op jit(solution)/shard_map/ppermute | solution.py:462
  282.8 12.6 %collective-permute-start.15 = (bf16[160,2048]{1,0:T(8,128)(2,1)}, bf16[160,2048]{1,0:T(8,128)(2,1)}, u32[]{:S(2)}, u32[]{:S(2)}) collective-permute-start(bf16[160,2048]{1,0:T(8,128)(2,1)} %slice.282), channel_id=1, source_target_pairs={{0,8},{8,0},{16,24},{24,16},{1,9},{9,1},{17,25},{25,17},{2,10},{10... | collective-permute-start | bytes 1966088 | tf_op jit(solution)/shard_map/ppermute | solution.py:462
  350.7 22.7 %collective-permute-start.21 = (bf16[4,1,192,2048]{3,2,1,0:T(8,128)(2,1)}, bf16[4,1,192,2048]{3,2,1,0:T(8,128)(2,1)}, u32[]{:S(2)}, u32[]{:S(2)}) collective-permute-start(bf16[4,1,192,2048]{3,2,1,0:T(8,128)(2,1)} %get-tuple-element.134), channel_id=1, source_target_pairs={{0,4},{4,0},{1,5},{5,1},{2,6},{6,2},{3,7},{7,3},{8,12},{12,8},{9,1... | collective-permute-start | bytes 9437192 | tf_op jit(solution)/shard_map/ppermute | solution.py:493
  378.6 124.5 %reduce-scatter.9.cloned.1.call-start = ((), (), s32[]{:S(2)}) async-start(), calls=%async_computation.17 | async-start | bytes 3932160 | tf_op jit(solution)/shard_map/reduce_scatter | solution.py:506
  379.7 19.8 %collective-permute-start.18 = (bf16[160,2048]{1,0:T(8,128)(2,1)S(1)}, bf16[160,2048]{1,0:T(8,128)(2,1)S(1)}, u32[]{:S(2)}, u32[]{:S(2)}) collective-permute-start(bf16[160,2048]{1,0:T(8,128)(2,1)S(1)} %copy-done.83), channel_id=1, source_target_pairs={{0,8},{8,0},{16,24},{24,16},{1,9},{9,1},{17,25},{25,17},{2,10},{10... | collective-permute-start | bytes 1966088 | tf_op jit(solution)/shard_map/ppermute | solution.py:462
  381.2 17.1 %collective-permute-start.16 = (bf16[160,2048]{1,0:T(8,128)(2,1)}, bf16[160,2048]{1,0:T(8,128)(2,1)S(1)}, u32[]{:S(2)}, u32[]{:S(2)}) collective-permute-start(bf16[160,2048]{1,0:T(8,128)(2,1)} %get-tuple-element.139), channel_id=1, source_target_pairs={{0,16},{8,24},{16,0},{24,8},{1,17},{9,25},{17,1},{25,9},{2,18},{10... | collective-permute-start | bytes 1966088 | tf_op jit(solution)/shard_map/ppermute | solution.py:462
  398.1 34.9 %collective-permute-start.20 = (bf16[4,4,64,1536]{3,2,1,0:T(8,128)(2,1)}, bf16[4,4,64,1536]{3,2,1,0:T(8,128)(2,1)S(1)}, u32[]{:S(2)}, u32[]{:S(2)}) collective-permute-start(bf16[4,4,64,1536]{3,2,1,0:T(8,128)(2,1)} %get-tuple-element.144), channel_id=1, source_target_pairs={{0,4},{4,0},{1,5},{5,1},{2,6},{6,2},{3,7},{7,3},{8,12},{12,8},{9,1... | collective-permute-start | bytes 9437192 | tf_op jit(solution)/shard_map/ppermute | solution.py:493
  398.6 31.2 %collective-permute-start.17 = (bf16[320,2048]{1,0:T(8,128)(2,1)S(1)}, bf16[320,2048]{1,0:T(8,128)(2,1)S(1)}, u32[]{:S(2)}, u32[]{:S(2)}) collective-permute-start(bf16[320,2048]{1,0:T(8,128)(2,1)S(1)} %pad_maximum_fusion.4), channel_id=1, source_target_pairs={{0,8},{8,0},{16,24},{24,16},{1,9},{9,1},{17,25},{25,17},{2,10},{10... | collective-permute-start | bytes 3932168 | tf_op jit(solution)/shard_map/ppermute | solution.py:462
  399.9 31.0 %collective-permute-start.19 = (bf16[320,2048]{1,0:T(8,128)(2,1)S(1)}, bf16[320,2048]{1,0:T(8,128)(2,1)S(1)}, u32[]{:S(2)}, u32[]{:S(2)}) collective-permute-start(bf16[320,2048]{1,0:T(8,128)(2,1)S(1)} %pad_maximum_fusion.5), channel_id=1, source_target_pairs={{0,16},{8,24},{16,0},{24,8},{1,17},{9,25},{17,1},{25,9},{2,18},{10... | collective-permute-start | bytes 3932168 | tf_op jit(solution)/shard_map/ppermute | solution.py:462
  437.3 147.9 %reduce-scatter.11.cloned.1.call-start = ((), (), s32[]{:S(2)}) async-start(), calls=%async_computation.18 | async-start | bytes 3932160 | tf_op jit(solution)/shard_map/reduce_scatter | solution.py:506
  442.1 30.7 %collective-permute-start.22 = (bf16[320,2048]{1,0:T(8,128)(2,1)}, bf16[320,2048]{1,0:T(8,128)(2,1)}, u32[]{:S(2)}, u32[]{:S(2)}) collective-permute-start(bf16[320,2048]{1,0:T(8,128)(2,1)} %fusion.45), channel_id=1, source_target_pairs={{0,8},{8,0},{16,24},{24,16},{1,9},{9,1},{17,25},{25,17},{2,10},{10... | collective-permute-start | bytes 3932168 | tf_op jit(solution)/shard_map/ppermute | solution.py:462
  443.6 31.9 %collective-permute-start.24 = (bf16[320,2048]{1,0:T(8,128)(2,1)}, bf16[320,2048]{1,0:T(8,128)(2,1)}, u32[]{:S(2)}, u32[]{:S(2)}) collective-permute-start(bf16[320,2048]{1,0:T(8,128)(2,1)} %fusion.45), channel_id=1, source_target_pairs={{0,16},{8,24},{16,0},{24,8},{1,17},{9,25},{17,1},{25,9},{2,18},{10... | collective-permute-start | bytes 3932168 | tf_op jit(solution)/shard_map/ppermute | solution.py:462
  460.6 40.0 %collective-permute-start.26 = (bf16[4,4,64,1536]{3,2,1,0:T(8,128)(2,1)}, bf16[4,4,64,1536]{3,2,1,0:T(8,128)(2,1)S(1)}, u32[]{:S(2)}, u32[]{:S(2)}) collective-permute-start(bf16[4,4,64,1536]{3,2,1,0:T(8,128)(2,1)} %get-tuple-element.156), channel_id=1, source_target_pairs={{0,4},{4,0},{1,5},{5,1},{2,6},{6,2},{3,7},{7,3},{8,12},{12,8},{9,1... | collective-permute-start | bytes 9437192 | tf_op jit(solution)/shard_map/ppermute | solution.py:493
  473.9 16.7 %collective-permute-start.23 = (bf16[160,2048]{1,0:T(8,128)(2,1)S(1)}, bf16[160,2048]{1,0:T(8,128)(2,1)S(1)}, u32[]{:S(2)}, u32[]{:S(2)}) collective-permute-start(bf16[160,2048]{1,0:T(8,128)(2,1)S(1)} %slice.287), channel_id=1, source_target_pairs={{0,16},{8,24},{16,0},{24,8},{1,17},{9,25},{17,1},{25,9},{2,18},{10... | collective-permute-start | bytes 1966088 | tf_op jit(solution)/shard_map/ppermute | solution.py:462
  476.6 15.2 %collective-permute-start.25 = (bf16[160,2048]{1,0:T(8,128)(2,1)S(1)}, bf16[160,2048]{1,0:T(8,128)(2,1)S(1)}, u32[]{:S(2)}, u32[]{:S(2)}) collective-permute-start(bf16[160,2048]{1,0:T(8,128)(2,1)S(1)} %slice.288), channel_id=1, source_target_pairs={{0,8},{8,0},{16,24},{24,16},{1,9},{9,1},{17,25},{25,17},{2,10},{10... | collective-permute-start | bytes 1966088 | tf_op jit(solution)/shard_map/ppermute | solution.py:462
  549.1 71.3 %all-to-all-start.5 = ((bf16[4,64,1,1536]{3,1,2,0:T(8,128)(2,1)}), bf16[4,64,1,1536]{3,1,2,0:T(8,128)(2,1)}, u32[]{:S(2)}, u32[]{:S(2)}) async-start(bf16[4,64,1,1536]{3,1,2,0:T(8,128)(2,1)} %bitcast.205), calls=%async_computation.9 | async-start | bytes 1572864 | tf_op jit(solution)/shard_map/all_to_all | solution.py:509
  553.3 92.2 %reduce-scatter.13.cloned.1.call-start = ((), (), s32[]{:S(2)}) async-start(), calls=%async_computation.19 | async-start | bytes 1638400 | tf_op jit(solution)/shard_map/reduce_scatter | solution.py:506
  561.8 19.8 %collective-permute-start.31 = (bf16[4,80,2048]{2,1,0:T(8,128)(2,1)}, bf16[4,80,2048]{2,1,0:T(8,128)(2,1)}, u32[]{:S(2)}, u32[]{:S(2)}) collective-permute-start(bf16[4,80,2048]{2,1,0:T(8,128)(2,1)} %dynamic-slice_bitcast_fusion), channel_id=1, source_target_pairs={{0,4},{4,0},{1,5},{5,1},{2,6},{6,2},{3,7},{7,3},{8,12},{12,8},{9,1... | collective-permute-start | bytes 3932168 | tf_op jit(solution)/shard_map/ppermute | solution.py:502
  573.5 26.4 %collective-permute-start.27 = (bf16[160,2048]{1,0:T(8,128)(2,1)}, bf16[160,2048]{1,0:T(8,128)(2,1)}, u32[]{:S(2)}, u32[]{:S(2)}) collective-permute-start(bf16[160,2048]{1,0:T(8,128)(2,1)} %get-tuple-element.164), channel_id=1, source_target_pairs={{0,16},{8,24},{16,0},{24,8},{1,17},{9,25},{17,1},{25,9},{2,18},{10... | collective-permute-start | bytes 1966088 | tf_op jit(solution)/shard_map/ppermute | solution.py:462
  576.4 26.6 %collective-permute-start.29 = (bf16[160,2048]{1,0:T(8,128)(2,1)}, bf16[160,2048]{1,0:T(8,128)(2,1)}, u32[]{:S(2)}, u32[]{:S(2)}) collective-permute-start(bf16[160,2048]{1,0:T(8,128)(2,1)} %get-tuple-element.167), channel_id=1, source_target_pairs={{0,8},{8,0},{16,24},{24,16},{1,9},{9,1},{17,25},{25,17},{2,10},{10... | collective-permute-start | bytes 1966088 | tf_op jit(solution)/shard_map/ppermute | solution.py:462
  599.9 24.7 %collective-permute-start.32 = (bf16[4,4,64,1280]{3,2,1,0:T(8,128)(2,1)}, bf16[4,4,64,1280]{3,2,1,0:T(8,128)(2,1)}, u32[]{:S(2)}, u32[]{:S(2)}) collective-permute-start(bf16[4,4,64,1280]{3,2,1,0:T(8,128)(2,1)} %get-tuple-element.175), channel_id=1, source_target_pairs={{0,4},{4,0},{1,5},{5,1},{2,6},{6,2},{3,7},{7,3},{8,12},{12,8},{9,1... | collective-permute-start | bytes 7864328 | tf_op jit(solution)/shard_map/ppermute | solution.py:493
  602.4 110.5 %collective-permute-start.28 = (bf16[320,2048]{1,0:T(8,128)(2,1)}, bf16[320,2048]{1,0:T(8,128)(2,1)}, u32[]{:S(2)}, u32[]{:S(2)}) collective-permute-start(bf16[320,2048]{1,0:T(8,128)(2,1)} %pad_maximum_fusion.6), channel_id=1, source_target_pairs={{0,8},{8,0},{16,24},{24,16},{1,9},{9,1},{17,25},{25,17},{2,10},{10... | collective-permute-start | bytes 3932168 | tf_op jit(solution)/shard_map/ppermute | solution.py:462
  605.9 107.1 %collective-permute-start.30 = (bf16[320,2048]{1,0:T(8,128)(2,1)}, bf16[320,2048]{1,0:T(8,128)(2,1)}, u32[]{:S(2)}, u32[]{:S(2)}) collective-permute-start(bf16[320,2048]{1,0:T(8,128)(2,1)} %pad_maximum_fusion.7), channel_id=1, source_target_pairs={{0,16},{8,24},{16,0},{24,8},{1,17},{9,25},{17,1},{25,9},{2,18},{10... | collective-permute-start | bytes 3932168 | tf_op jit(solution)/shard_map/ppermute | solution.py:462
  620.3 25.1 %all-to-all-start.4 = ((bf16[4,64,1,1536]{3,1,2,0:T(8,128)(2,1)}), bf16[4,64,1,1536]{3,1,2,0:T(8,128)(2,1)}, u32[]{:S(2)}, u32[]{:S(2)}) async-start(bf16[4,64,1,1536]{3,1,2,0:T(8,128)(2,1)} %bitcast.47), calls=%async_computation.8 | async-start | bytes 1572864 | tf_op jit(solution)/shard_map/all_to_all | solution.py:509
  624.6 98.7 %reduce-scatter.15.cloned.1.call-start = ((), (), s32[]{:S(2)}) async-start(), calls=%async_computation.20 | async-start | bytes 3276800 | tf_op jit(solution)/shard_map/reduce_scatter | solution.py:506
  649.6 91.5 %reduce-scatter.17.cloned.1.call-start = ((), (), s32[]{:S(2)}) async-start(), calls=%async_computation.21 | async-start | bytes 614400 | tf_op jit(solution)/shard_map/reduce_scatter | solution.py:506
  649.7 16.4 %collective-permute-start.33 = (bf16[160,2048]{1,0:T(8,128)(2,1)}, bf16[160,2048]{1,0:T(8,128)(2,1)}, u32[]{:S(2)}, u32[]{:S(2)}) collective-permute-start(bf16[160,2048]{1,0:T(8,128)(2,1)} %get-tuple-element.190), channel_id=1, source_target_pairs={{0,16},{8,24},{16,0},{24,8},{1,17},{9,25},{17,1},{25,9},{2,18},{10... | collective-permute-start | bytes 1966088 | tf_op jit(solution)/shard_map/ppermute | solution.py:462
  652.0 18.2 %collective-permute-start.35 = (bf16[160,2048]{1,0:T(8,128)(2,1)}, bf16[160,2048]{1,0:T(8,128)(2,1)}, u32[]{:S(2)}, u32[]{:S(2)}) collective-permute-start(bf16[160,2048]{1,0:T(8,128)(2,1)} %get-tuple-element.192), channel_id=1, source_target_pairs={{0,8},{8,0},{16,24},{24,16},{1,9},{9,1},{17,25},{25,17},{2,10},{10... | collective-permute-start | bytes 1966088 | tf_op jit(solution)/shard_map/ppermute | solution.py:462
  668.7 29.4 %collective-permute-start.34 = (bf16[320,2048]{1,0:T(8,128)(2,1)}, bf16[320,2048]{1,0:T(8,128)(2,1)S(1)}, u32[]{:S(2)}, u32[]{:S(2)}) collective-permute-start(bf16[320,2048]{1,0:T(8,128)(2,1)} %pad_maximum_fusion.8), channel_id=1, source_target_pairs={{0,8},{8,0},{16,24},{24,16},{1,9},{9,1},{17,25},{25,17},{2,10},{10... | collective-permute-start | bytes 3932168 | tf_op jit(solution)/shard_map/ppermute | solution.py:462
  672.7 29.2 %collective-permute-start.36 = (bf16[320,2048]{1,0:T(8,128)(2,1)}, bf16[320,2048]{1,0:T(8,128)(2,1)}, u32[]{:S(2)}, u32[]{:S(2)}) collective-permute-start(bf16[320,2048]{1,0:T(8,128)(2,1)} %pad_maximum_fusion.9), channel_id=1, source_target_pairs={{0,16},{8,24},{16,0},{24,8},{1,17},{9,25},{17,1},{25,9},{2,18},{10... | collective-permute-start | bytes 3932168 | tf_op jit(solution)/shard_map/ppermute | solution.py:462
  673.7 32.1 %collective-permute-start.43 = (f32[4,80,384]{2,1,0:T(8,128)S(1)}, f32[4,80,384]{2,1,0:T(8,128)S(1)}, u32[]{:S(2)}, u32[]{:S(2)}) collective-permute-start(f32[4,80,384]{2,1,0:T(8,128)S(1)} %dynamic-slice_bitcast_fusion.1), channel_id=1, source_target_pairs={{0,4},{4,0},{1,5},{5,1},{2,6},{6,2},{3,7},{7,3},{8,12},{12,8},{9,1... | collective-permute-start | bytes 1474568 | tf_op jit(solution)/shard_map/ppermute | solution.py:502
  705.2 3.8 collective-permute-start.37
  709.0 3.8 collective-permute-start.38
  712.8 4.6 collective-permute-start.39
  717.4 10.7 %collective-permute-start.40 = (f32[2,2048]{1,0:T(2,128)S(1)}, f32[2,2048]{1,0:T(2,128)S(1)}, u32[]{:S(2)}, u32[]{:S(2)}) collective-permute-start(f32[2,2048]{1,0:T(2,128)S(1)} %add.316), channel_id=1, source_target_pairs={{0,1},{1,2},{2,3},{3,0},{4,5},{5,6},{6,7},{7,4},{8,9},{9,10},{10,1... | collective-permute-start | bytes 49160 | tf_op jit(solution)/shard_map/ppermute | solution.py:541
  718.9 9.2 %collective-permute-start.41 = (f32[2,2048]{1,0:T(2,128)S(1)}, f32[2,2048]{1,0:T(2,128)S(1)}, u32[]{:S(2)}, u32[]{:S(2)}) collective-permute-start(f32[2,2048]{1,0:T(2,128)S(1)} %add.316), channel_id=1, source_target_pairs={{0,2},{1,3},{2,0},{3,1},{4,6},{5,7},{6,4},{7,5},{8,10},{9,11},{10,... | collective-permute-start | bytes 49160 | tf_op jit(solution)/shard_map/ppermute | solution.py:541
  720.8 7.3 collective-permute-start.42
  723.3 13.0 %all-to-all-start.6 = ((bf16[4,64,1,1280]{3,1,2,0:T(8,128)(2,1)}), bf16[4,64,1,1280]{3,1,2,0:T(8,128)(2,1)S(1)}, u32[]{:S(2)}, u32[]{:S(2)}) async-start(bf16[4,64,1,1280]{3,1,2,0:T(8,128)(2,1)} %bitcast.206), calls=%async_computation.11 | async-start | bytes 1310720 | tf_op jit(solution)/shard_map/all_to_all | solution.py:509
  (84 other events, 853.5 us)
Sparse Core Ops, SparseCore 0:
  25.0 66.4 all-gather.3
  93.7 84.9 all-gather.5
  185.7 115.9 all-gather.7
  378.8 58.4 reduce-scatter.6
  439.4 60.2 reduce-scatter.8
  503.3 59.8 reduce-scatter.10
  603.1 30.7 reduce-scatter.12
  649.7 51.6 reduce-scatter.14
  723.4 17.6 reduce-scatter.16

commit v4 on v3

--- a/solution.py
+++ b/solution.py
@@ -46,28 +46,27 @@
     return values * half, grad
 
 
-def minus_expm1(values):
-    series = 1.0 + values * (1.0 / 6.0) * (1.0 + values * (1.0 / 7.0))
-    for order in (5.0, 4.0, 3.0, 2.0):
-        series = 1.0 + values * (1.0 / order) * series
-    return jnp.where(values > -0.25, -values * series, 1.0 - jnp.exp(values))
-
-
 def softplus_minus(values):
     return jnp.maximum(-values, 0.0) + jnp.log(1.0 + jnp.exp(-jnp.abs(values)))
 
 
-def lru_terms(conv, rate_pre, input_pre, soft):
-    rate_gate = 1.0 / (1.0 + jnp.exp(-rate_pre))
-    input_gate = 1.0 / (1.0 + jnp.exp(-input_pre))
+def sigmoid(values):
+    return 1.0 / (1.0 + jnp.exp(jnp.minimum(-values, 80.0)))
+
+
+def lru_terms(rate_pre, input_pre, soft):
+    rate_gate = sigmoid(rate_pre)
+    input_gate = sigmoid(input_pre)
     log_decay = -RATE_SCALE * rate_gate * soft
     decay_now = jnp.exp(log_decay)
-    scale_in = jnp.sqrt(minus_expm1(2.0 * log_decay))
-    return rate_gate, input_gate, decay_now, scale_in
-
-
-CHUNK = 64
-UNROLL = 8
+    twice = 2.0 * log_decay
+    series = -twice * (1.0 + twice * 0.5 * (1.0 + twice * (1.0 / 3.0) * (1.0 + twice * 0.25)))
+    square = jnp.maximum(jnp.where(twice > -0.0625, series, 1.0 - decay_now * decay_now), 1e-30)
+    return rate_gate, input_gate, decay_now, square, lax.rsqrt(square)
+
+
+CHUNK = 160
+UNROLL = 16
 
 
 def lru_forward_kernel(seqs, conv_ref, rate_ref, input_ref, gate_ref, soft_ref, states_ref, mixed_ref, decay_s, drive_s):
@@ -78,17 +77,19 @@
     def prepare(i, carry):
         at = pl.ds(pl.multiple_of(i * CHUNK, CHUNK), CHUNK)
         conv = conv_ref[at, :].astype(jnp.float32)
-        _, input_gate, decay_now, scale_in = lru_terms(conv, rate_ref[at, :], input_ref[at, :], soft)
+        _, input_gate, decay_now, square, inverse = lru_terms(rate_ref[at, :], input_ref[at, :], soft)
         decay_s[at, :] = decay_now
-        drive_s[at, :] = scale_in * input_gate * conv
+        drive_s[at, :] = square * inverse * input_gate * conv
         return carry
 
     lax.fori_loop(0, rows // CHUNK, prepare, 0)
 
     def advance(i, state):
-        for j in range(UNROLL):
-            at = pl.ds(i * UNROLL + j, seqs, stride=length)
-            state = decay_s[at, :] * state + drive_s[at, :]
+        places = [pl.ds(i * UNROLL + j, seqs, stride=length) for j in range(UNROLL)]
+        decays = [decay_s[at, :] for at in places]
+        drives = [drive_s[at, :] for at in places]
+        for at, decay, drive in zip(places, decays, drives):
+            state = decay * state + drive
             states_ref[at, :] = state
         return state
 
@@ -119,7 +120,11 @@
     sums_ref,
     decay_s,
     flow_s,
-    before_s,
+    total_s,
+    gate_s,
+    drive_s,
+    input_s,
+    scale_s,
 ):
     rows = conv_ref.shape[0]
     length = rows // seqs
@@ -131,45 +136,46 @@
         grad = grad_ref[at, :]
         d_gate_ref[at, :] = (grad * states_ref[at, :] * slope).astype(jnp.bfloat16)
         flow_s[at, :] = grad * value
-        rate_gate = 1.0 / (1.0 + jnp.exp(-rate_ref[at, :]))
-        decay_s[at, :] = jnp.exp(-RATE_SCALE * rate_gate * soft)
+        conv = conv_ref[at, :].astype(jnp.float32)
+        rate_gate, input_gate, decay_now, square, inverse = lru_terms(rate_ref[at, :], input_ref[at, :], soft)
+        drive = square * inverse * input_gate
+        decay_s[at, :] = decay_now
+        gate_s[at, :] = rate_gate
+        drive_s[at, :] = drive
+        input_s[at, :] = drive * conv * (1.0 - input_gate)
+        scale_s[at, :] = input_gate * conv * decay_now * inverse
         return carry
 
     lax.fori_loop(0, rows // CHUNK, prepare, 0)
 
     def retreat(i, carry):
         flow, decay = carry
-        for j in range(UNROLL):
-            step = length - 1 - (i * UNROLL + j)
-            at = pl.ds(step, seqs, stride=length)
-            flow = flow_s[at, :] + decay * flow
-            flow_s[at, :] = flow
-            decay = decay_s[at, :]
-        return flow, decay
+        places = [pl.ds(length - 1 - (i * UNROLL + j), seqs, stride=length) for j in range(UNROLL)]
+        flows = [flow_s[at, :] for at in places]
+        decays = [decay_s[at, :] for at in places]
+        for at, here, later in zip(places, flows, [decay] + decays[:-1]):
+            flow = here + later * flow
+            total_s[at, :] = flow
+        return flow, decays[-1]
 
     nothing = jnp.zeros((seqs, LANES), jnp.float32)
     lax.fori_loop(0, length // UNROLL, retreat, (nothing, nothing))
 
-    def shift(i, last):
-        for j in range(UNROLL):
-            at = pl.ds(i * UNROLL + j, seqs, stride=length)
-            before_s[at, :] = last
-            last = states_ref[at, :]
-        return last
-
-    lax.fori_loop(0, length // UNROLL, shift, nothing)
+    first_row = lax.broadcasted_iota(jnp.int32, (CHUNK, LANES), 0) == 0
 
     def finish(i, carry):
-        rate_sum, input_sum, soft_sum = carry
+        rate_sum, input_sum, soft_sum, last = carry
         at = pl.ds(pl.multiple_of(i * CHUNK, CHUNK), CHUNK)
-        conv = conv_ref[at, :].astype(jnp.float32)
-        rate_gate, input_gate, decay_now, scale_in = lru_terms(conv, rate_ref[at, :], input_ref[at, :], soft)
-        flow = flow_s[at, :]
-        d_scale = flow * input_gate * conv
-        d_log = decay_now * (flow * before_s[at, :] - d_scale * decay_now / scale_in)
-        d_input = flow * scale_in * conv * input_gate * (1.0 - input_gate)
-        d_rate = d_log * (-RATE_SCALE) * soft * rate_gate * (1.0 - rate_gate)
-        d_conv_ref[at, :] = flow * scale_in * input_gate
+        states = states_ref[at, :]
+        last = jnp.where(lax.rem(i, length // CHUNK) == 0, jnp.zeros_like(last), last)
+        before = jnp.where(first_row, last, pltpu.roll(states, 1, 0))
+        flow = total_s[at, :]
+        rate_gate = gate_s[at, :]
+        d_log = flow * decay_s[at, :] * (before - scale_s[at, :])
+        d_soft = d_log * rate_gate * (-RATE_SCALE)
+        d_rate = d_soft * soft * (1.0 - rate_gate)
+        d_input = flow * input_s[at, :]
+        d_conv_ref[at, :] = flow * drive_s[at, :]
         d_rate_ref[at, :] = d_rate.astype(jnp.bfloat16)
         d_input_ref[at, :] = d_input.astype(jnp.bfloat16)
 
@@ -178,13 +184,12 @@
                 total = total + part[k * 8 : (k + 1) * 8, :]
             return total
 
-        return (fold(rate_sum, d_rate), fold(input_sum, d_input), fold(soft_sum, d_log * (-RATE_SCALE) * rate_gate))
+        return fold(rate_sum, d_rate), fold(input_sum, d_input), fold(soft_sum, d_soft), states[CHUNK - 1 :, :]
 
     blank = jnp.zeros((8, LANES), jnp.float32)
-    rate_sum, input_sum, soft_sum = lax.fori_loop(0, rows // CHUNK, finish, (blank, blank, blank))
-    sums_ref[0:8, :] = rate_sum
-    sums_ref[8:16, :] = input_sum
-    sums_ref[16:24, :] = soft_sum
+    sums = lax.fori_loop(0, rows // CHUNK, finish, (blank, blank, blank, jnp.zeros((1, LANES), jnp.float32)))
+    for k in range(3):
+        sums_ref[k * 8 : (k + 1) * 8, :] = sums[k]
 
 
 def lru_forward(seqs, conv, rate_pre, input_pre, gate_pre, soft):
@@ -221,7 +226,7 @@
         ),
         in_specs=[block, block, block, block, pl.BlockSpec((8, LANES), lambda i: (0, i)), block, block],
         out_specs=(block, block, block, block, pl.BlockSpec((24, LANES), lambda i: (0, i))),
-        scratch_shapes=[pltpu.VMEM((rows, LANES), jnp.float32)] * 3,
+        scratch_shapes=[pltpu.VMEM((rows, LANES), jnp.float32)] * 7,
         compiler_params=pltpu.CompilerParams(vmem_limit_bytes=48 * 2**20),
         cost_estimate=pl.CostEstimate(flops=200000 * rows * channels // 10, bytes_accessed=20 * rows * channels, transcendentals=16 * rows * channels),
         name="lru_backward",
@@ -236,19 +241,29 @@
     return max(w for w in range(LANES, most + 1, LANES) if columns % w == 0)
 
 
-def mlp_kernel(slots, n2_ref, low_ref, gate_ref, up_ref, down_ref, product_ref, d_gate_ref, d_up_ref, w_s):
+def mlp_kernel(slots, *refs):
+    parts, refs = refs[: slots + 1], refs[slots + 1 :]
+    low_ref, gate_ref, up_ref, down_ref, product_ref, d_gate_ref, d_up_ref, normed_ref, w_s = refs
     groups, rows = gate_ref.shape[1], gate_ref.shape[2]
     stride = gate_ref.shape[0] * rows
+
+    @pl.when(pl.program_id(0) == 0)
+    def _():
+        start = 0
+        for part in parts:
+            normed_ref[start : start + part.shape[0], :] = part[...]
+            start += part.shape[0]
+
     for c in range(groups):
         for k in range(gate_ref.shape[0]):
             at = pl.ds(c * stride + k * rows, rows)
             w_s[0, at, :] = gate_ref[k, c]
             w_s[1, at, :] = up_ref[k, c]
-    length = n2_ref.shape[0] // slots
+    length = low_ref.shape[0] // slots
 
     for i in range(slots):
         at = pl.ds(i * length, length)
-        here = n2_ref[at, :]
+        here = normed_ref[at, :]
         gate = jnp.dot(here, w_s[0], preferred_element_type=jnp.float32)
         up = jnp.dot(here, w_s[1], preferred_element_type=jnp.float32)
         grad = matmul_nt(low_ref[at, :], down_ref[...])
@@ -258,31 +273,65 @@
         d_up_ref[at, :] = (grad * value).astype(jnp.bfloat16)
 
 
-def mlp_both(slots, normed, low_res, weights, w_down):
-    tokens, width = normed.shape
+def mlp_both(parts, low_res, weights, w_down):
+    tokens, width = low_res.shape
     hidden = w_down.shape[0]
     block = column_block(hidden, 256)
     steps = hidden // block
     lead = weights.shape[:3]
     return pl.pallas_call(
-        functools.partial(mlp_kernel, slots),
+        functools.partial(mlp_kernel, PLANE),
         grid=(steps,),
-        out_shape=(jax.ShapeDtypeStruct((tokens, hidden), jnp.bfloat16),) * 3,
-        in_specs=[
-            pl.BlockSpec((tokens, width), lambda j: (0, 0), pipeline_mode=CONSTANT),
+        out_shape=(jax.ShapeDtypeStruct((tokens, hidden), jnp.bfloat16),) * 3
+        + (jax.ShapeDtypeStruct((tokens, width), jnp.bfloat16),),
+        in_specs=[pl.BlockSpec(p.shape, lambda j: (0, 0), pipeline_mode=CONSTANT) for p in parts]
+        + [
             pl.BlockSpec((tokens, width), lambda j: (0, 0), pipeline_mode=CONSTANT),
             pl.BlockSpec(lead + (block,), lambda j: (0, 0, 0, j)),
             pl.BlockSpec(lead + (block,), lambda j: (0, 0, 0, j + steps)),
             pl.BlockSpec((block, width), lambda j: (j, 0)),
         ],
-        out_specs=(pl.BlockSpec((tokens, block), lambda j: (0, j)),) * 3,
+        out_specs=(pl.BlockSpec((tokens, block), lambda j: (0, j)),) * 3
+        + (pl.BlockSpec((tokens, width), lambda j: (0, 0)),),
         scratch_shapes=[pltpu.VMEM((2, width, block), jnp.bfloat16)],
         compiler_params=pltpu.CompilerParams(vmem_limit_bytes=VMEM_BYTES),
         cost_estimate=pl.CostEstimate(
-            flops=6 * tokens * width * hidden, bytes_accessed=2 * (2 * tokens * width + 3 * width * hidden), transcendentals=tokens * hidden
+            flops=6 * tokens * width * hidden, bytes_accessed=2 * (3 * tokens * width + 3 * width * hidden), transcendentals=tokens * hidden
         ),
         name="mlp_both",
-    )(normed, low_res, weights, weights, w_down)
+    )(*parts, low_res, weights, weights, w_down)
+
+
+def mixed_grad_kernel(*refs):
+    parts, w_ref, grad_ref, whole_ref = refs[:-3], refs[-3], refs[-2], refs[-1]
+    start = 0
+    weight = w_ref[...].reshape(-1, w_ref.shape[-1])
+    for part in parts:
+        at = pl.ds(start, part.shape[0])
+        here = part[...]
+        whole_ref[at, :] = here
+        grad_ref[at, :] = matmul_nt(here, weight)
+        start += part.shape[0]
+
+
+def mixed_grad(parts, weight):
+    weight, rows = weight
+    width = parts[0].shape[1]
+    tokens = sum(p.shape[0] for p in parts)
+    inner = weight.shape[0] * rows
+    return pl.pallas_call(
+        mixed_grad_kernel,
+        grid=(1,),
+        out_shape=(jax.ShapeDtypeStruct((tokens, inner), jnp.float32), jax.ShapeDtypeStruct((tokens, width), jnp.bfloat16)),
+        in_specs=[pl.BlockSpec(p.shape, lambda j: (0, 0)) for p in parts]
+        + [pl.BlockSpec((weight.shape[0], rows, width), lambda j: (0, 0, 0))],
+        out_specs=(pl.BlockSpec((tokens, inner), lambda j: (0, 0)), pl.BlockSpec((tokens, width), lambda j: (0, 0))),
+        compiler_params=pltpu.CompilerParams(vmem_limit_bytes=VMEM_BYTES),
+        cost_estimate=pl.CostEstimate(
+            flops=2 * tokens * inner * width, bytes_accessed=4 * tokens * (width + inner) + 2 * inner * width, transcendentals=0
+        ),
+        name="mixed_grad",
+    )(*parts, weight)
 
 
 def store_parts(refs, length, part, value):
@@ -346,12 +395,14 @@
 
 
 def out_kernel(values_ref, w_ref, *refs):
-    store_all(refs, jnp.dot(values_ref[...], w_ref[...], preferred_element_type=jnp.float32))
+    weight = w_ref[...].reshape(-1, w_ref.shape[-1])
+    store_all(refs, jnp.dot(values_ref[...], weight, preferred_element_type=jnp.float32))
 
 
 def out_parts(values, weight):
+    weight, rows = weight
     tokens, inner = values.shape
-    width = weight.shape[1]
+    shares, _, width = weight.shape
     block = column_block(width, 512)
     shapes, specs = parts_out(tokens // PLANE, width, block)
     return pl.pallas_call(
@@ -360,7 +411,7 @@
         out_shape=shapes,
         in_specs=[
             pl.BlockSpec((tokens, inner), lambda j: (0, 0), pipeline_mode=CONSTANT),
-            pl.BlockSpec((inner, block), lambda j: (0, j)),
+            pl.BlockSpec((shares, rows, block), lambda j: (0, 0, j)),
         ],
         out_specs=specs,
         compiler_params=pltpu.CompilerParams(vmem_limit_bytes=VMEM_BYTES),
@@ -371,7 +422,9 @@
     )(values, weight)
 
 
-def weight_grad_kernel(rows, me_ref, left_ref, right_ref, mine_ref, theirs_ref, left_s):
+def weight_grad_kernel(rows, me_ref, left_ref, right_ref, mine_ref, *refs):
+    theirs, left_s = refs[:-1], refs[-1]
+
     @pl.when(pl.program_id(1) == 0)
     def _():
         left_s[...] = left_ref[...].T
@@ -380,19 +433,21 @@
     height = narrow * rows
     total = jnp.dot(left_s[...], right_ref[0], preferred_element_type=jnp.float32).astype(jnp.bfloat16)
 
-    def store(first_ref, second_ref):
+    def store(mine, other):
         for g in range(groups):
-            for share, ref in enumerate((first_ref, second_ref)):
-                start = (g * 2 + share) * height
-                ref[:, g] = total[start : start + height].reshape(narrow, rows, block)
+            start = (g * 2 + mine) * height
+            mine_ref[:, g] = total[start : start + height].reshape(narrow, rows, block)
+            start = (g * 2 + other) * height
+            for k, ref in enumerate(theirs):
+                ref[0, g] = total[start + k * rows : start + (k + 1) * rows]
 
     @pl.when(me_ref[0] == 0)
     def _():
-        store(mine_ref, theirs_ref)
+        store(0, 1)
 
     @pl.when(me_ref[0] != 0)
     def _():
-        store(theirs_ref, mine_ref)
+        store(1, 0)
 
 
 def weight_grad(me, left, right, narrow, groups, rows):
@@ -402,8 +457,7 @@
     steps = piece // block
     together = 2 if groups % 2 == 0 else 1
     height = together * 2 * narrow * rows
-    place = pl.BlockSpec((narrow, together, rows, block), lambda g, j, me_ref: (0, g, 0, j))
-    shape = jax.ShapeDtypeStruct((narrow, groups, rows, pieces * piece), jnp.bfloat16)
+    columns = pieces * piece
     return pl.pallas_call(
         functools.partial(weight_grad_kernel, rows),
         grid_spec=pltpu.PrefetchScalarGridSpec(
@@ -413,18 +467,41 @@
                 pl.BlockSpec((tokens, height), lambda g, j, me_ref: (0, g)),
                 pl.BlockSpec((1, tokens, block), lambda g, j, me_ref: (j // steps, 0, j % steps)),
             ],
-            out_specs=(place, place),
+            out_specs=(pl.BlockSpec((narrow, together, rows, block), lambda g, j, me_ref: (0, g, 0, j)),)
+            + (pl.BlockSpec((1, together, rows, block), lambda g, j, me_ref: (0, g, 0, j)),) * narrow,
             scratch_shapes=[pltpu.VMEM((height, tokens), jnp.bfloat16)],
         ),
-        out_shape=(shape, shape),
+        out_shape=(jax.ShapeDtypeStruct((narrow, groups, rows, columns), jnp.bfloat16),)
+        + (jax.ShapeDtypeStruct((1, groups, rows, columns), jnp.bfloat16),) * narrow,
         compiler_params=pltpu.CompilerParams(vmem_limit_bytes=VMEM_BYTES),
         cost_estimate=pl.CostEstimate(
-            flops=2 * tokens * left.shape[1] * pieces * piece,
-            bytes_accessed=2 * (left.size + groups // together * right.size + left.shape[1] * pieces * piece),
+            flops=2 * tokens * left.shape[1] * columns,
+            bytes_accessed=2 * (left.size + groups // together * right.size + left.shape[1] * columns),
             transcendentals=0,
         ),
         name="weight_grad",
     )(me, left, right)
+
+
+def add_pieces_kernel(mine_ref, *refs):
+    for k, ref in enumerate(refs[:-1]):
+        refs[-1][k] = (mine_ref[k].astype(jnp.float32) + ref[0].astype(jnp.float32)).astype(jnp.bfloat16)
+
+
+def add_pieces(mine, others):
+    narrow, groups, rows, columns = mine.shape
+    block = column_block(columns, 1024)
+    place = pl.BlockSpec((narrow, 1, rows, block), lambda g, j: (0, g, 0, j))
+    return pl.pallas_call(
+        add_pieces_kernel,
+        grid=(groups, columns // block),
+        out_shape=jax.ShapeDtypeStruct(mine.shape, jnp.bfloat16),
+        in_specs=[place] + [pl.BlockSpec((1, 1, rows, block), lambda g, j: (0, g, 0, j))] * narrow,
+        out_specs=place,
+        compiler_params=pltpu.CompilerParams(vmem_limit_bytes=VMEM_BYTES),
+        cost_estimate=pl.CostEstimate(flops=mine.size, bytes_accessed=6 * mine.size, transcendentals=0),
+        name="add_pieces",
+    )(mine, *others)
 
 
 def block_diagonal(table):
@@ -461,20 +538,27 @@
     def swap(values, mask):
         return lax.ppermute(values, "wide", [(i, i ^ mask) for i in range(PLANE)])
 
-    def gather_rows(shard):
+    def gather_parts(shard):
         half = shard.shape[0] // 2
         one, two = swap(shard, 1), swap(shard, 2)
-        far = [swap(one[:half], 2), swap(two[half:], 1)]
-        return jnp.concatenate(far + [one, two, shard], axis=0)
-
-    def scatter_rows(parts, *hold):
+        return [swap(one[:half], 2), swap(two[half:], 1), one, two, shard]
+
+    def gather_rows(shard):
+        return jnp.concatenate(gather_parts(shard), axis=0)
+
+    def scatter_start(parts):
         far_low, far_high, one, two, own = parts
         half = own.shape[0] // 2
         via_one, via_two = swap(far_low, 1), swap(far_high, 2)
-        one, two = after(one, *hold), after(two, *hold)
         one = jnp.concatenate([one[:half], (one[half:].astype(f32) + via_two.astype(f32)).astype(bf16)], axis=0)
         two = jnp.concatenate([(two[:half].astype(f32) + via_one.astype(f32)).astype(bf16), two[half:]], axis=0)
+        return one, two, own
+
+    def scatter_finish(one, two, own):
         return own.astype(f32) + swap(one, 1).astype(f32) + swap(two, 2).astype(f32)
+
+    def scatter_rows(parts):
+        return scatter_finish(*scatter_start(parts))
 
     def cut_columns(blocks):
         return lax.all_to_all(blocks, "wide", 0, 0, tiled=False)
@@ -489,9 +573,9 @@
             cut = grad.reshape(groups, rest_size, narrow_size, rows, -1).transpose(1, 2, 0, 3, 4)
             return grad, lambda *waits: lax.psum_scatter(after(cut, *waits), "rest", scatter_dimension=0, tiled=False)
         me = lax.axis_index("rest").astype(jnp.int32)[None]
-        mine, theirs = weight_grad(me, left, right, narrow_size, groups, rows)
-        other = lax.ppermute(theirs, "rest", [(0, 1), (1, 0)])
-        return theirs, lambda *waits: (after(mine, *waits).astype(f32) + other.astype(f32)).astype(bf16)
+        mine, *theirs = weight_grad(me, left, right, narrow_size, groups, rows)
+        others = [lax.ppermute(piece, "rest", [(0, 1), (1, 0)]) for piece in theirs]
+        return mine, lambda *waits: add_pieces(after(mine, *waits), others)
 
     def sum_rest(values):
         if rest_size != 2:
@@ -528,18 +612,6 @@
 
     def after(values, *others):
         return lax.optimization_barrier((values,) + others)[0]
-
-    def sum_all(values):
-        values = values + swap(values, 1)
-        values = values + swap(values, 2)
-        if rest_size == 2:
-            values = values + lax.ppermute(values, "rest", [(0, 1), (1, 0)])
-        else:
-            values = lax.psum(values, "rest")
-        total = values
-        for step in range(1, narrow_size):
-            total = total + lax.ppermute(values, "narrow", [(i, (i + step) % narrow_size) for i in range(narrow_size)])
-        return total
 
     def on_device(
         tokens,
@@ -603,13 +675,15 @@
             after(jnp.concatenate([out_proj, mlp_down], axis=0), w_rec), spread, axis=0, tiled=True
         ).reshape(rest_size * narrow_size, -1, width)
         low_res = (cotangent.astype(f32) * live).astype(bf16)
-        low_res_all = gather_rows(after(low_res, w_rec))
+        low_res_parts = gather_parts(after(low_res, w_rec))
+        low_res_all = jnp.concatenate(low_res_parts, axis=0)
         gains = gains.swapaxes(0, 1).reshape(2, width).astype(f32)
         gain_one, gain_two = gains[0:1], gains[1:2]
         table = table.reshape(channels, -1).T
         w_flat = w_rec.swapaxes(0, 1).reshape(width, columns)
         tokens_f = tokens_all.astype(f32)
-        normed1 = (tokens_f * rms_inverse(tokens_f) * gain_one).astype(bf16)
+        inverse_all = rms_inverse(tokens_f)
+        normed1 = (tokens_f * inverse_all * gain_one).astype(bf16)
         gate_pre = matmul_low(normed1, w_flat[:, :channels])
         branch_pre = matmul_low(normed1, w_flat[:, channels:])
         kernel, shift, rate_table, b_rate, input_table, b_input, decay = (
@@ -620,7 +694,7 @@
         w_input = block_diagonal(input_table)
         soft = softplus_minus(decay_f)
         soft_rows = jnp.broadcast_to(soft, (8, soft.shape[1]))
-        part_mlp = cut_columns(after(cut_mlp, low_res_all))
+        part_mlp = cut_columns(after(cut_mlp, *low_res_parts))
 
         conv = shift_f
         for tap in range(taps):
@@ -630,17 +704,20 @@
         input_pre = matmul_low(conv, w_input) + b_input
         states, mixed = lru_forward(seqs, conv, rate_pre, input_pre, gate_pre, soft_rows)
         mixed, part_mlp, out_and_down = fence(mixed, part_mlp, out_and_down)
-        w_out = out_and_down[:, : out_proj.shape[0]].reshape(-1, width)
-        w_down = out_and_down[:, out_proj.shape[0] :].reshape(-1, width)
+        out_rows = out_proj.shape[0]
+        if out_rows % 16 == 0:
+            w_out = (out_and_down, out_rows)
+        else:
+            w_out = (out_and_down[:, :out_rows].reshape(1, -1, width), shares * out_rows)
+        w_down = out_and_down[:, out_rows:].reshape(-1, width)
 
         w_mlp = gather_spread(part_mlp)
         merged = tokens.astype(f32) + scatter_rows(out_parts(mixed, w_out))
         inverse2 = rms_inverse(merged)
         normed2 = (merged * inverse2 * gain_two).astype(bf16)
-        normed2_all = gather_rows(normed2)
-        normed2_all, w_mlp = fence(normed2_all, w_mlp)
-
-        product, d_gate_two, d_up_two = mlp_both(PLANE, normed2_all, low_res_all, w_mlp, w_down)
+        *normed2_parts, w_mlp = fence(*gather_parts(normed2), w_mlp)
+
+        product, d_gate_two, d_up_two, normed2_all = mlp_both(normed2_parts, low_res_all, w_mlp, w_down)
         first, finish_down = grad_shares(product, low_res_all[None], mlp_down.shape[0], 1)
         parts2 = back_parts((after(d_gate_two, first), d_up_two), w_mlp)
         grad_down = finish_down(parts2[0])
@@ -653,47 +730,51 @@
         mgate_sum = sum_narrow(grad_mgate)
         grad_gain2 = jnp.sum(d_normed2 * merged * inverse2, axis=0)
         d_merged = low_res.astype(f32) + rms_back(merged, inverse2, gain_two, d_normed2)
-        low_merged_all = gather_rows(d_merged.astype(bf16))
-        _, finish = grad_shares(normed2_all, after(d_up_two, d_normed2)[None], rows, PLANE)
-        grad_mup = finish()
-        parts_result = out_parts(after(product, d_normed2), w_down)
-        low_merged_all, parts_result, grad_mup, mgate_sum = fence(low_merged_all, parts_result, grad_mup, mgate_sum)
+        low_merged = d_merged.astype(bf16)
+        low_merged_parts = gather_parts(low_merged)
+        _, finish = grad_shares(normed2_all, after(d_up_two, low_merged)[None], rows, PLANE)
+        grad_mup = finish(*low_merged_parts[2:4])
+        parts_result = out_parts(after(product, *low_merged_parts[2:4]), (w_down[None], w_down.shape[0]))
+        *low_merged_parts, parts_result, mgate_sum, grad_mup = fence(*low_merged_parts, parts_result, mgate_sum, grad_mup)
+        d_mixed, low_merged_all = mixed_grad(low_merged_parts, w_out)
         mup_sum = sum_narrow(grad_mup)
-        d_mixed = matmul_nt(low_merged_all, w_out)
+        sums_result = scatter_start(parts_result)
+        d_mixed, *sums_result = fence(d_mixed, *sums_result)
         d_conv_lru, d_rate, d_input, d_gate, sums = lru_backward(
             seqs, conv, rate_pre, input_pre, gate_pre, soft_rows, states, d_mixed
         )
-        result = merged + scatter_rows(parts_result, d_conv_lru)
         mgate_out = columns_home(after(mgate_sum, d_conv_lru), rows)
         sums = sums.reshape(3, 8, -1).sum(axis=1)
         grad_decay = sums[2] * (-1.0 / (1.0 + jnp.exp(decay_f[0])))
         d_conv = d_conv_lru + matmul_nt(d_rate, w_rate) + matmul_nt(d_input, w_input)
+        result = merged + scatter_finish(*sums_result)
         d_branch = jnp.zeros_like(d_conv)
         grad_taps = []
         for tap in range(taps):
             moved = shift_rows(d_conv, seqs, tap - (taps - 1))
             d_branch = d_branch + kernel_f[tap] * moved
             grad_taps.append(jnp.sum(branch_pre * moved, axis=0))
-        d_rec = jnp.stack([d_gate, d_branch.astype(bf16)])
-        grad_out = sum_rest(rows_cut(matmul_tn(mixed, after(low_merged_all, d_conv_lru)).astype(bf16)))
-
-        d_rec, mup_sum, grad_out = fence(d_rec, mup_sum, grad_out)
-        out_out = sum_narrow(grad_out)
-        first, finish = grad_shares(normed1, d_rec, rows, PLANE)
-        parts1 = back_parts((after(d_rec[0], first), d_rec[1]), w_rec)
-        grad_rec = finish(parts1[0])
+        low_branch = d_branch.astype(bf16)
+        d_rec = jnp.stack([d_gate, low_branch])
+
+        d_rec, mgate_out, result = fence(d_rec, mgate_out, result)
+        _, finish = grad_shares(normed1, d_rec, rows, PLANE)
+        grad_rec = finish(mup_sum)
+        rec_sum = sum_narrow(grad_rec)
         mup_out = columns_home(after(mup_sum, d_rec), rows)
-        grad_rec, parts1, out_out, mup_out, mgate_out = fence(grad_rec, parts1, out_out, mup_out, mgate_out)
-        rec_sum = sum_narrow(grad_rec)
-        d_normed1 = scatter_rows(parts1)
-        block_out = (after(result, d_normed1) * live).astype(bf16)
+        parts1 = back_parts((after(d_gate, grad_rec, mup_out), low_branch), w_rec)
+        one, two, own = scatter_start(parts1)
+        d_normed1 = scatter_finish(one, two, own)
+        grad_out = matmul_tn(mixed, after(low_merged_all, parts1)).astype(bf16)
+        normed_f = after(tokens_all, grad_rec).astype(f32) * inverse_all
+        grad_gain1 = jnp.zeros((width,), f32)
+        start = 0
+        for part in parts1:
+            grad_gain1 = grad_gain1 + jnp.sum(part.astype(f32) * normed_f[start : start + part.shape[0]], axis=0)
+            start += part.shape[0]
+        gain_grads = jnp.stack([grad_gain1, grad_gain2]).reshape(2, -1, rows).swapaxes(0, 1)
         grad_rate_weight = diagonal_blocks(matmul_tn(conv, after(d_rate, grad_rec)), head)
         grad_input_weight = diagonal_blocks(matmul_tn(conv, after(d_input, grad_rec)), head)
-        own = tokens.astype(f32)
-        inverse1 = rms_inverse(own)
-        grad_gain1 = jnp.sum(d_normed1 * own * inverse1, axis=0)
-        input_grad = d_merged + rms_back(own, inverse1, gain_one, d_normed1)
-
         table_grad = jnp.concatenate(
             [
                 jnp.stack(grad_taps),
@@ -706,16 +787,21 @@
             ],
             axis=0,
         )
-        table_grad = sum_rest(rows_cut(jnp.pad(table_grad, ((0, -places[-1] % LANES), (0, 0))).T))
-        table_out = sum_narrow(after(table_grad, rec_sum)).T
+        table_grad = jnp.pad(table_grad, ((0, -places[-1] % LANES), (0, 0))).T.astype(bf16)
+        last = sum_rest(rows_cut(jnp.concatenate([grad_out, table_grad], axis=1)))
+        rec_sum, d_normed1 = fence(rec_sum, d_normed1)
+        last = sum_narrow(after(last, rec_sum)).astype(f32)
+        out_out, table_out = last[:, :width], last[:, width:].T
+
         rec_out = columns_home(rec_sum, rows)
+        gain_out = lax.all_to_all(after(gain_grads, rec_out), ("wide",) + spread, 0, 0, tiled=False).sum(axis=0)
+        block_out = (result * live).astype(bf16)
+        own = tokens.astype(f32)
+        input_grad = d_merged + rms_back(own, rms_inverse(own), gain_one, d_normed1)
+
         kernel_out, shift_out, rate_out, rate_bias_out, input_out, input_bias_out, decay_out = (
             table_out[places[i] : places[i + 1]] for i in range(len(cuts))
         )
-        index = lax.axis_index(("wide",) + spread)
-        gain_sums = sum_all(jnp.stack([grad_gain1, grad_gain2]))
-        gain_out = lax.dynamic_slice_in_dim(gain_sums, index * rows, rows, axis=1)
-
         def whole_rows(cut):
             return cut.reshape(rows, -1).astype(f32)
 
@@ -732,7 +818,7 @@
             input_out,
             input_bias_out[0],
             decay_out[0],
-            out_out.astype(f32),
+            out_out,
             gain_out[1],
             whole_rows(mgate_out),
             whole_rows(mup_out),

time: 760 us -> 739 us (0.972)
  waiting for transfers between devices: 211 us -> 176 us
  Pallas kernels: 202 us -> 222 us
  other arithmetic: 83.7 us -> 92.5 us
  matrix products: 44.7 us -> 36.7 us
    pallas_call x1 -> x6, Pallas kernels: 34.6 us -> 70.8 us  [the longest x1 35 us: mlp_both(): pl.pallas_call(functools.partial(mlp_kernel, PLANE), grid=(steps,), out_s...]
    ppermute x34 -> x32, waiting for transfers between devices: 173 us -> 139 us  [swap(): return lax.ppermute(values, 'wide', [(i, i ^ mask) for i in range(PLANE)])]
    all_to_all x3, waiting for transfers between devices: 23.5 us -> 0.01 us  [columns_home(): lax.all_to_all(mine.reshape(PLANE, rows, -1), 'wide', 0, 1, tiled=False)]
    pallas_call x1, Pallas kernels: 34.5 us -> 21.1 us  [lru_backward(): pl.pallas_call(functools.partial(lru_backward_kernel, seqs), grid=(pl.cdi...]
    unnamed x197 -> x220, local copies, waits for them, and re-layouts: 41.2 us -> 28.1 us
    convert_element_type x16 -> x13, other arithmetic: 29.7 us -> 16.7 us  [the longest x4 4.16 us: scatter_start(): (two[:half].astype(f32) + via_one.astype(f32)).astype(bf16)]
    slice x1, local copies, waits for them, and re-layouts: 0.1 us -> 12.3 us  [on_device(): table[places[i]:places[i + 1]]]
    all_gather x2, waiting for transfers between devices: 9.46 us -> 19.2 us  [gather_spread(): lax.all_gather(part.reshape(-1, part.shape[-1]), spread, axis=0, tiled=True)]
  transfers between devices with their start and end apart: 59 -> 64, of which waited for: 24 -> 26; matrix products, arithmetic and copies ran while one was open for 28% -> 29% of each run, Pallas kernels for 20% -> 22%
where the time goes in v4:
time: 739 us; the launch traced here: 733 us
  Pallas kernels  222 us (30%)
  waiting for transfers between devices  176 us (24%)
  local copies, waits for them, and re-layouts  103 us (14%)
  other arithmetic  92.5 us (13%)
  starting transfers between devices  71 us (10%)
  matrix products  36.7 us (5%)
  between operations  16.7 us (2%)
  blocking collectives  15 us (2%)
    ppermute x32, waiting for transfers between devices, swap(): return lax.ppermute(values, 'wide', [(i, i ^ mask) for i in range(PLANE)])  139 us
    pallas_call x4, Pallas kernels, weight_grad(): pl.pallas_call(functools.partial(weight_grad_kernel, rows), grid_spec=plt...  60 us
    ppermute x32, starting transfers between devices, swap(): return lax.ppermute(values, 'wide', [(i, i ^ mask) for i in range(PLANE)])  35.7 us
    pallas_call x2, Pallas kernels, back_parts(): pl.pallas_call(functools.partial(back_kernel, len(grads)), grid=(groups,)...  35.4 us
    pallas_call x1, Pallas kernels, mlp_both(): pl.pallas_call(functools.partial(mlp_kernel, PLANE), grid=(steps,), out_s...  35 us
    unnamed x220, local copies, waits for them, and re-layouts  28.1 us
    pallas_call x4, Pallas kernels, add_pieces(): pl.pallas_call(add_pieces_kernel, grid=(groups, columns // block), out_sh...  25 us
    pallas_call x1, Pallas kernels, lru_backward(): pl.pallas_call(functools.partial(lru_backward_kernel, seqs), grid=(pl.cdi...  21.1 us
  transfers between devices with their start and end apart: 64, of which 26 were waited for; matrix products, arithmetic and copies ran while one was open for 29% of the time, Pallas kernels for 22%

profile of v4, /device:TPU:0, one launch (start us, length us, event | category | flops | bytes accessed | tf_op | source)
XLA Modules:
  0.0 733.1 jit_solution(15439181418796489366)
XLA Ops:
  9.9 15.0 %all_to_all.64 = bf16[4,64,1280]{2,1,0:T(8,128)(2,1)} all-to-all(bf16[4,64,1280]{2,1,0:T(8,128)(2,1)S(1)} %copy.110), channel_id=1, replica_groups=mesh['wide'=4,'rest'=2,'narrow'=4] {'wide'}, dimensions={0} | all-to-all | bytes 1310720 | tf_op jit(solution)/shard_map/all_to_all | solution.py:564
  28.1 4.9 all-to-all-start.1
  33.0 21.0 %collective-permute-done = bf16[320,2048]{1,0:T(8,128)(2,1)S(1)} collective-permute-done((bf16[320,2048]{1,0:T(8,128)(2,1)S(1)}, bf16[320,2048]{1,0:T(8,128)(2,1)S(1)}, u32[]{:S(2)}, u32[]{:S(2)}) %collective-permute-start) | collective-permute-done | bytes 1310752 | tf_op jit(solution)/shard_map/ppermute | solution.py:539
  56.2 2.3 pad_maximum_fusion.11
  68.2 5.1 all-to-all-start.2
  78.9 2.6 constant_dynamic-update-slice_fusion.1
  82.7 8.8 %all-gather.4.cloned.1.call-done = bf16[2048,1280]{1,0:T(8,128)(2,1)} async-done(((bf16[256,1280]{1,0:T(8,128)(2,1)}), bf16[2048,1280]{1,0:T(8,128)(2,1)}) %all-gather.4.cloned.1.call-update) | async-done | bytes 5242896 | tf_op jit(solution)/shard_map/all_gather | solution.py:567
  96.8 5.9 copy.113
  103.0 3.8 fusion
  106.8 3.9 fusion.2.left_ref
  110.8 4.3 fusion.26
  115.1 2.7 pad_slice_fusion.5
  117.8 7.9 %fusion.24.gate_ref = f32[1280,640]{1,0:T(8,128)} fusion(bf16[1280,2048]{1,0:T(8,128)(2,1)S(1)} %fusion.2.left_ref, bf16[2048,1280]{1,0:T(8,128)(2,1)} %bitcast.170), kind=kOutput, calls=%fused_computation.59 | convolution fusion | flops 3355443200 | bytes 11141120 | tf_op jit(solution)/shard_map/dot_general | solution.py:20
  125.9 12.3 %fusion.48 = (bf16[160,640]{1,0:T(8,128)(2,1)S(1)}, bf16[160,640]{1,0:T(8,128)(2,1)S(1)}) fusion(bf16[384,640]{1,0:T(8,128)(2,1)S(1)} %bitcast.181), kind=kLoop, calls=%fused_computation.165 | loop fusion | bytes 819200 | tf_op jit(solution)/shard_map/slice | solution.py:690
  143.6 3.6 convolution_add_fusion.3.rate_ref
  147.2 3.7 convolution_add_fusion.2.input_ref
  150.9 6.4 collective-permute-done.5
  160.9 3.6 all-to-all-start.3
  164.5 14.7 %lru_forward.1 = (f32[1280,640]{1,0:T(8,128)}, bf16[1280,640]{1,0:T(8,128)(2,1)S(1)}) custom-call(bf16[1280,640]{1,0:T(8,128)(2,1)S(1)} %fusion.12.conv_ref, f32[1280,640]{1,0:T(8,128)} %convolution_add_fusion.3.rate_ref, f32[1280,640]{1,0:T(8,128)} %convolution_add_fusion.2.input_ref, f32[1280,640]{1,0:T(8,128)} %fusion.24.gate_ref, ...), custom_call_target="tpu_custom_call" | custom-call | flops 16384000000 | bytes 16384000 | tf_op jit(solution)/shard_map/lru_forward/pallas_call | solution.py:198
  180.4 2.5 all-to-all-done.3
  184.1 7.5 %out_parts.2 = (bf16[160,2048]{1,0:T(8,128)(2,1)}, bf16[160,2048]{1,0:T(8,128)(2,1)}, bf16[320,2048]{1,0:T(8,128)(2,1)}, bf16[320,2048]{1,0:T(8,128)(2,1)}, bf16[320,2048]{1,0:T(8,128)(2,1)}) custom-call(bf16[1280,640]{1,0:T(8,128)(2,1)} %copy-done.5, bf16[8,272,2048]{2,1,0:T(8,128)(2,1)} %bitcast.152), custom_call_target="tpu_custom_call" | custom-call | flops 3355443200 | bytes 9502720 | tf_op jit(solution)/shard_map/out_parts/pallas_call | solution.py:408
  196.4 11.0 %collective-permute-done.10 = bf16[160,2048]{1,0:T(8,128)(2,1)S(1)} collective-permute-done((bf16[160,2048]{1,0:T(8,128)(2,1)}, bf16[160,2048]{1,0:T(8,128)(2,1)S(1)}, u32[]{:S(2)}, u32[]{:S(2)}) %collective-permute-start.10) | collective-permute-done | bytes 655392 | tf_op jit(solution)/shard_map/ppermute | solution.py:539
  209.5 3.8 collective-permute-start.9
  213.3 23.7 %collective-permute-done.11 = bf16[320,2048]{1,0:T(8,128)(2,1)} collective-permute-done((bf16[320,2048]{1,0:T(8,128)(2,1)S(1)}, bf16[320,2048]{1,0:T(8,128)(2,1)}, u32[]{:S(2)}, u32[]{:S(2)}) %collective-permute-start.11) | collective-permute-done | bytes 1310752 | tf_op jit(solution)/shard_map/ppermute | solution.py:539
  237.5 3.5 multiply_reduce_fusion.3
  246.6 24.0 %collective-permute-done.12.refs_2_ = bf16[320,2048]{1,0:T(8,128)(2,1)} collective-permute-done((bf16[320,2048]{1,0:T(8,128)(2,1)}, bf16[320,2048]{1,0:T(8,128)(2,1)}, u32[]{:S(2)}, u32[]{:S(2)}) %collective-permute-start.12) | collective-permute-done | bytes 1310752 | tf_op jit(solution)/shard_map/ppermute | solution.py:539
  279.3 8.5 %slice.237 = bf16[8,192,2048]{2,1,0:T(8,128)(2,1)} slice(bf16[8,272,2048]{2,1,0:T(8,128)(2,1)} %bitcast.153), slice={[0:8], [80:272], [0:2048]} | slice | bytes 12582912 | tf_op jit(solution)/shard_map/slice | solution.py:712
  287.8 10.4 %all-gather.8.cloned.1.call-done = bf16[2048,3072]{1,0:T(8,128)(2,1)} async-done(((bf16[256,3072]{1,0:T(8,128)(2,1)}), bf16[2048,3072]{1,0:T(8,128)(2,1)}) %all-gather.8.cloned.1.call-update) | async-done | bytes 12582928 | tf_op jit(solution)/shard_map/all_gather | solution.py:567
  298.2 35.0 %mlp_both.1 = (bf16[1280,1536]{1,0:T(8,128)(2,1)}, bf16[1280,1536]{1,0:T(8,128)(2,1)}, bf16[1280,1536]{1,0:T(8,128)(2,1)}, bf16[1280,2048]{1,0:T(8,128)(2,1)}) custom-call(bf16[160,2048]{1,0:T(8,128)(2,1)} %copy-done.98, bf16[160,2048]{1,0:T(8,128)(2,1)} %collective-permute-done.15.refs_1_, bf16[320,2048]{1,0:T(8,128)(2,1)} %collective-permute-done.12.refs_2_, ...), custom_call_target="tpu_custom_call" | custom-call | flops 24159191040 | bytes 34603008 | tf_op jit(solution)/shard_map/mlp_both/pallas_call | solution.py:282
  333.2 14.4 %weight_grad.4 = (bf16[4,1,192,2048]{3,2,1,0:T(8,128)(2,1)}, bf16[1,1,192,2048]{3,2,1,0:T(8,128)(2,1)}, bf16[1,1,192,2048]{3,2,1,0:T(8,128)(2,1)}, bf16[1,1,192,...) custom-call(s32[1]{0:T(128)} %bitcast.27.me_ref, bf16[1280,1536]{1,0:T(8,128)(2,1)} %get-tuple-element.180.left_ref.values_ref, ...), custom_call_target="tpu_custom_call" | custom-call | flops 8053063680 | bytes 15466496 | tf_op jit(solution)/shard_map/weight_grad/pallas_call | solution.py:461
  348.6 22.6 %back_parts.2 = (bf16[160,2048]{1,0:T(8,128)(2,1)}, bf16[160,2048]{1,0:T(8,128)(2,1)}, bf16[320,2048]{1,0:T(8,128)(2,1)}, bf16[320,2048]{1,0:T(8,128)(2,1)}, bf16[320,2048]{1,0:T(8,128)(2,1)}) custom-call(bf16[1280,1536]{1,0:T(8,128)(2,1)} %get-tuple-element.168.refs_0_, bf16[1280,1536]{1,0:T(8,128)(2,1)} %get-tuple-element.187.refs_1_, ...), custom_call_target="tpu_custom_call" | custom-call | flops 16106127360 | bytes 25690112 | tf_op jit(solution)/shard_map/back_parts/pallas_call | solution.py:380
  373.5 4.4 add_pieces.5
  383.4 15.2 %weight_grad.5 = (bf16[4,4,64,1536]{3,2,1,0:T(8,128)(2,1)}, bf16[1,4,64,1536]{3,2,1,0:T(8,128)(2,1)}, bf16[1,4,64,1536]{3,2,1,0:T(8,128)(2,1)}, bf16[1,4,64,1536]{3,2,1,0:T(8,128)(2,1)}, bf16[1,4,64,1536]{3,2,1,0:T(8,128)(2,1)}) custom-call(s32[1]{0:T(128)} %bitcast.27.me_ref, bf16[1280,2048]{1,0:T(8,128)(2,1)} %get-tuple-element.167.left_ref, ...), custom_call_target="tpu_custom_call" | custom-call | flops 8053063680 | bytes 19398656 | tf_op jit(solution)/shard_map/weight_grad/pallas_call | solution.py:461
  408.0 7.0 add_pieces.4
  415.0 16.4 %collective-permute-done.19 = bf16[320,2048]{1,0:T(8,128)(2,1)} collective-permute-done((bf16[320,2048]{1,0:T(8,128)(2,1)S(1)}, bf16[320,2048]{1,0:T(8,128)(2,1)}, u32[]{:S(2)}, u32[]{:S(2)}) %collective-permute-start.19) | collective-permute-done | bytes 1310752 | tf_op jit(solution)/shard_map/ppermute | solution.py:539
  433.5 3.9 convert_add_fusion.3
  437.6 2.7 multiply_reduce_fusion.1
  443.3 15.8 %weight_grad.6 = (bf16[4,4,64,1536]{3,2,1,0:T(8,128)(2,1)}, bf16[1,4,64,1536]{3,2,1,0:T(8,128)(2,1)}, bf16[1,4,64,1536]{3,2,1,0:T(8,128)(2,1)}, bf16[1,4,64,1536]{3,2,1,0:T(8,128)(2,1)}, bf16[1,4,64,1536]{3,2,1,0:T(8,128)(2,1)}) custom-call(s32[1]{0:T(128)} %bitcast.27.me_ref, bf16[1280,2048]{1,0:T(8,128)(2,1)} %get-tuple-element.167.left_ref, ...), custom_call_target="tpu_custom_call" | custom-call | flops 8053063680 | bytes 19398656 | tf_op jit(solution)/shard_map/weight_grad/pallas_call | solution.py:461
  459.7 11.8 %collective-permute-done.28.refs_2_ = bf16[320,2048]{1,0:T(8,128)(2,1)S(1)} collective-permute-done((bf16[320,2048]{1,0:T(8,128)(2,1)S(1)}, bf16[320,2048]{1,0:T(8,128)(2,1)S(1)}, u32[]{:S(2)}, u32[]{:S(2)}) %collective-permute-start.28) | collective-permute-done | bytes 1310752 | tf_op jit(solution)/shard_map/ppermute | solution.py:539
  476.8 6.9 add_pieces.6
  483.7 12.4 %out_parts.3 = (bf16[160,2048]{1,0:T(8,128)(2,1)}, bf16[160,2048]{1,0:T(8,128)(2,1)}, bf16[320,2048]{1,0:T(8,128)(2,1)}, bf16[320,2048]{1,0:T(8,128)(2,1)}, bf16[320,2048]{1,0:T(8,128)(2,1)}) custom-call(bf16[1280,1536]{1,0:T(8,128)(2,1)} %get-tuple-element.180.left_ref.values_ref, bf16[1,1536,2048]{2,1,0:T(8,128)(2,1)} %bitcast.164), custom_call_target="tpu_custom_call" | custom-call | flops 8053063680 | bytes 15466496 | tf_op jit(solution)/shard_map/out_parts/pallas_call | solution.py:408
  496.1 2.8 reduce-scatter.8.cloned.1.call-done
  505.3 10.8 %mixed_grad.1 = (f32[1280,640]{1,0:T(8,128)}, bf16[1280,2048]{1,0:T(8,128)(2,1)}) custom-call(bf16[160,2048]{1,0:T(8,128)(2,1)} %copy-done.57, bf16[160,2048]{1,0:T(8,128)(2,1)} %collective-permute-done.31.refs_1_, bf16[320,2048]{1,0:T(8,128)(2,1)} %copy-done.30, bf16[320,2048]{1,0:T(8,128)(2,1)} %copy-done.31, bf16[320,2048]{1,0:T(8,128)(2,1)} %copy-done.28, ...), custom_call_target="tpu_custom_call" | custom-call | flops 3355443200 | bytes 16384000 | tf_op jit(solution)/shard_map/mixed_grad/pallas_call | solution.py:322
  524.6 21.1 %lru_backward.1 = (f32[1280,640]{1,0:T(8,128)}, bf16[1280,640]{1,0:T(8,128)(2,1)S(1)}, bf16[1280,640]{1,0:T(8,128)(2,1)S(1)}, bf16[1280,640]{1,0:T(8,128)(2,1)S(1)}, f32[24,640]{1,0:T(8,128)S(1)}) custom-call(bf16[1280,640]{1,0:T(8,128)(2,1)} %copy-done, f32[1280,640]{1,0:T(8,128)} %convolution_add_fusion.3.rate_ref, ...), custom_call_target="tpu_custom_call" | custom-call | flops 16384000000 | bytes 16384000 | tf_op jit(solution)/shard_map/lru_backward/pallas_call | solution.py:217
  545.8 5.0 convolution_add_fusion.1
  552.7 4.0 pad_slice_fusion.2
  558.7 4.2 all-to-all-start.4
  563.0 6.7 fusion.47
  573.6 3.9 add_add_fusion
  577.5 14.7 %weight_grad.7 = (bf16[4,4,64,1280]{3,2,1,0:T(8,128)(2,1)}, bf16[1,4,64,1280]{3,2,1,0:T(8,128)(2,1)}, bf16[1,4,64,1280]{3,2,1,0:T(8,128)(2,1)}, bf16[1,4,64,1280]{3,2,1,0:T(8,128)(2,1)}, bf16[1,4,64,1280]{3,2,1,0:T(8,128)(2,1)}) custom-call(s32[1]{0:T(128)} %bitcast.27.me_ref, bf16[1280,2048]{1,0:T(8,128)(2,1)} %copy-done.29, ...), custom_call_target="tpu_custom_call" | custom-call | flops 6710886400 | bytes 17039360 | tf_op jit(solution)/shard_map/weight_grad/pallas_call | solution.py:461
  597.4 6.7 add_pieces.7
  604.2 12.8 %back_parts.3 = (bf16[160,2048]{1,0:T(8,128)(2,1)}, bf16[160,2048]{1,0:T(8,128)(2,1)}, bf16[320,2048]{1,0:T(8,128)(2,1)}, bf16[320,2048]{1,0:T(8,128)(2,1)}, bf16[320,2048]{1,0:T(8,128)(2,1)}) custom-call(bf16[1280,640]{1,0:T(8,128)(2,1)} %copy-done.2, bf16[1280,640]{1,0:T(8,128)(2,1)} %copy-done.19, bf16[8,4,64,1280]{3,2,1,0:T(8,128)(2,1)} %bitcast.169), custom_call_target="tpu_custom_call" | custom-call | flops 6710886400 | bytes 13762560 | tf_op jit(solution)/shard_map/back_parts/pallas_call | solution.py:380
  623.4 7.6 %convolution_convert_fusion = bf16[640,2048]{1,0:T(8,128)(2,1)} fusion(bf16[1280,640]{1,0:T(8,128)(2,1)S(1)} %copy-done.6, bf16[1280,2048]{1,0:T(8,128)(2,1)} %get-tuple-element.235), kind=kOutput, calls=%fused_computation.45 | convolution fusion | flops 3356753920 | bytes 9502720 | tf_op jit(solution)/shard_map/dot_general | solution.py:28
  645.4 7.3 convert_multiply_fusion.2
  652.7 4.2 all-to-all-start.7
  657.2 3.1 fusion.15
  660.3 14.0 %collective-permute-done.47 = bf16[320,2048]{1,0:T(8,128)(2,1)} collective-permute-done((bf16[320,2048]{1,0:T(8,128)(2,1)}, bf16[320,2048]{1,0:T(8,128)(2,1)}, u32[]{:S(2)}, u32[]{:S(2)}) %collective-permute-start.47) | collective-permute-done | bytes 1310752 | tf_op jit(solution)/shard_map/ppermute | solution.py:539
  674.3 3.0 collective-permute-done.45
  677.3 7.3 %fusion.23 = (f32[2048]{0:T(1024)S(1)}, f32[2048]{0:T(1024)S(1)}, f32[2048]{0:T(1024)S(1)}, f32[320,2048]{1,0:T(8,128)}) fusion(f32[1280,2048]{1,0:T(8,128)} %convert_multiply_fusion.2, bf16[320,2048]{1,0:T(8,128)(2,1)S(1)} %copy-done.24, bf16[320,2048]{1,0:T(8,128)(2,1)S(1)} %copy-done.38, bf16[320,2048]{1,0:T(8,128)(2,1)S(1)} %copy-done.27, ...), kind=kLoop, calls=%fused_computation.58 | loop fusion | flops 8513536 | bytes 17063936 | tf_op jit(solution)/shard_map/reduce_sum | solution.py:773
  693.7 3.8 all-to-all-start.5
  697.5 2.9 fusion.18
  700.5 5.3 fusion.21
  706.5 5.4 all-to-all-start.6
  713.8 5.4 all-to-all-done.6
  (444 shorter events, 158.6 us)
Async XLA Ops:
  7.2 84.4 %all-gather.4.cloned.1.call-start = ((), (), s32[]{:S(2)}) async-start(), calls=%async_computation.13 | async-start | bytes 5898240 | tf_op jit(solution)/shard_map/all_gather | solution.py:567
  24.9 29.0 %collective-permute-start = (bf16[320,2048]{1,0:T(8,128)(2,1)S(1)}, bf16[320,2048]{1,0:T(8,128)(2,1)S(1)}, u32[]{:S(2)}, u32[]{:S(2)}) collective-permute-start(bf16[320,2048]{1,0:T(8,128)(2,1)S(1)} %copy-done.13), channel_id=1, source_target_pairs={{0,8},{8,0},{16,24},{24,16},{1,9},{9,1},{17,25},{25,17},{2,10},{10... | collective-permute-start | bytes 3932168 | tf_op jit(solution)/shard_map/ppermute | solution.py:539
  25.9 32.6 %collective-permute-start.2 = (bf16[320,2048]{1,0:T(8,128)(2,1)S(1)}, bf16[320,2048]{1,0:T(8,128)(2,1)}, u32[]{:S(2)}, u32[]{:S(2)}) collective-permute-start(bf16[320,2048]{1,0:T(8,128)(2,1)S(1)} %copy-done.13), channel_id=1, source_target_pairs={{0,16},{8,24},{16,0},{24,8},{1,17},{9,25},{17,1},{25,9},{2,18},{10... | collective-permute-start | bytes 3932168 | tf_op jit(solution)/shard_map/ppermute | solution.py:539
  28.1 39.5 %all-to-all-start.1 = ((bf16[8,80,384]{2,1,0:T(8,128)(2,1)}), bf16[8,80,384]{2,1,0:T(8,128)(2,1)S(1)}, u32[]{:S(2)}, u32[]{:S(2)}) async-start(bf16[8,80,384]{2,1,0:T(8,128)(2,1)} %broadcast_in_dim.61), calls=%async_computation.1 | async-start | bytes 983040 | tf_op jit(solution)/shard_map/all_to_all | solution.py:605
  54.9 18.8 %collective-permute-start.1 = (bf16[160,2048]{1,0:T(8,128)(2,1)}, bf16[160,2048]{1,0:T(8,128)(2,1)}, u32[]{:S(2)}, u32[]{:S(2)}) collective-permute-start(bf16[160,2048]{1,0:T(8,128)(2,1)} %slice.276), channel_id=1, source_target_pairs={{0,16},{8,24},{16,0},{24,8},{1,17},{9,25},{17,1},{25,9},{2,18},{10... | collective-permute-start | bytes 1966088 | tf_op jit(solution)/shard_map/ppermute | solution.py:539
  60.5 15.3 %collective-permute-start.3 = (bf16[160,2048]{1,0:T(8,128)(2,1)}, bf16[160,2048]{1,0:T(8,128)(2,1)}, u32[]{:S(2)}, u32[]{:S(2)}) collective-permute-start(bf16[160,2048]{1,0:T(8,128)(2,1)} %slice.277), channel_id=1, source_target_pairs={{0,8},{8,0},{16,24},{24,16},{1,9},{9,1},{17,25},{25,17},{2,10},{10... | collective-permute-start | bytes 1966088 | tf_op jit(solution)/shard_map/ppermute | solution.py:539
  68.2 14.6 %all-to-all-start.2 = ((bf16[32,2,64]{2,1,0:T(2,128)(2,1)}), bf16[32,2,64]{2,1,0:T(2,128)(2,1)S(1)}, u32[]{:S(2)}, u32[]{:S(2)}) async-start(bf16[32,2,64]{2,1,0:T(2,128)(2,1)} %broadcast_in_dim.62), calls=%async_computation.2 | async-start | bytes 32768 | tf_op jit(solution)/shard_map/all_to_all | solution.py:605
  73.3 109.6 %all-gather.6.cloned.1.call-start = ((), (), s32[]{:S(2)}) async-start(), calls=%async_computation.14 | async-start | bytes 10027008 | tf_op jit(solution)/shard_map/all_gather | solution.py:674
  93.6 45.7 %collective-permute-start.4 = (bf16[320,2048]{1,0:T(8,128)(2,1)}, bf16[320,2048]{1,0:T(8,128)(2,1)}, u32[]{:S(2)}, u32[]{:S(2)}) collective-permute-start(bf16[320,2048]{1,0:T(8,128)(2,1)} %multiply_convert_fusion.2), channel_id=1, source_target_pairs={{0,8},{8,0},{16,24},{24,16},{1,9},{9,1},{17,25},{25,17},{2,10},{10... | collective-permute-start | bytes 3932168 | tf_op jit(solution)/shard_map/ppermute | solution.py:539
  95.1 46.5 %collective-permute-start.6 = (bf16[320,2048]{1,0:T(8,128)(2,1)}, bf16[320,2048]{1,0:T(8,128)(2,1)}, u32[]{:S(2)}, u32[]{:S(2)}) collective-permute-start(bf16[320,2048]{1,0:T(8,128)(2,1)} %multiply_convert_fusion.2), channel_id=1, source_target_pairs={{0,16},{8,24},{16,0},{24,8},{1,17},{9,25},{17,1},{25,9},{2,18},{10... | collective-permute-start | bytes 3932168 | tf_op jit(solution)/shard_map/ppermute | solution.py:539
  141.0 16.3 %collective-permute-start.5 = (bf16[160,2048]{1,0:T(8,128)(2,1)S(1)}, bf16[160,2048]{1,0:T(8,128)(2,1)}, u32[]{:S(2)}, u32[]{:S(2)}) collective-permute-start(bf16[160,2048]{1,0:T(8,128)(2,1)S(1)} %slice.292), channel_id=1, source_target_pairs={{0,16},{8,24},{16,0},{24,8},{1,17},{9,25},{17,1},{25,9},{2,18},{10... | collective-permute-start | bytes 1966088 | tf_op jit(solution)/shard_map/ppermute | solution.py:539
  142.8 16.5 %collective-permute-start.7 = (bf16[160,2048]{1,0:T(8,128)(2,1)S(1)}, bf16[160,2048]{1,0:T(8,128)(2,1)}, u32[]{:S(2)}, u32[]{:S(2)}) collective-permute-start(bf16[160,2048]{1,0:T(8,128)(2,1)S(1)} %slice.293), channel_id=1, source_target_pairs={{0,8},{8,0},{16,24},{24,16},{1,9},{9,1},{17,25},{25,17},{2,10},{10... | collective-permute-start | bytes 1966088 | tf_op jit(solution)/shard_map/ppermute | solution.py:539
  160.9 22.0 %all-to-all-start.3 = ((bf16[4,64,3072]{2,1,0:T(8,128)(2,1)}), bf16[4,64,3072]{2,1,0:T(8,128)(2,1)S(1)}, u32[]{:S(2)}, u32[]{:S(2)}) async-start(bf16[4,64,3072]{2,1,0:T(8,128)(2,1)} %copy.114), calls=%async_computation.3 | async-start | bytes 3145728 | tf_op jit(solution)/shard_map/all_to_all | solution.py:564
  164.5 133.7 %all-gather.8.cloned.1.call-start = ((), (), s32[]{:S(2)}) async-start(), calls=%async_computation.15 | async-start | bytes 14155776 | tf_op jit(solution)/shard_map/all_gather | solution.py:567
  184.1 253.4 %reduce-scatter.6.cloned.1.call-start = ((), (), s32[]{:S(2)}) async-start(), calls=%async_computation.16 | async-start | bytes 3932160 | tf_op jit(solution)/shard_map/reduce_scatter | solution.py:590
  191.6 15.8 %collective-permute-start.10 = (bf16[160,2048]{1,0:T(8,128)(2,1)}, bf16[160,2048]{1,0:T(8,128)(2,1)S(1)}, u32[]{:S(2)}, u32[]{:S(2)}) collective-permute-start(bf16[160,2048]{1,0:T(8,128)(2,1)} %get-tuple-element.149), channel_id=1, source_target_pairs={{0,8},{8,0},{16,24},{24,16},{1,9},{9,1},{17,25},{25,17},{2,10},{10... | collective-permute-start | bytes 1966088 | tf_op jit(solution)/shard_map/ppermute | solution.py:539
  194.2 15.0 %collective-permute-start.8 = (bf16[160,2048]{1,0:T(8,128)(2,1)}, bf16[160,2048]{1,0:T(8,128)(2,1)S(1)}, u32[]{:S(2)}, u32[]{:S(2)}) collective-permute-start(bf16[160,2048]{1,0:T(8,128)(2,1)} %get-tuple-element.147), channel_id=1, source_target_pairs={{0,16},{8,24},{16,0},{24,8},{1,17},{9,25},{17,1},{25,9},{2,18},{10... | collective-permute-start | bytes 1966088 | tf_op jit(solution)/shard_map/ppermute | solution.py:539
  207.7 29.3 %collective-permute-start.11 = (bf16[320,2048]{1,0:T(8,128)(2,1)S(1)}, bf16[320,2048]{1,0:T(8,128)(2,1)}, u32[]{:S(2)}, u32[]{:S(2)}) collective-permute-start(bf16[320,2048]{1,0:T(8,128)(2,1)S(1)} %pad_maximum_fusion.4), channel_id=1, source_target_pairs={{0,16},{8,24},{16,0},{24,8},{1,17},{9,25},{17,1},{25,9},{2,18},{10... | collective-permute-start | bytes 3932168 | tf_op jit(solution)/shard_map/ppermute | solution.py:539
  209.5 28.0 %collective-permute-start.9 = (bf16[320,2048]{1,0:T(8,128)(2,1)S(1)}, bf16[320,2048]{1,0:T(8,128)(2,1)}, u32[]{:S(2)}, u32[]{:S(2)}) collective-permute-start(bf16[320,2048]{1,0:T(8,128)(2,1)S(1)} %pad_maximum_fusion.3), channel_id=1, source_target_pairs={{0,8},{8,0},{16,24},{24,16},{1,9},{9,1},{17,25},{25,17},{2,10},{10... | collective-permute-start | bytes 3932168 | tf_op jit(solution)/shard_map/ppermute | solution.py:539
  242.6 28.0 %collective-permute-start.12 = (bf16[320,2048]{1,0:T(8,128)(2,1)}, bf16[320,2048]{1,0:T(8,128)(2,1)}, u32[]{:S(2)}, u32[]{:S(2)}) collective-permute-start(bf16[320,2048]{1,0:T(8,128)(2,1)} %multiply_convert_fusion.1.refs_4_), channel_id=1, source_target_pairs={{0,8},{8,0},{16,24},{24,16},{1,9},{9,1},{17,25},{25,17},{2,10},{10... | collective-permute-start | bytes 3932168 | tf_op jit(solution)/shard_map/ppermute | solution.py:539
  244.3 29.1 %collective-permute-start.14 = (bf16[320,2048]{1,0:T(8,128)(2,1)}, bf16[320,2048]{1,0:T(8,128)(2,1)}, u32[]{:S(2)}, u32[]{:S(2)}) collective-permute-start(bf16[320,2048]{1,0:T(8,128)(2,1)} %multiply_convert_fusion.1.refs_4_), channel_id=1, source_target_pairs={{0,16},{8,24},{16,0},{24,8},{1,17},{9,25},{17,1},{25,9},{2,18},{10... | collective-permute-start | bytes 3932168 | tf_op jit(solution)/shard_map/ppermute | solution.py:539
  271.7 16.1 %collective-permute-start.13 = (bf16[160,2048]{1,0:T(8,128)(2,1)S(1)}, bf16[160,2048]{1,0:T(8,128)(2,1)S(1)}, u32[]{:S(2)}, u32[]{:S(2)}) collective-permute-start(bf16[160,2048]{1,0:T(8,128)(2,1)S(1)} %slice.295), channel_id=1, source_target_pairs={{0,16},{8,24},{16,0},{24,8},{1,17},{9,25},{17,1},{25,9},{2,18},{10... | collective-permute-start | bytes 1966088 | tf_op jit(solution)/shard_map/ppermute | solution.py:539
  274.6 13.2 %collective-permute-start.15 = (bf16[160,2048]{1,0:T(8,128)(2,1)S(1)}, bf16[160,2048]{1,0:T(8,128)(2,1)}, u32[]{:S(2)}, u32[]{:S(2)}) collective-permute-start(bf16[160,2048]{1,0:T(8,128)(2,1)S(1)} %slice.296), channel_id=1, source_target_pairs={{0,8},{8,0},{16,24},{24,16},{1,9},{9,1},{17,25},{25,17},{2,10},{10... | collective-permute-start | bytes 1966088 | tf_op jit(solution)/shard_map/ppermute | solution.py:539
  347.5 23.6 %collective-permute-start.24 = (bf16[1,1,192,2048]{3,2,1,0:T(8,128)(2,1)}, bf16[1,1,192,2048]{3,2,1,0:T(8,128)(2,1)S(1)}, u32[]{:S(2)}, u32[]{:S(2)}) collective-permute-start(bf16[1,1,192,2048]{3,2,1,0:T(8,128)(2,1)} %get-tuple-element.175), channel_id=1, source_target_pairs={{0,4},{4,0},{1,5},{5,1},{2,6},{6,2},{3,7},{7,3},{8,12},{12,8},{9,1... | collective-permute-start | bytes 2359304 | tf_op jit(solution)/shard_map/ppermute | solution.py:577
  347.8 23.4 %collective-permute-start.25 = (bf16[1,1,192,2048]{3,2,1,0:T(8,128)(2,1)}, bf16[1,1,192,2048]{3,2,1,0:T(8,128)(2,1)S(1)}, u32[]{:S(2)}, u32[]{:S(2)}) collective-permute-start(bf16[1,1,192,2048]{3,2,1,0:T(8,128)(2,1)} %get-tuple-element.176), channel_id=1, source_target_pairs={{0,4},{4,0},{1,5},{5,1},{2,6},{6,2},{3,7},{7,3},{8,12},{12,8},{9,1... | collective-permute-start | bytes 2359304 | tf_op jit(solution)/shard_map/ppermute | solution.py:577
  348.1 23.1 %collective-permute-start.26 = (bf16[1,1,192,2048]{3,2,1,0:T(8,128)(2,1)}, bf16[1,1,192,2048]{3,2,1,0:T(8,128)(2,1)S(1)}, u32[]{:S(2)}, u32[]{:S(2)}) collective-permute-start(bf16[1,1,192,2048]{3,2,1,0:T(8,128)(2,1)} %get-tuple-element.177), channel_id=1, source_target_pairs={{0,4},{4,0},{1,5},{5,1},{2,6},{6,2},{3,7},{7,3},{8,12},{12,8},{9,1... | collective-permute-start | bytes 2359304 | tf_op jit(solution)/shard_map/ppermute | solution.py:577
  348.3 22.9 %collective-permute-start.27 = (bf16[1,1,192,2048]{3,2,1,0:T(8,128)(2,1)}, bf16[1,1,192,2048]{3,2,1,0:T(8,128)(2,1)S(1)}, u32[]{:S(2)}, u32[]{:S(2)}) collective-permute-start(bf16[1,1,192,2048]{3,2,1,0:T(8,128)(2,1)} %get-tuple-element.178), channel_id=1, source_target_pairs={{0,4},{4,0},{1,5},{5,1},{2,6},{6,2},{3,7},{7,3},{8,12},{12,8},{9,1... | collective-permute-start | bytes 2359304 | tf_op jit(solution)/shard_map/ppermute | solution.py:577
  377.9 121.1 %reduce-scatter.8.cloned.1.call-start = ((), (), s32[]{:S(2)}) async-start(), calls=%async_computation.17 | async-start | bytes 3932160 | tf_op jit(solution)/shard_map/reduce_scatter | solution.py:590
  377.9 20.7 %collective-permute-start.18 = (bf16[160,2048]{1,0:T(8,128)(2,1)}, bf16[160,2048]{1,0:T(8,128)(2,1)}, u32[]{:S(2)}, u32[]{:S(2)}) collective-permute-start(bf16[160,2048]{1,0:T(8,128)(2,1)} %get-tuple-element.166), channel_id=1, source_target_pairs={{0,8},{8,0},{16,24},{24,16},{1,9},{9,1},{17,25},{25,17},{2,10},{10... | collective-permute-start | bytes 1966088 | tf_op jit(solution)/shard_map/ppermute | solution.py:539
  380.6 20.4 %collective-permute-start.16 = (bf16[160,2048]{1,0:T(8,128)(2,1)}, bf16[160,2048]{1,0:T(8,128)(2,1)}, u32[]{:S(2)}, u32[]{:S(2)}) collective-permute-start(bf16[160,2048]{1,0:T(8,128)(2,1)} %get-tuple-element.164), channel_id=1, source_target_pairs={{0,16},{8,24},{16,0},{24,8},{1,17},{9,25},{17,1},{25,9},{2,18},{10... | collective-permute-start | bytes 1966088 | tf_op jit(solution)/shard_map/ppermute | solution.py:539
  398.6 5.3 collective-permute-start.20
  400.2 31.2 %collective-permute-start.19 = (bf16[320,2048]{1,0:T(8,128)(2,1)S(1)}, bf16[320,2048]{1,0:T(8,128)(2,1)}, u32[]{:S(2)}, u32[]{:S(2)}) collective-permute-start(bf16[320,2048]{1,0:T(8,128)(2,1)S(1)} %pad_maximum_fusion.6), channel_id=1, source_target_pairs={{0,16},{8,24},{16,0},{24,8},{1,17},{9,25},{17,1},{25,9},{2,18},{10... | collective-permute-start | bytes 3932168 | tf_op jit(solution)/shard_map/ppermute | solution.py:539
  402.4 31.2 %collective-permute-start.17 = (bf16[320,2048]{1,0:T(8,128)(2,1)S(1)}, bf16[320,2048]{1,0:T(8,128)(2,1)}, u32[]{:S(2)}, u32[]{:S(2)}) collective-permute-start(bf16[320,2048]{1,0:T(8,128)(2,1)S(1)} %pad_maximum_fusion.5), channel_id=1, source_target_pairs={{0,8},{8,0},{16,24},{24,16},{1,9},{9,1},{17,25},{25,17},{2,10},{10... | collective-permute-start | bytes 3932168 | tf_op jit(solution)/shard_map/ppermute | solution.py:539
  403.3 2.4 collective-permute-start.21
  403.4 3.5 collective-permute-start.22
  403.9 4.1 collective-permute-start.23
  437.5 157.1 %reduce-scatter.10.cloned.1.call-start = ((), (), s32[]{:S(2)}) async-start(), calls=%async_computation.18 | async-start | bytes 3932160 | tf_op jit(solution)/shard_map/reduce_scatter | solution.py:590
  441.2 30.2 %collective-permute-start.28 = (bf16[320,2048]{1,0:T(8,128)(2,1)S(1)}, bf16[320,2048]{1,0:T(8,128)(2,1)S(1)}, u32[]{:S(2)}, u32[]{:S(2)}) collective-permute-start(bf16[320,2048]{1,0:T(8,128)(2,1)S(1)} %fusion.46.refs_4_), channel_id=1, source_target_pairs={{0,8},{8,0},{16,24},{24,16},{1,9},{9,1},{17,25},{25,17},{2,10},{10... | collective-permute-start | bytes 3932168 | tf_op jit(solution)/shard_map/ppermute | solution.py:539
  442.0 30.4 %collective-permute-start.30 = (bf16[320,2048]{1,0:T(8,128)(2,1)S(1)}, bf16[320,2048]{1,0:T(8,128)(2,1)S(1)}, u32[]{:S(2)}, u32[]{:S(2)}) collective-permute-start(bf16[320,2048]{1,0:T(8,128)(2,1)S(1)} %fusion.46.refs_4_), channel_id=1, source_target_pairs={{0,16},{8,24},{16,0},{24,8},{1,17},{9,25},{17,1},{25,9},{2,18},{10... | collective-permute-start | bytes 3932168 | tf_op jit(solution)/shard_map/ppermute | solution.py:539
  459.0 14.4 %collective-permute-start.32 = (bf16[1,4,64,1536]{3,2,1,0:T(8,128)(2,1)}, bf16[1,4,64,1536]{3,2,1,0:T(8,128)(2,1)S(1)}, u32[]{:S(2)}, u32[]{:S(2)}) collective-permute-start(bf16[1,4,64,1536]{3,2,1,0:T(8,128)(2,1)} %get-tuple-element.190), channel_id=1, source_target_pairs={{0,4},{4,0},{1,5},{5,1},{2,6},{6,2},{3,7},{7,3},{8,12},{12,8},{9,1... | collective-permute-start | bytes 2359304 | tf_op jit(solution)/shard_map/ppermute | solution.py:577
  459.1 15.7 %collective-permute-start.33 = (bf16[1,4,64,1536]{3,2,1,0:T(8,128)(2,1)}, bf16[1,4,64,1536]{3,2,1,0:T(8,128)(2,1)S(1)}, u32[]{:S(2)}, u32[]{:S(2)}) collective-permute-start(bf16[1,4,64,1536]{3,2,1,0:T(8,128)(2,1)} %get-tuple-element.191), channel_id=1, source_target_pairs={{0,4},{4,0},{1,5},{5,1},{2,6},{6,2},{3,7},{7,3},{8,12},{12,8},{9,1... | collective-permute-start | bytes 2359304 | tf_op jit(solution)/shard_map/ppermute | solution.py:577
  459.6 15.2 %collective-permute-start.34 = (bf16[1,4,64,1536]{3,2,1,0:T(8,128)(2,1)}, bf16[1,4,64,1536]{3,2,1,0:T(8,128)(2,1)S(1)}, u32[]{:S(2)}, u32[]{:S(2)}) collective-permute-start(bf16[1,4,64,1536]{3,2,1,0:T(8,128)(2,1)} %get-tuple-element.192), channel_id=1, source_target_pairs={{0,4},{4,0},{1,5},{5,1},{2,6},{6,2},{3,7},{7,3},{8,12},{12,8},{9,1... | collective-permute-start | bytes 2359304 | tf_op jit(solution)/shard_map/ppermute | solution.py:577
  471.5 3.3 collective-permute-start.35
  472.4 23.7 %collective-permute-start.29 = (bf16[160,2048]{1,0:T(8,128)(2,1)}, bf16[160,2048]{1,0:T(8,128)(2,1)S(1)}, u32[]{:S(2)}, u32[]{:S(2)}) collective-permute-start(bf16[160,2048]{1,0:T(8,128)(2,1)} %slice.297), channel_id=1, source_target_pairs={{0,16},{8,24},{16,0},{24,8},{1,17},{9,25},{17,1},{25,9},{2,18},{10... | collective-permute-start | bytes 1966088 | tf_op jit(solution)/shard_map/ppermute | solution.py:539
  473.4 22.7 %collective-permute-start.31 = (bf16[160,2048]{1,0:T(8,128)(2,1)S(1)}, bf16[160,2048]{1,0:T(8,128)(2,1)}, u32[]{:S(2)}, u32[]{:S(2)}) collective-permute-start(bf16[160,2048]{1,0:T(8,128)(2,1)S(1)} %slice.298), channel_id=1, source_target_pairs={{0,8},{8,0},{16,24},{24,16},{1,9},{9,1},{17,25},{25,17},{2,10},{10... | collective-permute-start | bytes 1966088 | tf_op jit(solution)/shard_map/ppermute | solution.py:539
  499.0 17.1 %collective-permute-start.36 = (bf16[160,2048]{1,0:T(8,128)(2,1)}, bf16[160,2048]{1,0:T(8,128)(2,1)}, u32[]{:S(2)}, u32[]{:S(2)}) collective-permute-start(bf16[160,2048]{1,0:T(8,128)(2,1)} %get-tuple-element.201), channel_id=1, source_target_pairs={{0,16},{8,24},{16,0},{24,8},{1,17},{9,25},{17,1},{25,9},{2,18},{10... | collective-permute-start | bytes 1966088 | tf_op jit(solution)/shard_map/ppermute | solution.py:539
  503.7 16.4 %collective-permute-start.37 = (bf16[160,2048]{1,0:T(8,128)(2,1)}, bf16[160,2048]{1,0:T(8,128)(2,1)}, u32[]{:S(2)}, u32[]{:S(2)}) collective-permute-start(bf16[160,2048]{1,0:T(8,128)(2,1)} %get-tuple-element.203), channel_id=1, source_target_pairs={{0,8},{8,0},{16,24},{24,16},{1,9},{9,1},{17,25},{25,17},{2,10},{10... | collective-permute-start | bytes 1966088 | tf_op jit(solution)/shard_map/ppermute | solution.py:539
  522.6 49.6 %collective-permute-start.39 = (bf16[320,2048]{1,0:T(8,128)(2,1)}, bf16[320,2048]{1,0:T(8,128)(2,1)}, u32[]{:S(2)}, u32[]{:S(2)}) collective-permute-start(bf16[320,2048]{1,0:T(8,128)(2,1)} %pad_maximum_fusion.8), channel_id=1, source_target_pairs={{0,16},{8,24},{16,0},{24,8},{1,17},{9,25},{17,1},{25,9},{2,18},{10... | collective-permute-start | bytes 3932168 | tf_op jit(solution)/shard_map/ppermute | solution.py:539
  523.1 49.1 %collective-permute-start.38 = (bf16[320,2048]{1,0:T(8,128)(2,1)}, bf16[320,2048]{1,0:T(8,128)(2,1)}, u32[]{:S(2)}, u32[]{:S(2)}) collective-permute-start(bf16[320,2048]{1,0:T(8,128)(2,1)} %pad_maximum_fusion.7), channel_id=1, source_target_pairs={{0,8},{8,0},{16,24},{24,16},{1,9},{9,1},{17,25},{25,17},{2,10},{10... | collective-permute-start | bytes 3932168 | tf_op jit(solution)/shard_map/ppermute | solution.py:539
  558.7 18.9 %all-to-all-start.4 = ((bf16[4,64,1,1536]{3,1,2,0:T(8,128)(2,1)}), bf16[4,64,1,1536]{3,1,2,0:T(8,128)(2,1)}, u32[]{:S(2)}, u32[]{:S(2)}) async-start(bf16[4,64,1,1536]{3,1,2,0:T(8,128)(2,1)} %bitcast.190), calls=%async_computation.6 | async-start | bytes 1572864 | tf_op jit(solution)/shard_map/all_to_all | solution.py:593
  562.9 121.7 %reduce-scatter.12.cloned.1.call-start = ((), (), s32[]{:S(2)}) async-start(), calls=%async_computation.19 | async-start | bytes 3276800 | tf_op jit(solution)/shard_map/reduce_scatter | solution.py:590
  592.2 2.4 collective-permute-start.40
  592.2 4.2 collective-permute-start.41
  592.7 3.8 collective-permute-start.42
  592.8 4.7 collective-permute-start.43
  617.0 22.2 %collective-permute-start.46 = (bf16[160,2048]{1,0:T(8,128)(2,1)}, bf16[160,2048]{1,0:T(8,128)(2,1)}, u32[]{:S(2)}, u32[]{:S(2)}) collective-permute-start(bf16[160,2048]{1,0:T(8,128)(2,1)} %get-tuple-element.229), channel_id=1, source_target_pairs={{0,8},{8,0},{16,24},{24,16},{1,9},{9,1},{17,25},{25,17},{2,10},{10... | collective-permute-start | bytes 1966088 | tf_op jit(solution)/shard_map/ppermute | solution.py:539
  618.9 23.8 %collective-permute-start.44 = (bf16[160,2048]{1,0:T(8,128)(2,1)}, bf16[160,2048]{1,0:T(8,128)(2,1)}, u32[]{:S(2)}, u32[]{:S(2)}) collective-permute-start(bf16[160,2048]{1,0:T(8,128)(2,1)} %get-tuple-element.227), channel_id=1, source_target_pairs={{0,16},{8,24},{16,0},{24,8},{1,17},{9,25},{17,1},{25,9},{2,18},{10... | collective-permute-start | bytes 1966088 | tf_op jit(solution)/shard_map/ppermute | solution.py:539
  639.2 18.0 %collective-permute-start.48 = (bf16[4,80,2432]{2,1,0:T(8,128)(2,1)}, bf16[4,80,2432]{2,1,0:T(8,128)(2,1)}, u32[]{:S(2)}, u32[]{:S(2)}) collective-permute-start(bf16[4,80,2432]{2,1,0:T(8,128)(2,1)} %dynamic-slice_bitcast_fusion), channel_id=1, source_target_pairs={{0,4},{4,0},{1,5},{5,1},{2,6},{6,2},{3,7},{7,3},{8,12},{12,8},{9,1... | collective-permute-start | bytes 4669448 | tf_op jit(solution)/shard_map/ppermute | solution.py:586
  642.3 32.0 %collective-permute-start.47 = (bf16[320,2048]{1,0:T(8,128)(2,1)}, bf16[320,2048]{1,0:T(8,128)(2,1)}, u32[]{:S(2)}, u32[]{:S(2)}) collective-permute-start(bf16[320,2048]{1,0:T(8,128)(2,1)} %pad_maximum_fusion.10), channel_id=1, source_target_pairs={{0,16},{8,24},{16,0},{24,8},{1,17},{9,25},{17,1},{25,9},{2,18},{10... | collective-permute-start | bytes 3932168 | tf_op jit(solution)/shard_map/ppermute | solution.py:539
  645.3 32.0 %collective-permute-start.45 = (bf16[320,2048]{1,0:T(8,128)(2,1)}, bf16[320,2048]{1,0:T(8,128)(2,1)}, u32[]{:S(2)}, u32[]{:S(2)}) collective-permute-start(bf16[320,2048]{1,0:T(8,128)(2,1)} %pad_maximum_fusion.9), channel_id=1, source_target_pairs={{0,8},{8,0},{16,24},{24,16},{1,9},{9,1},{17,25},{25,17},{2,10},{10... | collective-permute-start | bytes 3932168 | tf_op jit(solution)/shard_map/ppermute | solution.py:539
  652.7 36.8 %all-to-all-start.7 = ((bf16[4,64,1,1536]{3,1,2,0:T(8,128)(2,1)}), bf16[4,64,1,1536]{3,1,2,0:T(8,128)(2,1)}, u32[]{:S(2)}, u32[]{:S(2)}) async-start(bf16[4,64,1,1536]{3,1,2,0:T(8,128)(2,1)} %bitcast.189), calls=%async_computation.12 | async-start | bytes 1572864 | tf_op jit(solution)/shard_map/all_to_all | solution.py:593
  656.9 64.2 %reduce-scatter.14.cloned.1.call-start = ((), (), s32[]{:S(2)}) async-start(), calls=%async_computation.20 | async-start | bytes 1945600 | tf_op jit(solution)/shard_map/reduce_scatter | solution.py:590
  693.7 12.1 %all-to-all-start.5 = ((bf16[4,64,1,1280]{3,1,2,0:T(8,128)(2,1)}), bf16[4,64,1,1280]{3,1,2,0:T(8,128)(2,1)S(1)}, u32[]{:S(2)}, u32[]{:S(2)}) async-start(bf16[4,64,1,1280]{3,1,2,0:T(8,128)(2,1)} %bitcast.191), calls=%async_computation.9 | async-start | bytes 1310720 | tf_op jit(solution)/shard_map/all_to_all | solution.py:593
  706.5 12.7 %all-to-all-start.6 = ((f32[32,1,128]{2,1,0:T(1,128)}), f32[32,1,128]{2,1,0:T(1,128)S(1)}, u32[]{:S(2)}, u32[]{:S(2)}) async-start(f32[32,1,128]{2,1,0:T(1,128)} %reshape.327), calls=%async_computation.10 | async-start | bytes 32768 | tf_op jit(solution)/shard_map/all_to_all | solution.py:797
  (103 other events, 1355.0 us)
Sparse Core Ops, SparseCore 0:
  25.0 66.4 all-gather.3
  93.7 84.9 all-gather.5
  184.2 113.9 all-gather.7
  378.0 58.4 reduce-scatter.5
  438.7 60.2 reduce-scatter.7
  505.4 58.4 reduce-scatter.9
  604.3 52.7 reduce-scatter.11
  684.8 34.8 reduce-scatter.13

commit v5 on v4

--- a/solution.py
+++ b/solution.py
@@ -349,8 +349,12 @@
         store_parts(refs, length, part, total[part * length : (part + 1) * length])
 
 
-def back_kernel(pieces, *refs):
-    grads, w_ref, outs = refs[:pieces], refs[pieces], refs[pieces + 1 :]
+def back_kernel(pieces, summed, *refs):
+    grads, w_ref, refs = refs[:pieces], refs[pieces], refs[pieces + 1 :]
+    if summed:
+        values_ref, inverse_ref, *outs, sums_ref = refs
+    else:
+        outs = refs
     shares, _, rows, _ = w_ref.shape
     total = None
     start = 0
@@ -361,6 +365,9 @@
         total = term if total is None else total + term
         start += cut
     store_all(outs, total)
+    if summed:
+        scaled = total * values_ref[...].astype(jnp.float32) * inverse_ref[...]
+        sums_ref[...] = jnp.sum(scaled, axis=0, keepdims=True)
 
 
 def parts_out(length, width, block):
@@ -371,18 +378,24 @@
     )
 
 
-def back_parts(grads, weights):
+def back_parts(grads, weights, summed=None):
     tokens = grads[0].shape[0]
     inner = sum(g.shape[1] for g in grads)
     shares, groups, rows, columns = weights.shape
     block = shares * rows
     shapes, specs = parts_out(tokens // PLANE, groups * block, block)
+    in_specs = [pl.BlockSpec(g.shape, lambda j: (0, 0), pipeline_mode=CONSTANT) for g in grads]
+    in_specs.append(pl.BlockSpec((shares, 1, rows, columns), lambda j: (0, j, 0, 0)))
+    if summed is not None:
+        in_specs.append(pl.BlockSpec((tokens, block), lambda j: (0, j)))
+        in_specs.append(pl.BlockSpec((tokens, 1), lambda j: (0, 0)))
+        shapes += (jax.ShapeDtypeStruct((1, groups * block), jnp.float32),)
+        specs += (pl.BlockSpec((1, block), lambda j: (0, j)),)
     return pl.pallas_call(
-        functools.partial(back_kernel, len(grads)),
+        functools.partial(back_kernel, len(grads), summed is not None),
         grid=(groups,),
         out_shape=shapes,
-        in_specs=[pl.BlockSpec(g.shape, lambda j: (0, 0), pipeline_mode=CONSTANT) for g in grads]
-        + [pl.BlockSpec((shares, 1, rows, columns), lambda j: (0, j, 0, 0))],
+        in_specs=in_specs,
         out_specs=specs,
         compiler_params=pltpu.CompilerParams(vmem_limit_bytes=VMEM_BYTES),
         cost_estimate=pl.CostEstimate(
@@ -391,7 +404,52 @@
             transcendentals=0,
         ),
         name="back_parts",
-    )(*grads, weights)
+    )(*grads, weights, *(summed or ()))
+
+
+def conv_back_kernel(seqs, taps, d_conv_ref, d_rate_ref, d_input_ref, rate_ref, input_ref, branch_ref, kernel_ref, out_ref, sums_ref, d_s):
+    rows, channels = branch_ref.shape
+    length = rows // seqs
+    total = d_conv_ref[...] + matmul_nt(d_rate_ref[...], rate_ref[...]) + matmul_nt(d_input_ref[...], input_ref[...])
+    nothing = jnp.zeros((8, channels), jnp.float32)
+    for q in range(seqs):
+        d_s[q, :length, :] = total[q * length : (q + 1) * length]
+        d_s[q, length:, :] = nothing
+    half = length // 2
+    sums = [jnp.zeros((1, channels), jnp.float32) for _ in range(taps + 1)]
+    for q in range(seqs):
+        for start in (0, half):
+            at = pl.ds(q * length + start, half)
+            branch = branch_ref[at, :]
+            d_branch = None
+            for tap in range(taps):
+                moved = d_s[q, pl.ds(start + taps - 1 - tap, half), :]
+                term = kernel_ref[tap : tap + 1, :] * moved
+                d_branch = term if d_branch is None else d_branch + term
+                sums[tap] = sums[tap] + jnp.sum(branch * moved, axis=0, keepdims=True)
+                if tap == taps - 1:
+                    sums[taps] = sums[taps] + jnp.sum(moved, axis=0, keepdims=True)
+            out_ref[at, :] = d_branch.astype(jnp.bfloat16)
+    for k in range(taps + 1):
+        sums_ref[k : k + 1, :] = sums[k]
+
+
+def conv_back(seqs, d_conv, d_rate, d_input, w_rate, w_input, branch, kernel):
+    rows, channels = branch.shape
+    taps = kernel.shape[0]
+    whole = lambda v: pl.BlockSpec(v.shape, lambda i: (0, 0))
+    args = (d_conv, d_rate, d_input, w_rate, w_input, branch, kernel)
+    return pl.pallas_call(
+        functools.partial(conv_back_kernel, seqs, taps),
+        grid=(1,),
+        out_shape=(jax.ShapeDtypeStruct((rows, channels), jnp.bfloat16), jax.ShapeDtypeStruct((taps + 1, channels), jnp.float32)),
+        in_specs=[whole(v) for v in args],
+        out_specs=(pl.BlockSpec((rows, channels), lambda i: (0, 0)), pl.BlockSpec((taps + 1, channels), lambda i: (0, 0))),
+        scratch_shapes=[pltpu.VMEM((seqs, rows // seqs + 8, channels), jnp.float32)],
+        compiler_params=pltpu.CompilerParams(vmem_limit_bytes=VMEM_BYTES),
+        cost_estimate=pl.CostEstimate(flops=8 * rows * channels * channels, bytes_accessed=16 * rows * channels, transcendentals=0),
+        name="conv_back",
+    )(*args)
 
 
 def out_kernel(values_ref, w_ref, *refs):
@@ -422,18 +480,16 @@
     )(values, weight)
 
 
-def weight_grad_kernel(rows, me_ref, left_ref, right_ref, mine_ref, *refs):
-    theirs, left_s = refs[:-1], refs[-1]
+def weight_grad_kernel(rows, rights, steps, me_ref, left_ref, *refs):
+    right_refs, mine_ref, theirs, left_s = refs[:rights], refs[rights], refs[rights + 1 : -1], refs[-1]
+    narrow, groups, _, block = mine_ref.shape
+    height = narrow * rows
 
     @pl.when(pl.program_id(1) == 0)
     def _():
         left_s[...] = left_ref[...].T
 
-    narrow, groups, _, block = mine_ref.shape
-    height = narrow * rows
-    total = jnp.dot(left_s[...], right_ref[0], preferred_element_type=jnp.float32).astype(jnp.bfloat16)
-
-    def store(mine, other):
+    def store(total, mine, other):
         for g in range(groups):
             start = (g * 2 + mine) * height
             mine_ref[:, g] = total[start : start + height].reshape(narrow, rows, block)
@@ -441,32 +497,39 @@
             for k, ref in enumerate(theirs):
                 ref[0, g] = total[start + k * rows : start + (k + 1) * rows]
 
-    @pl.when(me_ref[0] == 0)
-    def _():
-        store(0, 1)
-
-    @pl.when(me_ref[0] != 0)
-    def _():
-        store(1, 0)
-
-
-def weight_grad(me, left, right, narrow, groups, rows):
-    tokens = left.shape[0]
-    pieces, _, piece = right.shape
+    for k, right_ref in enumerate(right_refs):
+
+        @pl.when(pl.program_id(1) // steps == k)
+        def _(right_ref=right_ref):
+            total = jnp.dot(left_s[...], right_ref[...], preferred_element_type=jnp.float32).astype(jnp.bfloat16)
+
+            @pl.when(me_ref[0] == 0)
+            def _():
+                store(total, 0, 1)
+
+            @pl.when(me_ref[0] != 0)
+            def _():
+                store(total, 1, 0)
+
+
+def weight_grad(me, left, rights, narrow, groups, rows):
+    tokens, piece = rights[0].shape
     block = column_block(piece, 768)
     steps = piece // block
     together = 2 if groups % 2 == 0 else 1
     height = together * 2 * narrow * rows
-    columns = pieces * piece
+    columns = len(rights) * piece
+
+    def right_spec(k):
+        return pl.BlockSpec((tokens, block), lambda g, j, me_ref: (0, jnp.clip(j - k * steps, 0, steps - 1)))
+
     return pl.pallas_call(
-        functools.partial(weight_grad_kernel, rows),
+        functools.partial(weight_grad_kernel, rows, len(rights), steps),
         grid_spec=pltpu.PrefetchScalarGridSpec(
             num_scalar_prefetch=1,
-            grid=(groups // together, pieces * steps),
-            in_specs=[
-                pl.BlockSpec((tokens, height), lambda g, j, me_ref: (0, g)),
-                pl.BlockSpec((1, tokens, block), lambda g, j, me_ref: (j // steps, 0, j % steps)),
-            ],
+            grid=(groups // together, len(rights) * steps),
+            in_specs=[pl.BlockSpec((tokens, height), lambda g, j, me_ref: (0, g))]
+            + [right_spec(k) for k in range(len(rights))],
             out_specs=(pl.BlockSpec((narrow, together, rows, block), lambda g, j, me_ref: (0, g, 0, j)),)
             + (pl.BlockSpec((1, together, rows, block), lambda g, j, me_ref: (0, g, 0, j)),) * narrow,
             scratch_shapes=[pltpu.VMEM((height, tokens), jnp.bfloat16)],
@@ -476,11 +539,11 @@
         compiler_params=pltpu.CompilerParams(vmem_limit_bytes=VMEM_BYTES),
         cost_estimate=pl.CostEstimate(
             flops=2 * tokens * left.shape[1] * columns,
-            bytes_accessed=2 * (left.size + groups // together * right.size + left.shape[1] * columns),
+            bytes_accessed=2 * (left.size + groups // together * tokens * columns + left.shape[1] * columns),
             transcendentals=0,
         ),
         name="weight_grad",
-    )(me, left, right)
+    )(me, left, *rights)
 
 
 def add_pieces_kernel(mine_ref, *refs):
@@ -546,16 +609,19 @@
     def gather_rows(shard):
         return jnp.concatenate(gather_parts(shard), axis=0)
 
-    def scatter_start(parts):
+    def scatter_start(parts, *beside):
         far_low, far_high, one, two, own = parts
         half = own.shape[0] // 2
-        via_one, via_two = swap(far_low, 1), swap(far_high, 2)
+        via_one, via_two, *beside = fence(swap(far_low, 1), swap(far_high, 2), *beside)
         one = jnp.concatenate([one[:half], (one[half:].astype(f32) + via_two.astype(f32)).astype(bf16)], axis=0)
         two = jnp.concatenate([(two[:half].astype(f32) + via_one.astype(f32)).astype(bf16), two[half:]], axis=0)
-        return one, two, own
+        return (one, two, own, *beside)
+
+    def scatter_sum(own, one, two):
+        return own.astype(f32) + one.astype(f32) + two.astype(f32)
 
     def scatter_finish(one, two, own):
-        return own.astype(f32) + swap(one, 1).astype(f32) + swap(two, 2).astype(f32)
+        return scatter_sum(own, swap(one, 1), swap(two, 2))
 
     def scatter_rows(parts):
         return scatter_finish(*scatter_start(parts))
@@ -567,15 +633,15 @@
         whole = lax.all_gather(part.reshape(-1, part.shape[-1]), spread, axis=0, tiled=True)
         return whole.reshape((rest_size * narrow_size,) + part.shape)
 
-    def grad_shares(left, right, rows, groups):
+    def grad_shares(left, rights, rows, groups):
         if rest_size != 2:
-            grad = matmul_tn(left, right.swapaxes(0, 1).reshape(right.shape[1], -1)).astype(bf16)
+            grad = matmul_tn(left, jnp.concatenate(rights, axis=1)).astype(bf16)
             cut = grad.reshape(groups, rest_size, narrow_size, rows, -1).transpose(1, 2, 0, 3, 4)
-            return grad, lambda *waits: lax.psum_scatter(after(cut, *waits), "rest", scatter_dimension=0, tiled=False)
+            return cut, lambda term: lax.psum_scatter(term, "rest", scatter_dimension=0, tiled=False)
         me = lax.axis_index("rest").astype(jnp.int32)[None]
-        mine, *theirs = weight_grad(me, left, right, narrow_size, groups, rows)
+        mine, *theirs = weight_grad(me, left, rights, narrow_size, groups, rows)
         others = [lax.ppermute(piece, "rest", [(0, 1), (1, 0)]) for piece in theirs]
-        return mine, lambda *waits: add_pieces(after(mine, *waits), others)
+        return mine, lambda term: add_pieces(term, others)
 
     def sum_rest(values):
         if rest_size != 2:
@@ -718,23 +784,25 @@
         *normed2_parts, w_mlp = fence(*gather_parts(normed2), w_mlp)
 
         product, d_gate_two, d_up_two, normed2_all = mlp_both(normed2_parts, low_res_all, w_mlp, w_down)
-        first, finish_down = grad_shares(product, low_res_all[None], mlp_down.shape[0], 1)
-        parts2 = back_parts((after(d_gate_two, first), d_up_two), w_mlp)
-        grad_down = finish_down(parts2[0])
-        down_out = sum_narrow(grad_down)
-        d_normed2 = scatter_rows(parts2)
-        _, finish = grad_shares(normed2_all, after(d_gate_two, parts2)[None], rows, PLANE)
-        grad_mgate = finish()
-        d_normed2, grad_mgate, down_out = fence(d_normed2, grad_mgate, down_out)
+        mine, finish = grad_shares(product, (low_res_all,), mlp_down.shape[0], 1)
+        mine, late_gate_two = fence(mine, d_gate_two)
+        parts2 = back_parts((late_gate_two, d_up_two), w_mlp)
+        down_out = sum_narrow(finish(mine))
+        one, two, own = scatter_start(parts2)
+        mine, finish = grad_shares(normed2_all, (late_gate_two,), rows, PLANE)
+        grad_mgate = finish(mine)
+        d_normed2 = scatter_finish(one, two, own)
+        d_normed2, grad_mgate, down_out, late_up_two, late_product = fence(
+            d_normed2, grad_mgate, down_out, d_up_two, product
+        )
 
         mgate_sum = sum_narrow(grad_mgate)
         grad_gain2 = jnp.sum(d_normed2 * merged * inverse2, axis=0)
         d_merged = low_res.astype(f32) + rms_back(merged, inverse2, gain_two, d_normed2)
-        low_merged = d_merged.astype(bf16)
-        low_merged_parts = gather_parts(low_merged)
-        _, finish = grad_shares(normed2_all, after(d_up_two, low_merged)[None], rows, PLANE)
-        grad_mup = finish(*low_merged_parts[2:4])
-        parts_result = out_parts(after(product, *low_merged_parts[2:4]), (w_down[None], w_down.shape[0]))
+        low_merged_parts = gather_parts(d_merged.astype(bf16))
+        mine, finish = grad_shares(normed2_all, (late_up_two,), rows, PLANE)
+        grad_mup = finish(mine)
+        parts_result = out_parts(late_product, (w_down[None], w_down.shape[0]))
         *low_merged_parts, parts_result, mgate_sum, grad_mup = fence(*low_merged_parts, parts_result, mgate_sum, grad_mup)
         d_mixed, low_merged_all = mixed_grad(low_merged_parts, w_out)
         mup_sum = sum_narrow(grad_mup)
@@ -743,42 +811,28 @@
         d_conv_lru, d_rate, d_input, d_gate, sums = lru_backward(
             seqs, conv, rate_pre, input_pre, gate_pre, soft_rows, states, d_mixed
         )
-        mgate_out = columns_home(after(mgate_sum, d_conv_lru), rows)
+        mgate_out = columns_home(mgate_sum, rows)
         sums = sums.reshape(3, 8, -1).sum(axis=1)
         grad_decay = sums[2] * (-1.0 / (1.0 + jnp.exp(decay_f[0])))
-        d_conv = d_conv_lru + matmul_nt(d_rate, w_rate) + matmul_nt(d_input, w_input)
-        result = merged + scatter_finish(*sums_result)
-        d_branch = jnp.zeros_like(d_conv)
-        grad_taps = []
-        for tap in range(taps):
-            moved = shift_rows(d_conv, seqs, tap - (taps - 1))
-            d_branch = d_branch + kernel_f[tap] * moved
-            grad_taps.append(jnp.sum(branch_pre * moved, axis=0))
-        low_branch = d_branch.astype(bf16)
-        d_rec = jnp.stack([d_gate, low_branch])
-
-        d_rec, mgate_out, result = fence(d_rec, mgate_out, result)
-        _, finish = grad_shares(normed1, d_rec, rows, PLANE)
-        grad_rec = finish(mup_sum)
-        rec_sum = sum_narrow(grad_rec)
-        mup_out = columns_home(after(mup_sum, d_rec), rows)
-        parts1 = back_parts((after(d_gate, grad_rec, mup_out), low_branch), w_rec)
+        low_branch, conv_sums = conv_back(seqs, d_conv_lru, d_rate, d_input, w_rate, w_input, branch_pre, kernel_f)
+        one, two, own = sums_result
+        result_one, result_two = swap(one, 1), swap(two, 2)
+
+        low_branch, mgate_out, result_one, result_two = fence(low_branch, mgate_out, result_one, result_two)
+        result = merged + scatter_sum(own, result_one, result_two)
+        mine, finish = grad_shares(normed1, (d_gate, low_branch), rows, PLANE)
+        rec_sum = sum_narrow(finish(mine))
+        *parts1, grad_gain1 = back_parts((d_gate, low_branch), w_rec, (tokens_all, inverse_all))
         one, two, own = scatter_start(parts1)
+        one, two, late_mixed, late_rate, late_input = fence(one, two, mixed, d_rate, d_input)
         d_normed1 = scatter_finish(one, two, own)
-        grad_out = matmul_tn(mixed, after(low_merged_all, parts1)).astype(bf16)
-        normed_f = after(tokens_all, grad_rec).astype(f32) * inverse_all
-        grad_gain1 = jnp.zeros((width,), f32)
-        start = 0
-        for part in parts1:
-            grad_gain1 = grad_gain1 + jnp.sum(part.astype(f32) * normed_f[start : start + part.shape[0]], axis=0)
-            start += part.shape[0]
-        gain_grads = jnp.stack([grad_gain1, grad_gain2]).reshape(2, -1, rows).swapaxes(0, 1)
-        grad_rate_weight = diagonal_blocks(matmul_tn(conv, after(d_rate, grad_rec)), head)
-        grad_input_weight = diagonal_blocks(matmul_tn(conv, after(d_input, grad_rec)), head)
+        grad_out = matmul_tn(late_mixed, low_merged_all).astype(bf16)
+        gain_grads = jnp.stack([grad_gain1[0], grad_gain2]).reshape(2, -1, rows).swapaxes(0, 1)
+        grad_rate_weight = diagonal_blocks(matmul_tn(conv, late_rate), head)
+        grad_input_weight = diagonal_blocks(matmul_tn(conv, late_input), head)
         table_grad = jnp.concatenate(
             [
-                jnp.stack(grad_taps),
-                jnp.sum(d_conv, axis=0)[None],
+                conv_sums,
                 grad_rate_weight,
                 sums[0:1],
                 grad_input_weight,
@@ -789,12 +843,13 @@
         )
         table_grad = jnp.pad(table_grad, ((0, -places[-1] % LANES), (0, 0))).T.astype(bf16)
         last = sum_rest(rows_cut(jnp.concatenate([grad_out, table_grad], axis=1)))
-        rec_sum, d_normed1 = fence(rec_sum, d_normed1)
-        last = sum_narrow(after(last, rec_sum)).astype(f32)
+        rec_sum, d_normed1, last, gain_grads, mup_sum = fence(rec_sum, d_normed1, last, gain_grads, mup_sum)
+        last = sum_narrow(last).astype(f32)
         out_out, table_out = last[:, :width], last[:, width:].T
 
         rec_out = columns_home(rec_sum, rows)
-        gain_out = lax.all_to_all(after(gain_grads, rec_out), ("wide",) + spread, 0, 0, tiled=False).sum(axis=0)
+        mup_out = columns_home(mup_sum, rows)
+        gain_out = lax.all_to_all(gain_grads, ("wide",) + spread, 0, 0, tiled=False).sum(axis=0)
         block_out = (result * live).astype(bf16)
         own = tokens.astype(f32)
         input_grad = d_merged + rms_back(own, rms_inverse(own), gain_one, d_normed1)

time: 739 us -> 721 us (0.976)
  waiting for transfers between devices: 176 us -> 202 us
  other arithmetic: 92.5 us -> 66.9 us
  local copies, waits for them, and re-layouts: 103 us -> 82.5 us
  Pallas kernels: 222 us -> 234 us
  matrix products: 36.7 us -> 28.6 us
    reduce_sum x4 -> x1, other arithmetic: 16.2 us -> 0.05 us  [on_device(): lax.all_to_all(gain_grads, ('wide',) + spread, 0, 0, tiled=False)]
    slice x1, local copies, waits for them, and re-layouts: 12.3 us -> 0.1 us  [on_device(): table[places[i]:places[i + 1]]]
    pallas_call x6 -> x7, Pallas kernels: 95.4 us -> 107 us  [the longest x4 58.5 us: weight_grad(): pl.pallas_call(functools.partial(weight_grad_kernel, rows, len(rights), s...]
    all_gather x1, waiting for transfers between devices: 0.01 us -> 7.78 us  [on_device(): lax.all_gather(after(jnp.concatenate([out_proj, mlp_down], axis=0), w_rec...]
    unnamed x220 -> x174, local copies, waits for them, and re-layouts: 28.1 us -> 26.6 us
  transfers between devices with their start and end apart: 64 -> 64, of which waited for: 26 -> 31; matrix products, arithmetic and copies ran while one was open for 29% -> 23% of each run, Pallas kernels for 22% -> 25%
where the time goes in v5:
time: 721 us; the launch traced here: 714 us
  Pallas kernels  234 us (32%)
  waiting for transfers between devices  202 us (28%)
  local copies, waits for them, and re-layouts  82.5 us (11%)
  starting transfers between devices  68.8 us (10%)
  other arithmetic  66.9 us (9%)
  matrix products  28.6 us (4%)
  between operations  16.4 us (2%)
  blocking collectives  15 us (2%)
    ppermute x32, waiting for transfers between devices, swap(): return lax.ppermute(values, 'wide', [(i, i ^ mask) for i in range(PLANE)])  146 us
    pallas_call x4, Pallas kernels, weight_grad(): pl.pallas_call(functools.partial(weight_grad_kernel, rows, len(rights), s...  58.5 us
    pallas_call x2, Pallas kernels, back_parts(): pl.pallas_call(functools.partial(back_kernel, len(grads), summed is not N...  36.9 us
    ppermute x32, starting transfers between devices, swap(): return lax.ppermute(values, 'wide', [(i, i ^ mask) for i in range(PLANE)])  36.6 us
    pallas_call x1, Pallas kernels, mlp_both(): pl.pallas_call(functools.partial(mlp_kernel, PLANE), grid=(steps,), out_s...  35 us
    unnamed x174, local copies, waits for them, and re-layouts  26.6 us
    pallas_call x4, Pallas kernels, add_pieces(): pl.pallas_call(add_pieces_kernel, grid=(groups, columns // block), out_sh...  25.3 us
    pallas_call x1, Pallas kernels, lru_backward(): pl.pallas_call(functools.partial(lru_backward_kernel, seqs), grid=(pl.cdi...  21.2 us
  transfers between devices with their start and end apart: 64, of which 31 were waited for; matrix products, arithmetic and copies ran while one was open for 23% of the time, Pallas kernels for 25%

profile of v5, /device:TPU:0, one launch (start us, length us, event | category | flops | bytes accessed | tf_op | source)
XLA Modules:
  0.0 714.3 jit_solution(5709294260182547561)
XLA Ops:
  9.9 15.0 %all_to_all.64 = bf16[4,64,1280]{2,1,0:T(8,128)(2,1)} all-to-all(bf16[4,64,1280]{2,1,0:T(8,128)(2,1)S(1)} %copy.97), channel_id=1, replica_groups=mesh['wide'=4,'rest'=2,'narrow'=4] {'wide'}, dimensions={0} | all-to-all | bytes 1310720 | tf_op jit(solution)/shard_map/all_to_all | solution.py:630
  28.1 4.9 all-to-all-start.1
  33.0 21.0 %collective-permute-done = bf16[320,2048]{1,0:T(8,128)(2,1)S(1)} collective-permute-done((bf16[320,2048]{1,0:T(8,128)(2,1)S(1)}, bf16[320,2048]{1,0:T(8,128)(2,1)S(1)}, u32[]{:S(2)}, u32[]{:S(2)}) %collective-permute-start) | collective-permute-done | bytes 1310752 | tf_op jit(solution)/shard_map/ppermute | solution.py:602
  56.2 2.3 pad_maximum_fusion.10
  61.0 2.3 reshape.211
  68.2 5.1 all-to-all-start.2
  78.7 2.7 constant_dynamic-update-slice_fusion.1
  82.5 9.0 %all-gather.4.cloned.1.call-done = bf16[2048,1280]{1,0:T(8,128)(2,1)} async-done(((bf16[256,1280]{1,0:T(8,128)(2,1)}), bf16[2048,1280]{1,0:T(8,128)(2,1)}) %all-gather.4.cloned.1.call-update) | async-done | bytes 5242896 | tf_op jit(solution)/shard_map/all_gather | solution.py:633
  96.7 5.9 copy.100
  102.9 3.8 fusion
  106.8 3.9 fusion.2.left_ref
  110.8 4.3 fusion.15.branch_ref
  115.0 2.7 pad_slice_fusion.2
  117.8 7.9 %fusion.13.gate_ref = f32[1280,640]{1,0:T(8,128)} fusion(bf16[1280,2048]{1,0:T(8,128)(2,1)S(1)} %fusion.2.left_ref, bf16[2048,1280]{1,0:T(8,128)(2,1)} %bitcast.133), kind=kOutput, calls=%fused_computation.30 | convolution fusion | flops 3355443200 | bytes 11141120 | tf_op jit(solution)/shard_map/dot_general | solution.py:20
  131.7 3.7 convolution_add_fusion.input_ref
  135.4 3.6 convolution_add_fusion.1.rate_ref
  139.0 6.4 collective-permute-done.5
  149.0 3.6 all-to-all-start.3
  152.6 14.7 %lru_forward.1 = (f32[1280,640]{1,0:T(8,128)}, bf16[1280,640]{1,0:T(8,128)(2,1)S(1)}) custom-call(bf16[1280,640]{1,0:T(8,128)(2,1)S(1)} %fusion.5.conv_ref, f32[1280,640]{1,0:T(8,128)} %convolution_add_fusion.1.rate_ref, f32[1280,640]{1,0:T(8,128)} %convolution_add_fusion.input_ref, f32[1280,640]{1,0:T(8,128)} %fusion.13.gate_ref, ...), custom_call_target="tpu_custom_call" | custom-call | flops 16384000000 | bytes 16384000 | tf_op jit(solution)/shard_map/lru_forward/pallas_call | solution.py:198
  168.5 2.4 all-to-all-done.3
  170.9 7.8 %all-gather.6.cloned.1.call-done = bf16[2176,2048]{1,0:T(8,128)(2,1)} async-done(((bf16[272,2048]{1,0:T(8,128)(2,1)}), bf16[2176,2048]{1,0:T(8,128)(2,1)}) %all-gather.6.cloned.1.call-update) | async-done | bytes 8912912 | tf_op jit(solution)/shard_map/all_gather | solution.py:740
  178.8 7.4 %out_parts.2 = (bf16[160,2048]{1,0:T(8,128)(2,1)}, bf16[160,2048]{1,0:T(8,128)(2,1)}, bf16[320,2048]{1,0:T(8,128)(2,1)}, bf16[320,2048]{1,0:T(8,128)(2,1)}, bf16[320,2048]{1,0:T(8,128)(2,1)}) custom-call(bf16[1280,640]{1,0:T(8,128)(2,1)} %copy-done.2, bf16[8,272,2048]{2,1,0:T(8,128)(2,1)} %bitcast.116), custom_call_target="tpu_custom_call" | custom-call | flops 3355443200 | bytes 9502720 | tf_op jit(solution)/shard_map/out_parts/pallas_call | solution.py:466
  191.7 11.6 %collective-permute-done.8 = bf16[160,2048]{1,0:T(8,128)(2,1)S(1)} collective-permute-done((bf16[160,2048]{1,0:T(8,128)(2,1)}, bf16[160,2048]{1,0:T(8,128)(2,1)S(1)}, u32[]{:S(2)}, u32[]{:S(2)}) %collective-permute-start.8) | collective-permute-done | bytes 655392 | tf_op jit(solution)/shard_map/ppermute | solution.py:602
  207.3 27.5 %collective-permute-done.10 = bf16[320,2048]{1,0:T(8,128)(2,1)} collective-permute-done((bf16[320,2048]{1,0:T(8,128)(2,1)S(1)}, bf16[320,2048]{1,0:T(8,128)(2,1)}, u32[]{:S(2)}, u32[]{:S(2)}) %collective-permute-start.10) | collective-permute-done | bytes 1310752 | tf_op jit(solution)/shard_map/ppermute | solution.py:602
  235.5 3.5 multiply_reduce_fusion.2
  245.8 23.8 %collective-permute-done.12.refs_2_ = bf16[320,2048]{1,0:T(8,128)(2,1)} collective-permute-done((bf16[320,2048]{1,0:T(8,128)(2,1)}, bf16[320,2048]{1,0:T(8,128)(2,1)}, u32[]{:S(2)}, u32[]{:S(2)}) %collective-permute-start.12) | collective-permute-done | bytes 1310752 | tf_op jit(solution)/shard_map/ppermute | solution.py:602
  279.1 8.5 %slice.209 = bf16[8,192,2048]{2,1,0:T(8,128)(2,1)} slice(bf16[8,272,2048]{2,1,0:T(8,128)(2,1)} %bitcast.117), slice={[0:8], [80:272], [0:2048]} | slice | bytes 12582912 | tf_op jit(solution)/shard_map/slice | solution.py:778
  287.6 8.6 %all-gather.8.cloned.1.call-done = bf16[2048,3072]{1,0:T(8,128)(2,1)} async-done(((bf16[256,3072]{1,0:T(8,128)(2,1)}), bf16[2048,3072]{1,0:T(8,128)(2,1)}) %all-gather.8.cloned.1.call-update) | async-done | bytes 12582928 | tf_op jit(solution)/shard_map/all_gather | solution.py:633
  296.1 35.0 %mlp_both.1 = (bf16[1280,1536]{1,0:T(8,128)(2,1)}, bf16[1280,1536]{1,0:T(8,128)(2,1)}, bf16[1280,1536]{1,0:T(8,128)(2,1)}, bf16[1280,2048]{1,0:T(8,128)(2,1)}) custom-call(bf16[160,2048]{1,0:T(8,128)(2,1)} %copy-done.75, bf16[160,2048]{1,0:T(8,128)(2,1)} %collective-permute-done.15.refs_1_, bf16[320,2048]{1,0:T(8,128)(2,1)} %collective-permute-done.12.refs_2_, ...), custom_call_target="tpu_custom_call" | custom-call | flops 24159191040 | bytes 34603008 | tf_op jit(solution)/shard_map/mlp_both/pallas_call | solution.py:282
  331.1 14.4 %weight_grad.4 = (bf16[4,1,192,2048]{3,2,1,0:T(8,128)(2,1)}, bf16[1,1,192,2048]{3,2,1,0:T(8,128)(2,1)}, bf16[1,1,192,2048]{3,2,1,0:T(8,128)(2,1)}, bf16[1,1,192,...) custom-call(s32[1]{0:T(128)} %bitcast.24.me_ref, bf16[1280,1536]{1,0:T(8,128)(2,1)} %get-tuple-element.190.left_ref.values_ref, ...), custom_call_target="tpu_custom_call" | custom-call | flops 8053063680 | bytes 15466496 | tf_op jit(solution)/shard_map/weight_grad/pallas_call | solution.py:526
  352.3 4.4 add_pieces.5
  356.7 22.5 %back_parts.2 = (bf16[160,2048]{1,0:T(8,128)(2,1)}, bf16[160,2048]{1,0:T(8,128)(2,1)}, bf16[320,2048]{1,0:T(8,128)(2,1)}, bf16[320,2048]{1,0:T(8,128)(2,1)}, bf16[320,2048]{1,0:T(8,128)(2,1)}) custom-call(bf16[1280,1536]{1,0:T(8,128)(2,1)} %get-tuple-element.169.refs_0_, bf16[1280,1536]{1,0:T(8,128)(2,1)} %get-tuple-element.197.refs_1_.refs_0_, ...), custom_call_target="tpu_custom_call" | custom-call | flops 16106127360 | bytes 25690112 | tf_op jit(solution)/shard_map/back_parts/pallas_call | solution.py:394
  382.0 15.2 %weight_grad.5 = (bf16[4,4,64,1536]{3,2,1,0:T(8,128)(2,1)}, bf16[1,4,64,1536]{3,2,1,0:T(8,128)(2,1)}, bf16[1,4,64,1536]{3,2,1,0:T(8,128)(2,1)}, bf16[1,4,64,1536]{3,2,1,0:T(8,128)(2,1)}, bf16[1,4,64,1536]{3,2,1,0:T(8,128)(2,1)}) custom-call(s32[1]{0:T(128)} %bitcast.24.me_ref, bf16[1280,2048]{1,0:T(8,128)(2,1)} %get-tuple-element.178.left_ref, ...), custom_call_target="tpu_custom_call" | custom-call | flops 8053063680 | bytes 19398656 | tf_op jit(solution)/shard_map/weight_grad/pallas_call | solution.py:526
  405.6 7.1 add_pieces.4
  412.7 16.4 %collective-permute-done.18 = bf16[320,2048]{1,0:T(8,128)(2,1)} collective-permute-done((bf16[320,2048]{1,0:T(8,128)(2,1)S(1)}, bf16[320,2048]{1,0:T(8,128)(2,1)}, u32[]{:S(2)}, u32[]{:S(2)}) %collective-permute-start.18) | collective-permute-done | bytes 1310752 | tf_op jit(solution)/shard_map/ppermute | solution.py:602
  429.7 3.9 convert_add_fusion.3
  433.6 2.7 multiply_reduce_fusion
  439.4 15.2 %weight_grad.6 = (bf16[4,4,64,1536]{3,2,1,0:T(8,128)(2,1)}, bf16[1,4,64,1536]{3,2,1,0:T(8,128)(2,1)}, bf16[1,4,64,1536]{3,2,1,0:T(8,128)(2,1)}, bf16[1,4,64,1536]{3,2,1,0:T(8,128)(2,1)}, bf16[1,4,64,1536]{3,2,1,0:T(8,128)(2,1)}) custom-call(s32[1]{0:T(128)} %bitcast.24.me_ref, bf16[1280,2048]{1,0:T(8,128)(2,1)} %get-tuple-element.178.left_ref, ...), custom_call_target="tpu_custom_call" | custom-call | flops 8053063680 | bytes 19398656 | tf_op jit(solution)/shard_map/weight_grad/pallas_call | solution.py:526
  455.2 12.2 %collective-permute-done.28.refs_2_ = bf16[320,2048]{1,0:T(8,128)(2,1)S(1)} collective-permute-done((bf16[320,2048]{1,0:T(8,128)(2,1)S(1)}, bf16[320,2048]{1,0:T(8,128)(2,1)S(1)}, u32[]{:S(2)}, u32[]{:S(2)}) %collective-permute-start.28) | collective-permute-done | bytes 1310752 | tf_op jit(solution)/shard_map/ppermute | solution.py:602
  471.3 12.4 %out_parts.3 = (bf16[160,2048]{1,0:T(8,128)(2,1)}, bf16[160,2048]{1,0:T(8,128)(2,1)}, bf16[320,2048]{1,0:T(8,128)(2,1)}, bf16[320,2048]{1,0:T(8,128)(2,1)}, bf16[320,2048]{1,0:T(8,128)(2,1)}) custom-call(bf16[1280,1536]{1,0:T(8,128)(2,1)} %get-tuple-element.190.left_ref.values_ref, bf16[1,1536,2048]{2,1,0:T(8,128)(2,1)} %bitcast.127), custom_call_target="tpu_custom_call" | custom-call | flops 8053063680 | bytes 15466496 | tf_op jit(solution)/shard_map/out_parts/pallas_call | solution.py:466
  485.0 7.1 add_pieces.6
  494.8 2.5 fusion.17
  497.5 3.5 all-to-all-start.4
  501.6 10.9 %mixed_grad.1 = (f32[1280,640]{1,0:T(8,128)}, bf16[1280,2048]{1,0:T(8,128)(2,1)}) custom-call(bf16[160,2048]{1,0:T(8,128)(2,1)} %collective-permute-done.29.refs_0_, bf16[160,2048]{1,0:T(8,128)(2,1)} %collective-permute-done.31.refs_1_, bf16[320,2048]{1,0:T(8,128)(2,1)} %copy-done.23, bf16[320,2048]{1,0:T(8,128)(2,1)} %copy-done.24, ...), custom_call_target="tpu_custom_call" | custom-call | flops 3355443200 | bytes 16384000 | tf_op jit(solution)/shard_map/mixed_grad/pallas_call | solution.py:322
  519.5 2.5 collective-permute-start.39
  522.0 21.2 %lru_backward.1 = (f32[1280,640]{1,0:T(8,128)}, bf16[1280,640]{1,0:T(8,128)(2,1)S(1)}, bf16[1280,640]{1,0:T(8,128)(2,1)S(1)}, bf16[1280,640]{1,0:T(8,128)(2,1)S(1)}, f32[24,640]{1,0:T(8,128)S(1)}) custom-call(bf16[1280,640]{1,0:T(8,128)(2,1)} %copy-done, f32[1280,640]{1,0:T(8,128)} %convolution_add_fusion.1.rate_ref, ...), custom_call_target="tpu_custom_call" | custom-call | flops 16384000000 | bytes 16384000 | tf_op jit(solution)/shard_map/lru_backward/pallas_call | solution.py:217
  546.7 12.1 %conv_back.1 = (bf16[1280,640]{1,0:T(8,128)(2,1)}, f32[5,640]{1,0:T(8,128)}) custom-call(f32[1280,640]{1,0:T(8,128)} %get-tuple-element.219.d_conv_ref, bf16[1280,640]{1,0:T(8,128)(2,1)} %copy-done.6, bf16[1280,640]{1,0:T(8,128)(2,1)} %copy-done.4, bf16[640,640]{1,0:T(8,128)(2,1)} %get-tuple-element.378.rate_ref, ...), custom_call_target="tpu_custom_call" | custom-call | flops 4194304000 | bytes 13107200 | tf_op jit(solution)/shard_map/conv_back/pallas_call | solution.py:442
  558.9 14.4 %back_parts.3 = (bf16[160,2048]{1,0:T(8,128)(2,1)}, bf16[160,2048]{1,0:T(8,128)(2,1)}, bf16[320,2048]{1,0:T(8,128)(2,1)}, bf16[320,2048]{1,0:T(8,128)(2,1)}, bf1...) custom-call(bf16[1280,640]{1,0:T(8,128)(2,1)} %copy-done.8, bf16[1280,640]{1,0:T(8,128)(2,1)} %get-tuple-element.229.refs_1_, ...), custom_call_target="tpu_custom_call" | custom-call | flops 6710886400 | bytes 13762560 | tf_op jit(solution)/shard_map/back_parts/pallas_call | solution.py:394
  575.5 13.7 %weight_grad.7 = (bf16[4,4,64,1280]{3,2,1,0:T(8,128)(2,1)}, bf16[1,4,64,1280]{3,2,1,0:T(8,128)(2,1)}, bf16[1,4,64,1280]{3,2,1,0:T(8,128)(2,1)}, bf16[1,4,64,1280]{3,2,1,0:T(8,128)(2,1)}, bf16[1,4,64,1280]{3,2,1,0:T(8,128)(2,1)}) custom-call(s32[1]{0:T(128)} %bitcast.24.me_ref, bf16[1280,2048]{1,0:T(8,128)(2,1)} %copy-done.20, bf16[1280,640]{1,0:T(8,128)(2,1)} %copy-done.8, ...), custom_call_target="tpu_custom_call" | custom-call | flops 6710886400 | bytes 17039360 | tf_op jit(solution)/shard_map/weight_grad/pallas_call | solution.py:526
  594.5 6.6 add_pieces.7
  604.7 2.6 pad_maximum_fusion.8
  614.9 6.2 convolution_convert_fusion
  624.0 20.1 %collective-permute-done.46 = bf16[320,2048]{1,0:T(8,128)(2,1)} collective-permute-done((bf16[320,2048]{1,0:T(8,128)(2,1)}, bf16[320,2048]{1,0:T(8,128)(2,1)}, u32[]{:S(2)}, u32[]{:S(2)}) %collective-permute-start.46) | collective-permute-done | bytes 1310752 | tf_op jit(solution)/shard_map/ppermute | solution.py:602
  644.2 4.3 convert_add_fusion.2
  648.5 2.9 fusion.8
  651.4 4.4 reduce-scatter.10.cloned.1.call-done
  655.8 2.5 convert_element_type.295
  659.0 4.3 all-to-all-start.5
  664.8 5.7 all-to-all-done.5
  670.4 3.5 all-to-all-start.6
  673.9 2.9 fusion.9
  676.8 6.7 all-to-all-done.6
  684.4 3.5 all-to-all-start.7
  687.9 6.7 fusion.12
  (389 shorter events, 142.4 us)
Async XLA Ops:
  7.2 84.4 %all-gather.4.cloned.1.call-start = ((), (), s32[]{:S(2)}) async-start(), calls=%async_computation.13 | async-start | bytes 5898240 | tf_op jit(solution)/shard_map/all_gather | solution.py:633
  24.9 29.0 %collective-permute-start = (bf16[320,2048]{1,0:T(8,128)(2,1)S(1)}, bf16[320,2048]{1,0:T(8,128)(2,1)S(1)}, u32[]{:S(2)}, u32[]{:S(2)}) collective-permute-start(bf16[320,2048]{1,0:T(8,128)(2,1)S(1)} %copy-done.12), channel_id=1, source_target_pairs={{0,8},{8,0},{16,24},{24,16},{1,9},{9,1},{17,25},{25,17},{2,10},{10... | collective-permute-start | bytes 3932168 | tf_op jit(solution)/shard_map/ppermute | solution.py:602
  25.9 32.6 %collective-permute-start.2 = (bf16[320,2048]{1,0:T(8,128)(2,1)S(1)}, bf16[320,2048]{1,0:T(8,128)(2,1)}, u32[]{:S(2)}, u32[]{:S(2)}) collective-permute-start(bf16[320,2048]{1,0:T(8,128)(2,1)S(1)} %copy-done.12), channel_id=1, source_target_pairs={{0,16},{8,24},{16,0},{24,8},{1,17},{9,25},{17,1},{25,9},{2,18},{10... | collective-permute-start | bytes 3932168 | tf_op jit(solution)/shard_map/ppermute | solution.py:602
  28.1 39.4 %all-to-all-start.1 = ((bf16[8,80,384]{2,1,0:T(8,128)(2,1)}), bf16[8,80,384]{2,1,0:T(8,128)(2,1)S(1)}, u32[]{:S(2)}, u32[]{:S(2)}) async-start(bf16[8,80,384]{2,1,0:T(8,128)(2,1)} %broadcast_in_dim.22), calls=%async_computation.1 | async-start | bytes 983040 | tf_op jit(solution)/shard_map/all_to_all | solution.py:671
  54.9 18.6 %collective-permute-start.1 = (bf16[160,2048]{1,0:T(8,128)(2,1)}, bf16[160,2048]{1,0:T(8,128)(2,1)}, u32[]{:S(2)}, u32[]{:S(2)}) collective-permute-start(bf16[160,2048]{1,0:T(8,128)(2,1)} %slice.240), channel_id=1, source_target_pairs={{0,16},{8,24},{16,0},{24,8},{1,17},{9,25},{17,1},{25,9},{2,18},{10... | collective-permute-start | bytes 1966088 | tf_op jit(solution)/shard_map/ppermute | solution.py:602
  60.5 15.1 %collective-permute-start.3 = (bf16[160,2048]{1,0:T(8,128)(2,1)}, bf16[160,2048]{1,0:T(8,128)(2,1)}, u32[]{:S(2)}, u32[]{:S(2)}) collective-permute-start(bf16[160,2048]{1,0:T(8,128)(2,1)} %slice.241), channel_id=1, source_target_pairs={{0,8},{8,0},{16,24},{24,16},{1,9},{9,1},{17,25},{25,17},{2,10},{10... | collective-permute-start | bytes 1966088 | tf_op jit(solution)/shard_map/ppermute | solution.py:602
  68.2 14.4 %all-to-all-start.2 = ((bf16[32,2,64]{2,1,0:T(2,128)(2,1)}), bf16[32,2,64]{2,1,0:T(2,128)(2,1)S(1)}, u32[]{:S(2)}, u32[]{:S(2)}) async-start(bf16[32,2,64]{2,1,0:T(2,128)(2,1)} %broadcast_in_dim.23), calls=%async_computation.2 | async-start | bytes 32768 | tf_op jit(solution)/shard_map/all_to_all | solution.py:671
  73.3 105.4 %all-gather.6.cloned.1.call-start = ((), (), s32[]{:S(2)}) async-start(), calls=%async_computation.14 | async-start | bytes 10027008 | tf_op jit(solution)/shard_map/all_gather | solution.py:740
  93.6 33.8 %collective-permute-start.4 = (bf16[320,2048]{1,0:T(8,128)(2,1)}, bf16[320,2048]{1,0:T(8,128)(2,1)}, u32[]{:S(2)}, u32[]{:S(2)}) collective-permute-start(bf16[320,2048]{1,0:T(8,128)(2,1)} %multiply_convert_fusion.2), channel_id=1, source_target_pairs={{0,8},{8,0},{16,24},{24,16},{1,9},{9,1},{17,25},{25,17},{2,10},{10... | collective-permute-start | bytes 3932168 | tf_op jit(solution)/shard_map/ppermute | solution.py:602
  95.1 34.7 %collective-permute-start.6 = (bf16[320,2048]{1,0:T(8,128)(2,1)}, bf16[320,2048]{1,0:T(8,128)(2,1)}, u32[]{:S(2)}, u32[]{:S(2)}) collective-permute-start(bf16[320,2048]{1,0:T(8,128)(2,1)} %multiply_convert_fusion.2), channel_id=1, source_target_pairs={{0,16},{8,24},{16,0},{24,8},{1,17},{9,25},{17,1},{25,9},{2,18},{10... | collective-permute-start | bytes 3932168 | tf_op jit(solution)/shard_map/ppermute | solution.py:602
  129.1 16.3 %collective-permute-start.5 = (bf16[160,2048]{1,0:T(8,128)(2,1)S(1)}, bf16[160,2048]{1,0:T(8,128)(2,1)}, u32[]{:S(2)}, u32[]{:S(2)}) collective-permute-start(bf16[160,2048]{1,0:T(8,128)(2,1)S(1)} %slice.256), channel_id=1, source_target_pairs={{0,16},{8,24},{16,0},{24,8},{1,17},{9,25},{17,1},{25,9},{2,18},{10... | collective-permute-start | bytes 1966088 | tf_op jit(solution)/shard_map/ppermute | solution.py:602
  130.9 16.4 %collective-permute-start.7 = (bf16[160,2048]{1,0:T(8,128)(2,1)S(1)}, bf16[160,2048]{1,0:T(8,128)(2,1)}, u32[]{:S(2)}, u32[]{:S(2)}) collective-permute-start(bf16[160,2048]{1,0:T(8,128)(2,1)S(1)} %slice.257), channel_id=1, source_target_pairs={{0,8},{8,0},{16,24},{24,16},{1,9},{9,1},{17,25},{25,17},{2,10},{10... | collective-permute-start | bytes 1966088 | tf_op jit(solution)/shard_map/ppermute | solution.py:602
  149.0 21.9 %all-to-all-start.3 = ((bf16[4,64,3072]{2,1,0:T(8,128)(2,1)}), bf16[4,64,3072]{2,1,0:T(8,128)(2,1)S(1)}, u32[]{:S(2)}, u32[]{:S(2)}) async-start(bf16[4,64,3072]{2,1,0:T(8,128)(2,1)} %copy.101), calls=%async_computation.3 | async-start | bytes 3145728 | tf_op jit(solution)/shard_map/all_to_all | solution.py:630
  152.5 143.6 %all-gather.8.cloned.1.call-start = ((), (), s32[]{:S(2)}) async-start(), calls=%async_computation.15 | async-start | bytes 14155776 | tf_op jit(solution)/shard_map/all_gather | solution.py:633
  178.7 254.9 %reduce-scatter.6.cloned.1.call-start = ((), (), s32[]{:S(2)}) async-start(), calls=%async_computation.16 | async-start | bytes 3932160 | tf_op jit(solution)/shard_map/reduce_scatter | solution.py:656
  186.1 17.1 %collective-permute-start.8 = (bf16[160,2048]{1,0:T(8,128)(2,1)}, bf16[160,2048]{1,0:T(8,128)(2,1)S(1)}, u32[]{:S(2)}, u32[]{:S(2)}) collective-permute-start(bf16[160,2048]{1,0:T(8,128)(2,1)} %get-tuple-element.154), channel_id=1, source_target_pairs={{0,8},{8,0},{16,24},{24,16},{1,9},{9,1},{17,25},{25,17},{2,10},{10... | collective-permute-start | bytes 1966088 | tf_op jit(solution)/shard_map/ppermute | solution.py:602
  187.7 16.8 %collective-permute-start.9 = (bf16[160,2048]{1,0:T(8,128)(2,1)}, bf16[160,2048]{1,0:T(8,128)(2,1)S(1)}, u32[]{:S(2)}, u32[]{:S(2)}) collective-permute-start(bf16[160,2048]{1,0:T(8,128)(2,1)} %get-tuple-element.155), channel_id=1, source_target_pairs={{0,16},{8,24},{16,0},{24,8},{1,17},{9,25},{17,1},{25,9},{2,18},{10... | collective-permute-start | bytes 1966088 | tf_op jit(solution)/shard_map/ppermute | solution.py:602
  204.8 30.1 %collective-permute-start.10 = (bf16[320,2048]{1,0:T(8,128)(2,1)S(1)}, bf16[320,2048]{1,0:T(8,128)(2,1)}, u32[]{:S(2)}, u32[]{:S(2)}) collective-permute-start(bf16[320,2048]{1,0:T(8,128)(2,1)S(1)} %pad_maximum_fusion.2), channel_id=1, source_target_pairs={{0,8},{8,0},{16,24},{24,16},{1,9},{9,1},{17,25},{25,17},{2,10},{10... | collective-permute-start | bytes 3932168 | tf_op jit(solution)/shard_map/ppermute | solution.py:602
  205.7 29.9 %collective-permute-start.11 = (bf16[320,2048]{1,0:T(8,128)(2,1)S(1)}, bf16[320,2048]{1,0:T(8,128)(2,1)}, u32[]{:S(2)}, u32[]{:S(2)}) collective-permute-start(bf16[320,2048]{1,0:T(8,128)(2,1)S(1)} %pad_maximum_fusion.3), channel_id=1, source_target_pairs={{0,16},{8,24},{16,0},{24,8},{1,17},{9,25},{17,1},{25,9},{2,18},{10... | collective-permute-start | bytes 3932168 | tf_op jit(solution)/shard_map/ppermute | solution.py:602
  240.6 29.0 %collective-permute-start.12 = (bf16[320,2048]{1,0:T(8,128)(2,1)}, bf16[320,2048]{1,0:T(8,128)(2,1)}, u32[]{:S(2)}, u32[]{:S(2)}) collective-permute-start(bf16[320,2048]{1,0:T(8,128)(2,1)} %multiply_convert_fusion.1.refs_4_), channel_id=1, source_target_pairs={{0,8},{8,0},{16,24},{24,16},{1,9},{9,1},{17,25},{25,17},{2,10},{10... | collective-permute-start | bytes 3932168 | tf_op jit(solution)/shard_map/ppermute | solution.py:602
  242.0 30.3 %collective-permute-start.14 = (bf16[320,2048]{1,0:T(8,128)(2,1)}, bf16[320,2048]{1,0:T(8,128)(2,1)}, u32[]{:S(2)}, u32[]{:S(2)}) collective-permute-start(bf16[320,2048]{1,0:T(8,128)(2,1)} %multiply_convert_fusion.1.refs_4_), channel_id=1, source_target_pairs={{0,16},{8,24},{16,0},{24,8},{1,17},{9,25},{17,1},{25,9},{2,18},{10... | collective-permute-start | bytes 3932168 | tf_op jit(solution)/shard_map/ppermute | solution.py:602
  270.8 16.8 %collective-permute-start.13 = (bf16[160,2048]{1,0:T(8,128)(2,1)S(1)}, bf16[160,2048]{1,0:T(8,128)(2,1)S(1)}, u32[]{:S(2)}, u32[]{:S(2)}) collective-permute-start(bf16[160,2048]{1,0:T(8,128)(2,1)S(1)} %slice.259), channel_id=1, source_target_pairs={{0,16},{8,24},{16,0},{24,8},{1,17},{9,25},{17,1},{25,9},{2,18},{10... | collective-permute-start | bytes 1966088 | tf_op jit(solution)/shard_map/ppermute | solution.py:602
  273.4 14.1 %collective-permute-start.15 = (bf16[160,2048]{1,0:T(8,128)(2,1)S(1)}, bf16[160,2048]{1,0:T(8,128)(2,1)}, u32[]{:S(2)}, u32[]{:S(2)}) collective-permute-start(bf16[160,2048]{1,0:T(8,128)(2,1)S(1)} %slice.260), channel_id=1, source_target_pairs={{0,8},{8,0},{16,24},{24,16},{1,9},{9,1},{17,25},{25,17},{2,10},{10... | collective-permute-start | bytes 1966088 | tf_op jit(solution)/shard_map/ppermute | solution.py:602
  345.5 2.5 collective-permute-start.24
  345.7 3.4 collective-permute-start.25
  346.0 4.2 collective-permute-start.26
  346.2 5.1 collective-permute-start.27
  356.6 135.6 %reduce-scatter.8.cloned.1.call-start = ((), (), s32[]{:S(2)}) async-start(), calls=%async_computation.17 | async-start | bytes 3932160 | tf_op jit(solution)/shard_map/reduce_scatter | solution.py:656
  379.2 18.2 %collective-permute-start.16 = (bf16[160,2048]{1,0:T(8,128)(2,1)}, bf16[160,2048]{1,0:T(8,128)(2,1)S(1)}, u32[]{:S(2)}, u32[]{:S(2)}) collective-permute-start(bf16[160,2048]{1,0:T(8,128)(2,1)} %get-tuple-element.173), channel_id=1, source_target_pairs={{0,8},{8,0},{16,24},{24,16},{1,9},{9,1},{17,25},{25,17},{2,10},{10... | collective-permute-start | bytes 1966088 | tf_op jit(solution)/shard_map/ppermute | solution.py:602
  380.6 16.8 %collective-permute-start.17 = (bf16[160,2048]{1,0:T(8,128)(2,1)}, bf16[160,2048]{1,0:T(8,128)(2,1)S(1)}, u32[]{:S(2)}, u32[]{:S(2)}) collective-permute-start(bf16[160,2048]{1,0:T(8,128)(2,1)} %get-tuple-element.174), channel_id=1, source_target_pairs={{0,16},{8,24},{16,0},{24,8},{1,17},{9,25},{17,1},{25,9},{2,18},{10... | collective-permute-start | bytes 1966088 | tf_op jit(solution)/shard_map/ppermute | solution.py:602
  397.3 3.4 collective-permute-start.20
  397.7 31.4 %collective-permute-start.18 = (bf16[320,2048]{1,0:T(8,128)(2,1)S(1)}, bf16[320,2048]{1,0:T(8,128)(2,1)}, u32[]{:S(2)}, u32[]{:S(2)}) collective-permute-start(bf16[320,2048]{1,0:T(8,128)(2,1)S(1)} %pad_maximum_fusion.4), channel_id=1, source_target_pairs={{0,8},{8,0},{16,24},{24,16},{1,9},{9,1},{17,25},{25,17},{2,10},{10... | collective-permute-start | bytes 3932168 | tf_op jit(solution)/shard_map/ppermute | solution.py:602
  398.7 31.1 %collective-permute-start.19 = (bf16[320,2048]{1,0:T(8,128)(2,1)S(1)}, bf16[320,2048]{1,0:T(8,128)(2,1)}, u32[]{:S(2)}, u32[]{:S(2)}) collective-permute-start(bf16[320,2048]{1,0:T(8,128)(2,1)S(1)} %pad_maximum_fusion.5), channel_id=1, source_target_pairs={{0,16},{8,24},{16,0},{24,8},{1,17},{9,25},{17,1},{25,9},{2,18},{10... | collective-permute-start | bytes 3932168 | tf_op jit(solution)/shard_map/ppermute | solution.py:602
  400.2 2.3 collective-permute-start.21
  400.2 3.4 collective-permute-start.22
  400.7 4.0 collective-permute-start.23
  437.3 30.1 %collective-permute-start.28 = (bf16[320,2048]{1,0:T(8,128)(2,1)S(1)}, bf16[320,2048]{1,0:T(8,128)(2,1)S(1)}, u32[]{:S(2)}, u32[]{:S(2)}) collective-permute-start(bf16[320,2048]{1,0:T(8,128)(2,1)S(1)} %fusion.29.refs_4_), channel_id=1, source_target_pairs={{0,8},{8,0},{16,24},{24,16},{1,9},{9,1},{17,25},{25,17},{2,10},{10... | collective-permute-start | bytes 3932168 | tf_op jit(solution)/shard_map/ppermute | solution.py:602
  438.9 30.7 %collective-permute-start.30 = (bf16[320,2048]{1,0:T(8,128)(2,1)S(1)}, bf16[320,2048]{1,0:T(8,128)(2,1)S(1)}, u32[]{:S(2)}, u32[]{:S(2)}) collective-permute-start(bf16[320,2048]{1,0:T(8,128)(2,1)S(1)} %fusion.29.refs_4_), channel_id=1, source_target_pairs={{0,16},{8,24},{16,0},{24,8},{1,17},{9,25},{17,1},{25,9},{2,18},{10... | collective-permute-start | bytes 3932168 | tf_op jit(solution)/shard_map/ppermute | solution.py:602
  454.6 15.1 %collective-permute-start.32 = (bf16[1,4,64,1536]{3,2,1,0:T(8,128)(2,1)}, bf16[1,4,64,1536]{3,2,1,0:T(8,128)(2,1)S(1)}, u32[]{:S(2)}, u32[]{:S(2)}) collective-permute-start(bf16[1,4,64,1536]{3,2,1,0:T(8,128)(2,1)} %get-tuple-element.199), channel_id=1, source_target_pairs={{0,4},{4,0},{1,5},{5,1},{2,6},{6,2},{3,7},{7,3},{8,12},{12,8},{9,1... | collective-permute-start | bytes 2359304 | tf_op jit(solution)/shard_map/ppermute | solution.py:643
  454.7 29.0 %collective-permute-start.33 = (bf16[1,4,64,1536]{3,2,1,0:T(8,128)(2,1)}, bf16[1,4,64,1536]{3,2,1,0:T(8,128)(2,1)S(1)}, u32[]{:S(2)}, u32[]{:S(2)}) collective-permute-start(bf16[1,4,64,1536]{3,2,1,0:T(8,128)(2,1)} %get-tuple-element.200), channel_id=1, source_target_pairs={{0,4},{4,0},{1,5},{5,1},{2,6},{6,2},{3,7},{7,3},{8,12},{12,8},{9,1... | collective-permute-start | bytes 2359304 | tf_op jit(solution)/shard_map/ppermute | solution.py:643
  455.2 28.5 %collective-permute-start.34 = (bf16[1,4,64,1536]{3,2,1,0:T(8,128)(2,1)}, bf16[1,4,64,1536]{3,2,1,0:T(8,128)(2,1)S(1)}, u32[]{:S(2)}, u32[]{:S(2)}) collective-permute-start(bf16[1,4,64,1536]{3,2,1,0:T(8,128)(2,1)} %get-tuple-element.201), channel_id=1, source_target_pairs={{0,4},{4,0},{1,5},{5,1},{2,6},{6,2},{3,7},{7,3},{8,12},{12,8},{9,1... | collective-permute-start | bytes 2359304 | tf_op jit(solution)/shard_map/ppermute | solution.py:643
  467.4 16.3 %collective-permute-start.35 = (bf16[1,4,64,1536]{3,2,1,0:T(8,128)(2,1)}, bf16[1,4,64,1536]{3,2,1,0:T(8,128)(2,1)S(1)}, u32[]{:S(2)}, u32[]{:S(2)}) collective-permute-start(bf16[1,4,64,1536]{3,2,1,0:T(8,128)(2,1)} %get-tuple-element.202), channel_id=1, source_target_pairs={{0,4},{4,0},{1,5},{5,1},{2,6},{6,2},{3,7},{7,3},{8,12},{12,8},{9,1... | collective-permute-start | bytes 2359304 | tf_op jit(solution)/shard_map/ppermute | solution.py:643
  469.6 22.6 %collective-permute-start.29 = (bf16[160,2048]{1,0:T(8,128)(2,1)}, bf16[160,2048]{1,0:T(8,128)(2,1)}, u32[]{:S(2)}, u32[]{:S(2)}) collective-permute-start(bf16[160,2048]{1,0:T(8,128)(2,1)} %slice.261), channel_id=1, source_target_pairs={{0,16},{8,24},{16,0},{24,8},{1,17},{9,25},{17,1},{25,9},{2,18},{10... | collective-permute-start | bytes 1966088 | tf_op jit(solution)/shard_map/ppermute | solution.py:602
  469.7 22.5 %collective-permute-start.31 = (bf16[160,2048]{1,0:T(8,128)(2,1)S(1)}, bf16[160,2048]{1,0:T(8,128)(2,1)}, u32[]{:S(2)}, u32[]{:S(2)}) collective-permute-start(bf16[160,2048]{1,0:T(8,128)(2,1)S(1)} %slice.262), channel_id=1, source_target_pairs={{0,8},{8,0},{16,24},{24,16},{1,9},{9,1},{17,25},{25,17},{2,10},{10... | collective-permute-start | bytes 1966088 | tf_op jit(solution)/shard_map/ppermute | solution.py:602
  492.2 20.3 %collective-permute-start.36 = (bf16[160,2048]{1,0:T(8,128)(2,1)}, bf16[160,2048]{1,0:T(8,128)(2,1)}, u32[]{:S(2)}, u32[]{:S(2)}) collective-permute-start(bf16[160,2048]{1,0:T(8,128)(2,1)} %get-tuple-element.210), channel_id=1, source_target_pairs={{0,8},{8,0},{16,24},{24,16},{1,9},{9,1},{17,25},{25,17},{2,10},{10... | collective-permute-start | bytes 1966088 | tf_op jit(solution)/shard_map/ppermute | solution.py:602
  492.9 21.7 %collective-permute-start.37 = (bf16[160,2048]{1,0:T(8,128)(2,1)}, bf16[160,2048]{1,0:T(8,128)(2,1)}, u32[]{:S(2)}, u32[]{:S(2)}) collective-permute-start(bf16[160,2048]{1,0:T(8,128)(2,1)} %get-tuple-element.211), channel_id=1, source_target_pairs={{0,16},{8,24},{16,0},{24,8},{1,17},{9,25},{17,1},{25,9},{2,18},{10... | collective-permute-start | bytes 1966088 | tf_op jit(solution)/shard_map/ppermute | solution.py:602
  497.5 61.3 %all-to-all-start.4 = ((bf16[4,64,1,1536]{3,1,2,0:T(8,128)(2,1)}), bf16[4,64,1,1536]{3,1,2,0:T(8,128)(2,1)S(1)}, u32[]{:S(2)}, u32[]{:S(2)}) async-start(bf16[4,64,1,1536]{3,1,2,0:T(8,128)(2,1)} %bitcast.154), calls=%async_computation.6 | async-start | bytes 1572864 | tf_op jit(solution)/shard_map/all_to_all | solution.py:659
  501.0 150.4 %reduce-scatter.12.cloned.1.call-start = ((), (), s32[]{:S(2)}) async-start(), calls=%async_computation.19 | async-start | bytes 3932160 | tf_op jit(solution)/shard_map/reduce_scatter | solution.py:656
  501.6 154.2 %reduce-scatter.10.cloned.1.call-start = ((), (), s32[]{:S(2)}) async-start(), calls=%async_computation.18 | async-start | bytes 3276800 | tf_op jit(solution)/shard_map/reduce_scatter | solution.py:656
  519.5 39.3 %collective-permute-start.38 = (bf16[320,2048]{1,0:T(8,128)(2,1)}, bf16[320,2048]{1,0:T(8,128)(2,1)S(1)}, u32[]{:S(2)}, u32[]{:S(2)}) collective-permute-start(bf16[320,2048]{1,0:T(8,128)(2,1)} %pad_maximum_fusion.6), channel_id=1, source_target_pairs={{0,8},{8,0},{16,24},{24,16},{1,9},{9,1},{17,25},{25,17},{2,10},{10... | collective-permute-start | bytes 3932168 | tf_op jit(solution)/shard_map/ppermute | solution.py:602
  519.5 39.4 %collective-permute-start.39 = (bf16[320,2048]{1,0:T(8,128)(2,1)}, bf16[320,2048]{1,0:T(8,128)(2,1)S(1)}, u32[]{:S(2)}, u32[]{:S(2)}) collective-permute-start(bf16[320,2048]{1,0:T(8,128)(2,1)} %pad_maximum_fusion.7), channel_id=1, source_target_pairs={{0,16},{8,24},{16,0},{24,8},{1,17},{9,25},{17,1},{25,9},{2,18},{10... | collective-permute-start | bytes 3932168 | tf_op jit(solution)/shard_map/ppermute | solution.py:602
  573.3 16.4 %collective-permute-start.44 = (bf16[160,2048]{1,0:T(8,128)(2,1)}, bf16[160,2048]{1,0:T(8,128)(2,1)}, u32[]{:S(2)}, u32[]{:S(2)}) collective-permute-start(bf16[160,2048]{1,0:T(8,128)(2,1)} %get-tuple-element.237), channel_id=1, source_target_pairs={{0,8},{8,0},{16,24},{24,16},{1,9},{9,1},{17,25},{25,17},{2,10},{10... | collective-permute-start | bytes 1966088 | tf_op jit(solution)/shard_map/ppermute | solution.py:602
  575.5 16.5 %collective-permute-start.45 = (bf16[160,2048]{1,0:T(8,128)(2,1)}, bf16[160,2048]{1,0:T(8,128)(2,1)S(1)}, u32[]{:S(2)}, u32[]{:S(2)}) collective-permute-start(bf16[160,2048]{1,0:T(8,128)(2,1)} %get-tuple-element.238), channel_id=1, source_target_pairs={{0,16},{8,24},{16,0},{24,8},{1,17},{9,25},{17,1},{25,9},{2,18},{10... | collective-permute-start | bytes 1966088 | tf_op jit(solution)/shard_map/ppermute | solution.py:602
  589.2 2.8 collective-permute-start.40
  589.2 3.4 collective-permute-start.41
  589.7 3.8 collective-permute-start.42
  589.8 4.7 collective-permute-start.43
  604.6 97.6 %reduce-scatter.14.cloned.1.call-start = ((), (), s32[]{:S(2)}) async-start(), calls=%async_computation.20 | async-start | bytes 1945600 | tf_op jit(solution)/shard_map/reduce_scatter | solution.py:656
  612.9 31.1 %collective-permute-start.46 = (bf16[320,2048]{1,0:T(8,128)(2,1)}, bf16[320,2048]{1,0:T(8,128)(2,1)}, u32[]{:S(2)}, u32[]{:S(2)}) collective-permute-start(bf16[320,2048]{1,0:T(8,128)(2,1)} %pad_maximum_fusion.8), channel_id=1, source_target_pairs={{0,8},{8,0},{16,24},{24,16},{1,9},{9,1},{17,25},{25,17},{2,10},{10... | collective-permute-start | bytes 3932168 | tf_op jit(solution)/shard_map/ppermute | solution.py:602
  613.0 31.1 %collective-permute-start.47 = (bf16[320,2048]{1,0:T(8,128)(2,1)}, bf16[320,2048]{1,0:T(8,128)(2,1)}, u32[]{:S(2)}, u32[]{:S(2)}) collective-permute-start(bf16[320,2048]{1,0:T(8,128)(2,1)} %pad_maximum_fusion.9), channel_id=1, source_target_pairs={{0,16},{8,24},{16,0},{24,8},{1,17},{9,25},{17,1},{25,9},{2,18},{10... | collective-permute-start | bytes 3932168 | tf_op jit(solution)/shard_map/ppermute | solution.py:602
  622.6 25.8 %collective-permute-start.48 = (bf16[4,80,2432]{2,1,0:T(8,128)(2,1)}, bf16[4,80,2432]{2,1,0:T(8,128)(2,1)}, u32[]{:S(2)}, u32[]{:S(2)}) collective-permute-start(bf16[4,80,2432]{2,1,0:T(8,128)(2,1)} %dynamic-slice_bitcast_fusion), channel_id=1, source_target_pairs={{0,4},{4,0},{1,5},{5,1},{2,6},{6,2},{3,7},{7,3},{8,12},{12,8},{9,1... | collective-permute-start | bytes 4669448 | tf_op jit(solution)/shard_map/ppermute | solution.py:652
  659.0 11.4 %all-to-all-start.5 = ((f32[32,1,128]{2,1,0:T(1,128)}), f32[32,1,128]{2,1,0:T(1,128)S(1)}, u32[]{:S(2)}, u32[]{:S(2)}) async-start(f32[32,1,128]{2,1,0:T(1,128)} %reshape.272), calls=%async_computation.9 | async-start | bytes 32768 | tf_op jit(solution)/shard_map/all_to_all | solution.py:852
  670.4 13.1 %all-to-all-start.6 = ((bf16[4,64,1,1280]{3,1,2,0:T(8,128)(2,1)}), bf16[4,64,1,1280]{3,1,2,0:T(8,128)(2,1)S(1)}, u32[]{:S(2)}, u32[]{:S(2)}) async-start(bf16[4,64,1,1280]{3,1,2,0:T(8,128)(2,1)} %bitcast.47), calls=%async_computation.10 | async-start | bytes 1310720 | tf_op jit(solution)/shard_map/all_to_all | solution.py:659
  684.4 15.1 %all-to-all-start.7 = ((bf16[4,64,1,1536]{3,1,2,0:T(8,128)(2,1)}), bf16[4,64,1,1536]{3,1,2,0:T(8,128)(2,1)S(1)}, u32[]{:S(2)}, u32[]{:S(2)}) async-start(bf16[4,64,1,1536]{3,1,2,0:T(8,128)(2,1)} %bitcast.153), calls=%async_computation.12 | async-start | bytes 1572864 | tf_op jit(solution)/shard_map/all_to_all | solution.py:659
  (80 other events, 982.6 us)
Sparse Core Ops, SparseCore 0:
  25.0 66.4 all-gather.3
  93.7 84.9 all-gather.5
  180.9 115.2 all-gather.7
  356.8 58.4 reduce-scatter.5
  433.7 57.6 reduce-scatter.7
  503.8 60.2 reduce-scatter.11
  604.7 51.0 reduce-scatter.9
  658.1 35.0 reduce-scatter.13

commit v6 on v5

--- a/solution.py
+++ b/solution.py
@@ -553,7 +553,7 @@
 
 def add_pieces(mine, others):
     narrow, groups, rows, columns = mine.shape
-    block = column_block(columns, 1024)
+    block = column_block(columns, 2048 if groups > 1 else 512)
     place = pl.BlockSpec((narrow, 1, rows, block), lambda g, j: (0, g, 0, j))
     return pl.pallas_call(
         add_pieces_kernel,
@@ -820,9 +820,11 @@
 
         low_branch, mgate_out, result_one, result_two = fence(low_branch, mgate_out, result_one, result_two)
         result = merged + scatter_sum(own, result_one, result_two)
-        mine, finish = grad_shares(normed1, (d_gate, low_branch), rows, PLANE)
-        rec_sum = sum_narrow(finish(mine))
         *parts1, grad_gain1 = back_parts((d_gate, low_branch), w_rec, (tokens_all, inverse_all))
+        *parts1, late_gate = fence(*parts1, d_gate)
+        mine, finish = grad_shares(normed1, (late_gate, low_branch), rows, PLANE)
+        grad_rec = finish(mine)
+        rec_sum = sum_narrow(grad_rec)
         one, two, own = scatter_start(parts1)
         one, two, late_mixed, late_rate, late_input = fence(one, two, mixed, d_rate, d_input)
         d_normed1 = scatter_finish(one, two, own)
@@ -843,12 +845,12 @@
         )
         table_grad = jnp.pad(table_grad, ((0, -places[-1] % LANES), (0, 0))).T.astype(bf16)
         last = sum_rest(rows_cut(jnp.concatenate([grad_out, table_grad], axis=1)))
-        rec_sum, d_normed1, last, gain_grads, mup_sum = fence(rec_sum, d_normed1, last, gain_grads, mup_sum)
+        mup_out = columns_home(mup_sum, rows)
+        rec_sum, d_normed1, last, gain_grads, mup_out = fence(rec_sum, d_normed1, last, gain_grads, mup_out)
         last = sum_narrow(last).astype(f32)
         out_out, table_out = last[:, :width], last[:, width:].T
 
         rec_out = columns_home(rec_sum, rows)
-        mup_out = columns_home(mup_sum, rows)
         gain_out = lax.all_to_all(gain_grads, ("wide",) + spread, 0, 0, tiled=False).sum(axis=0)
         block_out = (result * live).astype(bf16)
         own = tokens.astype(f32)

time: 721 us -> 717 us (level)
  other arithmetic: 66.9 us -> 78.4 us
    convert_element_type x1, other arithmetic: 1.51 us -> 13.5 us  [on_device(): conv = conv.astype(bf16)]
    all_gather x1, waiting for transfers between devices: 7.78 us -> 0.01 us  [on_device(): lax.all_gather(after(jnp.concatenate([out_proj, mlp_down], axis=0), w_rec...]
    unnamed x174 -> x173, local copies, waits for them, and re-layouts: 26.6 us -> 25.3 us
  transfers between devices with their start and end apart: 64 -> 64, of which waited for: 31 -> 30; matrix products, arithmetic and copies ran while one was open for 23% -> 24% of each run, Pallas kernels for 25% -> 25%
where the time goes in v6:
time: 717 us; the launch traced here: 711 us
  Pallas kernels  229 us (32%)
  waiting for transfers between devices  197 us (27%)
  local copies, waits for them, and re-layouts  81.2 us (11%)
  other arithmetic  78.4 us (11%)
  starting transfers between devices  65 us (9%)
  matrix products  28.6 us (4%)
  between operations  16.3 us (2%)
  blocking collectives  15 us (2%)
    ppermute x32, waiting for transfers between devices, swap(): return lax.ppermute(values, 'wide', [(i, i ^ mask) for i in range(PLANE)])  148 us
    pallas_call x4, Pallas kernels, weight_grad(): pl.pallas_call(functools.partial(weight_grad_kernel, rows, len(rights), s...  58.5 us
    pallas_call x2, Pallas kernels, back_parts(): pl.pallas_call(functools.partial(back_kernel, len(grads), summed is not N...  36.9 us
    pallas_call x1, Pallas kernels, mlp_both(): pl.pallas_call(functools.partial(mlp_kernel, PLANE), grid=(steps,), out_s...  35 us
    ppermute x32, starting transfers between devices, swap(): return lax.ppermute(values, 'wide', [(i, i ^ mask) for i in range(PLANE)])  31.6 us
    unnamed x173, local copies, waits for them, and re-layouts  25.3 us
    pallas_call x1, Pallas kernels, lru_backward(): pl.pallas_call(functools.partial(lru_backward_kernel, seqs), grid=(pl.cdi...  21.1 us
    pallas_call x4, Pallas kernels, add_pieces(): pl.pallas_call(add_pieces_kernel, grid=(groups, columns // block), out_sh...  20.3 us
  transfers between devices with their start and end apart: 64, of which 30 were waited for; matrix products, arithmetic and copies ran while one was open for 24% of the time, Pallas kernels for 25%

profile of v6, /device:TPU:0, one launch (start us, length us, event | category | flops | bytes accessed | tf_op | source)
XLA Modules:
  0.0 711.1 jit_solution(12701512532724787145)
XLA Ops:
  9.9 15.0 %all_to_all.70 = bf16[4,64,1280]{2,1,0:T(8,128)(2,1)} all-to-all(bf16[4,64,1280]{2,1,0:T(8,128)(2,1)S(1)} %copy.97), channel_id=1, replica_groups=mesh['wide'=4,'rest'=2,'narrow'=4] {'wide'}, dimensions={0} | all-to-all | bytes 1310720 | tf_op jit(solution)/shard_map/all_to_all | solution.py:630
  28.1 4.9 all-to-all-start.1
  33.0 21.0 %collective-permute-done = bf16[320,2048]{1,0:T(8,128)(2,1)S(1)} collective-permute-done((bf16[320,2048]{1,0:T(8,128)(2,1)S(1)}, bf16[320,2048]{1,0:T(8,128)(2,1)S(1)}, u32[]{:S(2)}, u32[]{:S(2)}) %collective-permute-start) | collective-permute-done | bytes 1310752 | tf_op jit(solution)/shard_map/ppermute | solution.py:602
  56.2 2.3 pad_maximum_fusion.10
  61.0 2.3 reshape.210
  63.4 2.3 reshape.211
  68.2 5.1 all-to-all-start.2
  78.9 2.7 constant_dynamic-update-slice_fusion.1
  82.7 8.8 %all-gather.4.cloned.1.call-done = bf16[2048,1280]{1,0:T(8,128)(2,1)} async-done(((bf16[256,1280]{1,0:T(8,128)(2,1)}), bf16[2048,1280]{1,0:T(8,128)(2,1)}) %all-gather.4.cloned.1.call-update) | async-done | bytes 5242896 | tf_op jit(solution)/shard_map/all_gather | solution.py:633
  96.7 5.9 copy.100
  102.9 3.8 fusion
  106.8 3.9 fusion.2.left_ref
  110.8 4.3 fusion.15.branch_ref
  115.0 2.7 pad_slice_fusion.2
  117.8 7.9 %fusion.13.gate_ref = f32[1280,640]{1,0:T(8,128)} fusion(bf16[1280,2048]{1,0:T(8,128)(2,1)S(1)} %fusion.2.left_ref, bf16[2048,1280]{1,0:T(8,128)(2,1)} %bitcast.131), kind=kOutput, calls=%fused_computation.30 | convolution fusion | flops 3355443200 | bytes 11141120 | tf_op jit(solution)/shard_map/dot_general | solution.py:20
  125.9 13.5 %fusion.5.conv_ref = bf16[1280,640]{1,0:T(8,128)(2,1)S(1)} fusion(f32[4,320,640]{2,1,0:T(8,128)S(1)} %get-tuple-element.379, f32[4,320,640]{2,1,0:T(8,128)S(1)} %copy-done.15, f32[4,320,640]{2,1,0:T(8,128)S(1)} %get-tuple-element.378, f32[1280,640]{1,0:T(8,128)S(1)} %fusion.15.branch_ref, f32[640]{0:T(1024)S(1)} %get-tuple-element.371, ...), kind=kLoop, calls=%fused_computation.17 | loop fusion | flops 7372800 | bytes 14758400 | tf_op jit(solution)/shard_map/convert_element_type | solution.py:768
  143.7 3.7 convolution_add_fusion.input_ref
  147.4 3.6 convolution_add_fusion.1.rate_ref
  150.9 6.4 collective-permute-done.5
  160.9 3.6 all-to-all-start.3
  164.6 14.7 %lru_forward.1 = (f32[1280,640]{1,0:T(8,128)}, bf16[1280,640]{1,0:T(8,128)(2,1)S(1)}) custom-call(bf16[1280,640]{1,0:T(8,128)(2,1)S(1)} %fusion.5.conv_ref, f32[1280,640]{1,0:T(8,128)} %convolution_add_fusion.1.rate_ref, f32[1280,640]{1,0:T(8,128)} %convolution_add_fusion.input_ref, f32[1280,640]{1,0:T(8,128)} %fusion.13.gate_ref, ...), custom_call_target="tpu_custom_call" | custom-call | flops 16384000000 | bytes 16384000 | tf_op jit(solution)/shard_map/lru_forward/pallas_call | solution.py:198
  180.5 2.4 all-to-all-done.3
  184.1 7.5 %out_parts.2 = (bf16[160,2048]{1,0:T(8,128)(2,1)}, bf16[160,2048]{1,0:T(8,128)(2,1)}, bf16[320,2048]{1,0:T(8,128)(2,1)}, bf16[320,2048]{1,0:T(8,128)(2,1)}, bf16[320,2048]{1,0:T(8,128)(2,1)}) custom-call(bf16[1280,640]{1,0:T(8,128)(2,1)} %copy-done.2, bf16[8,272,2048]{2,1,0:T(8,128)(2,1)} %bitcast.115), custom_call_target="tpu_custom_call" | custom-call | flops 3355443200 | bytes 9502720 | tf_op jit(solution)/shard_map/out_parts/pallas_call | solution.py:466
  195.8 11.6 %collective-permute-done.8 = bf16[160,2048]{1,0:T(8,128)(2,1)S(1)} collective-permute-done((bf16[160,2048]{1,0:T(8,128)(2,1)}, bf16[160,2048]{1,0:T(8,128)(2,1)S(1)}, u32[]{:S(2)}, u32[]{:S(2)}) %collective-permute-start.8) | collective-permute-done | bytes 655392 | tf_op jit(solution)/shard_map/ppermute | solution.py:602
  210.2 26.4 %collective-permute-done.10 = bf16[320,2048]{1,0:T(8,128)(2,1)} collective-permute-done((bf16[320,2048]{1,0:T(8,128)(2,1)S(1)}, bf16[320,2048]{1,0:T(8,128)(2,1)}, u32[]{:S(2)}, u32[]{:S(2)}) %collective-permute-start.10) | collective-permute-done | bytes 1310752 | tf_op jit(solution)/shard_map/ppermute | solution.py:602
  238.2 3.4 multiply_reduce_fusion.2
  246.3 24.5 %collective-permute-done.12.refs_2_ = bf16[320,2048]{1,0:T(8,128)(2,1)} collective-permute-done((bf16[320,2048]{1,0:T(8,128)(2,1)}, bf16[320,2048]{1,0:T(8,128)(2,1)}, u32[]{:S(2)}, u32[]{:S(2)}) %collective-permute-start.12) | collective-permute-done | bytes 1310752 | tf_op jit(solution)/shard_map/ppermute | solution.py:602
  279.2 8.5 %slice.209 = bf16[8,192,2048]{2,1,0:T(8,128)(2,1)} slice(bf16[8,272,2048]{2,1,0:T(8,128)(2,1)} %bitcast.116), slice={[0:8], [80:272], [0:2048]} | slice | bytes 12582912 | tf_op jit(solution)/shard_map/slice | solution.py:778
  287.7 10.4 %all-gather.8.cloned.1.call-done = bf16[2048,3072]{1,0:T(8,128)(2,1)} async-done(((bf16[256,3072]{1,0:T(8,128)(2,1)}), bf16[2048,3072]{1,0:T(8,128)(2,1)}) %all-gather.8.cloned.1.call-update) | async-done | bytes 12582928 | tf_op jit(solution)/shard_map/all_gather | solution.py:633
  298.2 35.0 %mlp_both.1 = (bf16[1280,1536]{1,0:T(8,128)(2,1)}, bf16[1280,1536]{1,0:T(8,128)(2,1)}, bf16[1280,1536]{1,0:T(8,128)(2,1)}, bf16[1280,2048]{1,0:T(8,128)(2,1)}) custom-call(bf16[160,2048]{1,0:T(8,128)(2,1)} %copy-done.75, bf16[160,2048]{1,0:T(8,128)(2,1)} %collective-permute-done.15.refs_1_, bf16[320,2048]{1,0:T(8,128)(2,1)} %collective-permute-done.12.refs_2_, ...), custom_call_target="tpu_custom_call" | custom-call | flops 24159191040 | bytes 34603008 | tf_op jit(solution)/shard_map/mlp_both/pallas_call | solution.py:282
  333.1 14.4 %weight_grad.4 = (bf16[4,1,192,2048]{3,2,1,0:T(8,128)(2,1)}, bf16[1,1,192,2048]{3,2,1,0:T(8,128)(2,1)}, bf16[1,1,192,2048]{3,2,1,0:T(8,128)(2,1)}, bf16[1,1,192,...) custom-call(s32[1]{0:T(128)} %bitcast.24.me_ref, bf16[1280,1536]{1,0:T(8,128)(2,1)} %get-tuple-element.196.left_ref.values_ref, ...), custom_call_target="tpu_custom_call" | custom-call | flops 8053063680 | bytes 15466496 | tf_op jit(solution)/shard_map/weight_grad/pallas_call | solution.py:526
  354.3 5.2 add_pieces.5
  360.0 22.5 %back_parts.2 = (bf16[160,2048]{1,0:T(8,128)(2,1)}, bf16[160,2048]{1,0:T(8,128)(2,1)}, bf16[320,2048]{1,0:T(8,128)(2,1)}, bf16[320,2048]{1,0:T(8,128)(2,1)}, bf16[320,2048]{1,0:T(8,128)(2,1)}) custom-call(bf16[1280,1536]{1,0:T(8,128)(2,1)} %get-tuple-element.175.refs_0_, bf16[1280,1536]{1,0:T(8,128)(2,1)} %get-tuple-element.203.refs_1_.refs_0_, ...), custom_call_target="tpu_custom_call" | custom-call | flops 16106127360 | bytes 25690112 | tf_op jit(solution)/shard_map/back_parts/pallas_call | solution.py:394
  385.2 15.2 %weight_grad.5 = (bf16[4,4,64,1536]{3,2,1,0:T(8,128)(2,1)}, bf16[1,4,64,1536]{3,2,1,0:T(8,128)(2,1)}, bf16[1,4,64,1536]{3,2,1,0:T(8,128)(2,1)}, bf16[1,4,64,1536]{3,2,1,0:T(8,128)(2,1)}, bf16[1,4,64,1536]{3,2,1,0:T(8,128)(2,1)}) custom-call(s32[1]{0:T(128)} %bitcast.24.me_ref, bf16[1280,2048]{1,0:T(8,128)(2,1)} %get-tuple-element.184.left_ref, ...), custom_call_target="tpu_custom_call" | custom-call | flops 8053063680 | bytes 19398656 | tf_op jit(solution)/shard_map/weight_grad/pallas_call | solution.py:526
  408.7 5.2 add_pieces.4
  414.0 18.2 %collective-permute-done.18 = bf16[320,2048]{1,0:T(8,128)(2,1)} collective-permute-done((bf16[320,2048]{1,0:T(8,128)(2,1)S(1)}, bf16[320,2048]{1,0:T(8,128)(2,1)}, u32[]{:S(2)}, u32[]{:S(2)}) %collective-permute-start.18) | collective-permute-done | bytes 1310752 | tf_op jit(solution)/shard_map/ppermute | solution.py:602
  432.8 3.9 convert_add_fusion.3
  436.8 2.7 multiply_reduce_fusion
  442.5 15.2 %weight_grad.6 = (bf16[4,4,64,1536]{3,2,1,0:T(8,128)(2,1)}, bf16[1,4,64,1536]{3,2,1,0:T(8,128)(2,1)}, bf16[1,4,64,1536]{3,2,1,0:T(8,128)(2,1)}, bf16[1,4,64,1536]{3,2,1,0:T(8,128)(2,1)}, bf16[1,4,64,1536]{3,2,1,0:T(8,128)(2,1)}) custom-call(s32[1]{0:T(128)} %bitcast.24.me_ref, bf16[1280,2048]{1,0:T(8,128)(2,1)} %get-tuple-element.184.left_ref, ...), custom_call_target="tpu_custom_call" | custom-call | flops 8053063680 | bytes 19398656 | tf_op jit(solution)/shard_map/weight_grad/pallas_call | solution.py:526
  458.3 12.1 %collective-permute-done.28.refs_2_ = bf16[320,2048]{1,0:T(8,128)(2,1)S(1)} collective-permute-done((bf16[320,2048]{1,0:T(8,128)(2,1)S(1)}, bf16[320,2048]{1,0:T(8,128)(2,1)S(1)}, u32[]{:S(2)}, u32[]{:S(2)}) %collective-permute-start.28) | collective-permute-done | bytes 1310752 | tf_op jit(solution)/shard_map/ppermute | solution.py:602
  474.4 12.3 %out_parts.3 = (bf16[160,2048]{1,0:T(8,128)(2,1)}, bf16[160,2048]{1,0:T(8,128)(2,1)}, bf16[320,2048]{1,0:T(8,128)(2,1)}, bf16[320,2048]{1,0:T(8,128)(2,1)}, bf16[320,2048]{1,0:T(8,128)(2,1)}) custom-call(bf16[1280,1536]{1,0:T(8,128)(2,1)} %get-tuple-element.196.left_ref.values_ref, bf16[1,1536,2048]{2,1,0:T(8,128)(2,1)} %bitcast.126), custom_call_target="tpu_custom_call" | custom-call | flops 8053063680 | bytes 15466496 | tf_op jit(solution)/shard_map/out_parts/pallas_call | solution.py:466
  488.1 5.2 add_pieces.6
  497.4 2.5 fusion.17
  500.1 3.5 all-to-all-start.4
  504.2 10.9 %mixed_grad.1 = (f32[1280,640]{1,0:T(8,128)}, bf16[1280,2048]{1,0:T(8,128)(2,1)}) custom-call(bf16[160,2048]{1,0:T(8,128)(2,1)} %collective-permute-done.29.refs_0_, bf16[160,2048]{1,0:T(8,128)(2,1)} %collective-permute-done.31.refs_1_, bf16[320,2048]{1,0:T(8,128)(2,1)} %copy-done.24, bf16[320,2048]{1,0:T(8,128)(2,1)} %copy-done.25, ...), custom_call_target="tpu_custom_call" | custom-call | flops 3355443200 | bytes 16384000 | tf_op jit(solution)/shard_map/mixed_grad/pallas_call | solution.py:322
  515.1 3.0 collective-permute-done.37
  524.6 21.1 %lru_backward.1 = (f32[1280,640]{1,0:T(8,128)}, bf16[1280,640]{1,0:T(8,128)(2,1)S(1)}, bf16[1280,640]{1,0:T(8,128)(2,1)S(1)}, bf16[1280,640]{1,0:T(8,128)(2,1)S(1)}, f32[24,640]{1,0:T(8,128)S(1)}) custom-call(bf16[1280,640]{1,0:T(8,128)(2,1)} %copy-done, f32[1280,640]{1,0:T(8,128)} %convolution_add_fusion.1.rate_ref, ...), custom_call_target="tpu_custom_call" | custom-call | flops 16384000000 | bytes 16384000 | tf_op jit(solution)/shard_map/lru_backward/pallas_call | solution.py:217
  549.1 12.1 %conv_back.1 = (bf16[1280,640]{1,0:T(8,128)(2,1)}, f32[5,640]{1,0:T(8,128)}) custom-call(f32[1280,640]{1,0:T(8,128)} %get-tuple-element.225.d_conv_ref, bf16[1280,640]{1,0:T(8,128)(2,1)} %copy-done.6, bf16[1280,640]{1,0:T(8,128)(2,1)} %copy-done.4, bf16[640,640]{1,0:T(8,128)(2,1)} %get-tuple-element.390.rate_ref, ...), custom_call_target="tpu_custom_call" | custom-call | flops 4194304000 | bytes 13107200 | tf_op jit(solution)/shard_map/conv_back/pallas_call | solution.py:442
  561.3 14.4 %back_parts.3 = (bf16[160,2048]{1,0:T(8,128)(2,1)}, bf16[160,2048]{1,0:T(8,128)(2,1)}, bf16[320,2048]{1,0:T(8,128)(2,1)}, bf16[320,2048]{1,0:T(8,128)(2,1)}, bf1...) custom-call(bf16[1280,640]{1,0:T(8,128)(2,1)} %copy-done.8, bf16[1280,640]{1,0:T(8,128)(2,1)} %get-tuple-element.235.refs_1_, ...), custom_call_target="tpu_custom_call" | custom-call | flops 6710886400 | bytes 13762560 | tf_op jit(solution)/shard_map/back_parts/pallas_call | solution.py:394
  578.5 13.8 %weight_grad.7 = (bf16[4,4,64,1280]{3,2,1,0:T(8,128)(2,1)}, bf16[1,4,64,1280]{3,2,1,0:T(8,128)(2,1)}, bf16[1,4,64,1280]{3,2,1,0:T(8,128)(2,1)}, bf16[1,4,64,1280]{3,2,1,0:T(8,128)(2,1)}, bf16[1,4,64,1280]{3,2,1,0:T(8,128)(2,1)}) custom-call(s32[1]{0:T(128)} %bitcast.24.me_ref, bf16[1280,2048]{1,0:T(8,128)(2,1)} %copy-done.21, bf16[1280,640]{1,0:T(8,128)(2,1)} %copy-done.8, ...), custom_call_target="tpu_custom_call" | custom-call | flops 6710886400 | bytes 17039360 | tf_op jit(solution)/shard_map/weight_grad/pallas_call | solution.py:526
  597.5 4.6 add_pieces.7
  605.7 2.6 pad_maximum_fusion.8
  615.4 6.1 convolution_convert_fusion
  624.5 20.6 %collective-permute-done.46 = bf16[320,2048]{1,0:T(8,128)(2,1)} collective-permute-done((bf16[320,2048]{1,0:T(8,128)(2,1)}, bf16[320,2048]{1,0:T(8,128)(2,1)}, u32[]{:S(2)}, u32[]{:S(2)}) %collective-permute-start.46) | collective-permute-done | bytes 1310752 | tf_op jit(solution)/shard_map/ppermute | solution.py:602
  645.1 4.3 convert_add_fusion.2
  649.4 4.2 all-to-all-start.5
  653.7 2.9 fusion.8
  656.6 7.6 %all-to-all-done.5 = bf16[4,64,1,1536]{3,1,2,0:T(8,128)(2,1)} async-done(((bf16[4,64,1,1536]{3,1,2,0:T(8,128)(2,1)}), bf16[4,64,1,1536]{3,1,2,0:T(8,128)(2,1)}, u32[]{:S(2)}, u32[]{:S(2)}) %all-to-all-start.5) | async-done | bytes 786464 | tf_op jit(solution)/shard_map/all_to_all | solution.py:659
  664.2 2.5 convert_element_type.287
  668.9 3.7 all-to-all-start.6
  672.6 2.8 fusion.9
  675.5 6.3 fusion.12
  681.8 3.9 all-to-all-start.7
  690.2 5.3 all-to-all-done.7
  (388 shorter events, 135.6 us)
Async XLA Ops:
  7.2 84.4 %all-gather.4.cloned.1.call-start = ((), (), s32[]{:S(2)}) async-start(), calls=%async_computation.13 | async-start | bytes 5898240 | tf_op jit(solution)/shard_map/all_gather | solution.py:633
  24.9 29.0 %collective-permute-start = (bf16[320,2048]{1,0:T(8,128)(2,1)S(1)}, bf16[320,2048]{1,0:T(8,128)(2,1)S(1)}, u32[]{:S(2)}, u32[]{:S(2)}) collective-permute-start(bf16[320,2048]{1,0:T(8,128)(2,1)S(1)} %copy-done.12), channel_id=1, source_target_pairs={{0,8},{8,0},{16,24},{24,16},{1,9},{9,1},{17,25},{25,17},{2,10},{10... | collective-permute-start | bytes 3932168 | tf_op jit(solution)/shard_map/ppermute | solution.py:602
  25.9 32.6 %collective-permute-start.2 = (bf16[320,2048]{1,0:T(8,128)(2,1)S(1)}, bf16[320,2048]{1,0:T(8,128)(2,1)}, u32[]{:S(2)}, u32[]{:S(2)}) collective-permute-start(bf16[320,2048]{1,0:T(8,128)(2,1)S(1)} %copy-done.12), channel_id=1, source_target_pairs={{0,16},{8,24},{16,0},{24,8},{1,17},{9,25},{17,1},{25,9},{2,18},{10... | collective-permute-start | bytes 3932168 | tf_op jit(solution)/shard_map/ppermute | solution.py:602
  28.1 39.4 %all-to-all-start.1 = ((bf16[8,80,384]{2,1,0:T(8,128)(2,1)}), bf16[8,80,384]{2,1,0:T(8,128)(2,1)S(1)}, u32[]{:S(2)}, u32[]{:S(2)}) async-start(bf16[8,80,384]{2,1,0:T(8,128)(2,1)} %broadcast_in_dim.22), calls=%async_computation.1 | async-start | bytes 983040 | tf_op jit(solution)/shard_map/all_to_all | solution.py:671
  54.9 18.8 %collective-permute-start.1 = (bf16[160,2048]{1,0:T(8,128)(2,1)}, bf16[160,2048]{1,0:T(8,128)(2,1)}, u32[]{:S(2)}, u32[]{:S(2)}) collective-permute-start(bf16[160,2048]{1,0:T(8,128)(2,1)} %slice.240), channel_id=1, source_target_pairs={{0,16},{8,24},{16,0},{24,8},{1,17},{9,25},{17,1},{25,9},{2,18},{10... | collective-permute-start | bytes 1966088 | tf_op jit(solution)/shard_map/ppermute | solution.py:602
  60.5 15.3 %collective-permute-start.3 = (bf16[160,2048]{1,0:T(8,128)(2,1)}, bf16[160,2048]{1,0:T(8,128)(2,1)}, u32[]{:S(2)}, u32[]{:S(2)}) collective-permute-start(bf16[160,2048]{1,0:T(8,128)(2,1)} %slice.241), channel_id=1, source_target_pairs={{0,8},{8,0},{16,24},{24,16},{1,9},{9,1},{17,25},{25,17},{2,10},{10... | collective-permute-start | bytes 1966088 | tf_op jit(solution)/shard_map/ppermute | solution.py:602
  68.2 14.6 %all-to-all-start.2 = ((bf16[32,2,64]{2,1,0:T(2,128)(2,1)}), bf16[32,2,64]{2,1,0:T(2,128)(2,1)S(1)}, u32[]{:S(2)}, u32[]{:S(2)}) async-start(bf16[32,2,64]{2,1,0:T(2,128)(2,1)} %broadcast_in_dim.23), calls=%async_computation.2 | async-start | bytes 32768 | tf_op jit(solution)/shard_map/all_to_all | solution.py:671
  73.3 109.6 %all-gather.6.cloned.1.call-start = ((), (), s32[]{:S(2)}) async-start(), calls=%async_computation.14 | async-start | bytes 10027008 | tf_op jit(solution)/shard_map/all_gather | solution.py:740
  93.6 45.8 %collective-permute-start.4 = (bf16[320,2048]{1,0:T(8,128)(2,1)}, bf16[320,2048]{1,0:T(8,128)(2,1)}, u32[]{:S(2)}, u32[]{:S(2)}) collective-permute-start(bf16[320,2048]{1,0:T(8,128)(2,1)} %multiply_convert_fusion.2), channel_id=1, source_target_pairs={{0,8},{8,0},{16,24},{24,16},{1,9},{9,1},{17,25},{25,17},{2,10},{10... | collective-permute-start | bytes 3932168 | tf_op jit(solution)/shard_map/ppermute | solution.py:602
  95.1 46.7 %collective-permute-start.6 = (bf16[320,2048]{1,0:T(8,128)(2,1)}, bf16[320,2048]{1,0:T(8,128)(2,1)}, u32[]{:S(2)}, u32[]{:S(2)}) collective-permute-start(bf16[320,2048]{1,0:T(8,128)(2,1)} %multiply_convert_fusion.2), channel_id=1, source_target_pairs={{0,16},{8,24},{16,0},{24,8},{1,17},{9,25},{17,1},{25,9},{2,18},{10... | collective-permute-start | bytes 3932168 | tf_op jit(solution)/shard_map/ppermute | solution.py:602
  141.0 16.3 %collective-permute-start.5 = (bf16[160,2048]{1,0:T(8,128)(2,1)S(1)}, bf16[160,2048]{1,0:T(8,128)(2,1)}, u32[]{:S(2)}, u32[]{:S(2)}) collective-permute-start(bf16[160,2048]{1,0:T(8,128)(2,1)S(1)} %slice.256), channel_id=1, source_target_pairs={{0,16},{8,24},{16,0},{24,8},{1,17},{9,25},{17,1},{25,9},{2,18},{10... | collective-permute-start | bytes 1966088 | tf_op jit(solution)/shard_map/ppermute | solution.py:602
  142.9 16.4 %collective-permute-start.7 = (bf16[160,2048]{1,0:T(8,128)(2,1)S(1)}, bf16[160,2048]{1,0:T(8,128)(2,1)}, u32[]{:S(2)}, u32[]{:S(2)}) collective-permute-start(bf16[160,2048]{1,0:T(8,128)(2,1)S(1)} %slice.257), channel_id=1, source_target_pairs={{0,8},{8,0},{16,24},{24,16},{1,9},{9,1},{17,25},{25,17},{2,10},{10... | collective-permute-start | bytes 1966088 | tf_op jit(solution)/shard_map/ppermute | solution.py:602
  160.9 21.9 %all-to-all-start.3 = ((bf16[4,64,3072]{2,1,0:T(8,128)(2,1)}), bf16[4,64,3072]{2,1,0:T(8,128)(2,1)S(1)}, u32[]{:S(2)}, u32[]{:S(2)}) async-start(bf16[4,64,3072]{2,1,0:T(8,128)(2,1)} %copy.101), calls=%async_computation.3 | async-start | bytes 3145728 | tf_op jit(solution)/shard_map/all_to_all | solution.py:630
  164.5 133.6 %all-gather.8.cloned.1.call-start = ((), (), s32[]{:S(2)}) async-start(), calls=%async_computation.15 | async-start | bytes 14155776 | tf_op jit(solution)/shard_map/all_gather | solution.py:633
  184.0 252.7 %reduce-scatter.6.cloned.1.call-start = ((), (), s32[]{:S(2)}) async-start(), calls=%async_computation.16 | async-start | bytes 3932160 | tf_op jit(solution)/shard_map/reduce_scatter | solution.py:656
  191.6 15.8 %collective-permute-start.8 = (bf16[160,2048]{1,0:T(8,128)(2,1)}, bf16[160,2048]{1,0:T(8,128)(2,1)S(1)}, u32[]{:S(2)}, u32[]{:S(2)}) collective-permute-start(bf16[160,2048]{1,0:T(8,128)(2,1)} %get-tuple-element.160), channel_id=1, source_target_pairs={{0,8},{8,0},{16,24},{24,16},{1,9},{9,1},{17,25},{25,17},{2,10},{10... | collective-permute-start | bytes 1966088 | tf_op jit(solution)/shard_map/ppermute | solution.py:602
  193.0 14.4 %collective-permute-start.9 = (bf16[160,2048]{1,0:T(8,128)(2,1)}, bf16[160,2048]{1,0:T(8,128)(2,1)S(1)}, u32[]{:S(2)}, u32[]{:S(2)}) collective-permute-start(bf16[160,2048]{1,0:T(8,128)(2,1)} %get-tuple-element.161), channel_id=1, source_target_pairs={{0,16},{8,24},{16,0},{24,8},{1,17},{9,25},{17,1},{25,9},{2,18},{10... | collective-permute-start | bytes 1966088 | tf_op jit(solution)/shard_map/ppermute | solution.py:602
  207.7 28.9 %collective-permute-start.10 = (bf16[320,2048]{1,0:T(8,128)(2,1)S(1)}, bf16[320,2048]{1,0:T(8,128)(2,1)}, u32[]{:S(2)}, u32[]{:S(2)}) collective-permute-start(bf16[320,2048]{1,0:T(8,128)(2,1)S(1)} %pad_maximum_fusion.2), channel_id=1, source_target_pairs={{0,8},{8,0},{16,24},{24,16},{1,9},{9,1},{17,25},{25,17},{2,10},{10... | collective-permute-start | bytes 3932168 | tf_op jit(solution)/shard_map/ppermute | solution.py:602
  209.8 28.4 %collective-permute-start.11 = (bf16[320,2048]{1,0:T(8,128)(2,1)S(1)}, bf16[320,2048]{1,0:T(8,128)(2,1)}, u32[]{:S(2)}, u32[]{:S(2)}) collective-permute-start(bf16[320,2048]{1,0:T(8,128)(2,1)S(1)} %pad_maximum_fusion.3), channel_id=1, source_target_pairs={{0,16},{8,24},{16,0},{24,8},{1,17},{9,25},{17,1},{25,9},{2,18},{10... | collective-permute-start | bytes 3932168 | tf_op jit(solution)/shard_map/ppermute | solution.py:602
  243.2 27.6 %collective-permute-start.12 = (bf16[320,2048]{1,0:T(8,128)(2,1)}, bf16[320,2048]{1,0:T(8,128)(2,1)}, u32[]{:S(2)}, u32[]{:S(2)}) collective-permute-start(bf16[320,2048]{1,0:T(8,128)(2,1)} %multiply_convert_fusion.1.refs_4_), channel_id=1, source_target_pairs={{0,8},{8,0},{16,24},{24,16},{1,9},{9,1},{17,25},{25,17},{2,10},{10... | collective-permute-start | bytes 3932168 | tf_op jit(solution)/shard_map/ppermute | solution.py:602
  243.8 28.4 %collective-permute-start.14 = (bf16[320,2048]{1,0:T(8,128)(2,1)}, bf16[320,2048]{1,0:T(8,128)(2,1)}, u32[]{:S(2)}, u32[]{:S(2)}) collective-permute-start(bf16[320,2048]{1,0:T(8,128)(2,1)} %multiply_convert_fusion.1.refs_4_), channel_id=1, source_target_pairs={{0,16},{8,24},{16,0},{24,8},{1,17},{9,25},{17,1},{25,9},{2,18},{10... | collective-permute-start | bytes 3932168 | tf_op jit(solution)/shard_map/ppermute | solution.py:602
  271.9 15.8 %collective-permute-start.13 = (bf16[160,2048]{1,0:T(8,128)(2,1)S(1)}, bf16[160,2048]{1,0:T(8,128)(2,1)S(1)}, u32[]{:S(2)}, u32[]{:S(2)}) collective-permute-start(bf16[160,2048]{1,0:T(8,128)(2,1)S(1)} %slice.259), channel_id=1, source_target_pairs={{0,16},{8,24},{16,0},{24,8},{1,17},{9,25},{17,1},{25,9},{2,18},{10... | collective-permute-start | bytes 1966088 | tf_op jit(solution)/shard_map/ppermute | solution.py:602
  273.4 14.3 %collective-permute-start.15 = (bf16[160,2048]{1,0:T(8,128)(2,1)S(1)}, bf16[160,2048]{1,0:T(8,128)(2,1)}, u32[]{:S(2)}, u32[]{:S(2)}) collective-permute-start(bf16[160,2048]{1,0:T(8,128)(2,1)S(1)} %slice.260), channel_id=1, source_target_pairs={{0,8},{8,0},{16,24},{24,16},{1,9},{9,1},{17,25},{25,17},{2,10},{10... | collective-permute-start | bytes 1966088 | tf_op jit(solution)/shard_map/ppermute | solution.py:602
  347.5 2.5 collective-permute-start.24
  347.7 3.4 collective-permute-start.25
  348.0 4.2 collective-permute-start.26
  348.3 5.1 collective-permute-start.27
  359.5 134.9 %reduce-scatter.8.cloned.1.call-start = ((), (), s32[]{:S(2)}) async-start(), calls=%async_computation.17 | async-start | bytes 3932160 | tf_op jit(solution)/shard_map/reduce_scatter | solution.py:656
  382.5 18.0 %collective-permute-start.16 = (bf16[160,2048]{1,0:T(8,128)(2,1)}, bf16[160,2048]{1,0:T(8,128)(2,1)S(1)}, u32[]{:S(2)}, u32[]{:S(2)}) collective-permute-start(bf16[160,2048]{1,0:T(8,128)(2,1)} %get-tuple-element.179), channel_id=1, source_target_pairs={{0,8},{8,0},{16,24},{24,16},{1,9},{9,1},{17,25},{25,17},{2,10},{10... | collective-permute-start | bytes 1966088 | tf_op jit(solution)/shard_map/ppermute | solution.py:602
  383.7 16.8 %collective-permute-start.17 = (bf16[160,2048]{1,0:T(8,128)(2,1)}, bf16[160,2048]{1,0:T(8,128)(2,1)S(1)}, u32[]{:S(2)}, u32[]{:S(2)}) collective-permute-start(bf16[160,2048]{1,0:T(8,128)(2,1)} %get-tuple-element.180), channel_id=1, source_target_pairs={{0,16},{8,24},{16,0},{24,8},{1,17},{9,25},{17,1},{25,9},{2,18},{10... | collective-permute-start | bytes 1966088 | tf_op jit(solution)/shard_map/ppermute | solution.py:602
  400.4 3.4 collective-permute-start.20
  400.9 31.4 %collective-permute-start.18 = (bf16[320,2048]{1,0:T(8,128)(2,1)S(1)}, bf16[320,2048]{1,0:T(8,128)(2,1)}, u32[]{:S(2)}, u32[]{:S(2)}) collective-permute-start(bf16[320,2048]{1,0:T(8,128)(2,1)S(1)} %pad_maximum_fusion.4), channel_id=1, source_target_pairs={{0,8},{8,0},{16,24},{24,16},{1,9},{9,1},{17,25},{25,17},{2,10},{10... | collective-permute-start | bytes 3932168 | tf_op jit(solution)/shard_map/ppermute | solution.py:602
  401.9 30.9 %collective-permute-start.19 = (bf16[320,2048]{1,0:T(8,128)(2,1)S(1)}, bf16[320,2048]{1,0:T(8,128)(2,1)}, u32[]{:S(2)}, u32[]{:S(2)}) collective-permute-start(bf16[320,2048]{1,0:T(8,128)(2,1)S(1)} %pad_maximum_fusion.5), channel_id=1, source_target_pairs={{0,16},{8,24},{16,0},{24,8},{1,17},{9,25},{17,1},{25,9},{2,18},{10... | collective-permute-start | bytes 3932168 | tf_op jit(solution)/shard_map/ppermute | solution.py:602
  403.3 2.3 collective-permute-start.21
  403.3 3.4 collective-permute-start.22
  403.8 4.0 collective-permute-start.23
  440.4 30.0 %collective-permute-start.28 = (bf16[320,2048]{1,0:T(8,128)(2,1)S(1)}, bf16[320,2048]{1,0:T(8,128)(2,1)S(1)}, u32[]{:S(2)}, u32[]{:S(2)}) collective-permute-start(bf16[320,2048]{1,0:T(8,128)(2,1)S(1)} %fusion.29.refs_4_), channel_id=1, source_target_pairs={{0,8},{8,0},{16,24},{24,16},{1,9},{9,1},{17,25},{25,17},{2,10},{10... | collective-permute-start | bytes 3932168 | tf_op jit(solution)/shard_map/ppermute | solution.py:602
  442.0 30.6 %collective-permute-start.30 = (bf16[320,2048]{1,0:T(8,128)(2,1)S(1)}, bf16[320,2048]{1,0:T(8,128)(2,1)S(1)}, u32[]{:S(2)}, u32[]{:S(2)}) collective-permute-start(bf16[320,2048]{1,0:T(8,128)(2,1)S(1)} %fusion.29.refs_4_), channel_id=1, source_target_pairs={{0,16},{8,24},{16,0},{24,8},{1,17},{9,25},{17,1},{25,9},{2,18},{10... | collective-permute-start | bytes 3932168 | tf_op jit(solution)/shard_map/ppermute | solution.py:602
  457.7 15.2 %collective-permute-start.32 = (bf16[1,4,64,1536]{3,2,1,0:T(8,128)(2,1)}, bf16[1,4,64,1536]{3,2,1,0:T(8,128)(2,1)S(1)}, u32[]{:S(2)}, u32[]{:S(2)}) collective-permute-start(bf16[1,4,64,1536]{3,2,1,0:T(8,128)(2,1)} %get-tuple-element.205), channel_id=1, source_target_pairs={{0,4},{4,0},{1,5},{5,1},{2,6},{6,2},{3,7},{7,3},{8,12},{12,8},{9,1... | collective-permute-start | bytes 2359304 | tf_op jit(solution)/shard_map/ppermute | solution.py:643
  457.7 29.0 %collective-permute-start.33 = (bf16[1,4,64,1536]{3,2,1,0:T(8,128)(2,1)}, bf16[1,4,64,1536]{3,2,1,0:T(8,128)(2,1)S(1)}, u32[]{:S(2)}, u32[]{:S(2)}) collective-permute-start(bf16[1,4,64,1536]{3,2,1,0:T(8,128)(2,1)} %get-tuple-element.206), channel_id=1, source_target_pairs={{0,4},{4,0},{1,5},{5,1},{2,6},{6,2},{3,7},{7,3},{8,12},{12,8},{9,1... | collective-permute-start | bytes 2359304 | tf_op jit(solution)/shard_map/ppermute | solution.py:643
  458.2 28.5 %collective-permute-start.34 = (bf16[1,4,64,1536]{3,2,1,0:T(8,128)(2,1)}, bf16[1,4,64,1536]{3,2,1,0:T(8,128)(2,1)S(1)}, u32[]{:S(2)}, u32[]{:S(2)}) collective-permute-start(bf16[1,4,64,1536]{3,2,1,0:T(8,128)(2,1)} %get-tuple-element.207), channel_id=1, source_target_pairs={{0,4},{4,0},{1,5},{5,1},{2,6},{6,2},{3,7},{7,3},{8,12},{12,8},{9,1... | collective-permute-start | bytes 2359304 | tf_op jit(solution)/shard_map/ppermute | solution.py:643
  470.4 16.4 %collective-permute-start.35 = (bf16[1,4,64,1536]{3,2,1,0:T(8,128)(2,1)}, bf16[1,4,64,1536]{3,2,1,0:T(8,128)(2,1)S(1)}, u32[]{:S(2)}, u32[]{:S(2)}) collective-permute-start(bf16[1,4,64,1536]{3,2,1,0:T(8,128)(2,1)} %get-tuple-element.208), channel_id=1, source_target_pairs={{0,4},{4,0},{1,5},{5,1},{2,6},{6,2},{3,7},{7,3},{8,12},{12,8},{9,1... | collective-permute-start | bytes 2359304 | tf_op jit(solution)/shard_map/ppermute | solution.py:643
  472.6 20.8 %collective-permute-start.29 = (bf16[160,2048]{1,0:T(8,128)(2,1)}, bf16[160,2048]{1,0:T(8,128)(2,1)}, u32[]{:S(2)}, u32[]{:S(2)}) collective-permute-start(bf16[160,2048]{1,0:T(8,128)(2,1)} %slice.261), channel_id=1, source_target_pairs={{0,16},{8,24},{16,0},{24,8},{1,17},{9,25},{17,1},{25,9},{2,18},{10... | collective-permute-start | bytes 1966088 | tf_op jit(solution)/shard_map/ppermute | solution.py:602
  472.9 20.4 %collective-permute-start.31 = (bf16[160,2048]{1,0:T(8,128)(2,1)S(1)}, bf16[160,2048]{1,0:T(8,128)(2,1)}, u32[]{:S(2)}, u32[]{:S(2)}) collective-permute-start(bf16[160,2048]{1,0:T(8,128)(2,1)S(1)} %slice.262), channel_id=1, source_target_pairs={{0,8},{8,0},{16,24},{24,16},{1,9},{9,1},{17,25},{25,17},{2,10},{10... | collective-permute-start | bytes 1966088 | tf_op jit(solution)/shard_map/ppermute | solution.py:602
  494.5 20.7 %collective-permute-start.36 = (bf16[160,2048]{1,0:T(8,128)(2,1)}, bf16[160,2048]{1,0:T(8,128)(2,1)}, u32[]{:S(2)}, u32[]{:S(2)}) collective-permute-start(bf16[160,2048]{1,0:T(8,128)(2,1)} %get-tuple-element.216), channel_id=1, source_target_pairs={{0,8},{8,0},{16,24},{24,16},{1,9},{9,1},{17,25},{25,17},{2,10},{10... | collective-permute-start | bytes 1966088 | tf_op jit(solution)/shard_map/ppermute | solution.py:602
  495.9 22.2 %collective-permute-start.37 = (bf16[160,2048]{1,0:T(8,128)(2,1)}, bf16[160,2048]{1,0:T(8,128)(2,1)}, u32[]{:S(2)}, u32[]{:S(2)}) collective-permute-start(bf16[160,2048]{1,0:T(8,128)(2,1)} %get-tuple-element.217), channel_id=1, source_target_pairs={{0,16},{8,24},{16,0},{24,8},{1,17},{9,25},{17,1},{25,9},{2,18},{10... | collective-permute-start | bytes 1966088 | tf_op jit(solution)/shard_map/ppermute | solution.py:602
  500.1 61.2 %all-to-all-start.4 = ((bf16[4,64,1,1536]{3,1,2,0:T(8,128)(2,1)}), bf16[4,64,1,1536]{3,1,2,0:T(8,128)(2,1)S(1)}, u32[]{:S(2)}, u32[]{:S(2)}) async-start(bf16[4,64,1,1536]{3,1,2,0:T(8,128)(2,1)} %bitcast.152), calls=%async_computation.6 | async-start | bytes 1572864 | tf_op jit(solution)/shard_map/all_to_all | solution.py:659
  503.6 145.8 %reduce-scatter.12.cloned.1.call-start = ((), (), s32[]{:S(2)}) async-start(), calls=%async_computation.19 | async-start | bytes 3932160 | tf_op jit(solution)/shard_map/reduce_scatter | solution.py:656
  504.2 160.1 %reduce-scatter.10.cloned.1.call-start = ((), (), s32[]{:S(2)}) async-start(), calls=%async_computation.18 | async-start | bytes 3276800 | tf_op jit(solution)/shard_map/reduce_scatter | solution.py:656
  523.1 38.2 %collective-permute-start.38 = (bf16[320,2048]{1,0:T(8,128)(2,1)}, bf16[320,2048]{1,0:T(8,128)(2,1)S(1)}, u32[]{:S(2)}, u32[]{:S(2)}) collective-permute-start(bf16[320,2048]{1,0:T(8,128)(2,1)} %pad_maximum_fusion.6), channel_id=1, source_target_pairs={{0,8},{8,0},{16,24},{24,16},{1,9},{9,1},{17,25},{25,17},{2,10},{10... | collective-permute-start | bytes 3932168 | tf_op jit(solution)/shard_map/ppermute | solution.py:602
  523.1 38.2 %collective-permute-start.39 = (bf16[320,2048]{1,0:T(8,128)(2,1)}, bf16[320,2048]{1,0:T(8,128)(2,1)S(1)}, u32[]{:S(2)}, u32[]{:S(2)}) collective-permute-start(bf16[320,2048]{1,0:T(8,128)(2,1)} %pad_maximum_fusion.7), channel_id=1, source_target_pairs={{0,16},{8,24},{16,0},{24,8},{1,17},{9,25},{17,1},{25,9},{2,18},{10... | collective-permute-start | bytes 3932168 | tf_op jit(solution)/shard_map/ppermute | solution.py:602
  575.8 17.1 %collective-permute-start.44 = (bf16[160,2048]{1,0:T(8,128)(2,1)}, bf16[160,2048]{1,0:T(8,128)(2,1)}, u32[]{:S(2)}, u32[]{:S(2)}) collective-permute-start(bf16[160,2048]{1,0:T(8,128)(2,1)} %get-tuple-element.249), channel_id=1, source_target_pairs={{0,8},{8,0},{16,24},{24,16},{1,9},{9,1},{17,25},{25,17},{2,10},{10... | collective-permute-start | bytes 1966088 | tf_op jit(solution)/shard_map/ppermute | solution.py:602
  577.9 17.2 %collective-permute-start.45 = (bf16[160,2048]{1,0:T(8,128)(2,1)}, bf16[160,2048]{1,0:T(8,128)(2,1)S(1)}, u32[]{:S(2)}, u32[]{:S(2)}) collective-permute-start(bf16[160,2048]{1,0:T(8,128)(2,1)} %get-tuple-element.250), channel_id=1, source_target_pairs={{0,16},{8,24},{16,0},{24,8},{1,17},{9,25},{17,1},{25,9},{2,18},{10... | collective-permute-start | bytes 1966088 | tf_op jit(solution)/shard_map/ppermute | solution.py:602
  592.3 2.8 collective-permute-start.40
  592.3 3.4 collective-permute-start.41
  592.8 3.8 collective-permute-start.42
  592.9 4.7 collective-permute-start.43
  613.9 31.1 %collective-permute-start.46 = (bf16[320,2048]{1,0:T(8,128)(2,1)}, bf16[320,2048]{1,0:T(8,128)(2,1)}, u32[]{:S(2)}, u32[]{:S(2)}) collective-permute-start(bf16[320,2048]{1,0:T(8,128)(2,1)} %pad_maximum_fusion.8), channel_id=1, source_target_pairs={{0,8},{8,0},{16,24},{24,16},{1,9},{9,1},{17,25},{25,17},{2,10},{10... | collective-permute-start | bytes 3932168 | tf_op jit(solution)/shard_map/ppermute | solution.py:602
  614.0 31.1 %collective-permute-start.47 = (bf16[320,2048]{1,0:T(8,128)(2,1)}, bf16[320,2048]{1,0:T(8,128)(2,1)}, u32[]{:S(2)}, u32[]{:S(2)}) collective-permute-start(bf16[320,2048]{1,0:T(8,128)(2,1)} %pad_maximum_fusion.9), channel_id=1, source_target_pairs={{0,16},{8,24},{16,0},{24,8},{1,17},{9,25},{17,1},{25,9},{2,18},{10... | collective-permute-start | bytes 3932168 | tf_op jit(solution)/shard_map/ppermute | solution.py:602
  623.1 30.5 %collective-permute-start.48 = (bf16[4,80,2432]{2,1,0:T(8,128)(2,1)}, bf16[4,80,2432]{2,1,0:T(8,128)(2,1)}, u32[]{:S(2)}, u32[]{:S(2)}) collective-permute-start(bf16[4,80,2432]{2,1,0:T(8,128)(2,1)} %dynamic-slice_bitcast_fusion), channel_id=1, source_target_pairs={{0,4},{4,0},{1,5},{5,1},{2,6},{6,2},{3,7},{7,3},{8,12},{12,8},{9,1... | collective-permute-start | bytes 4669448 | tf_op jit(solution)/shard_map/ppermute | solution.py:652
  649.4 14.8 %all-to-all-start.5 = ((bf16[4,64,1,1536]{3,1,2,0:T(8,128)(2,1)}), bf16[4,64,1,1536]{3,1,2,0:T(8,128)(2,1)}, u32[]{:S(2)}, u32[]{:S(2)}) async-start(bf16[4,64,1,1536]{3,1,2,0:T(8,128)(2,1)} %bitcast.151), calls=%async_computation.9 | async-start | bytes 1572864 | tf_op jit(solution)/shard_map/all_to_all | solution.py:659
  653.6 45.4 %reduce-scatter.14.cloned.1.call-start = ((), (), s32[]{:S(2)}) async-start(), calls=%async_computation.20 | async-start | bytes 1945600 | tf_op jit(solution)/shard_map/reduce_scatter | solution.py:656
  668.9 13.0 %all-to-all-start.6 = ((f32[32,1,128]{2,1,0:T(1,128)}), f32[32,1,128]{2,1,0:T(1,128)S(1)}, u32[]{:S(2)}, u32[]{:S(2)}) async-start(f32[32,1,128]{2,1,0:T(1,128)} %reshape.270), calls=%async_computation.10 | async-start | bytes 32768 | tf_op jit(solution)/shard_map/all_to_all | solution.py:854
  681.8 13.7 %all-to-all-start.7 = ((bf16[4,64,1,1280]{3,1,2,0:T(8,128)(2,1)}), bf16[4,64,1,1280]{3,1,2,0:T(8,128)(2,1)S(1)}, u32[]{:S(2)}, u32[]{:S(2)}) async-start(bf16[4,64,1,1280]{3,1,2,0:T(8,128)(2,1)} %bitcast.51), calls=%async_computation.11 | async-start | bytes 1310720 | tf_op jit(solution)/shard_map/all_to_all | solution.py:659
  (80 other events, 997.5 us)
Sparse Core Ops, SparseCore 0:
  25.0 66.4 all-gather.3
  93.7 84.9 all-gather.5
  184.2 113.9 all-gather.7
  359.6 58.4 reduce-scatter.5
  436.9 57.5 reduce-scatter.7
  506.4 60.7 reduce-scatter.11
  605.8 51.1 reduce-scatter.9
  664.4 34.6 reduce-scatter.13

commit v7 on v6

--- a/solution.py
+++ b/solution.py
@@ -826,7 +826,8 @@
         grad_rec = finish(mine)
         rec_sum = sum_narrow(grad_rec)
         one, two, own = scatter_start(parts1)
-        one, two, late_mixed, late_rate, late_input = fence(one, two, mixed, d_rate, d_input)
+        mup_out = columns_home(mup_sum, rows)
+        one, two, late_mixed, late_rate, late_input, mup_out = fence(one, two, mixed, d_rate, d_input, mup_out)
         d_normed1 = scatter_finish(one, two, own)
         grad_out = matmul_tn(late_mixed, low_merged_all).astype(bf16)
         gain_grads = jnp.stack([grad_gain1[0], grad_gain2]).reshape(2, -1, rows).swapaxes(0, 1)
@@ -845,8 +846,7 @@
         )
         table_grad = jnp.pad(table_grad, ((0, -places[-1] % LANES), (0, 0))).T.astype(bf16)
         last = sum_rest(rows_cut(jnp.concatenate([grad_out, table_grad], axis=1)))
-        mup_out = columns_home(mup_sum, rows)
-        rec_sum, d_normed1, last, gain_grads, mup_out = fence(rec_sum, d_normed1, last, gain_grads, mup_out)
+        rec_sum, d_normed1, last, gain_grads = fence(rec_sum, d_normed1, last, gain_grads)
         last = sum_narrow(last).astype(f32)
         out_out, table_out = last[:, :width], last[:, width:].T
 

time: 717 us -> 717 us (level)
  other arithmetic: 78.4 us -> 69.2 us
    all_to_all x3, waiting for transfers between devices: 12.9 us -> 0.9 us  [columns_home(): lax.all_to_all(mine.reshape(PLANE, rows, -1), 'wide', 0, 1, tiled=False)]
    convert_element_type x1, other arithmetic: 13.5 us -> 1.5 us  [on_device(): conv = conv.astype(bf16)]
    all_gather x1, waiting for transfers between devices: 0.01 us -> 7.91 us  [on_device(): lax.all_gather(after(jnp.concatenate([out_proj, mlp_down], axis=0), w_rec...]
    unnamed x173 -> x167, local copies, waits for them, and re-layouts: 25.3 us -> 23.8 us
  transfers between devices with their start and end apart: 64 -> 64, of which waited for: 30 -> 30; matrix products, arithmetic and copies ran while one was open for 24% -> 23% of each run, Pallas kernels for 25% -> 25%
where the time goes in v7:
time: 717 us; the launch traced here: 710 us
  Pallas kernels  229 us (32%)
  waiting for transfers between devices  199 us (28%)
  local copies, waits for them, and re-layouts  82.1 us (11%)
  starting transfers between devices  71.3 us (10%)
  other arithmetic  69.2 us (10%)
  matrix products  28.5 us (4%)
  between operations  16.3 us (2%)
  blocking collectives  15 us (2%)
    ppermute x32, waiting for transfers between devices, swap(): return lax.ppermute(values, 'wide', [(i, i ^ mask) for i in range(PLANE)])  149 us
    pallas_call x4, Pallas kernels, weight_grad(): pl.pallas_call(functools.partial(weight_grad_kernel, rows, len(rights), s...  58.1 us
    ppermute x32, starting transfers between devices, swap(): return lax.ppermute(values, 'wide', [(i, i ^ mask) for i in range(PLANE)])  37.8 us
    pallas_call x2, Pallas kernels, back_parts(): pl.pallas_call(functools.partial(back_kernel, len(grads), summed is not N...  36.7 us
    pallas_call x1, Pallas kernels, mlp_both(): pl.pallas_call(functools.partial(mlp_kernel, PLANE), grid=(steps,), out_s...  35.1 us
    unnamed x167, local copies, waits for them, and re-layouts  23.8 us
    pallas_call x1, Pallas kernels, lru_backward(): pl.pallas_call(functools.partial(lru_backward_kernel, seqs), grid=(pl.cdi...  20.8 us
    pallas_call x4, Pallas kernels, add_pieces(): pl.pallas_call(add_pieces_kernel, grid=(groups, columns // block), out_sh...  20.2 us
  transfers between devices with their start and end apart: 64, of which 30 were waited for; matrix products, arithmetic and copies ran while one was open for 23% of the time, Pallas kernels for 25%

profile of v7, /device:TPU:0, one launch (start us, length us, event | category | flops | bytes accessed | tf_op | source)
XLA Modules:
  0.0 710.0 jit_solution(5786548145199060394)
XLA Ops:
  9.9 15.0 %all_to_all.70 = bf16[4,64,1280]{2,1,0:T(8,128)(2,1)} all-to-all(bf16[4,64,1280]{2,1,0:T(8,128)(2,1)S(1)} %copy.97), channel_id=1, replica_groups=mesh['wide'=4,'rest'=2,'narrow'=4] {'wide'}, dimensions={0} | all-to-all | bytes 1310720 | tf_op jit(solution)/shard_map/all_to_all | solution.py:630
  28.1 4.9 all-to-all-start.1
  33.0 21.0 %collective-permute-done = bf16[320,2048]{1,0:T(8,128)(2,1)S(1)} collective-permute-done((bf16[320,2048]{1,0:T(8,128)(2,1)S(1)}, bf16[320,2048]{1,0:T(8,128)(2,1)S(1)}, u32[]{:S(2)}, u32[]{:S(2)}) %collective-permute-start) | collective-permute-done | bytes 1310752 | tf_op jit(solution)/shard_map/ppermute | solution.py:602
  56.2 2.3 pad_maximum_fusion.10
  61.0 2.3 reshape.210
  68.2 5.1 all-to-all-start.2
  78.7 2.7 constant_dynamic-update-slice_fusion.1
  82.6 9.0 %all-gather.4.cloned.1.call-done = bf16[2048,1280]{1,0:T(8,128)(2,1)} async-done(((bf16[256,1280]{1,0:T(8,128)(2,1)}), bf16[2048,1280]{1,0:T(8,128)(2,1)}) %all-gather.4.cloned.1.call-update) | async-done | bytes 5242896 | tf_op jit(solution)/shard_map/all_gather | solution.py:633
  96.7 5.9 copy.100
  102.9 3.8 fusion
  106.8 3.9 fusion.2.left_ref
  110.8 4.3 fusion.15.branch_ref
  115.0 2.7 pad_slice_fusion.2
  117.7 7.9 %fusion.13.gate_ref = f32[1280,640]{1,0:T(8,128)} fusion(bf16[1280,2048]{1,0:T(8,128)(2,1)S(1)} %fusion.2.left_ref, bf16[2048,1280]{1,0:T(8,128)(2,1)} %bitcast.131), kind=kOutput, calls=%fused_computation.30 | convolution fusion | flops 3355443200 | bytes 11141120 | tf_op jit(solution)/shard_map/dot_general | solution.py:20
  131.6 3.6 convolution_add_fusion.input_ref
  135.2 3.6 convolution_add_fusion.1.rate_ref
  138.8 6.5 collective-permute-done.5
  148.8 3.6 all-to-all-start.3
  152.5 14.7 %lru_forward.1 = (f32[1280,640]{1,0:T(8,128)}, bf16[1280,640]{1,0:T(8,128)(2,1)S(1)}) custom-call(bf16[1280,640]{1,0:T(8,128)(2,1)S(1)} %fusion.5.conv_ref, f32[1280,640]{1,0:T(8,128)} %convolution_add_fusion.1.rate_ref, f32[1280,640]{1,0:T(8,128)} %convolution_add_fusion.input_ref, f32[1280,640]{1,0:T(8,128)} %fusion.13.gate_ref, ...), custom_call_target="tpu_custom_call" | custom-call | flops 16384000000 | bytes 16384000 | tf_op jit(solution)/shard_map/lru_forward/pallas_call | solution.py:198
  168.4 2.4 all-to-all-done.3
  170.8 7.9 %all-gather.6.cloned.1.call-done = bf16[2176,2048]{1,0:T(8,128)(2,1)} async-done(((bf16[272,2048]{1,0:T(8,128)(2,1)}), bf16[2176,2048]{1,0:T(8,128)(2,1)}) %all-gather.6.cloned.1.call-update) | async-done | bytes 8912912 | tf_op jit(solution)/shard_map/all_gather | solution.py:740
  178.8 7.4 %out_parts.2 = (bf16[160,2048]{1,0:T(8,128)(2,1)}, bf16[160,2048]{1,0:T(8,128)(2,1)}, bf16[320,2048]{1,0:T(8,128)(2,1)}, bf16[320,2048]{1,0:T(8,128)(2,1)}, bf16[320,2048]{1,0:T(8,128)(2,1)}) custom-call(bf16[1280,640]{1,0:T(8,128)(2,1)} %copy-done.2, bf16[8,272,2048]{2,1,0:T(8,128)(2,1)} %bitcast.115), custom_call_target="tpu_custom_call" | custom-call | flops 3355443200 | bytes 9502720 | tf_op jit(solution)/shard_map/out_parts/pallas_call | solution.py:466
  191.7 11.6 %collective-permute-done.8 = bf16[160,2048]{1,0:T(8,128)(2,1)S(1)} collective-permute-done((bf16[160,2048]{1,0:T(8,128)(2,1)}, bf16[160,2048]{1,0:T(8,128)(2,1)S(1)}, u32[]{:S(2)}, u32[]{:S(2)}) %collective-permute-start.8) | collective-permute-done | bytes 655392 | tf_op jit(solution)/shard_map/ppermute | solution.py:602
  207.3 27.5 %collective-permute-done.10 = bf16[320,2048]{1,0:T(8,128)(2,1)} collective-permute-done((bf16[320,2048]{1,0:T(8,128)(2,1)S(1)}, bf16[320,2048]{1,0:T(8,128)(2,1)}, u32[]{:S(2)}, u32[]{:S(2)}) %collective-permute-start.10) | collective-permute-done | bytes 1310752 | tf_op jit(solution)/shard_map/ppermute | solution.py:602
  235.5 3.5 multiply_reduce_fusion.2
  245.8 23.8 %collective-permute-done.12.refs_2_ = bf16[320,2048]{1,0:T(8,128)(2,1)} collective-permute-done((bf16[320,2048]{1,0:T(8,128)(2,1)}, bf16[320,2048]{1,0:T(8,128)(2,1)}, u32[]{:S(2)}, u32[]{:S(2)}) %collective-permute-start.12) | collective-permute-done | bytes 1310752 | tf_op jit(solution)/shard_map/ppermute | solution.py:602
  279.0 8.4 %slice.209 = bf16[8,192,2048]{2,1,0:T(8,128)(2,1)} slice(bf16[8,272,2048]{2,1,0:T(8,128)(2,1)} %bitcast.116), slice={[0:8], [80:272], [0:2048]} | slice | bytes 12582912 | tf_op jit(solution)/shard_map/slice | solution.py:778
  287.5 8.7 %all-gather.8.cloned.1.call-done = bf16[2048,3072]{1,0:T(8,128)(2,1)} async-done(((bf16[256,3072]{1,0:T(8,128)(2,1)}), bf16[2048,3072]{1,0:T(8,128)(2,1)}) %all-gather.8.cloned.1.call-update) | async-done | bytes 12582928 | tf_op jit(solution)/shard_map/all_gather | solution.py:633
  296.1 35.1 %mlp_both.1 = (bf16[1280,1536]{1,0:T(8,128)(2,1)}, bf16[1280,1536]{1,0:T(8,128)(2,1)}, bf16[1280,1536]{1,0:T(8,128)(2,1)}, bf16[1280,2048]{1,0:T(8,128)(2,1)}) custom-call(bf16[160,2048]{1,0:T(8,128)(2,1)} %copy-done.72, bf16[160,2048]{1,0:T(8,128)(2,1)} %collective-permute-done.15.refs_1_, bf16[320,2048]{1,0:T(8,128)(2,1)} %collective-permute-done.12.refs_2_, ...), custom_call_target="tpu_custom_call" | custom-call | flops 24159191040 | bytes 34603008 | tf_op jit(solution)/shard_map/mlp_both/pallas_call | solution.py:282
  331.2 14.4 %weight_grad.4 = (bf16[4,1,192,2048]{3,2,1,0:T(8,128)(2,1)}, bf16[1,1,192,2048]{3,2,1,0:T(8,128)(2,1)}, bf16[1,1,192,2048]{3,2,1,0:T(8,128)(2,1)}, bf16[1,1,192,...) custom-call(s32[1]{0:T(128)} %bitcast.24.me_ref, bf16[1280,1536]{1,0:T(8,128)(2,1)} %get-tuple-element.196.left_ref.values_ref, ...), custom_call_target="tpu_custom_call" | custom-call | flops 8053063680 | bytes 15466496 | tf_op jit(solution)/shard_map/weight_grad/pallas_call | solution.py:526
  352.3 5.2 add_pieces.5
  357.8 22.3 %back_parts.2 = (bf16[160,2048]{1,0:T(8,128)(2,1)}, bf16[160,2048]{1,0:T(8,128)(2,1)}, bf16[320,2048]{1,0:T(8,128)(2,1)}, bf16[320,2048]{1,0:T(8,128)(2,1)}, bf16[320,2048]{1,0:T(8,128)(2,1)}) custom-call(bf16[1280,1536]{1,0:T(8,128)(2,1)} %get-tuple-element.175.refs_0_, bf16[1280,1536]{1,0:T(8,128)(2,1)} %get-tuple-element.203.refs_1_.refs_0_, ...), custom_call_target="tpu_custom_call" | custom-call | flops 16106127360 | bytes 25690112 | tf_op jit(solution)/shard_map/back_parts/pallas_call | solution.py:394
  383.0 15.3 %weight_grad.5 = (bf16[4,4,64,1536]{3,2,1,0:T(8,128)(2,1)}, bf16[1,4,64,1536]{3,2,1,0:T(8,128)(2,1)}, bf16[1,4,64,1536]{3,2,1,0:T(8,128)(2,1)}, bf16[1,4,64,1536]{3,2,1,0:T(8,128)(2,1)}, bf16[1,4,64,1536]{3,2,1,0:T(8,128)(2,1)}) custom-call(s32[1]{0:T(128)} %bitcast.24.me_ref, bf16[1280,2048]{1,0:T(8,128)(2,1)} %get-tuple-element.184.left_ref, ...), custom_call_target="tpu_custom_call" | custom-call | flops 8053063680 | bytes 19398656 | tf_op jit(solution)/shard_map/weight_grad/pallas_call | solution.py:526
  406.5 5.2 add_pieces.4
  411.7 18.3 %collective-permute-done.18 = bf16[320,2048]{1,0:T(8,128)(2,1)} collective-permute-done((bf16[320,2048]{1,0:T(8,128)(2,1)S(1)}, bf16[320,2048]{1,0:T(8,128)(2,1)}, u32[]{:S(2)}, u32[]{:S(2)}) %collective-permute-start.18) | collective-permute-done | bytes 1310752 | tf_op jit(solution)/shard_map/ppermute | solution.py:602
  430.7 3.9 convert_add_fusion.3
  434.6 2.7 multiply_reduce_fusion
  441.4 15.0 %weight_grad.6 = (bf16[4,4,64,1536]{3,2,1,0:T(8,128)(2,1)}, bf16[1,4,64,1536]{3,2,1,0:T(8,128)(2,1)}, bf16[1,4,64,1536]{3,2,1,0:T(8,128)(2,1)}, bf16[1,4,64,1536]{3,2,1,0:T(8,128)(2,1)}, bf16[1,4,64,1536]{3,2,1,0:T(8,128)(2,1)}) custom-call(s32[1]{0:T(128)} %bitcast.24.me_ref, bf16[1280,2048]{1,0:T(8,128)(2,1)} %get-tuple-element.184.left_ref, ...), custom_call_target="tpu_custom_call" | custom-call | flops 8053063680 | bytes 19398656 | tf_op jit(solution)/shard_map/weight_grad/pallas_call | solution.py:526
  457.0 12.7 %collective-permute-done.28.refs_2_ = bf16[320,2048]{1,0:T(8,128)(2,1)S(1)} collective-permute-done((bf16[320,2048]{1,0:T(8,128)(2,1)}, bf16[320,2048]{1,0:T(8,128)(2,1)S(1)}, u32[]{:S(2)}, u32[]{:S(2)}) %collective-permute-start.28) | collective-permute-done | bytes 1310752 | tf_op jit(solution)/shard_map/ppermute | solution.py:602
  472.7 12.3 %out_parts.3 = (bf16[160,2048]{1,0:T(8,128)(2,1)}, bf16[160,2048]{1,0:T(8,128)(2,1)}, bf16[320,2048]{1,0:T(8,128)(2,1)}, bf16[320,2048]{1,0:T(8,128)(2,1)}, bf16[320,2048]{1,0:T(8,128)(2,1)}) custom-call(bf16[1280,1536]{1,0:T(8,128)(2,1)} %get-tuple-element.196.left_ref.values_ref, bf16[1,1536,2048]{2,1,0:T(8,128)(2,1)} %bitcast.126), custom_call_target="tpu_custom_call" | custom-call | flops 8053063680 | bytes 15466496 | tf_op jit(solution)/shard_map/out_parts/pallas_call | solution.py:466
  485.1 5.1 add_pieces.6
  495.3 2.6 fusion.17
  498.0 4.0 all-to-all-start.4
  502.0 10.9 %mixed_grad.1 = (f32[1280,640]{1,0:T(8,128)}, bf16[1280,2048]{1,0:T(8,128)(2,1)}) custom-call(bf16[160,2048]{1,0:T(8,128)(2,1)} %collective-permute-done.29.refs_0_, bf16[160,2048]{1,0:T(8,128)(2,1)} %collective-permute-done.31.refs_1_, bf16[320,2048]{1,0:T(8,128)(2,1)} %copy-done.22, bf16[320,2048]{1,0:T(8,128)(2,1)} %copy-done.23, ...), custom_call_target="tpu_custom_call" | custom-call | flops 3355443200 | bytes 16384000 | tf_op jit(solution)/shard_map/mixed_grad/pallas_call | solution.py:322
  512.9 3.0 collective-permute-done.37
  522.4 20.8 %lru_backward.1 = (f32[1280,640]{1,0:T(8,128)}, bf16[1280,640]{1,0:T(8,128)(2,1)S(1)}, bf16[1280,640]{1,0:T(8,128)(2,1)S(1)}, bf16[1280,640]{1,0:T(8,128)(2,1)S(1)}, f32[24,640]{1,0:T(8,128)S(1)}) custom-call(bf16[1280,640]{1,0:T(8,128)(2,1)} %copy-done, f32[1280,640]{1,0:T(8,128)} %convolution_add_fusion.1.rate_ref, ...), custom_call_target="tpu_custom_call" | custom-call | flops 16384000000 | bytes 16384000 | tf_op jit(solution)/shard_map/lru_backward/pallas_call | solution.py:217
  547.5 12.3 %conv_back.1 = (bf16[1280,640]{1,0:T(8,128)(2,1)}, f32[5,640]{1,0:T(8,128)}) custom-call(f32[1280,640]{1,0:T(8,128)} %get-tuple-element.225.d_conv_ref, bf16[1280,640]{1,0:T(8,128)(2,1)} %copy-done.6, bf16[1280,640]{1,0:T(8,128)(2,1)} %copy-done.4, bf16[640,640]{1,0:T(8,128)(2,1)} %get-tuple-element.390.rate_ref, ...), custom_call_target="tpu_custom_call" | custom-call | flops 4194304000 | bytes 13107200 | tf_op jit(solution)/shard_map/conv_back/pallas_call | solution.py:442
  559.9 14.4 %back_parts.3 = (bf16[160,2048]{1,0:T(8,128)(2,1)}, bf16[160,2048]{1,0:T(8,128)(2,1)}, bf16[320,2048]{1,0:T(8,128)(2,1)}, bf16[320,2048]{1,0:T(8,128)(2,1)}, bf1...) custom-call(bf16[1280,640]{1,0:T(8,128)(2,1)} %copy-done.8, bf16[1280,640]{1,0:T(8,128)(2,1)} %get-tuple-element.235.refs_1_, ...), custom_call_target="tpu_custom_call" | custom-call | flops 6710886400 | bytes 13762560 | tf_op jit(solution)/shard_map/back_parts/pallas_call | solution.py:394
  581.1 13.5 %weight_grad.7 = (bf16[4,4,64,1280]{3,2,1,0:T(8,128)(2,1)}, bf16[1,4,64,1280]{3,2,1,0:T(8,128)(2,1)}, bf16[1,4,64,1280]{3,2,1,0:T(8,128)(2,1)}, bf16[1,4,64,1280]{3,2,1,0:T(8,128)(2,1)}, bf16[1,4,64,1280]{3,2,1,0:T(8,128)(2,1)}) custom-call(s32[1]{0:T(128)} %bitcast.24.me_ref, bf16[1280,2048]{1,0:T(8,128)(2,1)} %copy-done.19, bf16[1280,640]{1,0:T(8,128)(2,1)} %copy-done.8, ...), custom_call_target="tpu_custom_call" | custom-call | flops 6710886400 | bytes 17039360 | tf_op jit(solution)/shard_map/weight_grad/pallas_call | solution.py:526
  596.7 4.2 all-to-all-start.5
  603.1 4.6 add_pieces.7
  607.8 2.6 pad_maximum_fusion.9
  610.5 2.5 pad_maximum_fusion.8
  622.0 6.1 convolution_convert_fusion
  631.1 18.5 %collective-permute-done.46 = bf16[320,2048]{1,0:T(8,128)(2,1)} collective-permute-done((bf16[320,2048]{1,0:T(8,128)(2,1)}, bf16[320,2048]{1,0:T(8,128)(2,1)}, u32[]{:S(2)}, u32[]{:S(2)}) %collective-permute-start.46) | collective-permute-done | bytes 1310752 | tf_op jit(solution)/shard_map/ppermute | solution.py:602
  651.0 4.4 convert_add_fusion.2
  655.4 2.9 fusion.8
  660.5 2.5 convert_element_type.287
  667.7 4.3 all-to-all-start.6
  672.0 2.9 fusion.9
  674.9 4.4 all-to-all-done.6
  679.3 3.5 all-to-all-start.7
  682.8 6.7 fusion.12
  694.2 3.7 reduce-scatter.14.cloned.1.call-done
  (382 shorter events, 146.9 us)
Async XLA Ops:
  7.2 84.4 %all-gather.4.cloned.1.call-start = ((), (), s32[]{:S(2)}) async-start(), calls=%async_computation.13 | async-start | bytes 5898240 | tf_op jit(solution)/shard_map/all_gather | solution.py:633
  24.9 29.0 %collective-permute-start = (bf16[320,2048]{1,0:T(8,128)(2,1)S(1)}, bf16[320,2048]{1,0:T(8,128)(2,1)S(1)}, u32[]{:S(2)}, u32[]{:S(2)}) collective-permute-start(bf16[320,2048]{1,0:T(8,128)(2,1)S(1)} %copy-done.12), channel_id=1, source_target_pairs={{0,8},{8,0},{16,24},{24,16},{1,9},{9,1},{17,25},{25,17},{2,10},{10... | collective-permute-start | bytes 3932168 | tf_op jit(solution)/shard_map/ppermute | solution.py:602
  25.9 32.6 %collective-permute-start.2 = (bf16[320,2048]{1,0:T(8,128)(2,1)S(1)}, bf16[320,2048]{1,0:T(8,128)(2,1)}, u32[]{:S(2)}, u32[]{:S(2)}) collective-permute-start(bf16[320,2048]{1,0:T(8,128)(2,1)S(1)} %copy-done.12), channel_id=1, source_target_pairs={{0,16},{8,24},{16,0},{24,8},{1,17},{9,25},{17,1},{25,9},{2,18},{10... | collective-permute-start | bytes 3932168 | tf_op jit(solution)/shard_map/ppermute | solution.py:602
  28.1 39.4 %all-to-all-start.1 = ((bf16[8,80,384]{2,1,0:T(8,128)(2,1)}), bf16[8,80,384]{2,1,0:T(8,128)(2,1)S(1)}, u32[]{:S(2)}, u32[]{:S(2)}) async-start(bf16[8,80,384]{2,1,0:T(8,128)(2,1)} %broadcast_in_dim.22), calls=%async_computation.1 | async-start | bytes 983040 | tf_op jit(solution)/shard_map/all_to_all | solution.py:671
  54.9 18.6 %collective-permute-start.1 = (bf16[160,2048]{1,0:T(8,128)(2,1)}, bf16[160,2048]{1,0:T(8,128)(2,1)}, u32[]{:S(2)}, u32[]{:S(2)}) collective-permute-start(bf16[160,2048]{1,0:T(8,128)(2,1)} %slice.240), channel_id=1, source_target_pairs={{0,16},{8,24},{16,0},{24,8},{1,17},{9,25},{17,1},{25,9},{2,18},{10... | collective-permute-start | bytes 1966088 | tf_op jit(solution)/shard_map/ppermute | solution.py:602
  60.5 15.1 %collective-permute-start.3 = (bf16[160,2048]{1,0:T(8,128)(2,1)}, bf16[160,2048]{1,0:T(8,128)(2,1)}, u32[]{:S(2)}, u32[]{:S(2)}) collective-permute-start(bf16[160,2048]{1,0:T(8,128)(2,1)} %slice.241), channel_id=1, source_target_pairs={{0,8},{8,0},{16,24},{24,16},{1,9},{9,1},{17,25},{25,17},{2,10},{10... | collective-permute-start | bytes 1966088 | tf_op jit(solution)/shard_map/ppermute | solution.py:602
  68.2 14.4 %all-to-all-start.2 = ((bf16[32,2,64]{2,1,0:T(2,128)(2,1)}), bf16[32,2,64]{2,1,0:T(2,128)(2,1)S(1)}, u32[]{:S(2)}, u32[]{:S(2)}) async-start(bf16[32,2,64]{2,1,0:T(2,128)(2,1)} %broadcast_in_dim.23), calls=%async_computation.2 | async-start | bytes 32768 | tf_op jit(solution)/shard_map/all_to_all | solution.py:671
  73.3 105.4 %all-gather.6.cloned.1.call-start = ((), (), s32[]{:S(2)}) async-start(), calls=%async_computation.14 | async-start | bytes 10027008 | tf_op jit(solution)/shard_map/all_gather | solution.py:740
  93.6 33.8 %collective-permute-start.4 = (bf16[320,2048]{1,0:T(8,128)(2,1)}, bf16[320,2048]{1,0:T(8,128)(2,1)}, u32[]{:S(2)}, u32[]{:S(2)}) collective-permute-start(bf16[320,2048]{1,0:T(8,128)(2,1)} %multiply_convert_fusion.2), channel_id=1, source_target_pairs={{0,8},{8,0},{16,24},{24,16},{1,9},{9,1},{17,25},{25,17},{2,10},{10... | collective-permute-start | bytes 3932168 | tf_op jit(solution)/shard_map/ppermute | solution.py:602
  95.1 34.6 %collective-permute-start.6 = (bf16[320,2048]{1,0:T(8,128)(2,1)}, bf16[320,2048]{1,0:T(8,128)(2,1)}, u32[]{:S(2)}, u32[]{:S(2)}) collective-permute-start(bf16[320,2048]{1,0:T(8,128)(2,1)} %multiply_convert_fusion.2), channel_id=1, source_target_pairs={{0,16},{8,24},{16,0},{24,8},{1,17},{9,25},{17,1},{25,9},{2,18},{10... | collective-permute-start | bytes 3932168 | tf_op jit(solution)/shard_map/ppermute | solution.py:602
  129.0 16.3 %collective-permute-start.5 = (bf16[160,2048]{1,0:T(8,128)(2,1)S(1)}, bf16[160,2048]{1,0:T(8,128)(2,1)}, u32[]{:S(2)}, u32[]{:S(2)}) collective-permute-start(bf16[160,2048]{1,0:T(8,128)(2,1)S(1)} %slice.256), channel_id=1, source_target_pairs={{0,16},{8,24},{16,0},{24,8},{1,17},{9,25},{17,1},{25,9},{2,18},{10... | collective-permute-start | bytes 1966088 | tf_op jit(solution)/shard_map/ppermute | solution.py:602
  130.8 16.4 %collective-permute-start.7 = (bf16[160,2048]{1,0:T(8,128)(2,1)S(1)}, bf16[160,2048]{1,0:T(8,128)(2,1)}, u32[]{:S(2)}, u32[]{:S(2)}) collective-permute-start(bf16[160,2048]{1,0:T(8,128)(2,1)S(1)} %slice.257), channel_id=1, source_target_pairs={{0,8},{8,0},{16,24},{24,16},{1,9},{9,1},{17,25},{25,17},{2,10},{10... | collective-permute-start | bytes 1966088 | tf_op jit(solution)/shard_map/ppermute | solution.py:602
  148.8 21.9 %all-to-all-start.3 = ((bf16[4,64,3072]{2,1,0:T(8,128)(2,1)}), bf16[4,64,3072]{2,1,0:T(8,128)(2,1)S(1)}, u32[]{:S(2)}, u32[]{:S(2)}) async-start(bf16[4,64,3072]{2,1,0:T(8,128)(2,1)} %copy.101), calls=%async_computation.3 | async-start | bytes 3145728 | tf_op jit(solution)/shard_map/all_to_all | solution.py:630
  152.4 143.7 %all-gather.8.cloned.1.call-start = ((), (), s32[]{:S(2)}) async-start(), calls=%async_computation.15 | async-start | bytes 14155776 | tf_op jit(solution)/shard_map/all_gather | solution.py:633
  178.7 255.8 %reduce-scatter.6.cloned.1.call-start = ((), (), s32[]{:S(2)}) async-start(), calls=%async_computation.16 | async-start | bytes 3932160 | tf_op jit(solution)/shard_map/reduce_scatter | solution.py:656
  186.1 17.1 %collective-permute-start.8 = (bf16[160,2048]{1,0:T(8,128)(2,1)}, bf16[160,2048]{1,0:T(8,128)(2,1)S(1)}, u32[]{:S(2)}, u32[]{:S(2)}) collective-permute-start(bf16[160,2048]{1,0:T(8,128)(2,1)} %get-tuple-element.160), channel_id=1, source_target_pairs={{0,8},{8,0},{16,24},{24,16},{1,9},{9,1},{17,25},{25,17},{2,10},{10... | collective-permute-start | bytes 1966088 | tf_op jit(solution)/shard_map/ppermute | solution.py:602
  187.7 16.8 %collective-permute-start.9 = (bf16[160,2048]{1,0:T(8,128)(2,1)}, bf16[160,2048]{1,0:T(8,128)(2,1)S(1)}, u32[]{:S(2)}, u32[]{:S(2)}) collective-permute-start(bf16[160,2048]{1,0:T(8,128)(2,1)} %get-tuple-element.161), channel_id=1, source_target_pairs={{0,16},{8,24},{16,0},{24,8},{1,17},{9,25},{17,1},{25,9},{2,18},{10... | collective-permute-start | bytes 1966088 | tf_op jit(solution)/shard_map/ppermute | solution.py:602
  204.8 30.1 %collective-permute-start.10 = (bf16[320,2048]{1,0:T(8,128)(2,1)S(1)}, bf16[320,2048]{1,0:T(8,128)(2,1)}, u32[]{:S(2)}, u32[]{:S(2)}) collective-permute-start(bf16[320,2048]{1,0:T(8,128)(2,1)S(1)} %pad_maximum_fusion.2), channel_id=1, source_target_pairs={{0,8},{8,0},{16,24},{24,16},{1,9},{9,1},{17,25},{25,17},{2,10},{10... | collective-permute-start | bytes 3932168 | tf_op jit(solution)/shard_map/ppermute | solution.py:602
  205.7 29.9 %collective-permute-start.11 = (bf16[320,2048]{1,0:T(8,128)(2,1)S(1)}, bf16[320,2048]{1,0:T(8,128)(2,1)}, u32[]{:S(2)}, u32[]{:S(2)}) collective-permute-start(bf16[320,2048]{1,0:T(8,128)(2,1)S(1)} %pad_maximum_fusion.3), channel_id=1, source_target_pairs={{0,16},{8,24},{16,0},{24,8},{1,17},{9,25},{17,1},{25,9},{2,18},{10... | collective-permute-start | bytes 3932168 | tf_op jit(solution)/shard_map/ppermute | solution.py:602
  240.6 29.0 %collective-permute-start.12 = (bf16[320,2048]{1,0:T(8,128)(2,1)}, bf16[320,2048]{1,0:T(8,128)(2,1)}, u32[]{:S(2)}, u32[]{:S(2)}) collective-permute-start(bf16[320,2048]{1,0:T(8,128)(2,1)} %multiply_convert_fusion.1.refs_4_), channel_id=1, source_target_pairs={{0,8},{8,0},{16,24},{24,16},{1,9},{9,1},{17,25},{25,17},{2,10},{10... | collective-permute-start | bytes 3932168 | tf_op jit(solution)/shard_map/ppermute | solution.py:602
  242.0 30.2 %collective-permute-start.14 = (bf16[320,2048]{1,0:T(8,128)(2,1)}, bf16[320,2048]{1,0:T(8,128)(2,1)}, u32[]{:S(2)}, u32[]{:S(2)}) collective-permute-start(bf16[320,2048]{1,0:T(8,128)(2,1)} %multiply_convert_fusion.1.refs_4_), channel_id=1, source_target_pairs={{0,16},{8,24},{16,0},{24,8},{1,17},{9,25},{17,1},{25,9},{2,18},{10... | collective-permute-start | bytes 3932168 | tf_op jit(solution)/shard_map/ppermute | solution.py:602
  270.7 16.7 %collective-permute-start.13 = (bf16[160,2048]{1,0:T(8,128)(2,1)S(1)}, bf16[160,2048]{1,0:T(8,128)(2,1)S(1)}, u32[]{:S(2)}, u32[]{:S(2)}) collective-permute-start(bf16[160,2048]{1,0:T(8,128)(2,1)S(1)} %slice.259), channel_id=1, source_target_pairs={{0,16},{8,24},{16,0},{24,8},{1,17},{9,25},{17,1},{25,9},{2,18},{10... | collective-permute-start | bytes 1966088 | tf_op jit(solution)/shard_map/ppermute | solution.py:602
  273.4 14.1 %collective-permute-start.15 = (bf16[160,2048]{1,0:T(8,128)(2,1)S(1)}, bf16[160,2048]{1,0:T(8,128)(2,1)}, u32[]{:S(2)}, u32[]{:S(2)}) collective-permute-start(bf16[160,2048]{1,0:T(8,128)(2,1)S(1)} %slice.260), channel_id=1, source_target_pairs={{0,8},{8,0},{16,24},{24,16},{1,9},{9,1},{17,25},{25,17},{2,10},{10... | collective-permute-start | bytes 1966088 | tf_op jit(solution)/shard_map/ppermute | solution.py:602
  345.6 2.5 collective-permute-start.24
  345.8 3.4 collective-permute-start.25
  346.1 4.2 collective-permute-start.26
  346.3 5.1 collective-permute-start.27
  357.6 134.8 %reduce-scatter.8.cloned.1.call-start = ((), (), s32[]{:S(2)}) async-start(), calls=%async_computation.17 | async-start | bytes 3932160 | tf_op jit(solution)/shard_map/reduce_scatter | solution.py:656
  380.1 18.3 %collective-permute-start.16 = (bf16[160,2048]{1,0:T(8,128)(2,1)}, bf16[160,2048]{1,0:T(8,128)(2,1)S(1)}, u32[]{:S(2)}, u32[]{:S(2)}) collective-permute-start(bf16[160,2048]{1,0:T(8,128)(2,1)} %get-tuple-element.179), channel_id=1, source_target_pairs={{0,8},{8,0},{16,24},{24,16},{1,9},{9,1},{17,25},{25,17},{2,10},{10... | collective-permute-start | bytes 1966088 | tf_op jit(solution)/shard_map/ppermute | solution.py:602
  381.5 16.9 %collective-permute-start.17 = (bf16[160,2048]{1,0:T(8,128)(2,1)}, bf16[160,2048]{1,0:T(8,128)(2,1)S(1)}, u32[]{:S(2)}, u32[]{:S(2)}) collective-permute-start(bf16[160,2048]{1,0:T(8,128)(2,1)} %get-tuple-element.180), channel_id=1, source_target_pairs={{0,16},{8,24},{16,0},{24,8},{1,17},{9,25},{17,1},{25,9},{2,18},{10... | collective-permute-start | bytes 1966088 | tf_op jit(solution)/shard_map/ppermute | solution.py:602
  398.2 3.4 collective-permute-start.20
  398.7 31.4 %collective-permute-start.18 = (bf16[320,2048]{1,0:T(8,128)(2,1)S(1)}, bf16[320,2048]{1,0:T(8,128)(2,1)}, u32[]{:S(2)}, u32[]{:S(2)}) collective-permute-start(bf16[320,2048]{1,0:T(8,128)(2,1)S(1)} %pad_maximum_fusion.4), channel_id=1, source_target_pairs={{0,8},{8,0},{16,24},{24,16},{1,9},{9,1},{17,25},{25,17},{2,10},{10... | collective-permute-start | bytes 3932168 | tf_op jit(solution)/shard_map/ppermute | solution.py:602
  399.6 31.1 %collective-permute-start.19 = (bf16[320,2048]{1,0:T(8,128)(2,1)S(1)}, bf16[320,2048]{1,0:T(8,128)(2,1)}, u32[]{:S(2)}, u32[]{:S(2)}) collective-permute-start(bf16[320,2048]{1,0:T(8,128)(2,1)S(1)} %pad_maximum_fusion.5), channel_id=1, source_target_pairs={{0,16},{8,24},{16,0},{24,8},{1,17},{9,25},{17,1},{25,9},{2,18},{10... | collective-permute-start | bytes 3932168 | tf_op jit(solution)/shard_map/ppermute | solution.py:602
  401.1 2.3 collective-permute-start.21
  401.1 3.4 collective-permute-start.22
  401.6 4.0 collective-permute-start.23
  434.6 162.2 %reduce-scatter.12.cloned.1.call-start = ((), (), s32[]{:S(2)}) async-start(), calls=%async_computation.19 | async-start | bytes 3932160 | tf_op jit(solution)/shard_map/reduce_scatter | solution.py:656
  439.4 30.3 %collective-permute-start.28 = (bf16[320,2048]{1,0:T(8,128)(2,1)}, bf16[320,2048]{1,0:T(8,128)(2,1)S(1)}, u32[]{:S(2)}, u32[]{:S(2)}) collective-permute-start(bf16[320,2048]{1,0:T(8,128)(2,1)} %fusion.29.refs_4_), channel_id=1, source_target_pairs={{0,8},{8,0},{16,24},{24,16},{1,9},{9,1},{17,25},{25,17},{2,10},{10... | collective-permute-start | bytes 3932168 | tf_op jit(solution)/shard_map/ppermute | solution.py:602
  440.9 30.1 %collective-permute-start.30 = (bf16[320,2048]{1,0:T(8,128)(2,1)}, bf16[320,2048]{1,0:T(8,128)(2,1)S(1)}, u32[]{:S(2)}, u32[]{:S(2)}) collective-permute-start(bf16[320,2048]{1,0:T(8,128)(2,1)} %fusion.29.refs_4_), channel_id=1, source_target_pairs={{0,16},{8,24},{16,0},{24,8},{1,17},{9,25},{17,1},{25,9},{2,18},{10... | collective-permute-start | bytes 3932168 | tf_op jit(solution)/shard_map/ppermute | solution.py:602
  456.4 14.9 %collective-permute-start.32 = (bf16[1,4,64,1536]{3,2,1,0:T(8,128)(2,1)}, bf16[1,4,64,1536]{3,2,1,0:T(8,128)(2,1)S(1)}, u32[]{:S(2)}, u32[]{:S(2)}) collective-permute-start(bf16[1,4,64,1536]{3,2,1,0:T(8,128)(2,1)} %get-tuple-element.205), channel_id=1, source_target_pairs={{0,4},{4,0},{1,5},{5,1},{2,6},{6,2},{3,7},{7,3},{8,12},{12,8},{9,1... | collective-permute-start | bytes 2359304 | tf_op jit(solution)/shard_map/ppermute | solution.py:643
  456.4 28.7 %collective-permute-start.33 = (bf16[1,4,64,1536]{3,2,1,0:T(8,128)(2,1)}, bf16[1,4,64,1536]{3,2,1,0:T(8,128)(2,1)}, u32[]{:S(2)}, u32[]{:S(2)}) collective-permute-start(bf16[1,4,64,1536]{3,2,1,0:T(8,128)(2,1)} %get-tuple-element.206), channel_id=1, source_target_pairs={{0,4},{4,0},{1,5},{5,1},{2,6},{6,2},{3,7},{7,3},{8,12},{12,8},{9,1... | collective-permute-start | bytes 2359304 | tf_op jit(solution)/shard_map/ppermute | solution.py:643
  456.9 28.2 %collective-permute-start.34 = (bf16[1,4,64,1536]{3,2,1,0:T(8,128)(2,1)}, bf16[1,4,64,1536]{3,2,1,0:T(8,128)(2,1)}, u32[]{:S(2)}, u32[]{:S(2)}) collective-permute-start(bf16[1,4,64,1536]{3,2,1,0:T(8,128)(2,1)} %get-tuple-element.207), channel_id=1, source_target_pairs={{0,4},{4,0},{1,5},{5,1},{2,6},{6,2},{3,7},{7,3},{8,12},{12,8},{9,1... | collective-permute-start | bytes 2359304 | tf_op jit(solution)/shard_map/ppermute | solution.py:643
  469.7 15.4 %collective-permute-start.35 = (bf16[1,4,64,1536]{3,2,1,0:T(8,128)(2,1)}, bf16[1,4,64,1536]{3,2,1,0:T(8,128)(2,1)}, u32[]{:S(2)}, u32[]{:S(2)}) collective-permute-start(bf16[1,4,64,1536]{3,2,1,0:T(8,128)(2,1)} %get-tuple-element.208), channel_id=1, source_target_pairs={{0,4},{4,0},{1,5},{5,1},{2,6},{6,2},{3,7},{7,3},{8,12},{12,8},{9,1... | collective-permute-start | bytes 2359304 | tf_op jit(solution)/shard_map/ppermute | solution.py:643
  471.0 19.2 %collective-permute-start.29 = (bf16[160,2048]{1,0:T(8,128)(2,1)S(1)}, bf16[160,2048]{1,0:T(8,128)(2,1)}, u32[]{:S(2)}, u32[]{:S(2)}) collective-permute-start(bf16[160,2048]{1,0:T(8,128)(2,1)S(1)} %slice.261), channel_id=1, source_target_pairs={{0,16},{8,24},{16,0},{24,8},{1,17},{9,25},{17,1},{25,9},{2,18},{10... | collective-permute-start | bytes 1966088 | tf_op jit(solution)/shard_map/ppermute | solution.py:602
  471.3 18.9 %collective-permute-start.31 = (bf16[160,2048]{1,0:T(8,128)(2,1)S(1)}, bf16[160,2048]{1,0:T(8,128)(2,1)}, u32[]{:S(2)}, u32[]{:S(2)}) collective-permute-start(bf16[160,2048]{1,0:T(8,128)(2,1)S(1)} %slice.262), channel_id=1, source_target_pairs={{0,8},{8,0},{16,24},{24,16},{1,9},{9,1},{17,25},{25,17},{2,10},{10... | collective-permute-start | bytes 1966088 | tf_op jit(solution)/shard_map/ppermute | solution.py:602
  492.3 20.6 %collective-permute-start.36 = (bf16[160,2048]{1,0:T(8,128)(2,1)}, bf16[160,2048]{1,0:T(8,128)(2,1)}, u32[]{:S(2)}, u32[]{:S(2)}) collective-permute-start(bf16[160,2048]{1,0:T(8,128)(2,1)} %get-tuple-element.216), channel_id=1, source_target_pairs={{0,8},{8,0},{16,24},{24,16},{1,9},{9,1},{17,25},{25,17},{2,10},{10... | collective-permute-start | bytes 1966088 | tf_op jit(solution)/shard_map/ppermute | solution.py:602
  493.8 22.2 %collective-permute-start.37 = (bf16[160,2048]{1,0:T(8,128)(2,1)}, bf16[160,2048]{1,0:T(8,128)(2,1)}, u32[]{:S(2)}, u32[]{:S(2)}) collective-permute-start(bf16[160,2048]{1,0:T(8,128)(2,1)} %get-tuple-element.217), channel_id=1, source_target_pairs={{0,16},{8,24},{16,0},{24,8},{1,17},{9,25},{17,1},{25,9},{2,18},{10... | collective-permute-start | bytes 1966088 | tf_op jit(solution)/shard_map/ppermute | solution.py:602
  498.0 61.8 %all-to-all-start.4 = ((bf16[4,64,1,1536]{3,1,2,0:T(8,128)(2,1)}), bf16[4,64,1,1536]{3,1,2,0:T(8,128)(2,1)S(1)}, u32[]{:S(2)}, u32[]{:S(2)}) async-start(bf16[4,64,1,1536]{3,1,2,0:T(8,128)(2,1)} %bitcast.152), calls=%async_computation.6 | async-start | bytes 1572864 | tf_op jit(solution)/shard_map/all_to_all | solution.py:659
  520.9 38.9 %collective-permute-start.38 = (bf16[320,2048]{1,0:T(8,128)(2,1)}, bf16[320,2048]{1,0:T(8,128)(2,1)S(1)}, u32[]{:S(2)}, u32[]{:S(2)}) collective-permute-start(bf16[320,2048]{1,0:T(8,128)(2,1)} %pad_maximum_fusion.6), channel_id=1, source_target_pairs={{0,8},{8,0},{16,24},{24,16},{1,9},{9,1},{17,25},{25,17},{2,10},{10... | collective-permute-start | bytes 3932168 | tf_op jit(solution)/shard_map/ppermute | solution.py:602
  520.9 39.0 %collective-permute-start.39 = (bf16[320,2048]{1,0:T(8,128)(2,1)}, bf16[320,2048]{1,0:T(8,128)(2,1)S(1)}, u32[]{:S(2)}, u32[]{:S(2)}) collective-permute-start(bf16[320,2048]{1,0:T(8,128)(2,1)} %pad_maximum_fusion.7), channel_id=1, source_target_pairs={{0,16},{8,24},{16,0},{24,8},{1,17},{9,25},{17,1},{25,9},{2,18},{10... | collective-permute-start | bytes 3932168 | tf_op jit(solution)/shard_map/ppermute | solution.py:602
  574.4 20.9 %collective-permute-start.44 = (bf16[160,2048]{1,0:T(8,128)(2,1)}, bf16[160,2048]{1,0:T(8,128)(2,1)S(1)}, u32[]{:S(2)}, u32[]{:S(2)}) collective-permute-start(bf16[160,2048]{1,0:T(8,128)(2,1)} %get-tuple-element.249), channel_id=1, source_target_pairs={{0,8},{8,0},{16,24},{24,16},{1,9},{9,1},{17,25},{25,17},{2,10},{10... | collective-permute-start | bytes 1966088 | tf_op jit(solution)/shard_map/ppermute | solution.py:602
  576.4 19.2 %collective-permute-start.45 = (bf16[160,2048]{1,0:T(8,128)(2,1)}, bf16[160,2048]{1,0:T(8,128)(2,1)S(1)}, u32[]{:S(2)}, u32[]{:S(2)}) collective-permute-start(bf16[160,2048]{1,0:T(8,128)(2,1)} %get-tuple-element.250), channel_id=1, source_target_pairs={{0,16},{8,24},{16,0},{24,8},{1,17},{9,25},{17,1},{25,9},{2,18},{10... | collective-permute-start | bytes 1966088 | tf_op jit(solution)/shard_map/ppermute | solution.py:602
  594.6 7.4 %collective-permute-start.40 = (bf16[1,4,64,1280]{3,2,1,0:T(8,128)(2,1)}, bf16[1,4,64,1280]{3,2,1,0:T(8,128)(2,1)S(1)}, u32[]{:S(2)}, u32[]{:S(2)}) collective-permute-start(bf16[1,4,64,1280]{3,2,1,0:T(8,128)(2,1)} %get-tuple-element.243), channel_id=1, source_target_pairs={{0,4},{4,0},{1,5},{5,1},{2,6},{6,2},{3,7},{7,3},{8,12},{12,8},{9,1... | collective-permute-start | bytes 1966088 | tf_op jit(solution)/shard_map/ppermute | solution.py:643
  594.7 7.4 %collective-permute-start.41 = (bf16[1,4,64,1280]{3,2,1,0:T(8,128)(2,1)}, bf16[1,4,64,1280]{3,2,1,0:T(8,128)(2,1)S(1)}, u32[]{:S(2)}, u32[]{:S(2)}) collective-permute-start(bf16[1,4,64,1280]{3,2,1,0:T(8,128)(2,1)} %get-tuple-element.244), channel_id=1, source_target_pairs={{0,4},{4,0},{1,5},{5,1},{2,6},{6,2},{3,7},{7,3},{8,12},{12,8},{9,1... | collective-permute-start | bytes 1966088 | tf_op jit(solution)/shard_map/ppermute | solution.py:643
  595.2 6.9 collective-permute-start.42
  595.2 6.8 collective-permute-start.43
  596.7 16.2 %all-to-all-start.5 = ((bf16[4,64,1,1536]{3,1,2,0:T(8,128)(2,1)}), bf16[4,64,1,1536]{3,1,2,0:T(8,128)(2,1)}, u32[]{:S(2)}, u32[]{:S(2)}) async-start(bf16[4,64,1,1536]{3,1,2,0:T(8,128)(2,1)} %bitcast.151), calls=%async_computation.9 | async-start | bytes 1572864 | tf_op jit(solution)/shard_map/all_to_all | solution.py:659
  600.9 59.5 %reduce-scatter.10.cloned.1.call-start = ((), (), s32[]{:S(2)}) async-start(), calls=%async_computation.18 | async-start | bytes 3276800 | tf_op jit(solution)/shard_map/reduce_scatter | solution.py:656
  607.8 90.2 %reduce-scatter.14.cloned.1.call-start = ((), (), s32[]{:S(2)}) async-start(), calls=%async_computation.20 | async-start | bytes 1945600 | tf_op jit(solution)/shard_map/reduce_scatter | solution.py:656
  618.6 31.1 %collective-permute-start.46 = (bf16[320,2048]{1,0:T(8,128)(2,1)}, bf16[320,2048]{1,0:T(8,128)(2,1)}, u32[]{:S(2)}, u32[]{:S(2)}) collective-permute-start(bf16[320,2048]{1,0:T(8,128)(2,1)} %pad_maximum_fusion.8), channel_id=1, source_target_pairs={{0,8},{8,0},{16,24},{24,16},{1,9},{9,1},{17,25},{25,17},{2,10},{10... | collective-permute-start | bytes 3932168 | tf_op jit(solution)/shard_map/ppermute | solution.py:602
  620.6 30.5 %collective-permute-start.47 = (bf16[320,2048]{1,0:T(8,128)(2,1)}, bf16[320,2048]{1,0:T(8,128)(2,1)}, u32[]{:S(2)}, u32[]{:S(2)}) collective-permute-start(bf16[320,2048]{1,0:T(8,128)(2,1)} %pad_maximum_fusion.9), channel_id=1, source_target_pairs={{0,16},{8,24},{16,0},{24,8},{1,17},{9,25},{17,1},{25,9},{2,18},{10... | collective-permute-start | bytes 3932168 | tf_op jit(solution)/shard_map/ppermute | solution.py:602
  629.7 25.7 %collective-permute-start.48 = (bf16[4,80,2432]{2,1,0:T(8,128)(2,1)}, bf16[4,80,2432]{2,1,0:T(8,128)(2,1)}, u32[]{:S(2)}, u32[]{:S(2)}) collective-permute-start(bf16[4,80,2432]{2,1,0:T(8,128)(2,1)} %dynamic-slice_bitcast_fusion), channel_id=1, source_target_pairs={{0,4},{4,0},{1,5},{5,1},{2,6},{6,2},{3,7},{7,3},{8,12},{12,8},{9,1... | collective-permute-start | bytes 4669448 | tf_op jit(solution)/shard_map/ppermute | solution.py:652
  667.7 11.6 %all-to-all-start.6 = ((f32[32,1,128]{2,1,0:T(1,128)}), f32[32,1,128]{2,1,0:T(1,128)S(1)}, u32[]{:S(2)}, u32[]{:S(2)}) async-start(f32[32,1,128]{2,1,0:T(1,128)} %reshape.270), calls=%async_computation.10 | async-start | bytes 32768 | tf_op jit(solution)/shard_map/all_to_all | solution.py:854
  679.3 13.0 %all-to-all-start.7 = ((bf16[4,64,1,1280]{3,1,2,0:T(8,128)(2,1)}), bf16[4,64,1,1280]{3,1,2,0:T(8,128)(2,1)S(1)}, u32[]{:S(2)}, u32[]{:S(2)}) async-start(bf16[4,64,1,1280]{3,1,2,0:T(8,128)(2,1)} %bitcast.153), calls=%async_computation.11 | async-start | bytes 1310720 | tf_op jit(solution)/shard_map/all_to_all | solution.py:659
  (77 other events, 932.2 us)
Sparse Core Ops, SparseCore 0:
  25.0 66.4 all-gather.3
  93.7 84.9 all-gather.5
  180.9 115.2 all-gather.7
  357.7 58.4 reduce-scatter.5
  434.7 57.6 reduce-scatter.7
  495.4 59.3 reduce-scatter.11
  607.9 52.5 reduce-scatter.9
  662.8 35.1 reduce-scatter.13
